TPU v7x, 32 devices: a whole 2x2x4 slice. The times are simulated.
32 devices in a mesh: seq: 8 (over y, x, core), fsdp: 4 (over z).
Axes of the slice: x: 2, y: 2, z: 4, core: 2. Of those that a mesh axis runs over, the one named last changes fastest.
Arguments:
- tokens: bfloat16 [4, 1024, 1536], P('fsdp', 'seq'), may hold values from -6 to 6
- cotangent: bfloat16 [4, 1024, 1536], P('fsdp', 'seq'), may hold values from -6 to 6
- doc_starts: int32 [4, 8], P('fsdp'), may hold values from 0 to 1023, as said below
- mix_gain: float32 [1536], replicated, may hold values from 0.5 to 1.5
- input_proj: bfloat16 [1536, 2048], P('fsdp'), may hold values from -0.15625 to 0.15625
- gelu_proj: bfloat16 [1536, 2048], P('fsdp'), may hold values from -0.15625 to 0.15625
- conv_taps: float32 [4, 2048], replicated, may hold values from -3 to 3
- conv_bias: float32 [2048], replicated, may hold values from -3 to 3
- decay_gate: bfloat16 [2048, 256], P('fsdp'), may hold values from -0.375 to 0.375
- decay_bias: float32 [2048], replicated, may hold values from -4 to 4
- input_gate: bfloat16 [2048, 256], P('fsdp'), may hold values from -0.375 to 0.375
- input_bias: float32 [2048], replicated, may hold values from -4 to 4
- decay_param: float32 [2048], replicated, may hold values from 4 to 11
- output_proj: bfloat16 [2048, 1536], P('fsdp'), may hold values from -0.375 to 0.375
- mlp_gain: float32 [1536], replicated, may hold values from 0.5 to 1.5
- mlp_gate: bfloat16 [1536, 4608], P('fsdp'), may hold values from -0.15625 to 0.15625
- mlp_up: bfloat16 [1536, 4608], P('fsdp'), may hold values from -0.15625 to 0.15625
- mlp_down: bfloat16 [4608, 1536], P('fsdp'), may hold values from -0.1875 to 0.1875
Outputs:
- mixed: bfloat16 [4, 1024, 1536], P('fsdp', 'seq')
- tokens_grad: bfloat16 [4, 1024, 1536], P('fsdp', 'seq')
- mix_gain_grad: float32 [1536], replicated
- input_proj_grad: float32 [1536, 2048], P('fsdp', 'seq')
- gelu_proj_grad: float32 [1536, 2048], P('fsdp', 'seq')
- conv_taps_grad: float32 [4, 2048], replicated
- conv_bias_grad: float32 [2048], replicated
- decay_gate_grad: float32 [2048, 256], P('fsdp', 'seq')
- decay_bias_grad: float32 [2048], replicated
- input_gate_grad: float32 [2048, 256], P('fsdp', 'seq')
- input_bias_grad: float32 [2048], replicated
- decay_param_grad: float32 [2048], replicated
- output_proj_grad: float32 [2048, 1536], P('fsdp', 'seq')
- mlp_gain_grad: float32 [1536], replicated
- mlp_gate_grad: float32 [1536, 4608], P('fsdp', 'seq')
- mlp_up_grad: float32 [1536, 4608], P('fsdp', 'seq')
- mlp_down_grad: float32 [4608, 1536], P('fsdp', 'seq')
Inputs may be any that keep to these rules, and one draw needn't show every extreme that they name: `doc_starts`: each row starts with 0 and rises strictly; its entries are the first positions of the documents of that sequence.
All inputs are finite; a program needn't handle non-finite values.
Results may differ from a plain program's by a relative error of at most 0.015.
Values may be sent and summed in bfloat16 or wider, within the bound.
No kernel may reach another device: no remote copies, remote signals or barrier semaphores. Data moves between devices by JAX's collectives and lax.ppermute only.
A program may use at most 448 MiB of HBM per device.

v0:
```python
import jax
import jax.numpy as jnp
from jax import lax
from jax.sharding import PartitionSpec as P

norm_eps = 1e-06
mult_floor = 0.0001


def from_behind(x, axis, by):
    devices = lax.axis_size(axis)
    pairs = [(i, i + by) for i in range(devices) if 0 <= i + by < devices]
    return lax.ppermute(x, axis, pairs)


def rms_scale(values, gain):
    scale = lax.rsqrt(jnp.mean(values * values, axis=-1, keepdims=True) + norm_eps)
    return values * scale * gain


def smooth_gelu(values):
    return jax.nn.gelu(values, approximate=True)


def gated_unit(gate, up_val):
    return smooth_gelu(gate) * up_val


def affine_pair(earlier, later):
    return (earlier[0] * later[0], earlier[1] * later[0] + later[1])


def decay_terms(conv_out, decay_pre, input_pre, decay_param, resets):
    log_a = -8.0 * jax.nn.sigmoid(decay_pre) * jax.nn.softplus(-decay_param)
    room = jnp.maximum(-jnp.expm1(2.0 * log_a), mult_floor)
    factor = jnp.where(resets, 1.0, jnp.sqrt(room))
    decay = jnp.where(resets, 0.0, jnp.exp(log_a))
    return (decay, jax.nn.sigmoid(input_pre) * conv_out * factor)


def conv_apply(extended, taps_w, bias, masks):
    taps = taps_w.shape[0]
    rows = masks.shape[1]
    total = jnp.zeros((rows, taps_w.shape[1]), jnp.float32) + bias
    for shift_k in range(taps):
        begin_row = taps - 1 - shift_k
        total = total + taps_w[shift_k] * extended[begin_row : begin_row + rows] * masks[shift_k]
    return total


def block_product(left, weight):
    width = weight.shape[1]
    blocks = weight.shape[0] // width
    result = jnp.einsum(
        "nhk,hkj->nhj",
        left.reshape(left.shape[0], blocks, width),
        weight.reshape(blocks, width, width),
        preferred_element_type=jnp.float32,
    )
    return result.reshape(left.shape[0], -1)


def block_back(grad, weight):
    width = weight.shape[1]
    blocks = weight.shape[0] // width
    result = jnp.einsum(
        "nhj,hkj->nhk",
        grad.reshape(grad.shape[0], blocks, width),
        weight.reshape(blocks, width, width),
        preferred_element_type=jnp.float32,
    )
    return result.reshape(grad.shape[0], -1)


def block_weight_grad(left, grad, width):
    blocks = left.shape[1] // width
    result = jnp.einsum(
        "nhk,nhj->hkj",
        left.reshape(left.shape[0], blocks, width),
        grad.reshape(grad.shape[0], blocks, width),
        preferred_element_type=jnp.float32,
    )
    return result.reshape(blocks * width, width)


def shards(
    tokens,
    cotangent,
    doc_starts,
    mix_gain,
    input_proj,
    gelu_proj,
    conv_taps,
    conv_bias,
    decay_gate,
    decay_bias,
    input_gate,
    input_bias,
    decay_param,
    output_proj,
    mlp_gain,
    mlp_gate,
    mlp_up,
    mlp_down,
):
    rows = tokens.shape[1]
    taps = conv_taps.shape[0]
    width = decay_gate.shape[1]
    input_w, gelu_w, output_w, decay_w, inputg_w, gate_w, up_w, down_w = (
        lax.all_gather(input_proj, "fsdp", axis=0, tiled=True),
        lax.all_gather(gelu_proj, "fsdp", axis=0, tiled=True),
        lax.all_gather(output_proj, "fsdp", axis=0, tiled=True),
        lax.all_gather(decay_gate, "fsdp", axis=0, tiled=True),
        lax.all_gather(input_gate, "fsdp", axis=0, tiled=True),
        lax.all_gather(mlp_gate, "fsdp", axis=0, tiled=True),
        lax.all_gather(mlp_up, "fsdp", axis=0, tiled=True),
        lax.all_gather(mlp_down, "fsdp", axis=0, tiled=True),
    )
    channels = input_w.shape[1]
    first = lax.axis_index("seq") * rows
    positions = first + jnp.arange(rows, dtype=jnp.int32)
    starts = doc_starts[0]
    begin = jnp.max(jnp.where(starts[None, :] <= positions[:, None], starts[None, :], 0), axis=1)
    resets = (begin == positions)[:, None]
    masks = jnp.stack([(positions - k >= begin)[:, None] for k in range(taps)]).astype(jnp.float32)
    values = tokens[0].astype(jnp.float32)
    normed = rms_scale(values, mix_gain).astype(jnp.bfloat16)
    branch = jnp.dot(normed, input_w, preferred_element_type=jnp.float32).astype(jnp.bfloat16)
    gelu_pre = jnp.dot(normed, gelu_w, preferred_element_type=jnp.float32)
    gelu_out = smooth_gelu(gelu_pre)
    previous = from_behind(branch[rows - (taps - 1) :], "seq", 1)
    extended = jnp.concatenate([previous, branch], axis=0).astype(jnp.float32)
    conv_f = conv_apply(extended, conv_taps, conv_bias, masks).astype(jnp.bfloat16)
    conv_val = conv_f.astype(jnp.float32)
    decay_pre = block_product(conv_f, decay_w) + decay_bias
    input_pre = block_product(conv_f, inputg_w) + input_bias
    decay, driven = decay_terms(conv_val, decay_pre, input_pre, decay_param, resets)
    decay_cols, driven_cols = (
        lax.all_to_all(decay, "seq", split_axis=1, concat_axis=0, tiled=True),
        lax.all_to_all(driven, "seq", split_axis=1, concat_axis=0, tiled=True),
    )
    states_cols = lax.associative_scan(affine_pair, (decay_cols, driven_cols), axis=0)[1]
    states_low = lax.all_to_all(
        states_cols.astype(jnp.bfloat16), "seq", split_axis=0, concat_axis=1, tiled=True
    )
    states_val = states_low.astype(jnp.float32)
    merged = (states_val * gelu_out).astype(jnp.bfloat16)
    middle = values + jnp.dot(merged, output_w, preferred_element_type=jnp.float32)
    normed2 = rms_scale(middle, mlp_gain).astype(jnp.bfloat16)
    gate = jnp.dot(normed2, gate_w, preferred_element_type=jnp.float32)
    up_val = jnp.dot(normed2, up_w, preferred_element_type=jnp.float32)
    hidden = gated_unit(gate, up_val).astype(jnp.bfloat16)
    mixed = (middle + jnp.dot(hidden, down_w, preferred_element_type=jnp.float32)).astype(
        jnp.bfloat16
    )
    out_grad = cotangent[0]
    down_grad = jnp.einsum("tf,td->fd", hidden, out_grad, preferred_element_type=jnp.float32)
    hidden_grad = jnp.einsum("td,fd->tf", out_grad, down_w, preferred_element_type=jnp.float32)
    unit_pull = jax.vjp(gated_unit, gate, up_val)[1]
    gate_grad, up_grad = unit_pull(hidden_grad)
    gate_low = gate_grad.astype(jnp.bfloat16)
    up_low = up_grad.astype(jnp.bfloat16)
    gate_w_grad = jnp.einsum("td,tf->df", normed2, gate_low, preferred_element_type=jnp.float32)
    up_w_grad = jnp.einsum("td,tf->df", normed2, up_low, preferred_element_type=jnp.float32)
    mlp_terms = (
        lax.psum_scatter(gate_w_grad, "seq", scatter_dimension=1, tiled=True),
        lax.psum_scatter(up_w_grad, "seq", scatter_dimension=1, tiled=True),
        lax.psum_scatter(down_grad, "seq", scatter_dimension=1, tiled=True),
    )
    mlp_gate_grad, mlp_up_grad, mlp_down_grad = (
        lax.psum_scatter(mlp_terms[0], "fsdp", scatter_dimension=0, tiled=True),
        lax.psum_scatter(mlp_terms[1], "fsdp", scatter_dimension=0, tiled=True),
        lax.psum_scatter(mlp_terms[2], "fsdp", scatter_dimension=0, tiled=True),
    )
    normed2_grad = jnp.einsum(
        "tf,df->td", gate_low, gate_w, preferred_element_type=jnp.float32
    ) + jnp.einsum("tf,df->td", up_low, up_w, preferred_element_type=jnp.float32)
    norm2_pull = jax.vjp(rms_scale, middle, mlp_gain)[1]
    middle_part, mlp_gain_term = norm2_pull(normed2_grad)
    middle_grad = out_grad.astype(jnp.float32) + middle_part
    mixer_grad = middle_grad.astype(jnp.bfloat16)
    output_w_grad = jnp.einsum("tr,td->rd", merged, mixer_grad, preferred_element_type=jnp.float32)
    merged_grad = jnp.einsum("td,rd->tr", mixer_grad, output_w, preferred_element_type=jnp.float32)
    state_low = (merged_grad * gelu_out).astype(jnp.bfloat16)
    gelu_pull = jax.vjp(smooth_gelu, gelu_pre)[1]
    gelu_pre_low = gelu_pull(merged_grad * states_val)[0].astype(jnp.bfloat16)
    grad_cols = lax.all_to_all(state_low, "seq", split_axis=1, concat_axis=0, tiled=True).astype(
        jnp.float32
    )
    width_cols = grad_cols.shape[1]
    next_decay = jnp.concatenate([decay_cols[1:], jnp.zeros((1, width_cols), jnp.float32)], axis=0)
    carried = lax.associative_scan(affine_pair, (next_decay, grad_cols), reverse=True, axis=0)[1]
    prior = jnp.concatenate([jnp.zeros((1, width_cols), jnp.float32), states_cols[:-1]], axis=0)
    decay_grad, driven_grad = (
        lax.all_to_all(carried * prior, "seq", split_axis=0, concat_axis=1, tiled=True),
        lax.all_to_all(carried, "seq", split_axis=0, concat_axis=1, tiled=True),
    )
    terms_pull = jax.vjp(
        lambda conv_in, dpre, ipre, dparam: decay_terms(conv_in, dpre, ipre, dparam, resets),
        conv_val,
        decay_pre,
        input_pre,
        decay_param,
    )[1]
    gate_conv_grad, dpre_grad, ipre_grad, decay_param_term = terms_pull((decay_grad, driven_grad))
    dpre_low = dpre_grad.astype(jnp.bfloat16)
    ipre_low = ipre_grad.astype(jnp.bfloat16)
    decay_w_grad = block_weight_grad(conv_f, dpre_low, width)
    inputg_w_grad = block_weight_grad(conv_f, ipre_low, width)
    conv_grad = gate_conv_grad + block_back(dpre_low, decay_w) + block_back(ipre_low, inputg_w)
    conv_pull = jax.vjp(
        lambda ext, taps_w, bias: conv_apply(ext, taps_w, bias, masks),
        extended,
        conv_taps,
        conv_bias,
    )[1]
    extended_grad, taps_term, conv_bias_term = conv_pull(conv_grad)
    returned = from_behind(extended_grad[: taps - 1], "seq", -1)
    branch_grad = extended_grad[taps - 1 :] + jnp.concatenate(
        [jnp.zeros((rows - (taps - 1), channels), jnp.float32), returned], axis=0
    )
    branch_low = branch_grad.astype(jnp.bfloat16)
    input_w_grad = jnp.einsum("td,tr->dr", normed, branch_low, preferred_element_type=jnp.float32)
    gelu_w_grad = jnp.einsum("td,tr->dr", normed, gelu_pre_low, preferred_element_type=jnp.float32)
    mix_terms = (
        lax.psum_scatter(input_w_grad, "seq", scatter_dimension=1, tiled=True),
        lax.psum_scatter(gelu_w_grad, "seq", scatter_dimension=1, tiled=True),
        lax.psum_scatter(output_w_grad, "seq", scatter_dimension=1, tiled=True),
        lax.psum_scatter(decay_w_grad, "seq", scatter_dimension=1, tiled=True),
        lax.psum_scatter(inputg_w_grad, "seq", scatter_dimension=1, tiled=True),
    )
    input_proj_grad, gelu_proj_grad, output_proj_grad, decay_gate_grad, input_gate_grad = (
        lax.psum_scatter(mix_terms[0], "fsdp", scatter_dimension=0, tiled=True),
        lax.psum_scatter(mix_terms[1], "fsdp", scatter_dimension=0, tiled=True),
        lax.psum_scatter(mix_terms[2], "fsdp", scatter_dimension=0, tiled=True),
        lax.psum_scatter(mix_terms[3], "fsdp", scatter_dimension=0, tiled=True),
        lax.psum_scatter(mix_terms[4], "fsdp", scatter_dimension=0, tiled=True),
    )
    normed_grad = jnp.einsum(
        "tr,dr->td", branch_low, input_w, preferred_element_type=jnp.float32
    ) + jnp.einsum("tr,dr->td", gelu_pre_low, gelu_w, preferred_element_type=jnp.float32)
    norm1_pull = jax.vjp(rms_scale, values, mix_gain)[1]
    values_part, mix_gain_term = norm1_pull(normed_grad)
    tokens_grad = (middle_grad + values_part).astype(jnp.bfloat16)
    (
        mix_gain_grad,
        conv_taps_grad,
        conv_bias_grad,
        decay_bias_grad,
        input_bias_grad,
        decay_param_grad,
        mlp_gain_grad,
    ) = lax.psum(
        (
            mix_gain_term,
            taps_term,
            conv_bias_term,
            jnp.sum(dpre_low.astype(jnp.float32), axis=0),
            jnp.sum(ipre_low.astype(jnp.float32), axis=0),
            decay_param_term,
            mlp_gain_term,
        ),
        ("seq", "fsdp"),
    )
    return (
        mixed[None],
        tokens_grad[None],
        mix_gain_grad,
        input_proj_grad,
        gelu_proj_grad,
        conv_taps_grad,
        conv_bias_grad,
        decay_gate_grad,
        decay_bias_grad,
        input_gate_grad,
        input_bias_grad,
        decay_param_grad,
        output_proj_grad,
        mlp_gain_grad,
        mlp_gate_grad,
        mlp_up_grad,
        mlp_down_grad,
    )


def solution(mesh):
    return jax.shard_map(
        shards,
        mesh=mesh,
        in_specs=(
            P("fsdp", "seq", None),
            P("fsdp", "seq", None),
            P("fsdp", None),
            P(),
            P("fsdp", None),
            P("fsdp", None),
            P(),
            P(),
            P("fsdp", None),
            P(),
            P("fsdp", None),
            P(),
            P(),
            P("fsdp", None),
            P(),
            P("fsdp", None),
            P("fsdp", None),
            P("fsdp", None),
        ),
        out_specs=(
            P("fsdp", "seq", None),
            P("fsdp", "seq", None),
            P(),
            P("fsdp", "seq"),
            P("fsdp", "seq"),
            P(),
            P(),
            P("fsdp", "seq"),
            P(),
            P("fsdp", "seq"),
            P(),
            P(),
            P("fsdp", "seq"),
            P(),
            P("fsdp", "seq"),
            P("fsdp", "seq"),
            P("fsdp", "seq"),
        ),
        check_vma=False,
    )
```

profile of v0, /device:TPU:0, one launch (start us, length us, event | category | flops | bytes accessed | tf_op | source)
XLA Modules:
  0.0 2809.6 jit_solution(8010894551462894261)
XLA Ops:
  13.8 113.8 %all-gather.9.cloned.1.call-done = bf16[1536,2048]{1,0:T(8,128)(2,1)} async-done(((bf16[384,2048]{1,0:T(8,128)(2,1)}), bf16[1536,2048]{1,0:T(8,128)(2,1)}) %all-gather.9.cloned.1.call-update) | async-done | bytes 6291472 | tf_op jit(solution)/shard_map/all_gather | solution.py:110
  135.5 19.9 all-gather.13.cloned.1.call-done
  162.8 21.7 all-gather.11.cloned.1.call-done
  268.7 12.2 all_to_all.99
  282.0 18.8 all-gather.15.cloned.1.call-done
  306.3 109.5 %all-gather.17.cloned.1.call-done = bf16[2048,1536]{1,0:T(8,128)(2,1)} async-done(((bf16[512,1536]{1,0:T(8,128)(2,1)}), bf16[2048,1536]{1,0:T(8,128)(2,1)}) %all-gather.17.cloned.1.call-update) | async-done | bytes 6291472 | tf_op jit(solution)/shard_map/all_gather | solution.py:112
  420.8 238.6 %all-gather.21.cloned.1.call-done = bf16[1536,4608]{1,0:T(8,128)(2,1)} async-done(((bf16[384,4608]{1,0:T(8,128)(2,1)}), bf16[1536,4608]{1,0:T(8,128)(2,1)}) %all-gather.21.cloned.1.call-update) | async-done | bytes 14155792 | tf_op jit(solution)/shard_map/all_gather | solution.py:116
  668.1 235.1 %all-gather.19.cloned.1.call-done = bf16[1536,4608]{1,0:T(8,128)(2,1)} async-done(((bf16[384,4608]{1,0:T(8,128)(2,1)}), bf16[1536,4608]{1,0:T(8,128)(2,1)}) %all-gather.19.cloned.1.call-update) | async-done | bytes 14155792 | tf_op jit(solution)/shard_map/all_gather | solution.py:115
  911.8 235.1 %all-gather.23.cloned.1.call-done = bf16[4608,1536]{1,0:T(8,128)(2,1)} async-done(((bf16[1152,1536]{1,0:T(8,128)(2,1)}), bf16[4608,1536]{1,0:T(8,128)(2,1)}) %all-gather.23.cloned.1.call-update) | async-done | bytes 14155792 | tf_op jit(solution)/shard_map/all_gather | solution.py:117
  1146.8 13.8 multiply_convert_fusion
  1160.6 10.8 fusion.131
  1171.4 11.9 multiply_reduce_fusion.5
  1348.6 19.4 all_to_all.100
  1374.7 12.9 all-to-all-done.4
  1442.6 12.1 fusion.59
  1456.0 11.6 fusion.134
  1468.9 11.6 fusion.133
  1495.1 82.1 %reduce-scatter.33.cloned.1.call-done = f32[2048,192]{0,1:T(8,128)} async-done(((f32[2048,1536]{0,1:T(8,128)}), f32[2048,192]{0,1:T(8,128)}) %reduce-scatter.33.cloned.1.call-update) | async-done | bytes 1572880 | tf_op jit(solution)/shard_map/reduce_scatter | solution.py:228
  1577.3 95.7 %reduce-scatter.21.cloned.1.call-done = f32[1536,256]{1,0:T(8,128)} async-done(((f32[1536,2048]{1,0:T(8,128)}), f32[1536,256]{1,0:T(8,128)}) %reduce-scatter.21.cloned.1.call-update) | async-done | bytes 1572880 | tf_op jit(solution)/shard_map/reduce_scatter | solution.py:227
  1673.1 95.9 %reduce-scatter.17.cloned.1.call-done = f32[1536,256]{1,0:T(8,128)} async-done(((f32[1536,2048]{1,0:T(8,128)}), f32[1536,256]{1,0:T(8,128)}) %reduce-scatter.17.cloned.1.call-update) | async-done | bytes 1572880 | tf_op jit(solution)/shard_map/reduce_scatter | solution.py:226
  1769.0 176.8 %reduce-scatter.45.cloned.1.call-done = f32[4608,192]{0,1:T(8,128)} async-done(((f32[4608,1536]{0,1:T(8,128)}), f32[4608,192]{0,1:T(8,128)}) %reduce-scatter.45.cloned.1.call-update) | async-done | bytes 3538960 | tf_op jit(solution)/shard_map/reduce_scatter | solution.py:168
  1945.8 176.8 %reduce-scatter.41.cloned.1.call-done = f32[1536,576]{0,1:T(8,128)} async-done(((f32[1536,4608]{0,1:T(8,128)}), f32[1536,576]{0,1:T(8,128)}) %reduce-scatter.41.cloned.1.call-update) | async-done | bytes 3538960 | tf_op jit(solution)/shard_map/reduce_scatter | solution.py:167
  2122.7 176.8 %reduce-scatter.37.cloned.1.call-done = f32[1536,576]{0,1:T(8,128)} async-done(((f32[1536,4608]{0,1:T(8,128)}), f32[1536,576]{0,1:T(8,128)}) %reduce-scatter.37.cloned.1.call-update) | async-done | bytes 3538960 | tf_op jit(solution)/shard_map/reduce_scatter | solution.py:166
  2308.4 122.0 %all-reduce.54.cloned.1.call-done = (f32[1536]{0:T(1024)}, f32[4,2048]{1,0:T(4,128)}, f32[2048]{0:T(1024)}, f32[2048]{0:T(1024)}, f32[2048]{0:T(1024)}, /*index=5*/f32[2048]{0:T(1024)}, f32[1536]{0:T(1024)}) async-done(((f32[1536]{0:T(1024)}, f32[4,2048]{1,0:T(4,128)}, f32[2048]{0:T(1024)}, f32[2048]{0:T(1024)}, f32[2048]{0:T(1024)}, /*index=5*/f32[2048]{0:T(1024)}, f32[1536]{0:T(1024)}), (f32[1536]{0:T(1024)}, ...) | async-done | bytes 77840 | tf_op jit(solution)/shard_map/psum | solution.py:253
  2430.4 23.6 reduce-scatter.31.cloned.1.call-done
  2454.0 20.8 reduce-scatter.27.cloned.1.call-done
  2474.8 36.4 %reduce-scatter.35.cloned.1.call-done = f32[512,192]{0,1:T(8,128)} async-done(((f32[2048,192]{0,1:T(8,128)}), f32[512,192]{0,1:T(8,128)}) %reduce-scatter.35.cloned.1.call-update) | async-done | bytes 393232 | tf_op jit(solution)/shard_map/reduce_scatter | solution.py:235
  2511.2 37.3 %reduce-scatter.23.cloned.1.call-done = f32[384,256]{1,0:T(8,128)} async-done(((f32[1536,256]{1,0:T(8,128)}), f32[384,256]{1,0:T(8,128)}) %reduce-scatter.23.cloned.1.call-update) | async-done | bytes 393232 | tf_op jit(solution)/shard_map/reduce_scatter | solution.py:234
  2548.5 37.3 %reduce-scatter.19.cloned.1.call-done = f32[384,256]{1,0:T(8,128)} async-done(((f32[1536,256]{1,0:T(8,128)}), f32[384,256]{1,0:T(8,128)}) %reduce-scatter.19.cloned.1.call-update) | async-done | bytes 393232 | tf_op jit(solution)/shard_map/reduce_scatter | solution.py:233
  2585.8 68.4 %reduce-scatter.47.cloned.1.call-done = f32[1152,192]{0,1:T(8,128)} async-done(((f32[4608,192]{0,1:T(8,128)}), f32[1152,192]{0,1:T(8,128)}) %reduce-scatter.47.cloned.1.call-update) | async-done | bytes 884752 | tf_op jit(solution)/shard_map/reduce_scatter | solution.py:173
  2654.2 69.6 %reduce-scatter.43.cloned.1.call-done = f32[384,576]{0,1:T(8,128)} async-done(((f32[1536,576]{0,1:T(8,128)}), f32[384,576]{0,1:T(8,128)}) %reduce-scatter.43.cloned.1.call-update) | async-done | bytes 884752 | tf_op jit(solution)/shard_map/reduce_scatter | solution.py:172
  2723.8 69.7 %reduce-scatter.39.cloned.1.call-done = f32[384,576]{0,1:T(8,128)} async-done(((f32[1536,576]{0,1:T(8,128)}), f32[384,576]{0,1:T(8,128)}) %reduce-scatter.39.cloned.1.call-update) | async-done | bytes 884752 | tf_op jit(solution)/shard_map/reduce_scatter | solution.py:171
  (534 shorter events, 395.6 us)
Async XLA Ops:
  7.2 120.5 %all-gather.9.cloned.1.call-start = ((), (), s32[]{:S(2)}) async-start(), calls=%async_computation.22 | async-start | bytes 7864320 | tf_op jit(solution)/shard_map/all_gather | solution.py:110
  7.9 147.5 %all-gather.13.cloned.1.call-start = ((), (), s32[]{:S(2)}) async-start(), calls=%async_computation.24 | async-start | bytes 1310720 | tf_op jit(solution)/shard_map/all_gather | solution.py:113
  8.7 175.8 %all-gather.11.cloned.1.call-start = ((), (), s32[]{:S(2)}) async-start(), calls=%async_computation.23 | async-start | bytes 1310720 | tf_op jit(solution)/shard_map/all_gather | solution.py:114
  9.4 291.4 %all-gather.15.cloned.1.call-start = ((), (), s32[]{:S(2)}) async-start(), calls=%async_computation.25 | async-start | bytes 7864320 | tf_op jit(solution)/shard_map/all_gather | solution.py:111
  10.0 405.8 %all-gather.17.cloned.1.call-start = ((), (), s32[]{:S(2)}) async-start(), calls=%async_computation.26 | async-start | bytes 7864320 | tf_op jit(solution)/shard_map/all_gather | solution.py:112
  10.6 648.9 %all-gather.21.cloned.1.call-start = ((), (), s32[]{:S(2)}) async-start(), calls=%async_computation.28 | async-start | bytes 17694720 | tf_op jit(solution)/shard_map/all_gather | solution.py:116
  11.1 892.0 %all-gather.19.cloned.1.call-start = ((), (), s32[]{:S(2)}) async-start(), calls=%async_computation.27 | async-start | bytes 17694720 | tf_op jit(solution)/shard_map/all_gather | solution.py:115
  11.9 1134.9 %all-gather.23.cloned.1.call-start = ((), (), s32[]{:S(2)}) async-start(), calls=%async_computation.29 | async-start | bytes 17694720 | tf_op jit(solution)/shard_map/all_gather | solution.py:117
  131.5 2.8 collective-permute-start
  158.5 31.7 %all-to-all-start.1 = ((f32[128,8,256]{2,0,1:T(8,128)}), f32[128,8,256]{2,0,1:T(8,128)}, u32[]{:S(2)}, u32[]{:S(2)}) async-start(f32[128,8,256]{2,0,1:T(8,128)} %get-tuple-element.104), calls=%async_computation.1 | async-start | bytes 2097152 | tf_op jit(solution)/shard_map/all_to_all | solution.py:139
  190.3 19.7 all-to-all-start
  1189.4 34.5 %all-to-all-start.3 = ((bf16[128,8,256]{2,0,1:T(8,128)(2,1)}), bf16[128,8,256]{2,0,1:T(8,128)(2,1)}, u32[]{:S(2)}, u32[]{:S(2)}) async-start(bf16[128,8,256]{2,0,1:T(8,128)(2,1)} %bitcast.236), calls=%async_computation.3 | async-start | bytes 1048576 | tf_op jit(solution)/shard_map/all_to_all | solution.py:187
  1367.9 19.7 all-to-all-start.4
  1372.3 121.5 %reduce-scatter.29.cloned.1.call-start = ((), (), s32[]{:S(2)}) async-start(), calls=%async_computation.36 | async-start | bytes 2359296 | tf_op jit(solution)/shard_map/reduce_scatter | solution.py:230
  1398.4 95.9 %reduce-scatter.25.cloned.1.call-start = ((), (), s32[]{:S(2)}) async-start(), calls=%async_computation.34 | async-start | bytes 2359296 | tf_op jit(solution)/shard_map/reduce_scatter | solution.py:229
  1406.5 170.7 %reduce-scatter.33.cloned.1.call-start = ((), (), s32[]{:S(2)}) async-start(), calls=%async_computation.38 | async-start | bytes 14155776 | tf_op jit(solution)/shard_map/reduce_scatter | solution.py:228
  1414.2 258.8 %reduce-scatter.21.cloned.1.call-start = ((), (), s32[]{:S(2)}) async-start(), calls=%async_computation.32 | async-start | bytes 14155776 | tf_op jit(solution)/shard_map/reduce_scatter | solution.py:227
  1422.4 346.5 %reduce-scatter.17.cloned.1.call-start = ((), (), s32[]{:S(2)}) async-start(), calls=%async_computation.30 | async-start | bytes 14155776 | tf_op jit(solution)/shard_map/reduce_scatter | solution.py:226
  1431.7 3.1 collective-permute-start.1
  1441.2 504.5 %reduce-scatter.45.cloned.1.call-start = ((), (), s32[]{:S(2)}) async-start(), calls=%async_computation.44 | async-start | bytes 31850496 | tf_op jit(solution)/shard_map/reduce_scatter | solution.py:168
  1454.7 667.9 %reduce-scatter.41.cloned.1.call-start = ((), (), s32[]{:S(2)}) async-start(), calls=%async_computation.42 | async-start | bytes 31850496 | tf_op jit(solution)/shard_map/reduce_scatter | solution.py:167
  1467.7 831.8 %reduce-scatter.37.cloned.1.call-start = ((), (), s32[]{:S(2)}) async-start(), calls=%async_computation.40 | async-start | bytes 31850496 | tf_op jit(solution)/shard_map/reduce_scatter | solution.py:166
  1480.6 949.9 %all-reduce.54.cloned.1.call-start = ((), (), s32[]{:S(2)}) async-start(), calls=%async_computation.46 | async-start | bytes 163840 | tf_op jit(solution)/shard_map/psum | solution.py:253
  1493.7 960.3 %reduce-scatter.31.cloned.1.call-start = ((), (), s32[]{:S(2)}) async-start(), calls=%async_computation.37 | async-start | bytes 327680 | tf_op jit(solution)/shard_map/reduce_scatter | solution.py:237
  1494.3 980.5 %reduce-scatter.27.cloned.1.call-start = ((), (), s32[]{:S(2)}) async-start(), calls=%async_computation.35 | async-start | bytes 327680 | tf_op jit(solution)/shard_map/reduce_scatter | solution.py:236
  1495.1 1016.2 %reduce-scatter.35.cloned.1.call-start = ((), (), s32[]{:S(2)}) async-start(), calls=%async_computation.39 | async-start | bytes 1966080 | tf_op jit(solution)/shard_map/reduce_scatter | solution.py:235
  1577.2 971.3 %reduce-scatter.23.cloned.1.call-start = ((), (), s32[]{:S(2)}) async-start(), calls=%async_computation.33 | async-start | bytes 1966080 | tf_op jit(solution)/shard_map/reduce_scatter | solution.py:234
  1673.0 912.8 %reduce-scatter.19.cloned.1.call-start = ((), (), s32[]{:S(2)}) async-start(), calls=%async_computation.31 | async-start | bytes 1966080 | tf_op jit(solution)/shard_map/reduce_scatter | solution.py:233
  1769.0 885.3 %reduce-scatter.47.cloned.1.call-start = ((), (), s32[]{:S(2)}) async-start(), calls=%async_computation.45 | async-start | bytes 4423680 | tf_op jit(solution)/shard_map/reduce_scatter | solution.py:173
  1945.8 778.0 %reduce-scatter.43.cloned.1.call-start = ((), (), s32[]{:S(2)}) async-start(), calls=%async_computation.43 | async-start | bytes 4423680 | tf_op jit(solution)/shard_map/reduce_scatter | solution.py:172
  2122.6 176.8 %copy-start.10 = (bf16[128,4608]{1,0:T(8,128)(2,1)S(1)}, bf16[128,4608]{1,0:T(8,128)(2,1)}, u32[]{:S(2)}) copy-start(bf16[128,4608]{1,0:T(8,128)(2,1)} %get-tuple-element.41) | copy-start | bytes 3538948
  2122.6 670.8 %reduce-scatter.39.cloned.1.call-start = ((), (), s32[]{:S(2)}) async-start(), calls=%async_computation.41 | async-start | bytes 4423680 | tf_op jit(solution)/shard_map/reduce_scatter | solution.py:171
  (77 other events, 2578.1 us)
Sparse Core Ops, SparseCore 0:
  9.6 118.0 all-gather.8
  129.2 26.1 all-gather.12
  157.0 27.4 all-gather.10
  185.9 114.8 all-gather.14
  302.2 113.5 all-gather.16
  417.2 242.1 all-gather.20
  661.0 242.1 all-gather.18
  904.7 242.1 all-gather.22
  1398.6 37.6 reduce-scatter.28
  1439.7 41.5 reduce-scatter.24
  1484.8 92.3 reduce-scatter.32
  1580.6 92.3 reduce-scatter.20
  1676.5 92.3 reduce-scatter.16
  1772.5 173.2 reduce-scatter.44
  1949.3 173.2 reduce-scatter.40
  2126.1 173.2 reduce-scatter.36
  2306.9 123.5 all-reduce.53
  2433.2 20.7 reduce-scatter.30
  2456.8 17.9 reduce-scatter.26
  2477.7 33.5 reduce-scatter.34
  2514.2 34.2 reduce-scatter.22
  2551.5 34.2 reduce-scatter.18
  2588.8 65.3 reduce-scatter.46
  2657.1 66.6 reduce-scatter.42
  2726.8 66.6 reduce-scatter.38
where the time goes:
time: 2820 us; the launch traced here: 2810 us
  waiting for transfers between devices  2310 us (82%)
  local copies, waits for them, and re-layouts  206 us (7%)
  matrix products  160 us (6%)
  other arithmetic  66.8 us (2%)
  blocking collectives  31.5 us (1%)
    all_gather x1, waiting for transfers between devices, shards(): lax.all_gather(mlp_up, 'fsdp', axis=0, tiled=True)  239 us
    all_gather x1, waiting for transfers between devices, shards(): lax.all_gather(mlp_gate, 'fsdp', axis=0, tiled=True)  235 us
    all_gather x1, waiting for transfers between devices, shards(): lax.all_gather(mlp_down, 'fsdp', axis=0, tiled=True)  235 us
    reduce_scatter x1, waiting for transfers between devices, shards(): lax.psum_scatter(down_grad, 'seq', scatter_dimension=1, tiled=True)  177 us
    reduce_scatter x1, waiting for transfers between devices, shards(): lax.psum_scatter(up_w_grad, 'seq', scatter_dimension=1, tiled=True)  177 us
    reduce_scatter x1, waiting for transfers between devices, shards(): lax.psum_scatter(gate_w_grad, 'seq', scatter_dimension=1, tiled=True)  177 us
    psum x1, waiting for transfers between devices, shards(): lax.psum((mix_gain_term, taps_term, conv_bias_term, jnp.sum(dpre_low.asty...  122 us
    all_gather x1, waiting for transfers between devices, shards(): lax.all_gather(input_proj, 'fsdp', axis=0, tiled=True)  114 us
  transfers between devices with their start and end apart: 31, of which 27 were waited for; matrix products, arithmetic and copies ran while one was open for 9% of the time, Pallas kernels for 0%

commit v1 on v0

--- a/solution.py
+++ b/solution.py
@@ -1,6 +1,10 @@
+import functools
+
 import jax
 import jax.numpy as jnp
 from jax import lax
+from jax.experimental import pallas as pl
+from jax.experimental.pallas import tpu as pltpu
 from jax.sharding import PartitionSpec as P
 
 norm_eps = 1e-06
@@ -83,7 +87,7 @@
     return result.reshape(blocks * width, width)
 
 
-def shards(
+def wide_shards(
     tokens,
     cotangent,
     doc_starts,
@@ -283,9 +287,813 @@
     )
 
 
+def chip_swap(x, k):
+    devices = lax.axis_size("seq")
+    return lax.ppermute(x, "seq", [(i, i ^ (2 * k)) for i in range(devices)])
+
+
+def core_swap(x):
+    devices = lax.axis_size("seq")
+    return lax.ppermute(x, "seq", [(i, i ^ 1) for i in range(devices)])
+
+
+def gather_blocks(x):
+    chips = lax.axis_size("seq") // 2
+    near = [x] + [chip_swap(x, k) for k in range(1, chips)]
+    return near, [core_swap(block) for block in near]
+
+
+def scatter_blocks(near, far):
+    chips = near.shape[0]
+    pair = near.astype(jnp.float32) + core_swap(far.astype(jnp.bfloat16)).astype(jnp.float32)
+    low = pair.astype(jnp.bfloat16)
+    total = pair[0]
+    for k in range(1, chips):
+        total = total + chip_swap(low[k], k).astype(jnp.float32)
+    return total
+
+
+def exchange(x, chip, core):
+    chips = x.shape[0]
+    parts = [lax.dynamic_index_in_dim(x, chip ^ k, 0, keepdims=False) for k in range(chips)]
+    got = jnp.stack([parts[0]] + [chip_swap(parts[k], k) for k in range(1, chips)])
+    keep = lax.dynamic_index_in_dim(got, core, 1, keepdims=False)
+    give = lax.dynamic_index_in_dim(got, 1 - core, 1, keepdims=False)
+    return keep, core_swap(give)
+
+
+def reorder(parts, index):
+    bit = 1
+    while bit < len(parts):
+        flip = (index & bit) != 0
+        parts = [jnp.where(flip, parts[i ^ bit], parts[i]) for i in range(len(parts))]
+        bit *= 2
+    return parts
+
+
+def total_over(x, axes):
+    for axis in axes:
+        devices = lax.axis_size(axis)
+        bit = 1
+        while bit < devices:
+            x = x + lax.ppermute(x, axis, [(i, i ^ bit) for i in range(devices)])
+            bit *= 2
+    return x
+
+
+def gelu_parts(v):
+    inner = 0.7978845608028654 * (v + 0.044715 * v * v * v)
+    th = jnp.tanh(inner)
+    value = 0.5 * v * (1.0 + th)
+    slope = 0.5 * (1.0 + th) + 0.5 * v * (1.0 - th * th) * (
+        0.7978845608028654 * (1.0 + 0.134145 * v * v)
+    )
+    return value, slope
+
+
+def sigmoid(v):
+    return 1.0 / (1.0 + jnp.exp(-v))
+
+
+def one_less_exp(v):
+    series = -v * (1.0 + v * (0.5 + v * (1.0 / 6.0 + v * (1.0 / 24.0 + v * (1.0 / 120.0)))))
+    return jnp.where(v > -0.1, series, 1.0 - jnp.exp(v))
+
+
+def dot_nn(a, b):
+    return lax.dot_general(a, b, (((1,), (0,)), ((), ())), preferred_element_type=jnp.float32)
+
+
+def dot_nt(a, b):
+    return lax.dot_general(a, b, (((1,), (1,)), ((), ())), preferred_element_type=jnp.float32)
+
+
+def dot_tn(a, b):
+    return lax.dot_general(a, b, (((0,), (0,)), ((), ())), preferred_element_type=jnp.float32)
+
+
+def scan_rows(a, b, later):
+    rows = a.shape[0]
+    row = lax.broadcasted_iota(jnp.int32, a.shape, 0)
+    step = 1
+    while step < rows:
+        turn = rows - step if later else step
+        there = (row < rows - step) if later else (row >= step)
+        a_next = jnp.where(there, pltpu.roll(a, turn, 0), 1.0)
+        b_next = jnp.where(there, pltpu.roll(b, turn, 0), 0.0)
+        b = a * b_next + b
+        a = a * a_next
+        step *= 2
+    return a, b
+
+
+def in_time(value, core):
+    rows = value.shape[0] // 2
+    near, far = value[:rows], value[rows:]
+    odd = core == 1
+    return jnp.concatenate([jnp.where(odd, far, near), jnp.where(odd, near, far)], axis=0)
+
+
+def by_core(value, ref, core):
+    rows = value.shape[0] // 2
+    first, second = value[:rows], value[rows:]
+    odd = core == 1
+    ref[0] = jnp.where(odd, second, first).astype(ref.dtype)
+    ref[1] = jnp.where(odd, first, second).astype(ref.dtype)
+
+
+def mix_forward_kernel(chips, *refs):
+    place = refs[0][0]
+    blocks = refs[1 : 1 + 2 * chips]
+    age_ref, chan_ref, in_ref, keep_ref, got_ref = refs[1 + 2 * chips : 6 + 2 * chips]
+    (
+        merged_ref,
+        normed_ref,
+        branch_ref,
+        gelu_pre_ref,
+        conv_ref,
+        decay_pre_ref,
+        input_pre_ref,
+        prior_ref,
+        low_ref,
+        weights_ref,
+        held,
+        extended,
+        carry,
+    ) = refs[-13:]
+    step = pl.program_id(0)
+    chip, core = place // 2, place % 2
+    rows, width = branch_ref.shape
+    planes, near_model, both = in_ref.shape
+    model = planes * near_model
+    parts = weights_ref.shape[1] // both
+    piece = keep_ref.shape[1] // parts
+
+    @pl.when(step == 0)
+    def _():
+        extended[pl.ds(0, 8), :] = jnp.zeros((8, width), jnp.float32)
+        carry[...] = jnp.zeros_like(carry)
+        for k in range(chips):
+            held[0, k] = blocks[k][...]
+            held[1, k] = blocks[chips + k][...]
+            home = pl.multiple_of(piece * 2 * (chip ^ k) + piece * core, piece)
+            away = pl.multiple_of(piece * 2 * (chip ^ k) + piece * (1 - core), piece)
+            for j in range(parts):
+                where = pl.ds(j * both, both)
+                weights_ref[pl.ds(home, piece), where] = keep_ref[k, pl.ds(j * piece, piece), :]
+                weights_ref[pl.ds(away, piece), where] = got_ref[k, pl.ds(j * piece, piece), :]
+
+    @pl.when(step > 0)
+    def _():
+        extended[pl.ds(0, 8), :] = extended[pl.ds(rows, 8), :]
+
+    turn = step ^ chip
+    near, far = held[0, turn], held[1, turn]
+    normed_ref[0] = near
+    normed_ref[1] = far
+    normed = jnp.concatenate([near, far], axis=0)
+    pre = dot_nn(normed[:, :near_model], in_ref[0])
+    for z in range(1, planes):
+        pre = pre + dot_nn(normed[:, z * near_model : (z + 1) * near_model], in_ref[z])
+    pre = in_time(pre, core)
+    branch = pre[:, :width].astype(jnp.bfloat16)
+    gelu_pre = pre[:, width:]
+    branch_ref[...] = branch
+    gelu_pre_ref[...] = gelu_pre
+    extended[pl.ds(8, rows), :] = branch.astype(jnp.float32)
+    age = age_ref[...]
+    total = jnp.zeros((rows, width), jnp.float32) + chan_ref[4:5, :]
+    for k in range(4):
+        shifted = extended[pl.ds(8 - k, rows), :]
+        total = total + chan_ref[k : k + 1, :] * shifted * jnp.where(age >= k, 1.0, 0.0)
+    conv_low = total.astype(jnp.bfloat16)
+    conv = conv_low.astype(jnp.float32)
+    conv_ref[...] = conv_low
+    decay_pre = dot_nn(conv_low, weights_ref[:, model : model + width]) + chan_ref[5:6, :]
+    input_pre = dot_nn(conv_low, weights_ref[:, model + width :]) + chan_ref[6:7, :]
+    decay_pre_ref[...] = decay_pre
+    input_pre_ref[...] = input_pre
+    log_a = -8.0 * sigmoid(decay_pre) * chan_ref[7:8, :]
+    reset = age < 0.5
+    room = jnp.maximum(one_less_exp(2.0 * log_a), mult_floor)
+    factor = jnp.where(reset, 1.0, jnp.sqrt(room))
+    decay = jnp.where(reset, 0.0, jnp.exp(log_a))
+    driven = sigmoid(input_pre) * conv * factor
+    grown, states = scan_rows(decay, driven, False)
+    before = carry[0:1, :]
+    states = states + grown * before
+    carry[0:1, :] = states[rows - 1 :, :]
+    row = lax.broadcasted_iota(jnp.int32, states.shape, 0)
+    prior_ref[...] = jnp.where(row == 0, before, pltpu.roll(states, 1, 0))
+    low = states.astype(jnp.bfloat16)
+    low_ref[...] = low
+    merged = low.astype(jnp.float32) * gelu_parts(gelu_pre)[0]
+    by_core(merged, merged_ref, core)
+
+
+def mix_forward(place, near, far, age, chan, pack, keep, got, ahead_of):
+    chips = len(near)
+    rows, model = near[0].shape
+    planes, _, both = pack.shape
+    width = both // 2
+    length = 2 * chips * rows
+    chunk = 2 * rows
+    columns = keep.shape[1] * both // (width // (2 * chips))
+    time_block = lambda i, s: (i, 0)
+    token_block = lambda i, s: (0, i ^ (s[0] // 2), 0, 0)
+    saved = lambda dtype: jax.ShapeDtypeStruct((length, width), dtype)
+    spec = pl.BlockSpec((chunk, width), time_block)
+    fixed = lambda shape: pl.BlockSpec(shape, lambda i, s: (0,) * len(shape))
+    return pl.pallas_call(
+        functools.partial(mix_forward_kernel, chips),
+        grid_spec=pltpu.PrefetchScalarGridSpec(
+            num_scalar_prefetch=1,
+            grid=(chips,),
+            in_specs=[fixed((rows, model))] * (2 * chips)
+            + [
+                pl.BlockSpec((chunk, 1), time_block),
+                pl.BlockSpec((chan.shape[0], width), lambda i, s: (0, s[0])),
+                fixed((planes, model // planes, both)),
+                fixed(keep.shape),
+                fixed(got.shape),
+            ]
+            + [pl.BlockSpec(memory_space=pl.ANY)] * len(ahead_of),
+            out_specs=[
+                pl.BlockSpec((2, None, rows, width), token_block),
+                pl.BlockSpec((2, None, rows, model), token_block),
+            ]
+            + [spec] * 7
+            + [fixed((width, columns))],
+            scratch_shapes=[
+                pltpu.VMEM((2, chips, rows, model), jnp.bfloat16),
+                pltpu.VMEM((chunk + 8, width), jnp.float32),
+                pltpu.VMEM((8, width), jnp.float32),
+            ],
+        ),
+        out_shape=[
+            jax.ShapeDtypeStruct((2, chips, rows, width), jnp.bfloat16),
+            jax.ShapeDtypeStruct((2, chips, rows, model), jnp.bfloat16),
+            saved(jnp.bfloat16),
+            saved(jnp.float32),
+            saved(jnp.bfloat16),
+            saved(jnp.float32),
+            saved(jnp.float32),
+            saved(jnp.float32),
+            saved(jnp.bfloat16),
+            jax.ShapeDtypeStruct((width, columns), jnp.bfloat16),
+        ],
+        compiler_params=pltpu.CompilerParams(vmem_limit_bytes=48 * 1024 * 1024),
+        name="mix_forward",
+    )(place, *near, *far, age, chan, pack, keep, got, *ahead_of)
+
+
+def mix_backward_kernel(chips, *refs):
+    place = refs[0][0]
+    blocks = refs[1 : 1 + 2 * chips]
+    (
+        age_ref,
+        chan_ref,
+        weights_ref,
+        branch_ref,
+        gelu_pre_ref,
+        conv_ref,
+        decay_pre_ref,
+        input_pre_ref,
+        prior_ref,
+        low_ref,
+        both_ref,
+        small_ref,
+        gate_grads_ref,
+        out_grad_ref,
+        held,
+        ahead,
+        carry,
+    ) = refs[1 + 2 * chips :]
+    step = pl.program_id(0)
+    chip, core = place // 2, place % 2
+    rows, width = branch_ref.shape
+    model = held.shape[-1]
+
+    @pl.when(step == 0)
+    def _():
+        carry[...] = jnp.zeros_like(carry)
+        ahead[:, pl.ds(rows, 8), :] = jnp.zeros((3, 8, width), jnp.float32)
+        small_ref[...] = jnp.zeros_like(small_ref)
+        gate_grads_ref[...] = jnp.zeros_like(gate_grads_ref)
+        out_grad_ref[...] = jnp.zeros_like(out_grad_ref)
+        for k in range(chips):
+            held[0, k] = blocks[k][...]
+            held[1, k] = blocks[chips + k][...]
+
+    @pl.when(step > 0)
+    def _():
+        ahead[:, pl.ds(rows, 8), :] = ahead[:, pl.ds(0, 8), :]
+
+    turn = (chips - 1 - step) ^ chip
+    mixer_grad = jnp.concatenate([held[0, turn], held[1, turn]], axis=0)
+    merged_grad = in_time(dot_nt(mixer_grad, weights_ref[:, :model]), core)
+    age = age_ref[...]
+    gelu_out, slope = gelu_parts(gelu_pre_ref[...])
+    state_grad = (merged_grad * gelu_out).astype(jnp.bfloat16).astype(jnp.float32)
+    low = low_ref[...].astype(jnp.float32)
+    gelu_pre_grad = merged_grad * low * slope
+    merged = in_time(low * gelu_out, core).astype(jnp.bfloat16)
+    out_grad_ref[...] += dot_tn(mixer_grad, merged)
+    reset = age < 0.5
+    sig_d = sigmoid(decay_pre_ref[...])
+    sig_i = sigmoid(input_pre_ref[...])
+    soft = chan_ref[7:8, :]
+    log_a = -8.0 * sig_d * soft
+    a = jnp.exp(log_a)
+    open_room = one_less_exp(2.0 * log_a)
+    room = jnp.maximum(open_room, mult_floor)
+    root = jnp.sqrt(room)
+    factor = jnp.where(reset, 1.0, root)
+    decay = jnp.where(reset, 0.0, a)
+    conv_low = conv_ref[...]
+    conv = conv_low.astype(jnp.float32)
+    row = lax.broadcasted_iota(jnp.int32, (rows, width), 0)
+    next_decay = jnp.where(row == rows - 1, carry[0:1, :], pltpu.roll(decay, rows - 1, 0))
+    grown, carried = scan_rows(next_decay, state_grad, True)
+    carried = carried + grown * carry[1:2, :]
+    carry[0:1, :] = decay[0:1, :]
+    carry[1:2, :] = carried[0:1, :]
+    decay_grad = carried * prior_ref[...]
+    input_pre_grad = carried * conv * factor * sig_i * (1.0 - sig_i)
+    gate_conv_grad = carried * sig_i * factor
+    room_grad = jnp.where(open_room > mult_floor, carried * sig_i * conv * 0.5 / root, 0.0)
+    log_a_grad = jnp.where(reset, 0.0, decay_grad * a - 2.0 * a * a * room_grad)
+    sig_grad = log_a_grad * sig_d
+    decay_pre_grad = -8.0 * soft * sig_grad * (1.0 - sig_d)
+    decay_low = decay_pre_grad.astype(jnp.bfloat16)
+    input_low = input_pre_grad.astype(jnp.bfloat16)
+    conv_grad = (
+        gate_conv_grad
+        + dot_nt(decay_low, weights_ref[:, model : model + width])
+        + dot_nt(input_low, weights_ref[:, model + width :])
+    )
+    gate_grads_ref[0] += dot_tn(decay_low, conv_low)
+    gate_grads_ref[1] += dot_tn(input_low, conv_low)
+    branch = branch_ref[...].astype(jnp.float32)
+    branch_grad = chan_ref[0:1, :] * conv_grad
+    small_ref[0:1, :] += jnp.sum(conv_grad * branch, axis=0, keepdims=True)
+    for k in range(1, 4):
+        ahead[k - 1, pl.ds(0, rows), :] = conv_grad * jnp.where(age >= k, 1.0, 0.0)
+        shifted = ahead[k - 1, pl.ds(k, rows), :]
+        branch_grad = branch_grad + chan_ref[k : k + 1, :] * shifted
+        small_ref[k : k + 1, :] += jnp.sum(shifted * branch, axis=0, keepdims=True)
+    small_ref[4:5, :] += jnp.sum(conv_grad, axis=0, keepdims=True)
+    small_ref[5:6, :] += jnp.sum(decay_low.astype(jnp.float32), axis=0, keepdims=True)
+    small_ref[6:7, :] += jnp.sum(input_low.astype(jnp.float32), axis=0, keepdims=True)
+    small_ref[7:8, :] += 8.0 * chan_ref[8:9, :] * jnp.sum(sig_grad, axis=0, keepdims=True)
+    by_core(jnp.concatenate([branch_grad, gelu_pre_grad], axis=1), both_ref, core)
+
+
+def mix_backward(place, near, far, age, chan, weights, saved):
+    chips = len(near)
+    rows, model = near[0].shape
+    width, columns = weights.shape
+    chunk = 2 * rows
+    last = chips - 1
+    time_block = lambda i, s: (last - i, 0)
+    token_block = lambda i, s: (0, (last - i) ^ (s[0] // 2), 0, 0)
+    spec = pl.BlockSpec((chunk, width), time_block)
+    fixed = lambda shape: pl.BlockSpec(shape, lambda i, s: (0,) * len(shape))
+    return pl.pallas_call(
+        functools.partial(mix_backward_kernel, chips),
+        grid_spec=pltpu.PrefetchScalarGridSpec(
+            num_scalar_prefetch=1,
+            grid=(chips,),
+            in_specs=[fixed((rows, model))] * (2 * chips)
+            + [
+                pl.BlockSpec((chunk, 1), time_block),
+                pl.BlockSpec((chan.shape[0], width), lambda i, s: (0, s[0])),
+                fixed((width, columns)),
+            ]
+            + [spec] * 7,
+            out_specs=[
+                pl.BlockSpec((2, None, rows, 2 * width), token_block),
+                fixed((8, width)),
+                fixed((2, width, width)),
+                fixed((model, width)),
+            ],
+            scratch_shapes=[
+                pltpu.VMEM((2, chips, rows, model), jnp.bfloat16),
+                pltpu.VMEM((3, chunk + 8, width), jnp.float32),
+                pltpu.VMEM((8, width), jnp.float32),
+            ],
+        ),
+        out_shape=[
+            jax.ShapeDtypeStruct((2, chips, rows, 2 * width), jnp.bfloat16),
+            jax.ShapeDtypeStruct((8, width), jnp.float32),
+            jax.ShapeDtypeStruct((2, width, width), jnp.float32),
+            jax.ShapeDtypeStruct((model, width), jnp.float32),
+        ],
+        compiler_params=pltpu.CompilerParams(vmem_limit_bytes=48 * 1024 * 1024),
+        name="mix_backward",
+    )(place, *near, *far, age, chan, weights, *saved)
+
+
+def unit_kernel(chips, *refs):
+    blocks, cots = refs[: 2 * chips], refs[2 * chips : 4 * chips]
+    pack_ref, pair_ref, hidden_ref, grads_ref, down_ref, normed, cot, gate_up, down = refs[4 * chips :]
+    rows = blocks[0].shape[0]
+    planes, tall, near_model = pack_ref.shape
+    both = pair_ref.shape[1]
+    part = both // 2
+    span = part // planes
+    side = near_model // 2
+    for k in range(2 * chips):
+        normed[pl.ds(k * rows, rows), :] = blocks[k][...]
+        cot[pl.ds(k * rows, rows), :] = cots[k][...]
+    for z in range(planes):
+        for j in range(3):
+            gate_up[pl.ds(z * near_model, near_model), pl.ds(j * near_model, near_model)] = pack_ref[
+                z, pl.ds(j * near_model, near_model), :
+            ]
+        for j in range(planes):
+            down[pl.ds(z * span, span), pl.ds(j * near_model, near_model)] = pack_ref[
+                z, pl.ds(3 * near_model + j * span, span), :
+            ]
+    down[pl.ds(part, side), :] = down[pl.ds(part - side, side), :]
+    down_ref[...] = down[pl.ds(0, part), :]
+    chunk = 2 * rows
+
+    def tokens_step(i, nothing):
+        here = pl.ds(pl.multiple_of(i * chunk, chunk), chunk)
+        pre = dot_nn(normed[here, :], gate_up[...])
+        hidden_grad = dot_nt(cot[here, :], down[...])
+        gate, mid, up = pre[:, :near_model], pre[:, near_model:-near_model], pre[:, -near_model:]
+        value, slope = gelu_parts(gate)
+        above = hidden_grad[:, :near_model]
+        hidden_ref[here, pl.ds(0, near_model)] = (value * up).astype(jnp.bfloat16)
+        pair_ref[here, pl.ds(0, near_model)] = (above * up * slope).astype(jnp.bfloat16)
+        pair_ref[here, pl.ds(2 * near_model, near_model)] = (above * value).astype(jnp.bfloat16)
+        first = lax.broadcasted_iota(jnp.int32, mid.shape, 1) < side
+        turned = pltpu.roll(mid, side, 1)
+        gate, up = jnp.where(first, mid, turned), jnp.where(first, turned, mid)
+        value, slope = gelu_parts(gate)
+        above = hidden_grad[:, near_model:]
+        hidden_ref[here, pl.ds(near_model, side)] = (value * up)[:, :side].astype(jnp.bfloat16)
+        pair_ref[here, pl.ds(near_model, near_model)] = jnp.where(
+            first, above * up * slope, above * value
+        ).astype(jnp.bfloat16)
+        return nothing
+
+    lax.fori_loop(0, chips, tokens_step, 0)
+    for z in range(planes):
+        here = pl.ds(z * near_model, near_model)
+        grad = dot_tn(normed[:, here], pair_ref[...]).astype(jnp.bfloat16)
+        for j in range(3):
+            grads_ref[z, pl.ds(j * near_model, near_model), :] = grad[
+                :, j * near_model : (j + 1) * near_model
+            ]
+        grad = dot_tn(hidden_ref[...], cot[:, here]).astype(jnp.bfloat16)
+        for j in range(planes):
+            grads_ref[j, pl.ds(3 * near_model + z * span, span), :] = grad[
+                j * span : (j + 1) * span
+            ]
+
+
+def unit_back_and_forth(near, far, cot_near, cot_far, pack, part):
+    chips = len(near)
+    rows, model = near[0].shape
+    length = 2 * chips * rows
+    _, _, near_model = pack.shape
+    bf16 = jnp.bfloat16
+    whole = pl.BlockSpec(memory_space=pltpu.VMEM)
+    return pl.pallas_call(
+        functools.partial(unit_kernel, chips),
+        in_specs=[whole] * (4 * chips + 1),
+        out_specs=[whole] * 4,
+        scratch_shapes=[
+            pltpu.VMEM((length, model), bf16),
+            pltpu.VMEM((length, model), bf16),
+            pltpu.VMEM((model, 2 * part), bf16),
+            pltpu.VMEM((part + near_model // 2, model), bf16),
+        ],
+        out_shape=[
+            jax.ShapeDtypeStruct((length, 2 * part), bf16),
+            jax.ShapeDtypeStruct((length, part), bf16),
+            jax.ShapeDtypeStruct(pack.shape, bf16),
+            jax.ShapeDtypeStruct((part, model), bf16),
+        ],
+        compiler_params=pltpu.CompilerParams(vmem_limit_bytes=58 * 1024 * 1024),
+        name="unit_back_and_forth",
+    )(*near, *far, *cot_near, *cot_far, pack)
+
+
+def pair_back_kernel(pair_ref, pack_ref, out_ref):
+    near_model = pack_ref.shape[1]
+    total = dot_nt(pair_ref[:, :near_model], pack_ref[:near_model, :])
+    for j in (1, 2):
+        here = slice(j * near_model, (j + 1) * near_model)
+        total = total + dot_nt(pair_ref[:, here], pack_ref[here, :])
+    out_ref[...] = total.astype(out_ref.dtype)
+
+
+def pair_back(pair, pack, half):
+    length, both = pair.shape
+    planes, _, near_model = pack.shape
+    rows = length // 2
+    return pl.pallas_call(
+        pair_back_kernel,
+        grid=(planes,),
+        in_specs=[
+            pl.BlockSpec((rows, both), lambda z: (half, 0)),
+            pl.BlockSpec((None, 3 * near_model, near_model), lambda z: (z, 0, 0)),
+        ],
+        out_specs=pl.BlockSpec((rows, near_model), lambda z: (0, z)),
+        out_shape=jax.ShapeDtypeStruct((rows, planes * near_model), jnp.bfloat16),
+        compiler_params=pltpu.CompilerParams(vmem_limit_bytes=32 * 1024 * 1024),
+        name="pair_back",
+    )(pair, pack)
+
+
+def norm_back(values, scale, gain, grad):
+    inner = jnp.mean(gain * grad * values, axis=-1, keepdims=True)
+    return scale * gain * grad - values * (scale * scale * scale) * inner
+
+
+def narrow_shards(
+    tokens,
+    cotangent,
+    doc_starts,
+    mix_gain,
+    input_proj,
+    gelu_proj,
+    conv_taps,
+    conv_bias,
+    decay_gate,
+    decay_bias,
+    input_gate,
+    input_bias,
+    decay_param,
+    output_proj,
+    mlp_gain,
+    mlp_gate,
+    mlp_up,
+    mlp_down,
+):
+    f32, bf16 = jnp.float32, jnp.bfloat16
+    devices, planes = lax.axis_size("seq"), lax.axis_size("fsdp")
+    chips = devices // 2
+    place = lax.axis_index("seq")
+    chip, core = place // 2, place % 2
+    rows, model = tokens.shape[1:]
+    length = rows * devices
+    channels = conv_taps.shape[1]
+    width = decay_gate.shape[1]
+    deep = mlp_gate.shape[1]
+    heads = output_proj.shape[0] // width
+    piece = width // devices
+    span = deep // (planes * devices)
+    part = deep // devices
+    near_model = model // planes
+
+    def along_fsdp(x):
+        return lax.all_gather(x, "fsdp", axis=0, tiled=True)
+
+    def columns(x, start, size):
+        return lax.dynamic_slice_in_dim(x, start, size, axis=1)
+
+    def own_rows(x):
+        mine = lax.dynamic_slice_in_dim(
+            x.reshape(heads, width, x.shape[1]), place * piece, piece, 1
+        )
+        return jnp.swapaxes(mine.reshape(heads, piece, -1, 2 * width), 1, 2)
+
+    rowset = jnp.concatenate(
+        [own_rows(output_proj), own_rows(jnp.concatenate([decay_gate, input_gate], axis=1))], axis=1
+    ).reshape(-1, 2 * width)
+    in_own = jnp.concatenate(
+        [columns(input_proj, place * width, width), columns(gelu_proj, place * width, width)],
+        axis=1,
+    )
+    mix_pack = lax.all_gather(jnp.concatenate([in_own, rowset], axis=0), "fsdp", axis=0)
+
+    def own_spans(x):
+        return jnp.concatenate(
+            [columns(x, z * (deep // planes) + place * span, span) for z in range(planes)], axis=1
+        )
+
+    gate_own, up_own = own_spans(mlp_gate), own_spans(mlp_up)
+    down_own = lax.dynamic_slice_in_dim(mlp_down, place * span, span, 0)
+    unit_pack = lax.all_gather(
+        jnp.concatenate(
+            [
+                gate_own[:, :near_model],
+                jnp.concatenate([gate_own[:, near_model:], up_own[:, near_model:]], axis=1),
+                up_own[:, :near_model],
+                jnp.swapaxes(down_own.reshape(span, planes, near_model), 0, 1).reshape(
+                    planes * span, near_model
+                ),
+            ],
+            axis=0,
+        ),
+        "fsdp",
+        axis=0,
+    )
+
+    values = tokens[0].astype(f32)
+    scale1 = lax.rsqrt(jnp.mean(values * values, axis=-1, keepdims=True) + norm_eps)
+    normed_near, normed_far = gather_blocks((values * scale1 * mix_gain).astype(bf16))
+    out_grad = cotangent[0]
+    cot_near, cot_far = gather_blocks(out_grad)
+
+    positions = jnp.arange(length, dtype=jnp.int32)
+    starts = doc_starts[0]
+    begin = jnp.max(jnp.where(starts[None, :] <= positions[:, None], starts[None, :], 0), axis=1)
+    age = (positions - begin).astype(f32)[:, None]
+    chan = jnp.concatenate(
+        [
+            conv_taps,
+            conv_bias[None],
+            decay_bias[None],
+            input_bias[None],
+            jax.nn.softplus(-decay_param)[None],
+            jax.nn.sigmoid(-decay_param)[None],
+            jnp.zeros((7, channels), f32),
+        ],
+        axis=0,
+    )
+    place_arg = place.astype(jnp.int32)[None]
+
+    keep, got = exchange(mix_pack[:, near_model:].reshape(chips, 2, -1, 2 * width), chip, core)
+    merged, normed, *saved, weights = mix_forward(
+        place_arg, normed_near, normed_far, age, chan, mix_pack, keep, got, cot_near + cot_far
+    )
+    out_weights = weights[:, :model]
+    in_weights = mix_pack[:, :near_model].reshape(model, 2 * width)
+    far = dot_nn(merged[1].reshape(-1, width), out_weights).astype(bf16)
+    near = dot_nn(merged[0].reshape(-1, width), out_weights)
+    middle = values + scatter_blocks(
+        near.reshape(chips, rows, model), far.reshape(chips, rows, model)
+    )
+
+    scale2 = lax.rsqrt(jnp.mean(middle * middle, axis=-1, keepdims=True) + norm_eps)
+    near, far = gather_blocks((middle * scale2 * mlp_gain).astype(bf16))
+    pair, hidden, unit_grads, down = unit_back_and_forth(
+        near, far, cot_near, cot_far, unit_pack, part
+    )
+    unit_sum = lax.psum_scatter(unit_grads, "fsdp", scatter_dimension=0, tiled=False)
+    far = pair_back(pair, unit_pack, 1)
+    near = pair_back(pair, unit_pack, 0)
+    normed2_grad = scatter_blocks(
+        near.reshape(chips, rows, model), far.reshape(chips, rows, model)
+    )
+    split = length // 2
+
+    mlp_gain_term = jnp.sum(normed2_grad * middle * scale2, axis=0)
+    middle_grad = out_grad.astype(f32) + norm_back(middle, scale2, mlp_gain, normed2_grad)
+    near, far = gather_blocks(middle_grad.astype(bf16))
+
+    both, small, gate_grads, out_w_grad = mix_backward(
+        place_arg, near, far, age, chan, weights, saved
+    )
+    normed = normed.reshape(length, model)
+    both = both.reshape(length, 2 * width)
+    far = dot_nt(both[split:], in_weights).astype(bf16)
+    near = dot_nt(both[:split], in_weights)
+    normed_grad = scatter_blocks(
+        near.reshape(chips, rows, model), far.reshape(chips, rows, model)
+    )
+    in_grad = dot_tn(normed, both)
+    turned = jnp.concatenate(
+        [
+            out_w_grad.astype(bf16).reshape(devices, model // devices, width),
+            gate_grads[0].astype(bf16).reshape(devices, piece, width),
+            gate_grads[1].astype(bf16).reshape(devices, piece, width),
+        ],
+        axis=1,
+    )
+    tall = turned.shape[1]
+    keep, got = exchange(turned.reshape(chips, 2, tall, width), chip, core)
+    home = reorder([keep[k] for k in range(chips)], chip)
+    away = reorder([got[k] for k in range(chips)], chip)
+    by_head = [
+        jnp.concatenate(
+            [jnp.where(core == 0, home[k], away[k]), jnp.where(core == 0, away[k], home[k])], axis=1
+        )
+        for k in range(chips)
+    ]
+    share = chips // planes
+    row_pack = jnp.stack(
+        [jnp.concatenate(by_head[z * share : (z + 1) * share], axis=1) for z in range(planes)]
+    )
+    grad_pack = jnp.concatenate(
+        [in_grad.astype(bf16).reshape(planes, near_model, 2 * width), row_pack], axis=1
+    )
+    grad_pack, unit_sum = lax.optimization_barrier((grad_pack, unit_sum))
+    mix_sum = lax.psum_scatter(grad_pack, "fsdp", scatter_dimension=0, tiled=False).astype(f32)
+    input_proj_grad = mix_sum[:near_model, :width]
+    gelu_proj_grad = mix_sum[:near_model, width:]
+    turned_sum = mix_sum[near_model:].T
+    slim = model // devices
+    output_proj_grad = turned_sum[:, :slim]
+    decay_gate_grad = turned_sum[:, slim : slim + piece]
+    input_gate_grad = turned_sum[:, slim + piece :]
+
+    first, mid, last, bottom = (
+        unit_sum[:near_model],
+        unit_sum[near_model : 2 * near_model],
+        unit_sum[2 * near_model : 3 * near_model],
+        unit_sum[3 * near_model :],
+    )
+    side = near_model // 2
+    gate_sum = jnp.concatenate([first, mid[:, :side]], axis=1)
+    up_sum = jnp.concatenate([last, mid[:, side:]], axis=1)
+    mlp_gate_grad, mlp_up_grad, mlp_down_grad = final_exchange(
+        jnp.stack([gate_sum.T, up_sum.T]).reshape(2, planes, span, near_model).swapaxes(0, 1),
+        bottom.reshape(planes, span, near_model),
+        chip,
+        core,
+        chips,
+    )
+
+    held = lax.optimization_barrier((hidden, down, both))
+    hidden, down = held[:2]
+    far = dot_nn(hidden[split:], down).astype(bf16)
+    near = dot_nn(hidden[:split], down)
+    mixed = (
+        middle
+        + scatter_blocks(near.reshape(chips, rows, model), far.reshape(chips, rows, model))
+    ).astype(bf16)
+
+    values_part = norm_back(values, scale1, mix_gain, normed_grad)
+    tokens_grad = (middle_grad + values_part).astype(bf16)
+    mix_gain_term = jnp.sum(in_grad * in_weights.astype(f32), axis=1) / mix_gain
+    where_mine = (jnp.arange(devices) == place)[None, :, None]
+    spread = jnp.where(where_mine, small[:, None, :], 0.0).reshape(8, channels)
+    gains = jnp.pad(jnp.stack([mix_gain_term, mlp_gain_term]), ((0, 0), (0, channels - model)))
+    sums = total_over(jnp.concatenate([spread, gains], axis=0), ("fsdp", "seq"))
+    return (
+        mixed[None],
+        tokens_grad[None],
+        sums[8, :model],
+        input_proj_grad,
+        gelu_proj_grad,
+        sums[:4],
+        sums[4],
+        decay_gate_grad,
+        sums[5],
+        input_gate_grad,
+        sums[6],
+        sums[7],
+        output_proj_grad,
+        sums[9, :model],
+        mlp_gate_grad,
+        mlp_up_grad,
+        mlp_down_grad,
+    )
+
+
+def final_exchange(gate_up_sum, down_sum, chip, core, chips):
+    f32 = jnp.float32
+    span, cols = down_sum.shape[1:]
+    half = cols // 2
+    sent = jnp.concatenate([gate_up_sum, down_sum[:, None]], axis=1)
+    parts = [lax.dynamic_index_in_dim(sent, chip ^ k, 0, keepdims=False) for k in range(chips)]
+    got = [parts[0]] + [chip_swap(parts[k], k) for k in range(1, chips)]
+    turn = core ^ (chip // 2)
+    low, high = jnp.stack(got[:2]), jnp.stack(got[2:])
+    keep_gu = jnp.where(turn == 0, low[:, :2], high[:, :2])
+    give_gu = jnp.where(turn == 0, high[:, :2], low[:, :2])
+    downs = jnp.stack([g[2] for g in got])
+    keep_d = jnp.where(core == 0, downs[:, :, :half], downs[:, :, half:])
+    give_d = jnp.where(core == 0, downs[:, :, half:], downs[:, :, :half])
+    got_gu, got_d = core_swap(give_gu), core_swap(give_d)
+    home = reorder([keep_gu[0], keep_gu[1]], chip & 1)
+    away = reorder([got_gu[0], got_gu[1]], chip & 1)
+    blocks = []
+    for x in range(2):
+        blocks.append(jnp.where(core == 0, home[x], away[x]))
+        blocks.append(jnp.where(core == 0, away[x], home[x]))
+    gate_up = jnp.concatenate(blocks, axis=1).astype(f32)
+    home = reorder([keep_d[k] for k in range(chips)], chip)
+    away = reorder([got_d[k] for k in range(chips)], chip)
+    blocks = []
+    for k in range(chips):
+        blocks.append(jnp.where(core == 0, home[k], away[k]))
+        blocks.append(jnp.where(core == 0, away[k], home[k]))
+    return gate_up[0].T, gate_up[1].T, jnp.concatenate(blocks, axis=0).astype(f32)
+
+
+def choose_plan(mesh):
+    devices, planes = mesh.shape["seq"], mesh.shape["fsdp"]
+
+    def plan(*args):
+        channels, width = args[6].shape[1], args[8].shape[1]
+        if channels == width * devices and devices == 2 * planes and planes == 4:
+            return narrow_shards(*args)
+        return wide_shards(*args)
+
+    return plan
+
+
 def solution(mesh):
     return jax.shard_map(
-        shards,
+        choose_plan(mesh),
         mesh=mesh,
         in_specs=(
             P("fsdp", "seq", None),

time: 2820 us -> 408 us (0.14)
  waiting for transfers between devices: 2310 us -> 185 us
  local copies, waits for them, and re-layouts: 206 us -> 46.7 us
  matrix products: 160 us -> 12.2 us
  Pallas kernels: 0 us -> 56.8 us
  blocking collectives: 31.5 us -> 0 us
  other arithmetic: 66.8 us -> 38.1 us
    reduce_scatter x16 -> x2, waiting for transfers between devices: 1170 us -> 5.11 us  [the longest x1 5.11 us: narrow_shards(): lax.psum_scatter(grad_pack, 'fsdp', scatter_dimension=0, tiled=False)]
    all_gather x8 -> x2, waiting for transfers between devices: 993 us -> 34.6 us  [the longest x1 34.6 us: narrow_shards(): lax.all_gather(jnp.concatenate([in_own, rowset], axis=0), 'fsdp', axis=0)]
    dot_general x24 -> x7, matrix products: 160 us -> 12.2 us  [the longest x4 6.88 us: dot_nn(): lax.dot_general(a, b, (((1,), (0,)), ((), ())), preferred_element_type=jn...]
    ppermute x2 -> x62, waiting for transfers between devices: 2.12 us -> 145 us  [the longest x33 125 us: chip_swap(): return lax.ppermute(x, 'seq', [(i, i ^ 2 * k) for i in range(devices)])]
    psum x1 -> x0, waiting for transfers between devices: 122 us -> none  [shards(): lax.psum((mix_gain_term, taps_term, conv_bias_term, jnp.sum(dpre_low.asty...]
    slice x129 -> x18, local copies, waits for them, and re-layouts: 132 us -> 11.7 us  [the longest x1 1.51 us: narrow_shards(): in_weights = mix_pack[:, :near_model].reshape(model, 2 * width)]
    pallas_call x0 -> x5, Pallas kernels: none -> 56.8 us  [the longest x1 22 us: unit_back_and_forth(): pl.pallas_call(functools.partial(unit_kernel, chips), in_specs=[whole] *...]
    ppermute x2 -> x62, starting transfers between devices: 3.25 us -> 47 us  [the longest x33 38.9 us: chip_swap(): return lax.ppermute(x, 'seq', [(i, i ^ 2 * k) for i in range(devices)])]
  transfers between devices with their start and end apart: 31 -> 66, of which waited for: 27 -> 35; matrix products, arithmetic and copies ran while one was open for 9% -> 18% of each run, Pallas kernels for 0% -> 8%
where the time goes in v1:
time: 408 us; the launch traced here: 401 us
  waiting for transfers between devices  185 us (45%)
  Pallas kernels  56.8 us (14%)
  starting transfers between devices  47.7 us (12%)
  local copies, waits for them, and re-layouts  46.7 us (11%)
  other arithmetic  38.1 us (9%)
  between operations  15.2 us (4%)
  matrix products  12.2 us (3%)
    ppermute x33, waiting for transfers between devices, chip_swap(): return lax.ppermute(x, 'seq', [(i, i ^ 2 * k) for i in range(devices)])  125 us
    ppermute x33, starting transfers between devices, chip_swap(): return lax.ppermute(x, 'seq', [(i, i ^ 2 * k) for i in range(devices)])  38.9 us
    all_gather x1, waiting for transfers between devices, narrow_shards(): lax.all_gather(jnp.concatenate([in_own, rowset], axis=0), 'fsdp', axis=0)  34.6 us
    pallas_call x1, Pallas kernels, unit_back_and_forth(): pl.pallas_call(functools.partial(unit_kernel, chips), in_specs=[whole] *...  22 us
    ppermute x5, waiting for transfers between devices, total_over(): x = x + lax.ppermute(x, axis, [(i, i ^ bit) for i in range(devices)])  14.7 us
    pallas_call x1, Pallas kernels, mix_backward(): pl.pallas_call(functools.partial(mix_backward_kernel, chips), grid_spec=p...  14.3 us
    unnamed x134, local copies, waits for them, and re-layouts  13.8 us
    pallas_call x1, Pallas kernels, mix_forward(): pl.pallas_call(functools.partial(mix_forward_kernel, chips), grid_spec=pl...  12.2 us
  transfers between devices with their start and end apart: 66, of which 35 were waited for; matrix products, arithmetic and copies ran while one was open for 18% of the time, Pallas kernels for 8%

profile of v1, /device:TPU:0, one launch (start us, length us, event | category | flops | bytes accessed | tf_op | source)
XLA Modules:
  0.0 401.5 jit_solution(15039664069086299634)
XLA Ops:
  22.8 11.6 %fusion.8 = bf16[1728,384]{1,0:T(8,128)(2,1)} fusion(bf16[384,144]{1,0:T(8,128)(2,1)S(1)} %get-tuple-element.165, bf16[384,144]{1,0:T(8,128)(2,1)S(1)} %get-tuple-element.166, bf16[384,144]{1,0:T(8,128)(2,1)S(1)} %get-tuple-element.167, bf16[384,144]{1,0:T(8,128)(2,1)S(1)} %get-tuple-element.164, bf16[384,144]{1,0:T(8,128)(2,1)S(1)} %get-tuple-element.162, ...), kind=kLoop, calls=%fused_computation.35 | loop fusion | flops 19243008 | bytes 2654208 | tf_op jit(solution)/shard_map/concatenate | solution.py:883
  36.4 3.5 collective-permute-start.2
  40.5 34.6 %all-gather.5.cloned.1.call-done = bf16[2560,512]{1,0:T(8,128)(2,1)} async-done(((bf16[640,512]{1,0:T(8,128)(2,1)}), bf16[2560,512]{1,0:T(8,128)(2,1)}) %all-gather.5.cloned.1.call-update) | async-done | bytes 2621456 | tf_op jit(solution)/shard_map/all_gather | solution.py:873
  83.8 3.7 collective-permute-done.9
  88.9 4.2 %collective-permute-done.8 = bf16[2,128,512]{2,1,0:T(8,128)(2,1)S(1)} collective-permute-done((bf16[2,128,512]{2,1,0:T(8,128)(2,1)S(1)}, bf16[2,128,512]{2,1,0:T(8,128)(2,1)S(1)}, u32[]{:S(2)}, u32[]{:S(2)}) %collective-permute-start.8) | collective-permute-done | bytes 262176 | tf_op jit(solution)/shard_map/ppermute | solution.py:292
  97.0 4.5 %collective-permute-done.13.refs_17_.refs_11_ = bf16[128,1536]{1,0:T(8,128)(2,1)S(1)} collective-permute-done((bf16[128,1536]{1,0:T(8,128)(2,1)S(1)}, bf16[128,1536]{1,0:T(8,128)(2,1)S(1)}, u32[]{:S(2)}, u32[]{:S(2)}) %collective-permute-start.13) | collective-permute-done | bytes 393248 | tf_op jit(solution)/shard_map/ppermute | solution.py:292
  102.7 6.0 %collective-permute-done.12.refs_16_.refs_10_ = bf16[128,1536]{1,0:T(8,128)(2,1)S(1)} collective-permute-done((bf16[128,1536]{1,0:T(8,128)(2,1)S(1)}, bf16[128,1536]{1,0:T(8,128)(2,1)S(1)}, u32[]{:S(2)}, u32[]{:S(2)}) %collective-permute-start.12) | collective-permute-done | bytes 393248 | tf_op jit(solution)/shard_map/ppermute | solution.py:292
  115.3 12.2 %mix_forward.1 = (bf16[2,4,128,256]{3,2,1,0:T(8,128)(2,1)}, bf16[2,4,128,1536]{3,2,1,0:T(8,128)(2,1)}, bf16[1024,256]{1,0:T(8,128)(2,1)}, f32[1024,256]{1,0:T(8,...) custom-call(s32[1]{0:T(128)} %bitcast.1.refs_0_, ...), custom_call_target="tpu_custom_call" | custom-call | tf_op jit(solution)/shard_map/mix_forward/pallas_call | solution.py:507
  138.1 8.5 %collective-permute-done.19 = bf16[128,1536]{1,0:T(8,128)(2,1)S(1)} collective-permute-done((bf16[128,1536]{1,0:T(8,128)(2,1)S(1)}, bf16[128,1536]{1,0:T(8,128)(2,1)S(1)}, u32[]{:S(2)}, u32[]{:S(2)}) %collective-permute-start.19) | collective-permute-done | bytes 393248 | tf_op jit(solution)/shard_map/ppermute | solution.py:292
  146.6 8.6 %collective-permute-done.21 = bf16[128,1536]{1,0:T(8,128)(2,1)S(1)} collective-permute-done((bf16[128,1536]{1,0:T(8,128)(2,1)S(1)}, bf16[128,1536]{1,0:T(8,128)(2,1)S(1)}, u32[]{:S(2)}, u32[]{:S(2)}) %collective-permute-start.21) | collective-permute-done | bytes 393248 | tf_op jit(solution)/shard_map/ppermute | solution.py:292
  161.2 9.5 %collective-permute-done.24.refs_3_ = bf16[128,1536]{1,0:T(8,128)(2,1)S(1)} collective-permute-done((bf16[128,1536]{1,0:T(8,128)(2,1)S(1)}, bf16[128,1536]{1,0:T(8,128)(2,1)S(1)}, u32[]{:S(2)}, u32[]{:S(2)}) %collective-permute-start.24) | collective-permute-done | bytes 393248 | tf_op jit(solution)/shard_map/ppermute | solution.py:292
  170.7 5.4 %collective-permute-done.23.refs_2_ = bf16[128,1536]{1,0:T(8,128)(2,1)S(1)} collective-permute-done((bf16[128,1536]{1,0:T(8,128)(2,1)S(1)}, bf16[128,1536]{1,0:T(8,128)(2,1)S(1)}, u32[]{:S(2)}, u32[]{:S(2)}) %collective-permute-start.23) | collective-permute-done | bytes 393248 | tf_op jit(solution)/shard_map/ppermute | solution.py:292
  178.6 22.0 %unit_back_and_forth.1 = (bf16[1024,1152]{1,0:T(8,128)(2,1)}, bf16[1024,576]{1,0:T(8,128)(2,1)}, bf16[4,1728,384]{2,1,0:T(8,128)(2,1)}, bf16[576,1536]{1,0:T(8,128)(2,1)}) custom-call(bf16[128,1536]{1,0:T(8,128)(2,1)} %copy-done.30, bf16[128,1536]{1,0:T(8,128)(2,1)} %copy-done.39, bf16[128,1536]{1,0:T(8,128)(2,1)} %copy-done.38, ...), custom_call_target="tpu_custom_call" | custom-call | tf_op jit(solution)/shard_map/unit_back_and_forth/pallas_call | solution.py:765
  202.2 4.4 %pair_back.3 = bf16[512,1536]{1,0:T(8,128)(2,1)} custom-call(bf16[1024,1152]{1,0:T(8,128)(2,1)S(1)} %copy-done.4, bf16[4,1728,384]{2,1,0:T(8,128)(2,1)S(1)} %bitcast.272), custom_call_target="tpu_custom_call" | custom-call | tf_op jit(solution)/shard_map/pair_back/pallas_call | solution.py:799
  210.1 3.4 copy-done.3
  213.5 4.0 pair_back.2
  227.5 5.9 %collective-permute-done.34 = bf16[128,1536]{1,0:T(8,128)(2,1)S(1)} collective-permute-done((bf16[128,1536]{1,0:T(8,128)(2,1)S(1)}, bf16[128,1536]{1,0:T(8,128)(2,1)S(1)}, u32[]{:S(2)}, u32[]{:S(2)}) %collective-permute-start.34) | collective-permute-done | bytes 393248 | tf_op jit(solution)/shard_map/ppermute | solution.py:292
  233.6 7.9 %collective-permute-done.36 = bf16[128,1536]{1,0:T(8,128)(2,1)S(1)} collective-permute-done((bf16[128,1536]{1,0:T(8,128)(2,1)S(1)}, bf16[128,1536]{1,0:T(8,128)(2,1)S(1)}, u32[]{:S(2)}, u32[]{:S(2)}) %collective-permute-start.36) | collective-permute-done | bytes 393248 | tf_op jit(solution)/shard_map/ppermute | solution.py:292
  244.6 5.7 %collective-permute-done.30 = bf16[128,1536]{1,0:T(8,128)(2,1)S(1)} collective-permute-done((bf16[128,1536]{1,0:T(8,128)(2,1)S(1)}, bf16[128,1536]{1,0:T(8,128)(2,1)S(1)}, u32[]{:S(2)}, u32[]{:S(2)}) %collective-permute-start.30) | collective-permute-done | bytes 393248 | tf_op jit(solution)/shard_map/ppermute | solution.py:292
  250.3 7.3 %collective-permute-done.32 = bf16[128,1536]{1,0:T(8,128)(2,1)S(1)} collective-permute-done((bf16[128,1536]{1,0:T(8,128)(2,1)S(1)}, bf16[128,1536]{1,0:T(8,128)(2,1)S(1)}, u32[]{:S(2)}, u32[]{:S(2)}) %collective-permute-start.32) | collective-permute-done | bytes 393248 | tf_op jit(solution)/shard_map/ppermute | solution.py:292
  264.1 9.5 %collective-permute-done.39.refs_4_ = bf16[128,1536]{1,0:T(8,128)(2,1)S(1)} collective-permute-done((bf16[128,1536]{1,0:T(8,128)(2,1)S(1)}, bf16[128,1536]{1,0:T(8,128)(2,1)S(1)}, u32[]{:S(2)}, u32[]{:S(2)}) %collective-permute-start.39) | collective-permute-done | bytes 393248 | tf_op jit(solution)/shard_map/ppermute | solution.py:292
  273.6 6.2 %collective-permute-done.38.refs_3_ = bf16[128,1536]{1,0:T(8,128)(2,1)S(1)} collective-permute-done((bf16[128,1536]{1,0:T(8,128)(2,1)S(1)}, bf16[128,1536]{1,0:T(8,128)(2,1)S(1)}, u32[]{:S(2)}, u32[]{:S(2)}) %collective-permute-start.38) | collective-permute-done | bytes 393248 | tf_op jit(solution)/shard_map/ppermute | solution.py:292
  282.4 14.3 %mix_backward.1 = (bf16[2,4,128,512]{3,2,1,0:T(8,128)(2,1)}, f32[8,256]{1,0:T(8,128)S(1)}, f32[2,256,256]{2,1,0:T(8,128)S(1)}, f32[1536,256]{1,0:T(8,128)}) custom-call(s32[1]{0:T(128)} %bitcast.1.refs_0_, bf16[128,1536]{1,0:T(8,128)(2,1)S(1)} %get-tuple-element.153.refs_1_, bf16[128,1536]{1,0:T(8,128)(2,1)} %collective-permute-done.37.refs_2_, ...), custom_call_target="tpu_custom_call" | custom-call | tf_op jit(solution)/shard_map/mix_backward/pallas_call | solution.py:662
  297.8 3.3 fusion.55
  301.5 5.3 %collective-permute-done.48 = f32[10,2048]{1,0:T(8,128)S(1)} collective-permute-done((f32[10,2048]{1,0:T(8,128)S(1)}, f32[10,2048]{1,0:T(8,128)S(1)}, u32[]{:S(2)}, u32[]{:S(2)}) %collective-permute-start.48) | collective-permute-done | bytes 81952 | tf_op jit(solution)/shard_map/ppermute | solution.py:339
  311.2 4.1 %collective-permute-done.49 = f32[10,2048]{1,0:T(8,128)S(1)} collective-permute-done((f32[10,2048]{1,0:T(8,128)S(1)}, f32[10,2048]{1,0:T(8,128)S(1)}, u32[]{:S(2)}, u32[]{:S(2)}) %collective-permute-start.49) | collective-permute-done | bytes 81952 | tf_op jit(solution)/shard_map/ppermute | solution.py:339
  325.1 3.5 collective-permute-done.52
  339.1 7.2 %collective-permute-done.45 = bf16[128,1536]{1,0:T(8,128)(2,1)} collective-permute-done((bf16[128,1536]{1,0:T(8,128)(2,1)}, bf16[128,1536]{1,0:T(8,128)(2,1)}, u32[]{:S(2)}, u32[]{:S(2)}) %collective-permute-start.45) | collective-permute-done | bytes 393248 | tf_op jit(solution)/shard_map/ppermute | solution.py:292
  346.2 5.9 %collective-permute-done.47 = bf16[128,1536]{1,0:T(8,128)(2,1)} collective-permute-done((bf16[128,1536]{1,0:T(8,128)(2,1)}, bf16[128,1536]{1,0:T(8,128)(2,1)}, u32[]{:S(2)}, u32[]{:S(2)}) %collective-permute-start.47) | collective-permute-done | bytes 393248 | tf_op jit(solution)/shard_map/ppermute | solution.py:292
  369.3 6.3 %collective-permute-done.58 = bf16[3,144,384]{2,1,0:T(8,128)(2,1)S(1)} collective-permute-done((bf16[3,144,384]{2,1,0:T(8,128)(2,1)S(1)}, bf16[3,144,384]{2,1,0:T(8,128)(2,1)S(1)}, u32[]{:S(2)}, u32[]{:S(2)}) %collective-permute-start.58) | collective-permute-done | bytes 331808 | tf_op jit(solution)/shard_map/ppermute | solution.py:292
  375.6 3.5 collective-permute-done.59
  385.7 5.1 %reduce-scatter.5.cloned.1.call-done = bf16[1,640,512]{2,1,0:T(8,128)(2,1)} async-done(((bf16[4,640,512]{2,1,0:T(8,128)(2,1)}), bf16[1,640,512]{2,1,0:T(8,128)(2,1)}) %reduce-scatter.5.cloned.1.call-update) | async-done | bytes 655376 | tf_op jit(solution)/shard_map/reduce_scatter | solution.py:988
  (360 shorter events, 139.3 us)
Async XLA Ops:
  7.2 68.0 %all-gather.5.cloned.1.call-start = ((), (), s32[]{:S(2)}) async-start(), calls=%async_computation.4 | async-start | bytes 3276800 | tf_op jit(solution)/shard_map/all_gather | solution.py:873
  17.5 161.1 %all-gather.7.cloned.1.call-start = ((), (), s32[]{:S(2)}) async-start(), calls=%async_computation.5 | async-start | bytes 6635520 | tf_op jit(solution)/shard_map/all_gather | solution.py:882
  34.4 304.6 %reduce-scatter.3.cloned.1.call-start = ((), (), s32[]{:S(2)}) async-start(), calls=%async_computation.2 | async-start | bytes 6635520 | tf_op jit(solution)/shard_map/reduce_scatter | solution.py:939
  35.8 40.7 %collective-permute-start.3 = (bf16[128,1536]{1,0:T(8,128)(2,1)S(1)}, bf16[128,1536]{1,0:T(8,128)(2,1)S(1)}, u32[]{:S(2)}, u32[]{:S(2)}) collective-permute-start(bf16[128,1536]{1,0:T(8,128)(2,1)S(1)} %fusion.11.refs_1_), channel_id=1, source_target_pairs={{0,4},{4,0},{8,12},{12,8},{16,20},{20,16},{24,28},{28,24},{1,5},{5... | collective-permute-start | bytes 1179656 | tf_op jit(solution)/shard_map/ppermute | solution.py:297
  36.4 43.4 %collective-permute-start.2 = (bf16[128,1536]{1,0:T(8,128)(2,1)S(1)}, bf16[128,1536]{1,0:T(8,128)(2,1)S(1)}, u32[]{:S(2)}, u32[]{:S(2)}) collective-permute-start(bf16[128,1536]{1,0:T(8,128)(2,1)S(1)} %fusion.11.refs_1_), channel_id=1, source_target_pairs={{0,24},{4,28},{8,16},{12,20},{16,8},{20,12},{24,0},{28,4},{1,25},{... | collective-permute-start | bytes 1179656 | tf_op jit(solution)/shard_map/ppermute | solution.py:292
  39.9 40.4 %collective-permute-start.1 = (bf16[128,1536]{1,0:T(8,128)(2,1)S(1)}, bf16[128,1536]{1,0:T(8,128)(2,1)S(1)}, u32[]{:S(2)}, u32[]{:S(2)}) collective-permute-start(bf16[128,1536]{1,0:T(8,128)(2,1)S(1)} %fusion.11.refs_1_), channel_id=1, source_target_pairs={{0,16},{4,20},{8,24},{12,28},{16,0},{20,4},{24,8},{28,12},{1,17},{... | collective-permute-start | bytes 1179656 | tf_op jit(solution)/shard_map/ppermute | solution.py:292
  40.4 40.4 %collective-permute-start = (bf16[128,1536]{1,0:T(8,128)(2,1)S(1)}, bf16[128,1536]{1,0:T(8,128)(2,1)}, u32[]{:S(2)}, u32[]{:S(2)}) collective-permute-start(bf16[128,1536]{1,0:T(8,128)(2,1)S(1)} %fusion.11.refs_1_), channel_id=1, source_target_pairs={{0,8},{4,12},{8,0},{12,4},{16,24},{20,28},{24,16},{28,20},{1,9},{5... | collective-permute-start | bytes 1179656 | tf_op jit(solution)/shard_map/ppermute | solution.py:292
  40.5 42.7 %collective-permute-start.14 = (bf16[128,1536]{1,0:T(8,128)(2,1)S(1)}, bf16[128,1536]{1,0:T(8,128)(2,1)S(1)}, u32[]{:S(2)}, u32[]{:S(2)}) collective-permute-start(bf16[128,1536]{1,0:T(8,128)(2,1)S(1)} %bitcast.276), channel_id=1, source_target_pairs={{0,4},{4,0},{8,12},{12,8},{16,20},{20,16},{24,28},{28,24},{1,5},{5... | collective-permute-start | bytes 1179656 | tf_op jit(solution)/shard_map/ppermute | solution.py:297
  79.7 13.4 %collective-permute-start.8 = (bf16[2,128,512]{2,1,0:T(8,128)(2,1)S(1)}, bf16[2,128,512]{2,1,0:T(8,128)(2,1)S(1)}, u32[]{:S(2)}, u32[]{:S(2)}) collective-permute-start(bf16[2,128,512]{2,1,0:T(8,128)(2,1)S(1)} %get-tuple-element.211), channel_id=1, source_target_pairs={{0,16},{4,20},{8,24},{12,28},{16,0},{20,4},{24,8},{28,12},{1,17},{... | collective-permute-start | bytes 786440 | tf_op jit(solution)/shard_map/ppermute | solution.py:292
  80.8 20.7 %collective-permute-start.13 = (bf16[128,1536]{1,0:T(8,128)(2,1)S(1)}, bf16[128,1536]{1,0:T(8,128)(2,1)S(1)}, u32[]{:S(2)}, u32[]{:S(2)}) collective-permute-start(bf16[128,1536]{1,0:T(8,128)(2,1)S(1)} %bitcast.277), channel_id=1, source_target_pairs={{0,24},{4,28},{8,16},{12,20},{16,8},{20,12},{24,0},{28,4},{1,25},{... | collective-permute-start | bytes 1179656 | tf_op jit(solution)/shard_map/ppermute | solution.py:292
  83.2 25.5 %collective-permute-start.12 = (bf16[128,1536]{1,0:T(8,128)(2,1)S(1)}, bf16[128,1536]{1,0:T(8,128)(2,1)S(1)}, u32[]{:S(2)}, u32[]{:S(2)}) collective-permute-start(bf16[128,1536]{1,0:T(8,128)(2,1)S(1)} %bitcast.278), channel_id=1, source_target_pairs={{0,16},{4,20},{8,24},{12,28},{16,0},{20,4},{24,8},{28,12},{1,17},{... | collective-permute-start | bytes 1179656 | tf_op jit(solution)/shard_map/ppermute | solution.py:292
  87.5 21.4 %collective-permute-start.11 = (bf16[128,1536]{1,0:T(8,128)(2,1)S(1)}, bf16[128,1536]{1,0:T(8,128)(2,1)S(1)}, u32[]{:S(2)}, u32[]{:S(2)}) collective-permute-start(bf16[128,1536]{1,0:T(8,128)(2,1)S(1)} %bitcast.279), channel_id=1, source_target_pairs={{0,8},{4,12},{8,0},{12,4},{16,24},{20,28},{24,16},{28,20},{1,9},{5... | collective-permute-start | bytes 1179656 | tf_op jit(solution)/shard_map/ppermute | solution.py:292
  93.2 16.1 %collective-permute-start.6 = (bf16[128,1536]{1,0:T(8,128)(2,1)S(1)}, bf16[128,1536]{1,0:T(8,128)(2,1)}, u32[]{:S(2)}, u32[]{:S(2)}) collective-permute-start(bf16[128,1536]{1,0:T(8,128)(2,1)S(1)} %collective-permute-done.2.refs_4_), channel_id=1, source_target_pairs={{0,4},{4,0},{8,12},{12,8},{16,20},{20,16},{24,28},{28,24},{1,5},{5... | collective-permute-start | bytes 1179656 | tf_op jit(solution)/shard_map/ppermute | solution.py:297
  94.6 14.8 %collective-permute-start.5 = (bf16[128,1536]{1,0:T(8,128)(2,1)S(1)}, bf16[128,1536]{1,0:T(8,128)(2,1)}, u32[]{:S(2)}, u32[]{:S(2)}) collective-permute-start(bf16[128,1536]{1,0:T(8,128)(2,1)S(1)} %collective-permute-done.1.refs_3_), channel_id=1, source_target_pairs={{0,4},{4,0},{8,12},{12,8},{16,20},{20,16},{24,28},{28,24},{1,5},{5... | collective-permute-start | bytes 1179656 | tf_op jit(solution)/shard_map/ppermute | solution.py:297
  136.1 19.1 %collective-permute-start.21 = (bf16[128,1536]{1,0:T(8,128)(2,1)S(1)}, bf16[128,1536]{1,0:T(8,128)(2,1)S(1)}, u32[]{:S(2)}, u32[]{:S(2)}) collective-permute-start(bf16[128,1536]{1,0:T(8,128)(2,1)S(1)} %get-tuple-element.189), channel_id=1, source_target_pairs={{0,24},{4,28},{8,16},{12,20},{16,8},{20,12},{24,0},{28,4},{1,25},{... | collective-permute-start | bytes 1179656 | tf_op jit(solution)/shard_map/ppermute | solution.py:292
  137.6 19.0 %collective-permute-start.20 = (bf16[128,1536]{1,0:T(8,128)(2,1)S(1)}, bf16[128,1536]{1,0:T(8,128)(2,1)S(1)}, u32[]{:S(2)}, u32[]{:S(2)}) collective-permute-start(bf16[128,1536]{1,0:T(8,128)(2,1)S(1)} %get-tuple-element.190), channel_id=1, source_target_pairs={{0,16},{4,20},{8,24},{12,28},{16,0},{20,4},{24,8},{28,12},{1,17},{... | collective-permute-start | bytes 1179656 | tf_op jit(solution)/shard_map/ppermute | solution.py:292
  159.2 16.9 %collective-permute-start.23 = (bf16[128,1536]{1,0:T(8,128)(2,1)S(1)}, bf16[128,1536]{1,0:T(8,128)(2,1)S(1)}, u32[]{:S(2)}, u32[]{:S(2)}) collective-permute-start(bf16[128,1536]{1,0:T(8,128)(2,1)S(1)} %multiply_convert_fusion.refs_0_), channel_id=1, source_target_pairs={{0,16},{4,20},{8,24},{12,28},{16,0},{20,4},{24,8},{28,12},{1,17},{... | collective-permute-start | bytes 1179656 | tf_op jit(solution)/shard_map/ppermute | solution.py:292
  160.0 16.0 %collective-permute-start.22 = (bf16[128,1536]{1,0:T(8,128)(2,1)S(1)}, bf16[128,1536]{1,0:T(8,128)(2,1)S(1)}, u32[]{:S(2)}, u32[]{:S(2)}) collective-permute-start(bf16[128,1536]{1,0:T(8,128)(2,1)S(1)} %multiply_convert_fusion.refs_0_), channel_id=1, source_target_pairs={{0,8},{4,12},{8,0},{12,4},{16,24},{20,28},{24,16},{28,20},{1,9},{5... | collective-permute-start | bytes 1179656 | tf_op jit(solution)/shard_map/ppermute | solution.py:292
  161.2 15.4 %collective-permute-start.25 = (bf16[128,1536]{1,0:T(8,128)(2,1)S(1)}, bf16[128,1536]{1,0:T(8,128)(2,1)S(1)}, u32[]{:S(2)}, u32[]{:S(2)}) collective-permute-start(bf16[128,1536]{1,0:T(8,128)(2,1)S(1)} %multiply_convert_fusion.refs_0_), channel_id=1, source_target_pairs={{0,4},{4,0},{8,12},{12,8},{16,20},{20,16},{24,28},{28,24},{1,5},{5... | collective-permute-start | bytes 1179656 | tf_op jit(solution)/shard_map/ppermute | solution.py:297
  206.8 184.1 %reduce-scatter.5.cloned.1.call-start = ((), (), s32[]{:S(2)}) async-start(), calls=%async_computation.3 | async-start | bytes 3276800 | tf_op jit(solution)/shard_map/reduce_scatter | solution.py:988
  222.2 19.3 %collective-permute-start.36 = (bf16[128,1536]{1,0:T(8,128)(2,1)S(1)}, bf16[128,1536]{1,0:T(8,128)(2,1)S(1)}, u32[]{:S(2)}, u32[]{:S(2)}) collective-permute-start(bf16[128,1536]{1,0:T(8,128)(2,1)S(1)} %get-tuple-element.183), channel_id=1, source_target_pairs={{0,24},{4,28},{8,16},{12,20},{16,8},{20,12},{24,0},{28,4},{1,25},{... | collective-permute-start | bytes 1179656 | tf_op jit(solution)/shard_map/ppermute | solution.py:292
  223.1 20.5 %collective-permute-start.35 = (bf16[128,1536]{1,0:T(8,128)(2,1)S(1)}, bf16[128,1536]{1,0:T(8,128)(2,1)S(1)}, u32[]{:S(2)}, u32[]{:S(2)}) collective-permute-start(bf16[128,1536]{1,0:T(8,128)(2,1)S(1)} %get-tuple-element.184), channel_id=1, source_target_pairs={{0,16},{4,20},{8,24},{12,28},{16,0},{20,4},{24,8},{28,12},{1,17},{... | collective-permute-start | bytes 1179656 | tf_op jit(solution)/shard_map/ppermute | solution.py:292
  225.7 24.6 %collective-permute-start.30 = (bf16[128,1536]{1,0:T(8,128)(2,1)S(1)}, bf16[128,1536]{1,0:T(8,128)(2,1)S(1)}, u32[]{:S(2)}, u32[]{:S(2)}) collective-permute-start(bf16[128,1536]{1,0:T(8,128)(2,1)S(1)} %get-tuple-element.185), channel_id=1, source_target_pairs={{0,8},{4,12},{8,0},{12,4},{16,24},{20,28},{24,16},{28,20},{1,9},{5... | collective-permute-start | bytes 1179656 | tf_op jit(solution)/shard_map/ppermute | solution.py:292
  226.6 31.0 %collective-permute-start.32 = (bf16[128,1536]{1,0:T(8,128)(2,1)S(1)}, bf16[128,1536]{1,0:T(8,128)(2,1)S(1)}, u32[]{:S(2)}, u32[]{:S(2)}) collective-permute-start(bf16[128,1536]{1,0:T(8,128)(2,1)S(1)} %get-tuple-element.186), channel_id=1, source_target_pairs={{0,24},{4,28},{8,16},{12,20},{16,8},{20,12},{24,0},{28,4},{1,25},{... | collective-permute-start | bytes 1179656 | tf_op jit(solution)/shard_map/ppermute | solution.py:292
  233.4 25.7 %collective-permute-start.31 = (bf16[128,1536]{1,0:T(8,128)(2,1)S(1)}, bf16[128,1536]{1,0:T(8,128)(2,1)S(1)}, u32[]{:S(2)}, u32[]{:S(2)}) collective-permute-start(bf16[128,1536]{1,0:T(8,128)(2,1)S(1)} %get-tuple-element.187), channel_id=1, source_target_pairs={{0,16},{4,20},{8,24},{12,28},{16,0},{20,4},{24,8},{28,12},{1,17},{... | collective-permute-start | bytes 1179656 | tf_op jit(solution)/shard_map/ppermute | solution.py:292
  260.5 13.1 %collective-permute-start.39 = (bf16[128,1536]{1,0:T(8,128)(2,1)S(1)}, bf16[128,1536]{1,0:T(8,128)(2,1)S(1)}, u32[]{:S(2)}, u32[]{:S(2)}) collective-permute-start(bf16[128,1536]{1,0:T(8,128)(2,1)S(1)} %get-tuple-element.153.refs_1_), channel_id=1, source_target_pairs={{0,24},{4,28},{8,16},{12,20},{16,8},{20,12},{24,0},{28,4},{1,25},{... | collective-permute-start | bytes 1179656 | tf_op jit(solution)/shard_map/ppermute | solution.py:292
  262.5 17.3 %collective-permute-start.38 = (bf16[128,1536]{1,0:T(8,128)(2,1)S(1)}, bf16[128,1536]{1,0:T(8,128)(2,1)S(1)}, u32[]{:S(2)}, u32[]{:S(2)}) collective-permute-start(bf16[128,1536]{1,0:T(8,128)(2,1)S(1)} %get-tuple-element.153.refs_1_), channel_id=1, source_target_pairs={{0,16},{4,20},{8,24},{12,28},{16,0},{20,4},{24,8},{28,12},{1,17},{... | collective-permute-start | bytes 1179656 | tf_op jit(solution)/shard_map/ppermute | solution.py:292
  263.4 16.5 %collective-permute-start.37 = (bf16[128,1536]{1,0:T(8,128)(2,1)S(1)}, bf16[128,1536]{1,0:T(8,128)(2,1)}, u32[]{:S(2)}, u32[]{:S(2)}) collective-permute-start(bf16[128,1536]{1,0:T(8,128)(2,1)S(1)} %get-tuple-element.153.refs_1_), channel_id=1, source_target_pairs={{0,8},{4,12},{8,0},{12,4},{16,24},{20,28},{24,16},{28,20},{1,9},{5... | collective-permute-start | bytes 1179656 | tf_op jit(solution)/shard_map/ppermute | solution.py:292
  264.1 17.8 %collective-permute-start.40 = (bf16[128,1536]{1,0:T(8,128)(2,1)S(1)}, bf16[128,1536]{1,0:T(8,128)(2,1)}, u32[]{:S(2)}, u32[]{:S(2)}) collective-permute-start(bf16[128,1536]{1,0:T(8,128)(2,1)S(1)} %get-tuple-element.153.refs_1_), channel_id=1, source_target_pairs={{0,4},{4,0},{8,12},{12,8},{16,20},{20,16},{24,28},{28,24},{1,5},{5... | collective-permute-start | bytes 1179656 | tf_op jit(solution)/shard_map/ppermute | solution.py:297
  316.4 14.3 %collective-permute-start.44 = (bf16[4,128,1536]{2,1,0:T(8,128)(2,1)S(1)}, bf16[4,128,1536]{2,1,0:T(8,128)(2,1)S(1)}, u32[]{:S(2)}, u32[]{:S(2)}) collective-permute-start(bf16[4,128,1536]{2,1,0:T(8,128)(2,1)S(1)} %bitcast.329), channel_id=1, source_target_pairs={{0,4},{4,0},{8,12},{12,8},{16,20},{20,16},{24,28},{28,24},{1,5},{5... | collective-permute-start | bytes 4718600 | tf_op jit(solution)/shard_map/ppermute | solution.py:297
  335.5 16.6 %collective-permute-start.47 = (bf16[128,1536]{1,0:T(8,128)(2,1)}, bf16[128,1536]{1,0:T(8,128)(2,1)}, u32[]{:S(2)}, u32[]{:S(2)}) collective-permute-start(bf16[128,1536]{1,0:T(8,128)(2,1)} %get-tuple-element.180), channel_id=1, source_target_pairs={{0,24},{4,28},{8,16},{12,20},{16,8},{20,12},{24,0},{28,4},{1,25},{... | collective-permute-start | bytes 1179656 | tf_op jit(solution)/shard_map/ppermute | solution.py:292
  336.7 16.8 %collective-permute-start.46 = (bf16[128,1536]{1,0:T(8,128)(2,1)}, bf16[128,1536]{1,0:T(8,128)(2,1)}, u32[]{:S(2)}, u32[]{:S(2)}) collective-permute-start(bf16[128,1536]{1,0:T(8,128)(2,1)} %get-tuple-element.181), channel_id=1, source_target_pairs={{0,16},{4,20},{8,24},{12,28},{16,0},{20,4},{24,8},{28,12},{1,17},{... | collective-permute-start | bytes 1179656 | tf_op jit(solution)/shard_map/ppermute | solution.py:292
  (100 other events, 982.4 us)
Sparse Core Ops, SparseCore 0:
  17.6 57.4 all-gather.4
  76.7 97.9 all-gather.6
  206.9 92.8 reduce-scatter.2
  339.2 51.6 reduce-scatter.4

commit v2 on v1

--- a/solution.py
+++ b/solution.py
@@ -299,23 +299,35 @@
 
 def gather_blocks(x):
     chips = lax.axis_size("seq") // 2
-    near = [x] + [chip_swap(x, k) for k in range(1, chips)]
-    return near, [core_swap(block) for block in near]
-
-
-def scatter_blocks(near, far):
-    chips = near.shape[0]
-    pair = near.astype(jnp.float32) + core_swap(far.astype(jnp.bfloat16)).astype(jnp.float32)
-    low = pair.astype(jnp.bfloat16)
-    total = pair[0]
-    for k in range(1, chips):
+    near = jnp.stack([x] + [chip_swap(x, k) for k in range(1, chips)])
+    return near, core_swap(near)
+
+
+def tie(*arrays):
+    return lax.optimization_barrier(arrays)
+
+
+def pair_blocks(near, far):
+    pair = near.astype(jnp.float32) + core_swap(far).astype(jnp.float32)
+    return pair.astype(jnp.bfloat16), pair[0]
+
+
+def spread_pairs(low, own):
+    total = own
+    for k in range(1, low.shape[0]):
         total = total + chip_swap(low[k], k).astype(jnp.float32)
     return total
 
 
-def exchange(x, chip, core):
+def scatter_blocks(near, far):
+    return spread_pairs(*pair_blocks(near, far))
+
+
+def exchange(x, chip, core, turn):
     chips = x.shape[0]
-    parts = [lax.dynamic_index_in_dim(x, chip ^ k, 0, keepdims=False) for k in range(chips)]
+    parts = [
+        lax.dynamic_index_in_dim(x, chip ^ k ^ turn, 0, keepdims=False) for k in range(chips)
+    ]
     got = jnp.stack([parts[0]] + [chip_swap(parts[k], k) for k in range(1, chips)])
     keep = lax.dynamic_index_in_dim(got, core, 1, keepdims=False)
     give = lax.dynamic_index_in_dim(got, 1 - core, 1, keepdims=False)
@@ -329,6 +341,14 @@
         parts = [jnp.where(flip, parts[i ^ bit], parts[i]) for i in range(len(parts))]
         bit *= 2
     return parts
+
+
+def over_planes(x):
+    planes = lax.axis_size("fsdp")
+    total = x
+    for k in range(1, planes):
+        total = total + lax.ppermute(x, "fsdp", [(i, i ^ k) for i in range(planes)])
+    return total
 
 
 def total_over(x, axes):
@@ -342,13 +362,11 @@
 
 
 def gelu_parts(v):
-    inner = 0.7978845608028654 * (v + 0.044715 * v * v * v)
-    th = jnp.tanh(inner)
-    value = 0.5 * v * (1.0 + th)
-    slope = 0.5 * (1.0 + th) + 0.5 * v * (1.0 - th * th) * (
-        0.7978845608028654 * (1.0 + 0.134145 * v * v)
-    )
-    return value, slope
+    root = 0.7978845608028654
+    square = v * v
+    h = 0.5 + 0.5 * jnp.tanh(v * (root + root * 0.044715 * square))
+    value = v * h
+    return value, h + value * (1.0 - h) * (2.0 * root + root * 0.26829 * square)
 
 
 def sigmoid(v):
@@ -372,19 +390,26 @@
     return lax.dot_general(a, b, (((0,), (0,)), ((), ())), preferred_element_type=jnp.float32)
 
 
-def scan_rows(a, b, later):
+def scan_rows(a, b, carry, later):
     rows = a.shape[0]
-    row = lax.broadcasted_iota(jnp.int32, a.shape, 0)
+    group = 8
+    row = lax.broadcasted_iota(jnp.int32, a.shape, 0) % group
     step = 1
-    while step < rows:
+    while step < group:
         turn = rows - step if later else step
-        there = (row < rows - step) if later else (row >= step)
+        there = (row < group - step) if later else (row >= step)
         a_next = jnp.where(there, pltpu.roll(a, turn, 0), 1.0)
         b_next = jnp.where(there, pltpu.roll(b, turn, 0), 0.0)
         b = a * b_next + b
         a = a * a_next
         step *= 2
-    return a, b
+    starts = list(range(0, rows, group))
+    done = {}
+    for start in reversed(starts) if later else starts:
+        states = a[start : start + group] * carry + b[start : start + group]
+        done[start] = states
+        carry = states[:1] if later else states[group - 1 :]
+    return jnp.concatenate([done[start] for start in starts], axis=0)
 
 
 def in_time(value, core):
@@ -402,25 +427,29 @@
     ref[1] = jnp.where(odd, first, second).astype(ref.dtype)
 
 
-def mix_forward_kernel(chips, *refs):
-    place = refs[0][0]
-    blocks = refs[1 : 1 + 2 * chips]
-    age_ref, chan_ref, in_ref, keep_ref, got_ref = refs[1 + 2 * chips : 6 + 2 * chips]
-    (
-        merged_ref,
-        normed_ref,
-        branch_ref,
-        gelu_pre_ref,
-        conv_ref,
-        decay_pre_ref,
-        input_pre_ref,
-        prior_ref,
-        low_ref,
-        weights_ref,
-        held,
-        extended,
-        carry,
-    ) = refs[-13:]
+def mix_forward_kernel(
+    seq_ref,
+    near_ref,
+    far_ref,
+    age_ref,
+    chan_ref,
+    in_ref,
+    keep_ref,
+    got_ref,
+    merged_ref,
+    branch_ref,
+    gelu_pre_ref,
+    conv_ref,
+    decay_pre_ref,
+    input_pre_ref,
+    prior_ref,
+    low_ref,
+    weights_ref,
+    extended,
+    carry,
+):
+    place = seq_ref[0]
+    chips = near_ref.shape[0]
     step = pl.program_id(0)
     chip, core = place // 2, place % 2
     rows, width = branch_ref.shape
@@ -434,8 +463,6 @@
         extended[pl.ds(0, 8), :] = jnp.zeros((8, width), jnp.float32)
         carry[...] = jnp.zeros_like(carry)
         for k in range(chips):
-            held[0, k] = blocks[k][...]
-            held[1, k] = blocks[chips + k][...]
             home = pl.multiple_of(piece * 2 * (chip ^ k) + piece * core, piece)
             away = pl.multiple_of(piece * 2 * (chip ^ k) + piece * (1 - core), piece)
             for j in range(parts):
@@ -448,10 +475,7 @@
         extended[pl.ds(0, 8), :] = extended[pl.ds(rows, 8), :]
 
     turn = step ^ chip
-    near, far = held[0, turn], held[1, turn]
-    normed_ref[0] = near
-    normed_ref[1] = far
-    normed = jnp.concatenate([near, far], axis=0)
+    normed = jnp.concatenate([near_ref[turn], far_ref[turn]], axis=0)
     pre = dot_nn(normed[:, :near_model], in_ref[0])
     for z in range(1, planes):
         pre = pre + dot_nn(normed[:, z * near_model : (z + 1) * near_model], in_ref[z])
@@ -479,9 +503,8 @@
     factor = jnp.where(reset, 1.0, jnp.sqrt(room))
     decay = jnp.where(reset, 0.0, jnp.exp(log_a))
     driven = sigmoid(input_pre) * conv * factor
-    grown, states = scan_rows(decay, driven, False)
     before = carry[0:1, :]
-    states = states + grown * before
+    states = scan_rows(decay, driven, before, False)
     carry[0:1, :] = states[rows - 1 :, :]
     row = lax.broadcasted_iota(jnp.int32, states.shape, 0)
     prior_ref[...] = jnp.where(row == 0, before, pltpu.roll(states, 1, 0))
@@ -491,9 +514,8 @@
     by_core(merged, merged_ref, core)
 
 
-def mix_forward(place, near, far, age, chan, pack, keep, got, ahead_of):
-    chips = len(near)
-    rows, model = near[0].shape
+def mix_forward(place, near, far, age, chan, pack, keep, got):
+    chips, rows, model = near.shape
     planes, _, both = pack.shape
     width = both // 2
     length = 2 * chips * rows
@@ -505,34 +527,29 @@
     spec = pl.BlockSpec((chunk, width), time_block)
     fixed = lambda shape: pl.BlockSpec(shape, lambda i, s: (0,) * len(shape))
     return pl.pallas_call(
-        functools.partial(mix_forward_kernel, chips),
+        mix_forward_kernel,
         grid_spec=pltpu.PrefetchScalarGridSpec(
             num_scalar_prefetch=1,
             grid=(chips,),
-            in_specs=[fixed((rows, model))] * (2 * chips)
-            + [
+            in_specs=[
+                fixed(near.shape),
+                fixed(far.shape),
                 pl.BlockSpec((chunk, 1), time_block),
                 pl.BlockSpec((chan.shape[0], width), lambda i, s: (0, s[0])),
                 fixed((planes, model // planes, both)),
                 fixed(keep.shape),
                 fixed(got.shape),
-            ]
-            + [pl.BlockSpec(memory_space=pl.ANY)] * len(ahead_of),
-            out_specs=[
-                pl.BlockSpec((2, None, rows, width), token_block),
-                pl.BlockSpec((2, None, rows, model), token_block),
-            ]
+            ],
+            out_specs=[pl.BlockSpec((2, None, rows, width), token_block)]
             + [spec] * 7
             + [fixed((width, columns))],
             scratch_shapes=[
-                pltpu.VMEM((2, chips, rows, model), jnp.bfloat16),
                 pltpu.VMEM((chunk + 8, width), jnp.float32),
                 pltpu.VMEM((8, width), jnp.float32),
             ],
         ),
         out_shape=[
             jax.ShapeDtypeStruct((2, chips, rows, width), jnp.bfloat16),
-            jax.ShapeDtypeStruct((2, chips, rows, model), jnp.bfloat16),
             saved(jnp.bfloat16),
             saved(jnp.float32),
             saved(jnp.bfloat16),
@@ -542,63 +559,59 @@
             saved(jnp.bfloat16),
             jax.ShapeDtypeStruct((width, columns), jnp.bfloat16),
         ],
-        compiler_params=pltpu.CompilerParams(vmem_limit_bytes=48 * 1024 * 1024),
+        compiler_params=pltpu.CompilerParams(vmem_limit_bytes=56 * 1024 * 1024),
         name="mix_forward",
-    )(place, *near, *far, age, chan, pack, keep, got, *ahead_of)
-
-
-def mix_backward_kernel(chips, *refs):
-    place = refs[0][0]
-    blocks = refs[1 : 1 + 2 * chips]
-    (
-        age_ref,
-        chan_ref,
-        weights_ref,
-        branch_ref,
-        gelu_pre_ref,
-        conv_ref,
-        decay_pre_ref,
-        input_pre_ref,
-        prior_ref,
-        low_ref,
-        both_ref,
-        small_ref,
-        gate_grads_ref,
-        out_grad_ref,
-        held,
-        ahead,
-        carry,
-    ) = refs[1 + 2 * chips :]
+    )(place, near, far, age, chan, pack, keep, got)
+
+
+def mix_backward_kernel(
+    seq_ref,
+    near_ref,
+    far_ref,
+    age_ref,
+    chan_ref,
+    weights_ref,
+    branch_ref,
+    gelu_pre_ref,
+    conv_ref,
+    decay_pre_ref,
+    input_pre_ref,
+    prior_ref,
+    low_ref,
+    both_ref,
+    small_ref,
+    *rest,
+):
+    place = seq_ref[0]
+    chips = near_ref.shape[0]
+    row_refs, (out_grad, gate_grads, ahead, carry) = rest[:chips], rest[chips:]
     step = pl.program_id(0)
     chip, core = place // 2, place % 2
     rows, width = branch_ref.shape
-    model = held.shape[-1]
+    model = near_ref.shape[-1]
 
     @pl.when(step == 0)
     def _():
         carry[...] = jnp.zeros_like(carry)
         ahead[:, pl.ds(rows, 8), :] = jnp.zeros((3, 8, width), jnp.float32)
         small_ref[...] = jnp.zeros_like(small_ref)
-        gate_grads_ref[...] = jnp.zeros_like(gate_grads_ref)
-        out_grad_ref[...] = jnp.zeros_like(out_grad_ref)
-        for k in range(chips):
-            held[0, k] = blocks[k][...]
-            held[1, k] = blocks[chips + k][...]
+        gate_grads[...] = jnp.zeros_like(gate_grads)
+        out_grad[...] = jnp.zeros_like(out_grad)
 
     @pl.when(step > 0)
     def _():
         ahead[:, pl.ds(rows, 8), :] = ahead[:, pl.ds(0, 8), :]
 
     turn = (chips - 1 - step) ^ chip
-    mixer_grad = jnp.concatenate([held[0, turn], held[1, turn]], axis=0)
+    mixer_grad = jnp.concatenate([near_ref[turn], far_ref[turn]], axis=0)
     merged_grad = in_time(dot_nt(mixer_grad, weights_ref[:, :model]), core)
     age = age_ref[...]
     gelu_out, slope = gelu_parts(gelu_pre_ref[...])
     state_grad = (merged_grad * gelu_out).astype(jnp.bfloat16).astype(jnp.float32)
     low = low_ref[...].astype(jnp.float32)
     gelu_pre_grad = merged_grad * low * slope
-    merged = in_time(low * gelu_out, core).astype(jnp.bfloat16)
-    out_grad_ref[...] += dot_tn(mixer_grad, merged)
+    merged = in_time((low * gelu_out).astype(jnp.bfloat16), core)
+    out_grad[...] += dot_tn(mixer_grad, merged)
     reset = age < 0.5
     sig_d = sigmoid(decay_pre_ref[...])
     sig_i = sigmoid(input_pre_ref[...])
@@ -614,8 +627,7 @@
     conv = conv_low.astype(jnp.float32)
     row = lax.broadcasted_iota(jnp.int32, (rows, width), 0)
     next_decay = jnp.where(row == rows - 1, carry[0:1, :], pltpu.roll(decay, rows - 1, 0))
-    grown, carried = scan_rows(next_decay, state_grad, True)
-    carried = carried + grown * carry[1:2, :]
+    carried = scan_rows(next_decay, state_grad, carry[1:2, :], True)
     carry[0:1, :] = decay[0:1, :]
     carry[1:2, :] = carried[0:1, :]
     decay_grad = carried * prior_ref[...]
@@ -632,8 +644,8 @@
         + dot_nt(decay_low, weights_ref[:, model : model + width])
         + dot_nt(input_low, weights_ref[:, model + width :])
     )
-    gate_grads_ref[0] += dot_tn(decay_low, conv_low)
-    gate_grads_ref[1] += dot_tn(input_low, conv_low)
+    gate_grads[0] += dot_tn(decay_low, conv_low)
+    gate_grads[1] += dot_tn(input_low, conv_low)
     branch = branch_ref[...].astype(jnp.float32)
     branch_grad = chan_ref[0:1, :] * conv_grad
     small_ref[0:1, :] += jnp.sum(conv_grad * branch, axis=0, keepdims=True)
@@ -648,11 +660,25 @@
     small_ref[7:8, :] += 8.0 * chan_ref[8:9, :] * jnp.sum(sig_grad, axis=0, keepdims=True)
     by_core(jnp.concatenate([branch_grad, gelu_pre_grad], axis=1), both_ref, core)
 
+    @pl.when(step == chips - 1)
+    def _():
+        slim, piece = model // (2 * chips), width // (2 * chips)
+        for k in range(chips):
+            for e in range(2):
+                target = 2 * (chip ^ k) + (core ^ e)
+                rows = pl.ds(pl.multiple_of(target * slim, slim), slim)
+                row_refs[k][e, pl.ds(0, slim), :] = out_grad[rows, :].astype(jnp.bfloat16)
+                rows = pl.ds(pl.multiple_of(target * piece, piece), piece)
+                for j in range(2):
+                    row_refs[k][e, pl.ds(slim + j * piece, piece), :] = gate_grads[j, rows, :].astype(
+                        jnp.bfloat16
+                    )
+
 
 def mix_backward(place, near, far, age, chan, weights, saved):
-    chips = len(near)
-    rows, model = near[0].shape
+    chips, rows, model = near.shape
     width, columns = weights.shape
+    tall = (model + 2 * width) // (2 * chips)
     chunk = 2 * rows
     last = chips - 1
     time_block = lambda i, s: (last - i, 0)
@@ -660,12 +686,13 @@
     spec = pl.BlockSpec((chunk, width), time_block)
     fixed = lambda shape: pl.BlockSpec(shape, lambda i, s: (0,) * len(shape))
     return pl.pallas_call(
-        functools.partial(mix_backward_kernel, chips),
+        mix_backward_kernel,
         grid_spec=pltpu.PrefetchScalarGridSpec(
             num_scalar_prefetch=1,
             grid=(chips,),
-            in_specs=[fixed((rows, model))] * (2 * chips)
-            + [
+            in_specs=[
+                fixed(near.shape),
+                fixed(far.shape),
                 pl.BlockSpec((chunk, 1), time_block),
                 pl.BlockSpec((chan.shape[0], width), lambda i, s: (0, s[0])),
                 fixed((width, columns)),
@@ -674,11 +701,11 @@
             out_specs=[
                 pl.BlockSpec((2, None, rows, 2 * width), token_block),
                 fixed((8, width)),
-                fixed((2, width, width)),
-                fixed((model, width)),
-            ],
+            ]
+            + [fixed((2, tall, width))] * chips,
             scratch_shapes=[
-                pltpu.VMEM((2, chips, rows, model), jnp.bfloat16),
+                pltpu.VMEM((model, width), jnp.float32),
+                pltpu.VMEM((2, width, width), jnp.float32),
                 pltpu.VMEM((3, chunk + 8, width), jnp.float32),
                 pltpu.VMEM((8, width), jnp.float32),
             ],
@@ -686,128 +713,326 @@
         out_shape=[
             jax.ShapeDtypeStruct((2, chips, rows, 2 * width), jnp.bfloat16),
             jax.ShapeDtypeStruct((8, width), jnp.float32),
-            jax.ShapeDtypeStruct((2, width, width), jnp.float32),
-            jax.ShapeDtypeStruct((model, width), jnp.float32),
-        ],
-        compiler_params=pltpu.CompilerParams(vmem_limit_bytes=48 * 1024 * 1024),
+        ]
+        + [jax.ShapeDtypeStruct((2, tall, width), jnp.bfloat16)] * chips,
+        compiler_params=pltpu.CompilerParams(vmem_limit_bytes=56 * 1024 * 1024),
+        cost_estimate=pl.CostEstimate(
+            flops=10**10, bytes_accessed=40 * 10**6, transcendentals=6 * width * 2 * chips * rows
+        ),
         name="mix_backward",
-    )(place, *near, *far, age, chan, weights, *saved)
-
-
-def unit_kernel(chips, *refs):
-    blocks, cots = refs[: 2 * chips], refs[2 * chips : 4 * chips]
-    pack_ref, pair_ref, hidden_ref, grads_ref, down_ref, normed, cot, gate_up, down = refs[4 * chips :]
-    rows = blocks[0].shape[0]
+    )(place, near, far, age, chan, weights, *saved)
+
+
+def unit_kernel(
+    near_ref,
+    far_ref,
+    cot_near_ref,
+    cot_far_ref,
+    pack_ref,
+    back_near_out,
+    back_far_out,
+    mixed_near_out,
+    mixed_far_out,
+    grads_out,
+    normed,
+    cot,
+    gate_up,
+    down,
+    pair,
+    hidden,
+    pair_t,
+    hidden_t,
+    grads,
+    back,
+    mixed,
+    in_sems,
+    out_sems,
+):
+    bf16 = jnp.bfloat16
+    chips, rows, _ = near_ref.shape
     planes, tall, near_model = pack_ref.shape
-    both = pair_ref.shape[1]
+    both = pair.shape[1]
     part = both // 2
     span = part // planes
     side = near_model // 2
-    for k in range(2 * chips):
-        normed[pl.ds(k * rows, rows), :] = blocks[k][...]
-        cot[pl.ds(k * rows, rows), :] = cots[k][...]
-    for z in range(planes):
-        for j in range(3):
-            gate_up[pl.ds(z * near_model, near_model), pl.ds(j * near_model, near_model)] = pack_ref[
-                z, pl.ds(j * near_model, near_model), :
-            ]
-        for j in range(planes):
-            down[pl.ds(z * span, span), pl.ds(j * near_model, near_model)] = pack_ref[
-                z, pl.ds(3 * near_model + j * span, span), :
-            ]
-    down[pl.ds(part, side), :] = down[pl.ds(part - side, side), :]
-    down_ref[...] = down[pl.ds(0, part), :]
+    half = chips * rows
+    incoming, outgoing = [], []
+
+    def fetch(source, target):
+        copy = pltpu.make_async_copy(source, target, in_sems.at[len(incoming)])
+        copy.start()
+        incoming.append(copy)
+        return copy
+
+    def send(source, target):
+        copy = pltpu.make_async_copy(source, target, out_sems.at[len(outgoing)])
+        copy.start()
+        outgoing.append(copy)
+
+    def fetch_half(source, target, i):
+        return [
+            fetch(source.at[k], target.at[pl.ds(i * half + k * rows, rows), :]) for k in range(chips)
+        ]
+
+    gate_up_copies = [
+        fetch(
+            pack_ref.at[z, pl.ds(j * near_model, near_model), :],
+            gate_up.at[pl.ds(z * near_model, near_model), pl.ds(j * near_model, near_model)],
+        )
+        for z in range(planes)
+        for j in range(3)
+    ]
+    normed_copies = [fetch_half(near_ref, normed, 0)]
+    for copy in gate_up_copies + normed_copies[0]:
+        copy.wait()
+    down_copies = [
+        fetch(
+            pack_ref.at[z, pl.ds(3 * near_model + j * span, span), :],
+            down.at[pl.ds(z * span, span), pl.ds(j * near_model, near_model)],
+        )
+        for z in range(planes)
+        for j in range(planes)
+    ]
+    cot_copies = [fetch_half(cot_near_ref, cot, 0)]
+    normed_copies.append(fetch_half(far_ref, normed, 1))
+    cot_copies.append(fetch_half(cot_far_ref, cot, 1))
     chunk = 2 * rows
-
-    def tokens_step(i, nothing):
-        here = pl.ds(pl.multiple_of(i * chunk, chunk), chunk)
+    first_unit, mid_unit, last_unit = (pl.ds(j * near_model, near_model) for j in range(3))
+    for i in range(chips):
+        here = pl.ds(i * chunk, chunk)
+        if i * chunk == half:
+            for copy in normed_copies[1] + cot_copies[1]:
+                copy.wait()
         pre = dot_nn(normed[here, :], gate_up[...])
-        hidden_grad = dot_nt(cot[here, :], down[...])
-        gate, mid, up = pre[:, :near_model], pre[:, near_model:-near_model], pre[:, -near_model:]
-        value, slope = gelu_parts(gate)
-        above = hidden_grad[:, :near_model]
-        hidden_ref[here, pl.ds(0, near_model)] = (value * up).astype(jnp.bfloat16)
-        pair_ref[here, pl.ds(0, near_model)] = (above * up * slope).astype(jnp.bfloat16)
-        pair_ref[here, pl.ds(2 * near_model, near_model)] = (above * value).astype(jnp.bfloat16)
+        if i == 0:
+            for copy in down_copies + cot_copies[0]:
+                copy.wait()
+            down[pl.ds(part, side), :] = down[pl.ds(part - side, side), :]
+        above = dot_nt(cot[here, :], down[...])
+        up = pre[:, 2 * near_model :]
+        value, slope = gelu_parts(pre[:, :near_model])
+        grad = above[:, :near_model]
+        hidden[here, first_unit] = (value * up).astype(bf16)
+        pair[here, first_unit] = (grad * up * slope).astype(bf16)
+        pair[here, last_unit] = (grad * value).astype(bf16)
+        mid = pre[:, near_model : 2 * near_model]
         first = lax.broadcasted_iota(jnp.int32, mid.shape, 1) < side
         turned = pltpu.roll(mid, side, 1)
         gate, up = jnp.where(first, mid, turned), jnp.where(first, turned, mid)
         value, slope = gelu_parts(gate)
-        above = hidden_grad[:, near_model:]
-        hidden_ref[here, pl.ds(near_model, side)] = (value * up)[:, :side].astype(jnp.bfloat16)
-        pair_ref[here, pl.ds(near_model, near_model)] = jnp.where(
-            first, above * up * slope, above * value
-        ).astype(jnp.bfloat16)
-        return nothing
-
-    lax.fori_loop(0, chips, tokens_step, 0)
+        grad = above[:, near_model:]
+        hidden[here, pl.ds(near_model, side)] = (value * up)[:, :side].astype(bf16)
+        pair[here, mid_unit] = jnp.where(first, grad * up * slope, grad * value).astype(bf16)
+        pair_t[:, here] = pair[here, :].T
+        hidden_t[:, here] = hidden[here, :].T
+    low = pl.ds(both, planes * span)
     for z in range(planes):
         here = pl.ds(z * near_model, near_model)
-        grad = dot_tn(normed[:, here], pair_ref[...]).astype(jnp.bfloat16)
-        for j in range(3):
-            grads_ref[z, pl.ds(j * near_model, near_model), :] = grad[
-                :, j * near_model : (j + 1) * near_model
-            ]
-        grad = dot_tn(hidden_ref[...], cot[:, here]).astype(jnp.bfloat16)
+        grad = dot_nn(hidden_t[...], cot[:, here]).astype(bf16)
         for j in range(planes):
-            grads_ref[j, pl.ds(3 * near_model + z * span, span), :] = grad[
-                j * span : (j + 1) * span
-            ]
+            grads[j, pl.ds(both + z * span, span), :] = grad[j * span : (j + 1) * span]
+    for z in range(planes):
+        send(grads.at[z, low, :], grads_out.at[z, low, :])
+    for z in range(planes):
+        here = pl.ds(z * near_model, near_model)
+        grads[z, pl.ds(0, both), :] = dot_nn(pair_t[...], normed[:, here]).astype(bf16)
+        send(grads.at[z, pl.ds(0, both), :], grads_out.at[z, pl.ds(0, both), :])
+    for i, out in ((0, mixed_near_out), (1, mixed_far_out)):
+        here = pl.ds(i * half, half)
+        mixed[here, :] = dot_nn(hidden[here, :], down[pl.ds(0, part), :]).astype(bf16)
+        for k in range(chips):
+            send(mixed.at[pl.ds(i * half + k * rows, rows), :], out.at[k])
+    for i, out in ((1, back_far_out), (0, back_near_out)):
+        here = pl.ds(i * half, half)
+        back[here, :] = dot_nt(pair[here, :], gate_up[...]).astype(bf16)
+        for k in range(chips):
+            send(back.at[pl.ds(i * half + k * rows, rows), :], out.at[k])
+    for copy in outgoing:
+        copy.wait()
 
 
 def unit_back_and_forth(near, far, cot_near, cot_far, pack, part):
-    chips = len(near)
-    rows, model = near[0].shape
+    chips, rows, model = near.shape
     length = 2 * chips * rows
-    _, _, near_model = pack.shape
+    planes, _, near_model = pack.shape
     bf16 = jnp.bfloat16
-    whole = pl.BlockSpec(memory_space=pltpu.VMEM)
+    there = pl.BlockSpec(memory_space=pl.ANY)
     return pl.pallas_call(
-        functools.partial(unit_kernel, chips),
-        in_specs=[whole] * (4 * chips + 1),
-        out_specs=[whole] * 4,
+        unit_kernel,
+        in_specs=[there] * 5,
+        out_specs=[there] * 5,
         scratch_shapes=[
             pltpu.VMEM((length, model), bf16),
             pltpu.VMEM((length, model), bf16),
             pltpu.VMEM((model, 2 * part), bf16),
             pltpu.VMEM((part + near_model // 2, model), bf16),
+            pltpu.VMEM((length, 2 * part), bf16),
+            pltpu.VMEM((length, part), bf16),
+            pltpu.VMEM((2 * part, length), bf16),
+            pltpu.VMEM((part, length), bf16),
+            pltpu.VMEM(pack.shape, bf16),
+            pltpu.VMEM((length, model), bf16),
+            pltpu.VMEM((length, model), bf16),
+            pltpu.SemaphoreType.DMA((4 * chips + planes * (3 + planes),)),
+            pltpu.SemaphoreType.DMA((4 * chips + 2 * planes,)),
         ],
-        out_shape=[
-            jax.ShapeDtypeStruct((length, 2 * part), bf16),
-            jax.ShapeDtypeStruct((length, part), bf16),
-            jax.ShapeDtypeStruct(pack.shape, bf16),
-            jax.ShapeDtypeStruct((part, model), bf16),
-        ],
+        out_shape=[jax.ShapeDtypeStruct(near.shape, bf16)] * 4
+        + [jax.ShapeDtypeStruct(pack.shape, bf16)],
         compiler_params=pltpu.CompilerParams(vmem_limit_bytes=58 * 1024 * 1024),
         name="unit_back_and_forth",
-    )(*near, *far, *cot_near, *cot_far, pack)
-
-
-def pair_back_kernel(pair_ref, pack_ref, out_ref):
-    near_model = pack_ref.shape[1]
-    total = dot_nt(pair_ref[:, :near_model], pack_ref[:near_model, :])
-    for j in (1, 2):
-        here = slice(j * near_model, (j + 1) * near_model)
-        total = total + dot_nt(pair_ref[:, here], pack_ref[here, :])
-    out_ref[...] = total.astype(out_ref.dtype)
-
-
-def pair_back(pair, pack, half):
-    length, both = pair.shape
-    planes, _, near_model = pack.shape
-    rows = length // 2
+    )(near, far, cot_near, cot_far, pack)
+
+
+def mix_pack_kernel(place_ref, input_ref, gelu_ref, out_ref, decay_ref, gate_ref, pack_ref):
+    near_model, width = input_ref.shape
+    heads, piece, model = out_ref.shape
+    pack_ref[pl.ds(0, near_model), pl.ds(0, width)] = input_ref[...]
+    pack_ref[pl.ds(0, near_model), pl.ds(width, width)] = gelu_ref[...]
+    row = near_model
+    for h in range(heads):
+        for j in range(model // (2 * width)):
+            pack_ref[pl.ds(row, piece), :] = out_ref[h, :, pl.ds(j * 2 * width, 2 * width)]
+            row += piece
+        pack_ref[pl.ds(row, piece), pl.ds(0, width)] = decay_ref[h]
+        pack_ref[pl.ds(row, piece), pl.ds(width, width)] = gate_ref[h]
+        row += piece
+
+
+def own_mix_pack(place, input_proj, gelu_proj, output_proj, decay_gate, input_gate):
+    near_model, channels = input_proj.shape
+    width = decay_gate.shape[1]
+    heads = decay_gate.shape[0] // width
+    model = output_proj.shape[1]
+    piece = width // (channels // width)
+    tall = near_model + heads * (model // (2 * width) + 1) * piece
+    mine = pl.BlockSpec((near_model, width), lambda i, s: (0, s[0]))
+    rows = lambda columns: pl.BlockSpec((heads, piece, columns), lambda i, s: (0, s[0], 0))
     return pl.pallas_call(
-        pair_back_kernel,
-        grid=(planes,),
-        in_specs=[
-            pl.BlockSpec((rows, both), lambda z: (half, 0)),
-            pl.BlockSpec((None, 3 * near_model, near_model), lambda z: (z, 0, 0)),
-        ],
-        out_specs=pl.BlockSpec((rows, near_model), lambda z: (0, z)),
-        out_shape=jax.ShapeDtypeStruct((rows, planes * near_model), jnp.bfloat16),
+        mix_pack_kernel,
+        grid_spec=pltpu.PrefetchScalarGridSpec(
+            num_scalar_prefetch=1,
+            grid=(1,),
+            in_specs=[mine, mine, rows(model), rows(width), rows(width)],
+            out_specs=pl.BlockSpec((tall, 2 * width), lambda i, s: (0, 0)),
+        ),
+        out_shape=jax.ShapeDtypeStruct((tall, 2 * width), input_proj.dtype),
+        name="own_mix_pack",
+    )(
+        place,
+        input_proj,
+        gelu_proj,
+        output_proj.reshape(heads, width, model),
+        decay_gate.reshape(heads, width, width),
+        input_gate.reshape(heads, width, width),
+    )
+
+
+def unit_pack_kernel(place_ref, gate_ref, up_ref, down_ref, pack_ref, windows, sems):
+    place = place_ref[0]
+    near_model, deep = gate_ref.shape
+    planes = windows.shape[1]
+    tile = 128
+    span = (pack_ref.shape[0] - 3 * near_model) // planes
+    extra = span - tile
+    copies = []
+
+    def fetch(source, target):
+        copies.append(pltpu.make_async_copy(source, target, sems.at[len(copies)]))
+        copies[-1].start()
+
+    for i, ref in enumerate((gate_ref, up_ref)):
+        for z in range(planes):
+            start = pl.multiple_of(z * (deep // planes) + place * tile, tile)
+            fetch(ref.at[:, pl.ds(start, 2 * tile)], windows.at[i, z])
+    rows = pl.ds(pl.multiple_of(place * span, 16), span)
+    for j in range(planes):
+        fetch(
+            down_ref.at[rows, pl.ds(j * near_model, near_model)],
+            pack_ref.at[pl.ds(3 * near_model + j * span, span), :],
+        )
+    lane = lax.broadcasted_iota(jnp.int32, (near_model, tile), 1)
+
+    def tiles(i):
+        parts = []
+        for z in range(planes):
+            copies[i * planes + z].wait()
+            turn = lax.rem((z - place) * extra + 2 * tile, 2 * tile)
+            parts.append(pltpu.roll(windows[i, z].astype(jnp.float32), turn, 1))
+        found = [parts[0][:, :tile]]
+        for z in range(1, planes):
+            found.append(jnp.where(lane < z * extra, parts[z - 1][:, tile:], parts[z][:, :tile]))
+        return found + [parts[planes - 1][:, tile:]]
+
+    gate, up = tiles(0), tiles(1)
+    half = tile // 2
+    turned = [pltpu.roll(up[j], half, 1) for j in (3, 4)]
+    mid = [
+        gate[3],
+        jnp.where(lane < half, gate[4], turned[0]),
+        jnp.where(lane < half, turned[0], turned[1]),
+    ]
+    for block, found in enumerate((gate[:3], mid, up[:3])):
+        for j in range(3):
+            pack_ref[pl.ds(block * near_model, near_model), pl.ds(j * tile, tile)] = found[
+                j
+            ].astype(pack_ref.dtype)
+    for copy in copies[2 * planes :]:
+        copy.wait()
+
+
+def own_unit_pack(place, mlp_gate, mlp_up, mlp_down, planes, span):
+    near_model = mlp_gate.shape[0]
+    tall = 3 * near_model + planes * span
+    there = pl.BlockSpec(memory_space=pl.ANY)
+    return pl.pallas_call(
+        unit_pack_kernel,
+        grid_spec=pltpu.PrefetchScalarGridSpec(
+            num_scalar_prefetch=1,
+            grid=(1,),
+            in_specs=[there] * 3,
+            out_specs=pl.BlockSpec((tall, near_model), lambda i, s: (0, 0)),
+            scratch_shapes=[
+                pltpu.VMEM((2, planes, near_model, 256), mlp_gate.dtype),
+                pltpu.SemaphoreType.DMA((3 * planes,)),
+            ],
+        ),
+        out_shape=jax.ShapeDtypeStruct((tall, near_model), mlp_gate.dtype),
+        compiler_params=pltpu.CompilerParams(vmem_limit_bytes=48 * 1024 * 1024),
+        name="own_unit_pack",
+    )(place, mlp_gate, mlp_up, mlp_down)
+
+
+def grad_pack_kernel(place_ref, in_ref, *refs):
+    *blocks, pack_ref = refs
+    place = place_ref[0]
+    chips = len(blocks) // 2
+    chip, core = place // 2, place % 2
+    near_model, both = in_ref.shape[1:]
+    tall, width = blocks[0].shape
+    pack_ref[:, pl.ds(0, near_model), :] = in_ref[...]
+    for k in range(chips):
+        home, away = blocks[k][...], blocks[chips + k][...]
+        odd = core == 1
+        pack_ref[chip ^ k, pl.ds(near_model, tall), pl.ds(0, width)] = jnp.where(odd, away, home)
+        pack_ref[chip ^ k, pl.ds(near_model, tall), pl.ds(width, width)] = jnp.where(odd, home, away)
+
+
+def grad_pack(place, in_grad, home, away):
+    planes, near_model, both = in_grad.shape
+    tall, width = home[0].shape
+    return pl.pallas_call(
+        grad_pack_kernel,
+        grid_spec=pltpu.PrefetchScalarGridSpec(
+            num_scalar_prefetch=1,
+            grid=(1,),
+            in_specs=[pl.BlockSpec(in_grad.shape, lambda i, s: (0, 0, 0))]
+            + [pl.BlockSpec((tall, width), lambda i, s: (0, 0))] * (2 * len(home)),
+            out_specs=pl.BlockSpec((planes, near_model + tall, both), lambda i, s: (0, 0, 0)),
+        ),
+        out_shape=jax.ShapeDtypeStruct((planes, near_model + tall, both), jnp.bfloat16),
         compiler_params=pltpu.CompilerParams(vmem_limit_bytes=32 * 1024 * 1024),
-        name="pair_back",
-    )(pair, pack)
+        name="grad_pack",
+    )(place, in_grad, *home, *away)
 
 
 def norm_back(values, scale, gain, grad):
@@ -857,48 +1082,23 @@
     def columns(x, start, size):
         return lax.dynamic_slice_in_dim(x, start, size, axis=1)
 
-    def own_rows(x):
-        mine = lax.dynamic_slice_in_dim(
-            x.reshape(heads, width, x.shape[1]), place * piece, piece, 1
-        )
-        return jnp.swapaxes(mine.reshape(heads, piece, -1, 2 * width), 1, 2)
-
-    rowset = jnp.concatenate(
-        [own_rows(output_proj), own_rows(jnp.concatenate([decay_gate, input_gate], axis=1))], axis=1
-    ).reshape(-1, 2 * width)
-    in_own = jnp.concatenate(
-        [columns(input_proj, place * width, width), columns(gelu_proj, place * width, width)],
-        axis=1,
-    )
-    mix_pack = lax.all_gather(jnp.concatenate([in_own, rowset], axis=0), "fsdp", axis=0)
-
-    def own_spans(x):
-        return jnp.concatenate(
-            [columns(x, z * (deep // planes) + place * span, span) for z in range(planes)], axis=1
-        )
-
-    gate_own, up_own = own_spans(mlp_gate), own_spans(mlp_up)
-    down_own = lax.dynamic_slice_in_dim(mlp_down, place * span, span, 0)
-    unit_pack = lax.all_gather(
-        jnp.concatenate(
-            [
-                gate_own[:, :near_model],
-                jnp.concatenate([gate_own[:, near_model:], up_own[:, near_model:]], axis=1),
-                up_own[:, :near_model],
-                jnp.swapaxes(down_own.reshape(span, planes, near_model), 0, 1).reshape(
-                    planes * span, near_model
-                ),
-            ],
-            axis=0,
-        ),
-        "fsdp",
-        axis=0,
-    )
+    place_arg = place.astype(jnp.int32)[None]
+    mix_pack, tokens = tie(
+        own_mix_pack(place_arg, input_proj, gelu_proj, output_proj, decay_gate, input_gate), tokens
+    )
+    mix_pack = lax.all_gather(mix_pack, "fsdp", axis=0)
 
     values = tokens[0].astype(f32)
     scale1 = lax.rsqrt(jnp.mean(values * values, axis=-1, keepdims=True) + norm_eps)
-    normed_near, normed_far = gather_blocks((values * scale1 * mix_gain).astype(bf16))
-    out_grad = cotangent[0]
+    normed_own, mlp_gate, mlp_up, mlp_down = tie(
+        (values * scale1 * mix_gain).astype(bf16), mlp_gate, mlp_up, mlp_down
+    )
+    normed_near, normed_far = gather_blocks(normed_own)
+    unit_pack = own_unit_pack(place_arg, mlp_gate, mlp_up, mlp_down, planes, span)
+    unit_pack, normed_near, normed_far, out_grad = tie(
+        unit_pack, normed_near, normed_far, cotangent[0]
+    )
+    unit_pack = lax.all_gather(unit_pack, "fsdp", axis=0)
     cot_near, cot_far = gather_blocks(out_grad)
 
     positions = jnp.arange(length, dtype=jnp.int32)
@@ -917,11 +1117,13 @@
         ],
         axis=0,
     )
-    place_arg = place.astype(jnp.int32)[None]
-
-    keep, got = exchange(mix_pack[:, near_model:].reshape(chips, 2, -1, 2 * width), chip, core)
-    merged, normed, *saved, weights = mix_forward(
-        place_arg, normed_near, normed_far, age, chan, mix_pack, keep, got, cot_near + cot_far
+
+    mix_pack, cot_near, cot_far, normed_near, normed_far = tie(
+        mix_pack, cot_near, cot_far, normed_near, normed_far
+    )
+    keep, got = exchange(mix_pack[:, near_model:].reshape(chips, 2, -1, 2 * width), chip, core, 0)
+    merged, *saved, weights = mix_forward(
+        place_arg, normed_near, normed_far, age, chan, mix_pack, keep, got
     )
     out_weights = weights[:, :model]
     in_weights = mix_pack[:, :near_model].reshape(model, 2 * width)
@@ -933,59 +1135,40 @@
 
     scale2 = lax.rsqrt(jnp.mean(middle * middle, axis=-1, keepdims=True) + norm_eps)
     near, far = gather_blocks((middle * scale2 * mlp_gain).astype(bf16))
-    pair, hidden, unit_grads, down = unit_back_and_forth(
+    back_near, back_far, mixed_near, mixed_far, unit_grads = unit_back_and_forth(
         near, far, cot_near, cot_far, unit_pack, part
     )
     unit_sum = lax.psum_scatter(unit_grads, "fsdp", scatter_dimension=0, tiled=False)
-    far = pair_back(pair, unit_pack, 1)
-    near = pair_back(pair, unit_pack, 0)
-    normed2_grad = scatter_blocks(
-        near.reshape(chips, rows, model), far.reshape(chips, rows, model)
-    )
-    split = length // 2
+    normed2_grad = scatter_blocks(back_near, back_far)
 
     mlp_gain_term = jnp.sum(normed2_grad * middle * scale2, axis=0)
     middle_grad = out_grad.astype(f32) + norm_back(middle, scale2, mlp_gain, normed2_grad)
-    near, far = gather_blocks(middle_grad.astype(bf16))
-
-    both, small, gate_grads, out_w_grad = mix_backward(
-        place_arg, near, far, age, chan, weights, saved
-    )
-    normed = normed.reshape(length, model)
-    both = both.reshape(length, 2 * width)
-    far = dot_nt(both[split:], in_weights).astype(bf16)
-    near = dot_nt(both[:split], in_weights)
-    normed_grad = scatter_blocks(
-        near.reshape(chips, rows, model), far.reshape(chips, rows, model)
-    )
-    in_grad = dot_tn(normed, both)
-    turned = jnp.concatenate(
-        [
-            out_w_grad.astype(bf16).reshape(devices, model // devices, width),
-            gate_grads[0].astype(bf16).reshape(devices, piece, width),
-            gate_grads[1].astype(bf16).reshape(devices, piece, width),
-        ],
-        axis=1,
-    )
-    tall = turned.shape[1]
-    keep, got = exchange(turned.reshape(chips, 2, tall, width), chip, core)
-    home = reorder([keep[k] for k in range(chips)], chip)
-    away = reorder([got[k] for k in range(chips)], chip)
-    by_head = [
-        jnp.concatenate(
-            [jnp.where(core == 0, home[k], away[k]), jnp.where(core == 0, away[k], home[k])], axis=1
-        )
-        for k in range(chips)
-    ]
-    share = chips // planes
-    row_pack = jnp.stack(
-        [jnp.concatenate(by_head[z * share : (z + 1) * share], axis=1) for z in range(planes)]
-    )
-    grad_pack = jnp.concatenate(
-        [in_grad.astype(bf16).reshape(planes, near_model, 2 * width), row_pack], axis=1
-    )
-    grad_pack, unit_sum = lax.optimization_barrier((grad_pack, unit_sum))
-    mix_sum = lax.psum_scatter(grad_pack, "fsdp", scatter_dimension=0, tiled=False).astype(f32)
+    middle_low, mixed_near, mixed_far = tie(middle_grad.astype(bf16), mixed_near, mixed_far)
+    near, far = gather_blocks(middle_low)
+    mixed_low, mixed_own = pair_blocks(mixed_near, mixed_far)
+    near, far, mixed_low, mixed_own = tie(near, far, mixed_low, mixed_own)
+
+    both, small, *by_chip = mix_backward(place_arg, near, far, age, chan, weights, saved)
+    mixed = (middle + spread_pairs(mixed_low, mixed_own)).astype(bf16)
+    mixed, *by_chip = tie(mixed, *by_chip)
+    arrived = [by_chip[0]] + [chip_swap(by_chip[k], k) for k in range(1, chips)]
+    in_grad = dot_tn(normed_near.reshape(-1, model), both[0].reshape(-1, 2 * width)) + dot_tn(
+        normed_far.reshape(-1, model), both[1].reshape(-1, 2 * width)
+    )
+    *arrived, both = tie(*arrived, both)
+    away = core_swap(jnp.stack([block[1] for block in arrived]))
+    pack, unit_sum, small, both = tie(
+        grad_pack(
+            place_arg,
+            in_grad.astype(bf16).reshape(planes, near_model, 2 * width),
+            [block[0] for block in arrived],
+            [away[k] for k in range(chips)],
+        ),
+        unit_sum,
+        small,
+        both,
+    )
+    mix_sum = lax.psum_scatter(pack, "fsdp", scatter_dimension=0, tiled=False).astype(f32)
     input_proj_grad = mix_sum[:near_model, :width]
     gelu_proj_grad = mix_sum[:near_model, width:]
     turned_sum = mix_sum[near_model:].T
@@ -994,39 +1177,31 @@
     decay_gate_grad = turned_sum[:, slim : slim + piece]
     input_gate_grad = turned_sum[:, slim + piece :]
 
-    first, mid, last, bottom = (
-        unit_sum[:near_model],
-        unit_sum[near_model : 2 * near_model],
-        unit_sum[2 * near_model : 3 * near_model],
-        unit_sum[3 * near_model :],
-    )
-    side = near_model // 2
-    gate_sum = jnp.concatenate([first, mid[:, :side]], axis=1)
-    up_sum = jnp.concatenate([last, mid[:, side:]], axis=1)
+    normed_grad = scatter_blocks(
+        dot_nt(both[0].reshape(-1, 2 * width), in_weights).reshape(chips, rows, model),
+        dot_nt(both[1].reshape(-1, 2 * width), in_weights).astype(bf16).reshape(chips, rows, model),
+    )
+
+    up_first = unit_sum[part + near_model // 2 : 2 * part]
+    up_sum = jnp.concatenate([up_first, unit_sum[part : part + near_model // 2]], axis=0)
+    gate_up_sum = jnp.stack([unit_sum[:part], up_sum]).reshape(2, planes, span, near_model)
     mlp_gate_grad, mlp_up_grad, mlp_down_grad = final_exchange(
-        jnp.stack([gate_sum.T, up_sum.T]).reshape(2, planes, span, near_model).swapaxes(0, 1),
-        bottom.reshape(planes, span, near_model),
+        gate_up_sum.swapaxes(0, 1),
+        unit_sum[2 * part :].reshape(planes, span, near_model),
         chip,
         core,
         chips,
     )
 
-    held = lax.optimization_barrier((hidden, down, both))
-    hidden, down = held[:2]
-    far = dot_nn(hidden[split:], down).astype(bf16)
-    near = dot_nn(hidden[:split], down)
-    mixed = (
-        middle
-        + scatter_blocks(near.reshape(chips, rows, model), far.reshape(chips, rows, model))
-    ).astype(bf16)
-
+    mix_gain_term = jnp.sum(in_grad * in_weights.astype(f32), axis=1) / mix_gain
+    gains = jnp.stack([mix_gain_term, mlp_gain_term]).reshape(-1, width)
+    small = over_planes(jnp.concatenate([small, gains], axis=0))
     values_part = norm_back(values, scale1, mix_gain, normed_grad)
     tokens_grad = (middle_grad + values_part).astype(bf16)
-    mix_gain_term = jnp.sum(in_grad * in_weights.astype(f32), axis=1) / mix_gain
     where_mine = (jnp.arange(devices) == place)[None, :, None]
-    spread = jnp.where(where_mine, small[:, None, :], 0.0).reshape(8, channels)
-    gains = jnp.pad(jnp.stack([mix_gain_term, mlp_gain_term]), ((0, 0), (0, channels - model)))
-    sums = total_over(jnp.concatenate([spread, gains], axis=0), ("fsdp", "seq"))
+    spread = jnp.where(where_mine, small[:8, None, :], 0.0).reshape(8, channels)
+    gains = jnp.pad(small[8:].reshape(2, model), ((0, 0), (0, channels - model)))
+    sums = total_over(jnp.concatenate([spread, gains], axis=0), ("seq",))
     return (
         mixed[None],
         tokens_grad[None],

time: 408 us -> 379 us (0.929)
  local copies, waits for them, and re-layouts: 46.7 us -> 22.9 us
  other arithmetic: 38.1 us -> 25.6 us
  waiting for transfers between devices: 185 us -> 190 us
    ppermute x33, waiting for transfers between devices: 125 us -> 142 us  [chip_swap(): return lax.ppermute(x, 'seq', [(i, i ^ 2 * k) for i in range(devices)])]
    concatenate x7 -> x2, other arithmetic: 16.6 us -> 0.06 us  [the longest x1 0.05 us: narrow_shards(): jnp.concatenate([up_first, unit_sum[part:part + near_model // 2]], axis=0)]
    all_gather x2, waiting for transfers between devices: 34.6 us -> 23 us  [the longest x1 12.5 us: narrow_shards(): unit_pack = lax.all_gather(unit_pack, 'fsdp', axis=0)]
    dynamic_slice x7 -> x0, local copies, waits for them, and re-layouts: 9.06 us -> none  [the longest x4 6.58 us: columns(): return lax.dynamic_slice_in_dim(x, start, size, axis=1)]
    unnamed x134 -> x65, local copies, waits for them, and re-layouts: 13.8 us -> 6.6 us
    ppermute x24 -> x12, waiting for transfers between devices: 5.03 us -> 11 us  [core_swap(): return lax.ppermute(x, 'seq', [(i, i ^ 1) for i in range(devices)])]
    another operation x6 -> x7, other arithmetic: 0.12 us -> 5.68 us  [the longest x5 5.6 us: gather_blocks(): near = jnp.stack([x] + [chip_swap(x, k) for k in range(1, chips)])]
    reduce_scatter x1, waiting for transfers between devices: 5.11 us -> 0.01 us  [narrow_shards(): lax.psum_scatter(pack, 'fsdp', scatter_dimension=0, tiled=False).astype(f32)]
  transfers between devices with their start and end apart: 66 -> 55, of which waited for: 35 -> 35; matrix products, arithmetic and copies ran while one was open for 18% -> 14% of each run, Pallas kernels for 8% -> 8%
where the time goes in v2:
time: 379 us; the launch traced here: 374 us
  waiting for transfers between devices  190 us (50%)
  Pallas kernels  60.3 us (16%)
  starting transfers between devices  47.9 us (13%)
  other arithmetic  25.6 us (7%)
  local copies, waits for them, and re-layouts  22.9 us (6%)
  between operations  15.1 us (4%)
  matrix products  12.1 us (3%)
    ppermute x33, waiting for transfers between devices, chip_swap(): return lax.ppermute(x, 'seq', [(i, i ^ 2 * k) for i in range(devices)])  142 us
    ppermute x33, starting transfers between devices, chip_swap(): return lax.ppermute(x, 'seq', [(i, i ^ 2 * k) for i in range(devices)])  39.8 us
    pallas_call x1, Pallas kernels, unit_back_and_forth(): pl.pallas_call(unit_kernel, in_specs=[there] * 5, out_specs=[there] * 5,...  27.4 us
    ppermute x3, waiting for transfers between devices, total_over(): x = x + lax.ppermute(x, axis, [(i, i ^ bit) for i in range(devices)])  14.1 us
    pallas_call x1, Pallas kernels, mix_backward(): pl.pallas_call(mix_backward_kernel, grid_spec=pltpu.PrefetchScalarGridSpe...  14 us
    all_gather x1, waiting for transfers between devices, narrow_shards(): unit_pack = lax.all_gather(unit_pack, 'fsdp', axis=0)  12.5 us
    pallas_call x1, Pallas kernels, mix_forward(): pl.pallas_call(mix_forward_kernel, grid_spec=pltpu.PrefetchScalarGridSpec...  12.2 us
    ppermute x12, waiting for transfers between devices, core_swap(): return lax.ppermute(x, 'seq', [(i, i ^ 1) for i in range(devices)])  11 us
  transfers between devices with their start and end apart: 55, of which 35 were waited for; matrix products, arithmetic and copies ran while one was open for 14% of the time, Pallas kernels for 8%

profile of v2, /device:TPU:0, one launch (start us, length us, event | category | flops | bytes accessed | tf_op | source)
XLA Modules:
  0.0 373.9 jit_solution(11429040316699841761)
XLA Ops:
  10.4 3.9 %collective-permute-start.2 = (bf16[128,1536]{1,0:T(8,128)(2,1)}, bf16[128,1536]{1,0:T(8,128)(2,1)}, u32[]{:S(2)}, u32[]{:S(2)}) collective-permute-start(bf16[128,1536]{1,0:T(8,128)(2,1)} %fusion.2), channel_id=1, source_target_pairs={{0,24},{4,28},{8,16},{12,20},{16,8},{20,12},{24,0},{28,4},{1,25},{... | collective-permute-start | bytes 1179656 | tf_op jit(solution)/shard_map/ppermute | solution.py:292
  14.9 9.7 %collective-permute-done.2 = bf16[128,1536]{1,0:T(8,128)(2,1)} collective-permute-done((bf16[128,1536]{1,0:T(8,128)(2,1)}, bf16[128,1536]{1,0:T(8,128)(2,1)}, u32[]{:S(2)}, u32[]{:S(2)}) %collective-permute-start.2) | collective-permute-done | bytes 393248 | tf_op jit(solution)/shard_map/ppermute | solution.py:292
  24.6 7.6 %collective-permute-done.1 = bf16[128,1536]{1,0:T(8,128)(2,1)} collective-permute-done((bf16[128,1536]{1,0:T(8,128)(2,1)}, bf16[128,1536]{1,0:T(8,128)(2,1)}, u32[]{:S(2)}, u32[]{:S(2)}) %collective-permute-start.1) | collective-permute-done | bytes 393248 | tf_op jit(solution)/shard_map/ppermute | solution.py:292
  32.5 2.7 pad_maximum_fusion.near_ref
  35.2 3.0 own_unit_pack.1
  42.4 9.6 %collective-permute-done.6 = bf16[128,1536]{1,0:T(8,128)(2,1)S(1)} collective-permute-done((bf16[128,1536]{1,0:T(8,128)(2,1)}, bf16[128,1536]{1,0:T(8,128)(2,1)S(1)}, u32[]{:S(2)}, u32[]{:S(2)}) %collective-permute-start.6) | collective-permute-done | bytes 393248 | tf_op jit(solution)/shard_map/ppermute | solution.py:292
  52.0 7.6 %collective-permute-done.5 = bf16[128,1536]{1,0:T(8,128)(2,1)S(1)} collective-permute-done((bf16[128,1536]{1,0:T(8,128)(2,1)}, bf16[128,1536]{1,0:T(8,128)(2,1)S(1)}, u32[]{:S(2)}, u32[]{:S(2)}) %collective-permute-start.5) | collective-permute-done | bytes 393248 | tf_op jit(solution)/shard_map/ppermute | solution.py:292
  61.1 10.5 %all-gather.5.cloned.1.call-done = bf16[2560,512]{1,0:T(8,128)(2,1)} async-done(((bf16[640,512]{1,0:T(8,128)(2,1)}), bf16[2560,512]{1,0:T(8,128)(2,1)}) %all-gather.5.cloned.1.call-update) | async-done | bytes 2621456 | tf_op jit(solution)/shard_map/all_gather | solution.py:1089
  77.1 6.7 %collective-permute-done.10 = bf16[2,128,512]{2,1,0:T(8,128)(2,1)S(1)} collective-permute-done((bf16[2,128,512]{2,1,0:T(8,128)(2,1)S(1)}, bf16[2,128,512]{2,1,0:T(8,128)(2,1)S(1)}, u32[]{:S(2)}, u32[]{:S(2)}) %collective-permute-start.10) | collective-permute-done | bytes 262176 | tf_op jit(solution)/shard_map/ppermute | solution.py:292
  83.8 4.4 %collective-permute-done.9 = bf16[2,128,512]{2,1,0:T(8,128)(2,1)S(1)} collective-permute-done((bf16[2,128,512]{2,1,0:T(8,128)(2,1)S(1)}, bf16[2,128,512]{2,1,0:T(8,128)(2,1)S(1)}, u32[]{:S(2)}, u32[]{:S(2)}) %collective-permute-start.9) | collective-permute-done | bytes 262176 | tf_op jit(solution)/shard_map/ppermute | solution.py:292
  92.8 12.2 %mix_forward.1 = (bf16[2,4,128,256]{3,2,1,0:T(8,128)(2,1)}, bf16[1024,256]{1,0:T(8,128)(2,1)}, f32[1024,256]{1,0:T(8,128)}, bf16[1024,256]{1,0:T(8,128)(2,1)}, f...) custom-call(s32[1]{0:T(128)} %bitcast.place_ref.seq_ref, ...), custom_call_target="tpu_custom_call" | custom-call | tf_op jit(solution)/shard_map/mix_forward/pallas_call | solution.py:529
  108.3 3.0 collective-permute-done.12
  115.6 8.4 %collective-permute-done.13 = bf16[128,1536]{1,0:T(8,128)(2,1)S(1)} collective-permute-done((bf16[128,1536]{1,0:T(8,128)(2,1)S(1)}, bf16[128,1536]{1,0:T(8,128)(2,1)S(1)}, u32[]{:S(2)}, u32[]{:S(2)}) %collective-permute-start.13) | collective-permute-done | bytes 393248 | tf_op jit(solution)/shard_map/ppermute | solution.py:292
  124.0 8.8 %collective-permute-done.15 = bf16[128,1536]{1,0:T(8,128)(2,1)S(1)} collective-permute-done((bf16[128,1536]{1,0:T(8,128)(2,1)S(1)}, bf16[128,1536]{1,0:T(8,128)(2,1)S(1)}, u32[]{:S(2)}, u32[]{:S(2)}) %collective-permute-start.15) | collective-permute-done | bytes 393248 | tf_op jit(solution)/shard_map/ppermute | solution.py:292
  138.7 7.5 %collective-permute-done.17 = bf16[128,1536]{1,0:T(8,128)(2,1)S(1)} collective-permute-done((bf16[128,1536]{1,0:T(8,128)(2,1)S(1)}, bf16[128,1536]{1,0:T(8,128)(2,1)S(1)}, u32[]{:S(2)}, u32[]{:S(2)}) %collective-permute-start.17) | collective-permute-done | bytes 393248 | tf_op jit(solution)/shard_map/ppermute | solution.py:292
  147.8 7.0 %collective-permute-done.18 = bf16[128,1536]{1,0:T(8,128)(2,1)S(1)} collective-permute-done((bf16[128,1536]{1,0:T(8,128)(2,1)S(1)}, bf16[128,1536]{1,0:T(8,128)(2,1)S(1)}, u32[]{:S(2)}, u32[]{:S(2)}) %collective-permute-start.18) | collective-permute-done | bytes 393248 | tf_op jit(solution)/shard_map/ppermute | solution.py:292
  155.1 3.5 collective-permute-done.19.far_ref
  158.6 12.5 %all-gather.7.cloned.1.call-done = bf16[6912,384]{1,0:T(8,128)(2,1)} async-done(((bf16[1728,384]{1,0:T(8,128)(2,1)}), bf16[6912,384]{1,0:T(8,128)(2,1)}) %all-gather.7.cloned.1.call-update) | async-done | bytes 5308432 | tf_op jit(solution)/shard_map/all_gather | solution.py:1101
  171.1 27.4 %unit_back_and_forth.1 = (bf16[4,128,1536]{2,1,0:T(8,128)(2,1)}, bf16[4,128,1536]{2,1,0:T(8,128)(2,1)}, bf16[4,128,1536]{2,1,0:T(8,128)(2,1)}, bf16[4,128,1536]{2,1,0:T(8,128)(2,1)}, bf16[4,1728,384]{2,1,0:T(8,128)(2,1)}) custom-call(bf16[4,128,1536]{2,1,0:T(8,128)(2,1)} %copy-done.8, bf16[4,128,1536]{2,1,0:T(8,128)(2,1)} %collective-permute-done.19.far_ref, ...), custom_call_target="tpu_custom_call" | custom-call | tf_op jit(solution)/shard_map/unit_back_and_forth/pallas_call | solution.py:860
  198.7 3.7 collective-permute-done.20
  208.4 8.5 %collective-permute-done.21 = bf16[128,1536]{1,0:T(8,128)(2,1)S(1)} collective-permute-done((bf16[128,1536]{1,0:T(8,128)(2,1)S(1)}, bf16[128,1536]{1,0:T(8,128)(2,1)S(1)}, u32[]{:S(2)}, u32[]{:S(2)}) %collective-permute-start.21) | collective-permute-done | bytes 393248 | tf_op jit(solution)/shard_map/ppermute | solution.py:292
  216.9 8.3 %collective-permute-done.23 = bf16[128,1536]{1,0:T(8,128)(2,1)S(1)} collective-permute-done((bf16[128,1536]{1,0:T(8,128)(2,1)S(1)}, bf16[128,1536]{1,0:T(8,128)(2,1)S(1)}, u32[]{:S(2)}, u32[]{:S(2)}) %collective-permute-start.23) | collective-permute-done | bytes 393248 | tf_op jit(solution)/shard_map/ppermute | solution.py:292
  232.2 9.4 %collective-permute-done.26 = bf16[128,1536]{1,0:T(8,128)(2,1)S(1)} collective-permute-done((bf16[128,1536]{1,0:T(8,128)(2,1)S(1)}, bf16[128,1536]{1,0:T(8,128)(2,1)S(1)}, u32[]{:S(2)}, u32[]{:S(2)}) %collective-permute-start.26) | collective-permute-done | bytes 393248 | tf_op jit(solution)/shard_map/ppermute | solution.py:292
  241.6 8.0 %collective-permute-done.25 = bf16[128,1536]{1,0:T(8,128)(2,1)S(1)} collective-permute-done((bf16[128,1536]{1,0:T(8,128)(2,1)S(1)}, bf16[128,1536]{1,0:T(8,128)(2,1)S(1)}, u32[]{:S(2)}, u32[]{:S(2)}) %collective-permute-start.25) | collective-permute-done | bytes 393248 | tf_op jit(solution)/shard_map/ppermute | solution.py:292
  259.6 14.0 %mix_backward.1 = (bf16[2,4,128,512]{3,2,1,0:T(8,128)(2,1)}, f32[8,256]{1,0:T(8,128)}, bf16[2,256,256]{2,1,0:T(8,128)(2,1)}, bf16[2,256,256]{2,1,0:T(8,128)(2,1)...) custom-call(s32[1]{0:T(128)} %bitcast.place_ref.seq_ref, bf16[4,128,1536]{2,1,0:T(8,128)(2,1)} %pad_maximum_fusion.3.near_ref, ...), custom_call_target="tpu_custom_call" | custom-call | flops 10000000000 | bytes 40000000 | tf_op jit(solution)/shard_map/mix_backward/pallas_call | solution.py:688
  284.4 3.1 collective-permute-done.32
  287.5 3.7 collective-permute-done.33
  291.4 2.8 multiply_reduce_fusion
  296.6 3.9 %collective-permute-start.40 = (f32[20,256]{1,0:T(8,128)S(1)}, f32[20,256]{1,0:T(8,128)S(1)}, u32[]{:S(2)}, u32[]{:S(2)}) collective-permute-start(f32[20,256]{1,0:T(8,128)S(1)} %constant_dynamic-update-slice_fusion), channel_id=1, source_target_pairs={{0,1},{1,0},{2,3},{3,2},{4,5},{5,4},{6,7},{7,6},{8,9},{9,8},{10,11... | collective-permute-start | bytes 61448 | tf_op jit(solution)/shard_map/ppermute | solution.py:350
  314.8 11.1 %collective-permute-done.45 = f32[10,2048]{1,0:T(8,128)S(1)} collective-permute-done((f32[10,2048]{1,0:T(8,128)S(1)}, f32[10,2048]{1,0:T(8,128)S(1)}, u32[]{:S(2)}, u32[]{:S(2)}) %collective-permute-start.45) | collective-permute-done | bytes 81952 | tf_op jit(solution)/shard_map/ppermute | solution.py:359
  345.0 7.0 %collective-permute-done.37 = bf16[128,1536]{1,0:T(8,128)(2,1)S(1)} collective-permute-done((bf16[128,1536]{1,0:T(8,128)(2,1)S(1)}, bf16[128,1536]{1,0:T(8,128)(2,1)S(1)}, u32[]{:S(2)}, u32[]{:S(2)}) %collective-permute-start.37) | collective-permute-done | bytes 393248 | tf_op jit(solution)/shard_map/ppermute | solution.py:292
  352.0 8.1 %collective-permute-done.39 = bf16[128,1536]{1,0:T(8,128)(2,1)S(1)} collective-permute-done((bf16[128,1536]{1,0:T(8,128)(2,1)S(1)}, bf16[128,1536]{1,0:T(8,128)(2,1)S(1)}, u32[]{:S(2)}, u32[]{:S(2)}) %collective-permute-start.39) | collective-permute-done | bytes 393248 | tf_op jit(solution)/shard_map/ppermute | solution.py:292
  (252 shorter events, 111.3 us)
Async XLA Ops:
  7.2 64.4 %all-gather.5.cloned.1.call-start = ((), (), s32[]{:S(2)}) async-start(), calls=%async_computation.4 | async-start | bytes 3276800 | tf_op jit(solution)/shard_map/all_gather | solution.py:1089
  10.4 14.2 %collective-permute-start.2 = (bf16[128,1536]{1,0:T(8,128)(2,1)}, bf16[128,1536]{1,0:T(8,128)(2,1)}, u32[]{:S(2)}, u32[]{:S(2)}) collective-permute-start(bf16[128,1536]{1,0:T(8,128)(2,1)} %fusion.2), channel_id=1, source_target_pairs={{0,24},{4,28},{8,16},{12,20},{16,8},{20,12},{24,0},{28,4},{1,25},{... | collective-permute-start | bytes 1179656 | tf_op jit(solution)/shard_map/ppermute | solution.py:292
  14.3 17.9 %collective-permute-start.1 = (bf16[128,1536]{1,0:T(8,128)(2,1)}, bf16[128,1536]{1,0:T(8,128)(2,1)}, u32[]{:S(2)}, u32[]{:S(2)}) collective-permute-start(bf16[128,1536]{1,0:T(8,128)(2,1)} %fusion.2), channel_id=1, source_target_pairs={{0,16},{4,20},{8,24},{12,28},{16,0},{20,4},{24,8},{28,12},{1,17},{... | collective-permute-start | bytes 1179656 | tf_op jit(solution)/shard_map/ppermute | solution.py:292
  14.8 17.6 %collective-permute-start = (bf16[128,1536]{1,0:T(8,128)(2,1)}, bf16[128,1536]{1,0:T(8,128)(2,1)}, u32[]{:S(2)}, u32[]{:S(2)}) collective-permute-start(bf16[128,1536]{1,0:T(8,128)(2,1)} %fusion.2), channel_id=1, source_target_pairs={{0,8},{4,12},{8,0},{12,4},{16,24},{20,28},{24,16},{28,20},{1,9},{5... | collective-permute-start | bytes 1179656 | tf_op jit(solution)/shard_map/ppermute | solution.py:292
  14.9 156.2 %all-gather.7.cloned.1.call-start = ((), (), s32[]{:S(2)}) async-start(), calls=%async_computation.5 | async-start | bytes 6635520 | tf_op jit(solution)/shard_map/all_gather | solution.py:1101
  38.9 13.1 %collective-permute-start.6 = (bf16[128,1536]{1,0:T(8,128)(2,1)}, bf16[128,1536]{1,0:T(8,128)(2,1)S(1)}, u32[]{:S(2)}, u32[]{:S(2)}) collective-permute-start(bf16[128,1536]{1,0:T(8,128)(2,1)} %bitcast.249), channel_id=1, source_target_pairs={{0,24},{4,28},{8,16},{12,20},{16,8},{20,12},{24,0},{28,4},{1,25},{... | collective-permute-start | bytes 1179656 | tf_op jit(solution)/shard_map/ppermute | solution.py:292
  40.4 19.2 %collective-permute-start.5 = (bf16[128,1536]{1,0:T(8,128)(2,1)}, bf16[128,1536]{1,0:T(8,128)(2,1)S(1)}, u32[]{:S(2)}, u32[]{:S(2)}) collective-permute-start(bf16[128,1536]{1,0:T(8,128)(2,1)} %bitcast.250), channel_id=1, source_target_pairs={{0,16},{4,20},{8,24},{12,28},{16,0},{20,4},{24,8},{28,12},{1,17},{... | collective-permute-start | bytes 1179656 | tf_op jit(solution)/shard_map/ppermute | solution.py:292
  41.9 17.7 %collective-permute-start.4 = (bf16[128,1536]{1,0:T(8,128)(2,1)}, bf16[128,1536]{1,0:T(8,128)(2,1)S(1)}, u32[]{:S(2)}, u32[]{:S(2)}) collective-permute-start(bf16[128,1536]{1,0:T(8,128)(2,1)} %bitcast.251), channel_id=1, source_target_pairs={{0,8},{4,12},{8,0},{12,4},{16,24},{20,28},{24,16},{28,20},{1,9},{5... | collective-permute-start | bytes 1179656 | tf_op jit(solution)/shard_map/ppermute | solution.py:292
  61.0 235.0 %reduce-scatter.3.cloned.1.call-start = ((), (), s32[]{:S(2)}) async-start(), calls=%async_computation.2 | async-start | bytes 6635520 | tf_op jit(solution)/shard_map/reduce_scatter | solution.py:1141
  76.0 12.1 %collective-permute-start.9 = (bf16[2,128,512]{2,1,0:T(8,128)(2,1)S(1)}, bf16[2,128,512]{2,1,0:T(8,128)(2,1)S(1)}, u32[]{:S(2)}, u32[]{:S(2)}) collective-permute-start(bf16[2,128,512]{2,1,0:T(8,128)(2,1)S(1)} %get-tuple-element.252), channel_id=1, source_target_pairs={{0,16},{4,20},{8,24},{12,28},{16,0},{20,4},{24,8},{28,12},{1,17},{... | collective-permute-start | bytes 786440 | tf_op jit(solution)/shard_map/ppermute | solution.py:292
  113.6 19.3 %collective-permute-start.15 = (bf16[128,1536]{1,0:T(8,128)(2,1)S(1)}, bf16[128,1536]{1,0:T(8,128)(2,1)S(1)}, u32[]{:S(2)}, u32[]{:S(2)}) collective-permute-start(bf16[128,1536]{1,0:T(8,128)(2,1)S(1)} %get-tuple-element.234), channel_id=1, source_target_pairs={{0,24},{4,28},{8,16},{12,20},{16,8},{20,12},{24,0},{28,4},{1,25},{... | collective-permute-start | bytes 1179656 | tf_op jit(solution)/shard_map/ppermute | solution.py:292
  115.0 19.2 %collective-permute-start.14 = (bf16[128,1536]{1,0:T(8,128)(2,1)S(1)}, bf16[128,1536]{1,0:T(8,128)(2,1)S(1)}, u32[]{:S(2)}, u32[]{:S(2)}) collective-permute-start(bf16[128,1536]{1,0:T(8,128)(2,1)S(1)} %get-tuple-element.235), channel_id=1, source_target_pairs={{0,16},{4,20},{8,24},{12,28},{16,0},{20,4},{24,8},{28,12},{1,17},{... | collective-permute-start | bytes 1179656 | tf_op jit(solution)/shard_map/ppermute | solution.py:292
  135.7 12.1 %collective-permute-start.16 = (bf16[128,1536]{1,0:T(8,128)(2,1)S(1)}, bf16[128,1536]{1,0:T(8,128)(2,1)S(1)}, u32[]{:S(2)}, u32[]{:S(2)}) collective-permute-start(bf16[128,1536]{1,0:T(8,128)(2,1)S(1)} %multiply_convert_fusion), channel_id=1, source_target_pairs={{0,8},{4,12},{8,0},{12,4},{16,24},{20,28},{24,16},{28,20},{1,9},{5... | collective-permute-start | bytes 1179656 | tf_op jit(solution)/shard_map/ppermute | solution.py:292
  137.2 17.6 %collective-permute-start.18 = (bf16[128,1536]{1,0:T(8,128)(2,1)S(1)}, bf16[128,1536]{1,0:T(8,128)(2,1)S(1)}, u32[]{:S(2)}, u32[]{:S(2)}) collective-permute-start(bf16[128,1536]{1,0:T(8,128)(2,1)S(1)} %multiply_convert_fusion), channel_id=1, source_target_pairs={{0,24},{4,28},{8,16},{12,20},{16,8},{20,12},{24,0},{28,4},{1,25},{... | collective-permute-start | bytes 1179656 | tf_op jit(solution)/shard_map/ppermute | solution.py:292
  198.6 164.5 %reduce-scatter.5.cloned.1.call-start = ((), (), s32[]{:S(2)}) async-start(), calls=%async_computation.3 | async-start | bytes 3276800 | tf_op jit(solution)/shard_map/reduce_scatter | solution.py:1171
  206.1 19.1 %collective-permute-start.23 = (bf16[128,1536]{1,0:T(8,128)(2,1)S(1)}, bf16[128,1536]{1,0:T(8,128)(2,1)S(1)}, u32[]{:S(2)}, u32[]{:S(2)}) collective-permute-start(bf16[128,1536]{1,0:T(8,128)(2,1)S(1)} %get-tuple-element.231), channel_id=1, source_target_pairs={{0,24},{4,28},{8,16},{12,20},{16,8},{20,12},{24,0},{28,4},{1,25},{... | collective-permute-start | bytes 1179656 | tf_op jit(solution)/shard_map/ppermute | solution.py:292
  207.6 19.0 %collective-permute-start.22 = (bf16[128,1536]{1,0:T(8,128)(2,1)S(1)}, bf16[128,1536]{1,0:T(8,128)(2,1)S(1)}, u32[]{:S(2)}, u32[]{:S(2)}) collective-permute-start(bf16[128,1536]{1,0:T(8,128)(2,1)S(1)} %get-tuple-element.232), channel_id=1, source_target_pairs={{0,16},{4,20},{8,24},{12,28},{16,0},{20,4},{24,8},{28,12},{1,17},{... | collective-permute-start | bytes 1179656 | tf_op jit(solution)/shard_map/ppermute | solution.py:292
  228.7 23.3 %collective-permute-start.28 = (bf16[4,128,1536]{2,1,0:T(8,128)(2,1)}, bf16[4,128,1536]{2,1,0:T(8,128)(2,1)}, u32[]{:S(2)}, u32[]{:S(2)}) collective-permute-start(bf16[4,128,1536]{2,1,0:T(8,128)(2,1)} %get-tuple-element.96), channel_id=1, source_target_pairs={{0,4},{4,0},{8,12},{12,8},{16,20},{20,16},{24,28},{28,24},{1,5},{5... | collective-permute-start | bytes 4718600 | tf_op jit(solution)/shard_map/ppermute | solution.py:297
  228.7 12.9 %collective-permute-start.26 = (bf16[128,1536]{1,0:T(8,128)(2,1)S(1)}, bf16[128,1536]{1,0:T(8,128)(2,1)S(1)}, u32[]{:S(2)}, u32[]{:S(2)}) collective-permute-start(bf16[128,1536]{1,0:T(8,128)(2,1)S(1)} %get-tuple-element.94), channel_id=1, source_target_pairs={{0,24},{4,28},{8,16},{12,20},{16,8},{20,12},{24,0},{28,4},{1,25},{... | collective-permute-start | bytes 1179656 | tf_op jit(solution)/shard_map/ppermute | solution.py:292
  230.2 19.4 %collective-permute-start.25 = (bf16[128,1536]{1,0:T(8,128)(2,1)S(1)}, bf16[128,1536]{1,0:T(8,128)(2,1)S(1)}, u32[]{:S(2)}, u32[]{:S(2)}) collective-permute-start(bf16[128,1536]{1,0:T(8,128)(2,1)S(1)} %get-tuple-element.94), channel_id=1, source_target_pairs={{0,16},{4,20},{8,24},{12,28},{16,0},{20,4},{24,8},{28,12},{1,17},{... | collective-permute-start | bytes 1179656 | tf_op jit(solution)/shard_map/ppermute | solution.py:292
  231.7 17.9 %collective-permute-start.24 = (bf16[128,1536]{1,0:T(8,128)(2,1)S(1)}, bf16[128,1536]{1,0:T(8,128)(2,1)S(1)}, u32[]{:S(2)}, u32[]{:S(2)}) collective-permute-start(bf16[128,1536]{1,0:T(8,128)(2,1)S(1)} %get-tuple-element.94), channel_id=1, source_target_pairs={{0,8},{4,12},{8,0},{12,4},{16,24},{20,28},{24,16},{28,20},{1,9},{5... | collective-permute-start | bytes 1179656 | tf_op jit(solution)/shard_map/ppermute | solution.py:292
  256.1 18.8 %collective-permute-start.29 = (bf16[128,1536]{1,0:T(8,128)(2,1)S(1)}, bf16[128,1536]{1,0:T(8,128)(2,1)S(1)}, u32[]{:S(2)}, u32[]{:S(2)}) collective-permute-start(bf16[128,1536]{1,0:T(8,128)(2,1)S(1)} %get-tuple-element.227), channel_id=1, source_target_pairs={{0,8},{4,12},{8,0},{12,4},{16,24},{20,28},{24,16},{28,20},{1,9},{5... | collective-permute-start | bytes 1179656 | tf_op jit(solution)/shard_map/ppermute | solution.py:292
  257.2 18.9 %collective-permute-start.31 = (bf16[128,1536]{1,0:T(8,128)(2,1)S(1)}, bf16[128,1536]{1,0:T(8,128)(2,1)S(1)}, u32[]{:S(2)}, u32[]{:S(2)}) collective-permute-start(bf16[128,1536]{1,0:T(8,128)(2,1)S(1)} %get-tuple-element.228), channel_id=1, source_target_pairs={{0,24},{4,28},{8,16},{12,20},{16,8},{20,12},{24,0},{28,4},{1,25},{... | collective-permute-start | bytes 1179656 | tf_op jit(solution)/shard_map/ppermute | solution.py:292
  258.3 19.1 %collective-permute-start.30 = (bf16[128,1536]{1,0:T(8,128)(2,1)S(1)}, bf16[128,1536]{1,0:T(8,128)(2,1)S(1)}, u32[]{:S(2)}, u32[]{:S(2)}) collective-permute-start(bf16[128,1536]{1,0:T(8,128)(2,1)S(1)} %get-tuple-element.229), channel_id=1, source_target_pairs={{0,16},{4,20},{8,24},{12,28},{16,0},{20,4},{24,8},{28,12},{1,17},{... | collective-permute-start | bytes 1179656 | tf_op jit(solution)/shard_map/ppermute | solution.py:292
  306.4 20.8 %collective-permute-start.47 = (bf16[3,144,384]{2,1,0:T(8,128)(2,1)S(1)}, bf16[3,144,384]{2,1,0:T(8,128)(2,1)S(1)}, u32[]{:S(2)}, u32[]{:S(2)}) collective-permute-start(bf16[3,144,384]{2,1,0:T(8,128)(2,1)S(1)} %get-tuple-element.238), channel_id=1, source_target_pairs={{0,16},{4,20},{8,24},{12,28},{16,0},{20,4},{24,8},{28,12},{1,17},{... | collective-permute-start | bytes 995336 | tf_op jit(solution)/shard_map/ppermute | solution.py:292
  307.5 19.7 %collective-permute-start.46 = (bf16[3,144,384]{2,1,0:T(8,128)(2,1)S(1)}, bf16[3,144,384]{2,1,0:T(8,128)(2,1)S(1)}, u32[]{:S(2)}, u32[]{:S(2)}) collective-permute-start(bf16[3,144,384]{2,1,0:T(8,128)(2,1)S(1)} %get-tuple-element.240), channel_id=1, source_target_pairs={{0,8},{4,12},{8,0},{12,4},{16,24},{20,28},{24,16},{28,20},{1,9},{5... | collective-permute-start | bytes 995336 | tf_op jit(solution)/shard_map/ppermute | solution.py:292
  308.3 18.9 %collective-permute-start.48 = (bf16[3,144,384]{2,1,0:T(8,128)(2,1)S(1)}, bf16[3,144,384]{2,1,0:T(8,128)(2,1)S(1)}, u32[]{:S(2)}, u32[]{:S(2)}) collective-permute-start(bf16[3,144,384]{2,1,0:T(8,128)(2,1)S(1)} %get-tuple-element.241), channel_id=1, source_target_pairs={{0,24},{4,28},{8,16},{12,20},{16,8},{20,12},{24,0},{28,4},{1,25},{... | collective-permute-start | bytes 995336 | tf_op jit(solution)/shard_map/ppermute | solution.py:292
  311.9 14.0 %collective-permute-start.45 = (f32[10,2048]{1,0:T(8,128)S(1)}, f32[10,2048]{1,0:T(8,128)S(1)}, u32[]{:S(2)}, u32[]{:S(2)}) collective-permute-start(f32[10,2048]{1,0:T(8,128)S(1)} %add.184), channel_id=1, source_target_pairs={{0,16},{4,20},{8,24},{12,28},{16,0},{20,4},{24,8},{28,12},{1,17},{... | collective-permute-start | bytes 245768 | tf_op jit(solution)/shard_map/ppermute | solution.py:359
  314.8 22.6 %collective-permute-start.36 = (bf16[4,128,1536]{2,1,0:T(8,128)(2,1)}, bf16[4,128,1536]{2,1,0:T(8,128)(2,1)}, u32[]{:S(2)}, u32[]{:S(2)}) collective-permute-start(bf16[4,128,1536]{2,1,0:T(8,128)(2,1)} %bitcast.76), channel_id=1, source_target_pairs={{0,4},{4,0},{8,12},{12,8},{16,20},{20,16},{24,28},{28,24},{1,5},{5... | collective-permute-start | bytes 4718600 | tf_op jit(solution)/shard_map/ppermute | solution.py:297
  340.0 12.0 %collective-permute-start.37 = (bf16[128,1536]{1,0:T(8,128)(2,1)S(1)}, bf16[128,1536]{1,0:T(8,128)(2,1)S(1)}, u32[]{:S(2)}, u32[]{:S(2)}) collective-permute-start(bf16[128,1536]{1,0:T(8,128)(2,1)S(1)} %get-tuple-element.224), channel_id=1, source_target_pairs={{0,8},{4,12},{8,0},{12,4},{16,24},{20,28},{24,16},{28,20},{1,9},{5... | collective-permute-start | bytes 1179656 | tf_op jit(solution)/shard_map/ppermute | solution.py:292
  341.2 18.9 %collective-permute-start.39 = (bf16[128,1536]{1,0:T(8,128)(2,1)S(1)}, bf16[128,1536]{1,0:T(8,128)(2,1)S(1)}, u32[]{:S(2)}, u32[]{:S(2)}) collective-permute-start(bf16[128,1536]{1,0:T(8,128)(2,1)S(1)} %get-tuple-element.225), channel_id=1, source_target_pairs={{0,24},{4,28},{8,16},{12,20},{16,8},{20,12},{24,0},{28,4},{1,25},{... | collective-permute-start | bytes 1179656 | tf_op jit(solution)/shard_map/ppermute | solution.py:292
  342.6 18.9 %collective-permute-start.38 = (bf16[128,1536]{1,0:T(8,128)(2,1)S(1)}, bf16[128,1536]{1,0:T(8,128)(2,1)S(1)}, u32[]{:S(2)}, u32[]{:S(2)}) collective-permute-start(bf16[128,1536]{1,0:T(8,128)(2,1)S(1)} %get-tuple-element.226), channel_id=1, source_target_pairs={{0,16},{4,20},{8,24},{12,28},{16,0},{20,4},{24,8},{28,12},{1,17},{... | collective-permute-start | bytes 1179656 | tf_op jit(solution)/shard_map/ppermute | solution.py:292
  (54 other events, 387.4 us)
Sparse Core Ops, SparseCore 0:
  15.0 56.5 all-gather.4
  73.2 97.9 all-gather.6
  198.8 93.3 reduce-scatter.2
  303.8 49.2 reduce-scatter.4

commit v3 on v2

--- a/solution.py
+++ b/solution.py
@@ -307,20 +307,14 @@
     return lax.optimization_barrier(arrays)
 
 
-def pair_blocks(near, far):
-    pair = near.astype(jnp.float32) + core_swap(far).astype(jnp.float32)
-    return pair.astype(jnp.bfloat16), pair[0]
-
-
-def spread_pairs(low, own):
-    total = own
-    for k in range(1, low.shape[0]):
-        total = total + chip_swap(low[k], k).astype(jnp.float32)
-    return total
-
-
-def scatter_blocks(near, far):
-    return spread_pairs(*pair_blocks(near, far))
+def pair_blocks(near, far, extra=None):
+    if extra is None:
+        extra = jnp.zeros((0, near.shape[2]), jnp.bfloat16)
+    return payloads(near, core_swap(far), extra)
+
+
+def spread_pairs(own, *low):
+    return own, *[chip_swap(block, k + 1) for k, block in enumerate(low)]
 
 
 def exchange(x, chip, core, turn):
@@ -334,31 +328,16 @@
     return keep, core_swap(give)
 
 
-def reorder(parts, index):
-    bit = 1
-    while bit < len(parts):
-        flip = (index & bit) != 0
-        parts = [jnp.where(flip, parts[i ^ bit], parts[i]) for i in range(len(parts))]
-        bit *= 2
-    return parts
-
-
 def over_planes(x):
     planes = lax.axis_size("fsdp")
     total = x
     for k in range(1, planes):
-        total = total + lax.ppermute(x, "fsdp", [(i, i ^ k) for i in range(planes)])
+        got = lax.ppermute(x.astype(jnp.bfloat16), "fsdp", [(i, i ^ k) for i in range(planes)])
+        total = total + got.astype(jnp.float32)
     return total
 
 
-def total_over(x, axes):
-    for axis in axes:
-        devices = lax.axis_size(axis)
-        bit = 1
-        while bit < devices:
-            x = x + lax.ppermute(x, axis, [(i, i ^ bit) for i in range(devices)])
-            bit *= 2
-    return x
+little = pl.CostEstimate(flops=0, bytes_accessed=0, transcendentals=0)
 
 
 def gelu_parts(v):
@@ -437,13 +416,17 @@
     keep_ref,
     got_ref,
     merged_ref,
+    middle_near_ref,
+    middle_far_ref,
     branch_ref,
-    gelu_pre_ref,
     conv_ref,
-    decay_pre_ref,
-    input_pre_ref,
-    prior_ref,
-    low_ref,
+    gelu_ref,
+    gelu_grad_ref,
+    decay_ref,
+    input_ref,
+    direct_ref,
+    sig_ref,
+    decay_grad_ref,
     weights_ref,
     extended,
     carry,
@@ -476,14 +459,10 @@
 
     turn = step ^ chip
     normed = jnp.concatenate([near_ref[turn], far_ref[turn]], axis=0)
-    pre = dot_nn(normed[:, :near_model], in_ref[0])
-    for z in range(1, planes):
-        pre = pre + dot_nn(normed[:, z * near_model : (z + 1) * near_model], in_ref[z])
-    pre = in_time(pre, core)
+    pre = in_time(dot_nn(normed, in_ref[...].reshape(model, both)), core)
     branch = pre[:, :width].astype(jnp.bfloat16)
     gelu_pre = pre[:, width:]
     branch_ref[...] = branch
-    gelu_pre_ref[...] = gelu_pre
     extended[pl.ds(8, rows), :] = branch.astype(jnp.float32)
     age = age_ref[...]
     total = jnp.zeros((rows, width), jnp.float32) + chan_ref[4:5, :]
@@ -495,23 +474,36 @@
     conv_ref[...] = conv_low
     decay_pre = dot_nn(conv_low, weights_ref[:, model : model + width]) + chan_ref[5:6, :]
     input_pre = dot_nn(conv_low, weights_ref[:, model + width :]) + chan_ref[6:7, :]
-    decay_pre_ref[...] = decay_pre
-    input_pre_ref[...] = input_pre
-    log_a = -8.0 * sigmoid(decay_pre) * chan_ref[7:8, :]
+    sig_d, sig_i = sigmoid(decay_pre), sigmoid(input_pre)
+    soft = chan_ref[7:8, :]
+    log_a = -8.0 * sig_d * soft
     reset = age < 0.5
-    room = jnp.maximum(one_less_exp(2.0 * log_a), mult_floor)
-    factor = jnp.where(reset, 1.0, jnp.sqrt(room))
-    decay = jnp.where(reset, 0.0, jnp.exp(log_a))
-    driven = sigmoid(input_pre) * conv * factor
+    open_room = one_less_exp(2.0 * log_a)
+    root = jnp.sqrt(jnp.maximum(open_room, mult_floor))
+    factor = jnp.where(reset, 1.0, root)
+    a = jnp.exp(log_a)
+    decay = jnp.where(reset, 0.0, a)
+    passed = sig_i * conv
     before = carry[0:1, :]
-    states = scan_rows(decay, driven, before, False)
+    states = scan_rows(decay, passed * factor, before, False)
     carry[0:1, :] = states[rows - 1 :, :]
     row = lax.broadcasted_iota(jnp.int32, states.shape, 0)
-    prior_ref[...] = jnp.where(row == 0, before, pltpu.roll(states, 1, 0))
-    low = states.astype(jnp.bfloat16)
-    low_ref[...] = low
-    merged = low.astype(jnp.float32) * gelu_parts(gelu_pre)[0]
-    by_core(merged, merged_ref, core)
+    prior = jnp.where(row == 0, before, pltpu.roll(states, 1, 0))
+    low = states.astype(jnp.bfloat16).astype(jnp.float32)
+    value, slope = gelu_parts(gelu_pre)
+    by_core(low * value, merged_ref, core)
+    product = dot_nn(merged_ref[...].reshape(rows, width), weights_ref[:, :model])
+    middle_near_ref[...] = product[: rows // 2].astype(jnp.bfloat16)
+    middle_far_ref[...] = product[rows // 2 :].astype(jnp.bfloat16)
+    gelu_ref[...] = value
+    gelu_grad_ref[...] = low * slope
+    decay_ref[...] = decay
+    input_ref[...] = passed * (1.0 - sig_i) * factor
+    direct_ref[...] = sig_i * factor
+    through_room = jnp.where(open_room > mult_floor, a * a * passed / root, 0.0)
+    sig_grad = jnp.where(reset, 0.0, (prior * a - through_room) * sig_d)
+    sig_ref[...] = sig_grad
+    decay_grad_ref[...] = -8.0 * soft * (1.0 - sig_d) * sig_grad
 
 
 def mix_forward(place, near, far, age, chan, pack, keep, got):
@@ -541,7 +533,8 @@
                 fixed(got.shape),
             ],
             out_specs=[pl.BlockSpec((2, None, rows, width), token_block)]
-            + [spec] * 7
+            + [pl.BlockSpec((None, rows, model), lambda i, s: (i ^ (s[0] // 2), 0, 0))] * 2
+            + [spec] * 9
             + [fixed((width, columns))],
             scratch_shapes=[
                 pltpu.VMEM((chunk + 8, width), jnp.float32),
@@ -550,15 +543,13 @@
         ),
         out_shape=[
             jax.ShapeDtypeStruct((2, chips, rows, width), jnp.bfloat16),
+            jax.ShapeDtypeStruct(near.shape, jnp.bfloat16),
+            jax.ShapeDtypeStruct(near.shape, jnp.bfloat16),
             saved(jnp.bfloat16),
-            saved(jnp.float32),
             saved(jnp.bfloat16),
-            saved(jnp.float32),
-            saved(jnp.float32),
-            saved(jnp.float32),
-            saved(jnp.bfloat16),
-            jax.ShapeDtypeStruct((width, columns), jnp.bfloat16),
-        ],
+        ]
+        + [saved(jnp.float32)] * 7
+        + [jax.ShapeDtypeStruct((width, columns), jnp.bfloat16)],
         compiler_params=pltpu.CompilerParams(vmem_limit_bytes=56 * 1024 * 1024),
         name="mix_forward",
     )(place, near, far, age, chan, pack, keep, got)
@@ -571,15 +562,21 @@
     age_ref,
     chan_ref,
     weights_ref,
+    in_ref,
+    merged_ref,
     branch_ref,
-    gelu_pre_ref,
     conv_ref,
-    decay_pre_ref,
-    input_pre_ref,
-    prior_ref,
-    low_ref,
+    gelu_ref,
+    gelu_grad_ref,
+    decay_ref,
+    input_ref,
+    direct_ref,
+    sig_ref,
+    decay_grad_ref,
     both_ref,
     small_ref,
+    back_near_ref,
+    back_far_ref,
     *rest,
 ):
     place = seq_ref[0]
@@ -606,39 +603,20 @@
     mixer_grad = jnp.concatenate([near_ref[turn], far_ref[turn]], axis=0)
     merged_grad = in_time(dot_nt(mixer_grad, weights_ref[:, :model]), core)
     age = age_ref[...]
-    gelu_out, slope = gelu_parts(gelu_pre_ref[...])
-    state_grad = (merged_grad * gelu_out).astype(jnp.bfloat16).astype(jnp.float32)
-    low = low_ref[...].astype(jnp.float32)
-    gelu_pre_grad = merged_grad * low * slope
-    merged = in_time((low * gelu_out).astype(jnp.bfloat16), core)
-    out_grad[...] += dot_tn(mixer_grad, merged)
-    reset = age < 0.5
-    sig_d = sigmoid(decay_pre_ref[...])
-    sig_i = sigmoid(input_pre_ref[...])
-    soft = chan_ref[7:8, :]
-    log_a = -8.0 * sig_d * soft
-    a = jnp.exp(log_a)
-    open_room = one_less_exp(2.0 * log_a)
-    room = jnp.maximum(open_room, mult_floor)
-    root = jnp.sqrt(room)
-    factor = jnp.where(reset, 1.0, root)
-    decay = jnp.where(reset, 0.0, a)
+    out_grad[...] += dot_tn(mixer_grad, merged_ref[...].reshape(rows, width))
+    state_grad = (merged_grad * gelu_ref[...]).astype(jnp.bfloat16).astype(jnp.float32)
+    gelu_pre_grad = merged_grad * gelu_grad_ref[...]
+    decay = decay_ref[...]
     conv_low = conv_ref[...]
-    conv = conv_low.astype(jnp.float32)
     row = lax.broadcasted_iota(jnp.int32, (rows, width), 0)
     next_decay = jnp.where(row == rows - 1, carry[0:1, :], pltpu.roll(decay, rows - 1, 0))
     carried = scan_rows(next_decay, state_grad, carry[1:2, :], True)
     carry[0:1, :] = decay[0:1, :]
     carry[1:2, :] = carried[0:1, :]
-    decay_grad = carried * prior_ref[...]
-    input_pre_grad = carried * conv * factor * sig_i * (1.0 - sig_i)
-    gate_conv_grad = carried * sig_i * factor
-    room_grad = jnp.where(open_room > mult_floor, carried * sig_i * conv * 0.5 / root, 0.0)
-    log_a_grad = jnp.where(reset, 0.0, decay_grad * a - 2.0 * a * a * room_grad)
-    sig_grad = log_a_grad * sig_d
-    decay_pre_grad = -8.0 * soft * sig_grad * (1.0 - sig_d)
-    decay_low = decay_pre_grad.astype(jnp.bfloat16)
-    input_low = input_pre_grad.astype(jnp.bfloat16)
+    gate_conv_grad = carried * direct_ref[...]
+    input_low = (carried * input_ref[...]).astype(jnp.bfloat16)
+    decay_low = (carried * decay_grad_ref[...]).astype(jnp.bfloat16)
+    sig_grad = carried * sig_ref[...]
     conv_grad = (
         gate_conv_grad
         + dot_nt(decay_low, weights_ref[:, model : model + width])
@@ -659,6 +637,10 @@
     small_ref[6:7, :] += jnp.sum(input_low.astype(jnp.float32), axis=0, keepdims=True)
     small_ref[7:8, :] += 8.0 * chan_ref[8:9, :] * jnp.sum(sig_grad, axis=0, keepdims=True)
     by_core(jnp.concatenate([branch_grad, gelu_pre_grad], axis=1), both_ref, core)
+    both = both_ref[...].reshape(rows, 2 * width)
+    back = dot_nt(both, in_ref[...].reshape(model, 2 * width)).astype(jnp.bfloat16)
+    back_near_ref[...] = back[: rows // 2]
+    back_far_ref[...] = back[rows // 2 :]
 
     @pl.when(step == chips - 1)
     def _():
@@ -675,7 +657,8 @@
                     )
 
 
-def mix_backward(place, near, far, age, chan, weights, saved):
+def mix_backward(place, near, far, age, chan, weights, pack, merged, saved):
+    planes, _, both = pack.shape
     chips, rows, model = near.shape
     width, columns = weights.shape
     tall = (model + 2 * width) // (2 * chips)
@@ -684,6 +667,7 @@
     time_block = lambda i, s: (last - i, 0)
     token_block = lambda i, s: (0, (last - i) ^ (s[0] // 2), 0, 0)
     spec = pl.BlockSpec((chunk, width), time_block)
+    back = pl.BlockSpec((None, rows, model), lambda i, s: ((last - i) ^ (s[0] // 2), 0, 0))
     fixed = lambda shape: pl.BlockSpec(shape, lambda i, s: (0,) * len(shape))
     return pl.pallas_call(
         mix_backward_kernel,
@@ -696,11 +680,15 @@
                 pl.BlockSpec((chunk, 1), time_block),
                 pl.BlockSpec((chan.shape[0], width), lambda i, s: (0, s[0])),
                 fixed((width, columns)),
+                fixed((planes, model // planes, both)),
+                pl.BlockSpec((2, None, rows, width), token_block),
             ]
-            + [spec] * 7,
+            + [spec] * 9,
             out_specs=[
                 pl.BlockSpec((2, None, rows, 2 * width), token_block),
                 fixed((8, width)),
+                back,
+                back,
             ]
             + [fixed((2, tall, width))] * chips,
             scratch_shapes=[
@@ -713,14 +701,16 @@
         out_shape=[
             jax.ShapeDtypeStruct((2, chips, rows, 2 * width), jnp.bfloat16),
             jax.ShapeDtypeStruct((8, width), jnp.float32),
+            jax.ShapeDtypeStruct(near.shape, jnp.bfloat16),
+            jax.ShapeDtypeStruct(near.shape, jnp.bfloat16),
         ]
         + [jax.ShapeDtypeStruct((2, tall, width), jnp.bfloat16)] * chips,
-        compiler_params=pltpu.CompilerParams(vmem_limit_bytes=56 * 1024 * 1024),
+        compiler_params=pltpu.CompilerParams(vmem_limit_bytes=50 * 1024 * 1024),
         cost_estimate=pl.CostEstimate(
-            flops=10**10, bytes_accessed=40 * 10**6, transcendentals=6 * width * 2 * chips * rows
+            flops=10**9, bytes_accessed=24 * 10**6, transcendentals=0
         ),
         name="mix_backward",
-    )(place, near, far, age, chan, weights, *saved)
+    )(place, near, far, age, chan, weights, pack, merged, *saved)
 
 
 def unit_kernel(
@@ -825,18 +815,37 @@
         pair[here, mid_unit] = jnp.where(first, grad * up * slope, grad * value).astype(bf16)
         pair_t[:, here] = pair[here, :].T
         hidden_t[:, here] = hidden[here, :].T
-    low = pl.ds(both, planes * span)
-    for z in range(planes):
-        here = pl.ds(z * near_model, near_model)
+    def unit_rows(start):
+        pieces, stop = [], start + span
+        if start < near_model:
+            pieces.append((2 * near_model + start, min(stop, near_model) - start))
+        if stop > near_model:
+            first = max(start, near_model)
+            pieces.append((part + first - near_model, stop - first))
+        return pieces
+
+    for first_z in range(0, planes, 2):
+        here = pl.ds(first_z * near_model, 2 * near_model)
         grad = dot_nn(hidden_t[...], cot[:, here]).astype(bf16)
-        for j in range(planes):
-            grads[j, pl.ds(both + z * span, span), :] = grad[j * span : (j + 1) * span]
-    for z in range(planes):
-        send(grads.at[z, low, :], grads_out.at[z, low, :])
-    for z in range(planes):
-        here = pl.ds(z * near_model, near_model)
-        grads[z, pl.ds(0, both), :] = dot_nn(pair_t[...], normed[:, here]).astype(bf16)
-        send(grads.at[z, pl.ds(0, both), :], grads_out.at[z, pl.ds(0, both), :])
+        for z in (first_z, first_z + 1):
+            columns = slice((z - first_z) * near_model, (z - first_z + 1) * near_model)
+            for j in range(planes):
+                grads[j, pl.ds((3 * z + 2) * span, span), :] = grad[
+                    j * span : (j + 1) * span, columns
+                ]
+    for first_z in range(0, planes, 2):
+        here = pl.ds(first_z * near_model, 2 * near_model)
+        grad = dot_nn(pair_t[...], normed[:, here]).astype(bf16)
+        for z in (first_z, first_z + 1):
+            columns = slice((z - first_z) * near_model, (z - first_z + 1) * near_model)
+            for j in range(planes):
+                row = 3 * j * span
+                grads[z, pl.ds(row, span), :] = grad[j * span : (j + 1) * span, columns]
+                row += span
+                for first, count in unit_rows(j * span):
+                    grads[z, pl.ds(row, count), :] = grad[first : first + count, columns]
+                    row += count
+            send(grads.at[z], grads_out.at[z])
     for i, out in ((0, mixed_near_out), (1, mixed_far_out)):
         here = pl.ds(i * half, half)
         mixed[here, :] = dot_nn(hidden[here, :], down[pl.ds(0, part), :]).astype(bf16)
@@ -874,7 +883,7 @@
             pltpu.VMEM((length, model), bf16),
             pltpu.VMEM((length, model), bf16),
             pltpu.SemaphoreType.DMA((4 * chips + planes * (3 + planes),)),
-            pltpu.SemaphoreType.DMA((4 * chips + 2 * planes,)),
+            pltpu.SemaphoreType.DMA((4 * chips + planes,)),
         ],
         out_shape=[jax.ShapeDtypeStruct(near.shape, bf16)] * 4
         + [jax.ShapeDtypeStruct(pack.shape, bf16)],
@@ -998,8 +1007,258 @@
         ),
         out_shape=jax.ShapeDtypeStruct((tall, near_model), mlp_gate.dtype),
         compiler_params=pltpu.CompilerParams(vmem_limit_bytes=48 * 1024 * 1024),
+        cost_estimate=pl.CostEstimate(flops=0, bytes_accessed=5 << 20, transcendentals=0),
         name="own_unit_pack",
     )(place, mlp_gate, mlp_up, mlp_down)
+
+
+def in_grads_kernel(
+    place_ref,
+    near_ref,
+    far_ref,
+    both_ref,
+    back_near_ref,
+    back_far_ref,
+    gain_ref,
+    later_gain_ref,
+    small_ref,
+    grads_ref,
+    sums_ref,
+):
+    place = place_ref[0]
+    chips, rows, model = near_ref.shape
+    planes, near_model, _ = grads_ref.shape
+    taken, width = small_ref.shape
+    near = near_ref[...].reshape(chips * rows, model)
+    far = far_ref[...].reshape(chips * rows, model)
+    for z in range(planes):
+        here = slice(z * near_model, (z + 1) * near_model)
+        total = dot_tn(near[:, here], both_ref[0].reshape(chips * rows, -1))
+        total = total + dot_tn(far[:, here], both_ref[1].reshape(chips * rows, -1))
+        grads_ref[z] = total.astype(grads_ref.dtype)
+    gain_sum = jnp.zeros((1, model), jnp.float32)
+    for ref, back_ref in ((near_ref, back_near_ref), (far_ref, back_far_ref)):
+        for k in range(chips):
+            product = ref[k].astype(jnp.float32) * back_ref[k].astype(jnp.float32)
+            gain_sum = gain_sum + jnp.sum(product, axis=0, keepdims=True)
+    sums_ref[...] = jnp.zeros_like(sums_ref)
+    across = model // width
+    row = pl.multiple_of(taken * (place // across), taken)
+    column = pl.multiple_of(width * lax.rem(place, across), width)
+    sums_ref[pl.ds(row, taken), pl.ds(column, width)] = small_ref[...]
+    band = model // 3
+    for j in range(3):
+        here = slice(j * band, (j + 1) * band)
+        sums_ref[pl.ds(taken + j, 1), pl.ds(band, band)] = gain_sum[:, here] / gain_ref[:, here]
+        sums_ref[pl.ds(taken + 3 + j, 1), pl.ds(band, band)] = later_gain_ref[:, here]
+
+
+def in_grads(place, near, far, both, back_near, back_far, gain, later_gain, small, planes):
+    chips, rows, model = near.shape
+    columns = both.shape[-1]
+    whole = lambda shape: pl.BlockSpec(shape, lambda i, s: (0,) * len(shape))
+    inputs = (near, far, both, back_near, back_far, gain[None], later_gain, small)
+    shapes = [
+        jax.ShapeDtypeStruct((planes, model // planes, columns), jnp.bfloat16),
+        jax.ShapeDtypeStruct((16, model), jnp.float32),
+    ]
+    return pl.pallas_call(
+        in_grads_kernel,
+        grid_spec=pltpu.PrefetchScalarGridSpec(
+            num_scalar_prefetch=1,
+            grid=(1,),
+            in_specs=[whole(x.shape) for x in inputs],
+            out_specs=[whole(x.shape) for x in shapes],
+        ),
+        out_shape=shapes,
+        compiler_params=pltpu.CompilerParams(vmem_limit_bytes=24 * 1024 * 1024),
+        name="in_grads",
+    )(place, *inputs)
+
+
+def payload_kernel(*refs):
+    near_ref, got_ref, *extra_refs = refs[: -near_count(refs)]
+    own_ref, *out_refs = refs[-near_count(refs) :]
+    chips, rows, _ = near_ref.shape
+    for k in range(chips):
+        total = near_ref[k].astype(jnp.float32) + got_ref[k].astype(jnp.float32)
+        if k == 0:
+            own_ref[...] = total
+        else:
+            out_refs[k - 1][pl.ds(0, rows), :] = total.astype(jnp.bfloat16)
+            for ref in extra_refs:
+                out_refs[k - 1][pl.ds(rows, ref.shape[0]), :] = ref[...]
+
+
+def near_count(refs):
+    return refs[0].shape[0]
+
+
+def payloads(near, got, extra):
+    chips, rows, model = near.shape
+    tall = rows + extra.shape[0]
+    whole = pl.BlockSpec(memory_space=pltpu.VMEM)
+    inputs = (near, got) + ((extra,) if extra.shape[0] else ())
+    return pl.pallas_call(
+        payload_kernel,
+        in_specs=[whole] * len(inputs),
+        out_specs=[whole] * chips,
+        out_shape=[jax.ShapeDtypeStruct((rows, model), jnp.float32)]
+        + [jax.ShapeDtypeStruct((tall, model), jnp.bfloat16)] * (chips - 1),
+        compiler_params=pltpu.CompilerParams(vmem_limit_bytes=20 * 1024 * 1024),
+        cost_estimate=little,
+        name="payloads",
+    )(*inputs)
+
+
+def middle_kernel(tokens_ref, gain_ref, *refs):
+    *parts, middle_ref, normed_ref = refs
+    total = tokens_ref[...].astype(jnp.float32)
+    for ref in parts:
+        total = total + ref[...].astype(jnp.float32)
+    middle_ref[...] = total
+    scale = lax.rsqrt(jnp.mean(total * total, axis=-1, keepdims=True) + norm_eps)
+    normed_ref[...] = (total * scale * gain_ref[...]).astype(jnp.bfloat16)
+
+
+def middle_and_normed(tokens, gain, parts):
+    rows, model = tokens.shape
+    whole = pl.BlockSpec(memory_space=pltpu.VMEM)
+    return pl.pallas_call(
+        middle_kernel,
+        in_specs=[whole] * (2 + len(parts)),
+        out_specs=[whole] * 2,
+        out_shape=[
+            jax.ShapeDtypeStruct((rows, model), jnp.float32),
+            jax.ShapeDtypeStruct((rows, model), jnp.bfloat16),
+        ],
+        cost_estimate=little,
+        name="middle_and_normed",
+    )(tokens, gain[None], *parts)
+
+
+def middle_back_kernel(cot_ref, middle_ref, gain_ref, *refs):
+    *parts, grad_ref, low_ref, gain_grad_ref = refs
+    middle, gain = middle_ref[...], gain_ref[...]
+    upper = parts[0][...]
+    for ref in parts[1:]:
+        upper = upper + ref[...].astype(jnp.float32)
+    scale = lax.rsqrt(jnp.mean(middle * middle, axis=-1, keepdims=True) + norm_eps)
+    gain_grad_ref[...] = jnp.sum(upper * middle * scale, axis=0, keepdims=True)
+    scaled = gain * upper
+    inner = jnp.mean(scaled * middle, axis=-1, keepdims=True)
+    grad = cot_ref[...].astype(jnp.float32) + scale * scaled - middle * (scale * scale * scale) * inner
+    grad_ref[...] = grad
+    low_ref[...] = grad.astype(jnp.bfloat16)
+
+
+def middle_back(cotangent, middle, gain, parts):
+    rows, model = middle.shape
+    whole = pl.BlockSpec(memory_space=pltpu.VMEM)
+    return pl.pallas_call(
+        middle_back_kernel,
+        in_specs=[whole] * (3 + len(parts)),
+        out_specs=[whole] * 3,
+        out_shape=[
+            jax.ShapeDtypeStruct((rows, model), jnp.float32),
+            jax.ShapeDtypeStruct((rows, model), jnp.bfloat16),
+            jax.ShapeDtypeStruct((1, model), jnp.float32),
+        ],
+        cost_estimate=little,
+        name="middle_back",
+    )(cotangent, middle, gain[None], *parts)
+
+
+def halves(value, wanted):
+    side = value.shape[1] // 2
+    return jnp.where(wanted == 1, pltpu.roll(value, side, 1), value)
+
+
+def unit_give_kernel(place_ref, *refs):
+    *piece_refs, give_ref = refs
+    place = place_ref[0]
+    chip, core = place // 2, place % 2
+    turn = core ^ (chip // 2)
+    span = piece_refs[0].shape[0] // 3
+    for e in range(2):
+        first, second = (piece_refs[i][pl.ds(0, 2 * span), :] for i in (e, 2 + e))
+        give_ref[pl.ds(2 * e * span, 2 * span), :] = jnp.where(turn == 0, second, first)
+    for e in range(2):
+        first, second = (
+            halves(piece_refs[2 * e + i][pl.ds(2 * span, span), :].astype(jnp.float32), 1 - core)
+            for i in range(2)
+        )
+        side = first.shape[1] // 2
+        lane = lax.broadcasted_iota(jnp.int32, first.shape, 1)
+        give_ref[pl.ds((4 + e) * span, span), :] = jnp.where(
+            lane < side, first, pltpu.roll(second, side, 1)
+        ).astype(give_ref.dtype)
+
+
+def unit_finish_kernel(place_ref, *refs):
+    *piece_refs, got_ref, gate_ref, up_ref, down_ref, down = refs
+    place = place_ref[0]
+    chip, core = place // 2, place % 2
+    turn = core ^ (chip // 2)
+    span = piece_refs[0].shape[0] // 3
+    side = piece_refs[0].shape[1] // 2
+    for e in range(2):
+        first, second = (piece_refs[i][pl.ds(0, 2 * span), :] for i in (e, 2 + e))
+        mine = jnp.where(turn == 0, first, second).astype(jnp.float32)
+        away = got_ref[pl.ds(2 * e * span, 2 * span), :].astype(jnp.float32)
+        column = 2 * ((chip % 2) ^ e)
+        for value, at in ((mine, column + core), (away, column + 1 - core)):
+            rows = pl.ds(pl.multiple_of(at * span, span), span)
+            gate_ref[rows, :] = value[:span]
+            up_ref[rows, :] = value[span:]
+    for k in range(4):
+        mine = halves(piece_refs[k][pl.ds(2 * span, span), :].astype(jnp.float32), core)
+        away = halves(got_ref[pl.ds((4 + k // 2) * span, span), :].astype(jnp.float32), k % 2)
+        for value, at in ((mine, core), (away, 1 - core)):
+            row = pl.multiple_of((2 * (chip ^ k) + at) * span, span)
+            down[pl.ds(row, span), :] = value[:, :side]
+    down_ref[...] = down[...].T
+
+
+def unit_pieces(total, chip):
+    chips = total.shape[0]
+    pieces = [
+        lax.dynamic_index_in_dim(total, chip ^ k, 0, keepdims=False) for k in range(chips)
+    ]
+    return [pieces[0]] + [chip_swap(pieces[k], k) for k in range(1, chips)]
+
+
+def unit_exchange(place, pieces):
+    chips = len(pieces)
+    tall, cols = pieces[0].shape
+    span = tall // 3
+    fixed = lambda shape: pl.BlockSpec(shape, lambda i, s: (0,) * len(shape))
+    give = pl.pallas_call(
+        unit_give_kernel,
+        grid_spec=pltpu.PrefetchScalarGridSpec(
+            num_scalar_prefetch=1,
+            grid=(1,),
+            in_specs=[fixed((tall, cols))] * chips,
+            out_specs=fixed((6 * span, cols)),
+        ),
+        out_shape=jax.ShapeDtypeStruct((6 * span, cols), pieces[0].dtype),
+        name="unit_give",
+    )(place, *pieces)
+    shapes = [(4 * span, cols), (4 * span, cols), (cols // 2, 2 * chips * span)]
+    grads = pl.pallas_call(
+        unit_finish_kernel,
+        grid_spec=pltpu.PrefetchScalarGridSpec(
+            num_scalar_prefetch=1,
+            grid=(1,),
+            in_specs=[fixed((tall, cols))] * chips + [fixed((6 * span, cols))],
+            out_specs=[fixed(shape) for shape in shapes],
+            scratch_shapes=[pltpu.VMEM((2 * chips * span, cols // 2), jnp.float32)],
+        ),
+        out_shape=[jax.ShapeDtypeStruct(shape, jnp.float32) for shape in shapes],
+        compiler_params=pltpu.CompilerParams(vmem_limit_bytes=32 * 1024 * 1024),
+        name="unit_finish",
+    )(place, *pieces, core_swap(give))
+    return [grad.T for grad in grads]
 
 
 def grad_pack_kernel(place_ref, in_ref, *refs):
@@ -1033,6 +1292,34 @@
         compiler_params=pltpu.CompilerParams(vmem_limit_bytes=32 * 1024 * 1024),
         name="grad_pack",
     )(place, in_grad, *home, *away)
+
+
+def mix_results_kernel(sum_ref, *refs):
+    row = 0
+    width = sum_ref.shape[1] // 2
+    for j, ref in enumerate(refs):
+        rows = ref.shape[0]
+        if j < 2:
+            ref[...] = sum_ref[pl.ds(0, rows), pl.ds(j * width, width)].astype(jnp.float32)
+            row = rows
+        else:
+            ref[...] = sum_ref[pl.ds(row, rows), :].astype(jnp.float32)
+            row += rows
+
+
+def mix_results(total, near_model, slim):
+    tall, both = total.shape
+    piece = (tall - near_model - slim) // 2
+    shapes = [(near_model, both // 2)] * 2 + [(slim, both), (piece, both), (piece, both)]
+    whole = pl.BlockSpec(memory_space=pltpu.VMEM)
+    found = pl.pallas_call(
+        mix_results_kernel,
+        in_specs=[whole],
+        out_specs=[whole] * len(shapes),
+        out_shape=[jax.ShapeDtypeStruct(shape, jnp.float32) for shape in shapes],
+        name="mix_results",
+    )(total)
+    return [*found[:2], *[grad.T for grad in found[2:]]]
 
 
 def norm_back(values, scale, gain, grad):
@@ -1095,11 +1382,9 @@
     )
     normed_near, normed_far = gather_blocks(normed_own)
     unit_pack = own_unit_pack(place_arg, mlp_gate, mlp_up, mlp_down, planes, span)
-    unit_pack, normed_near, normed_far, out_grad = tie(
-        unit_pack, normed_near, normed_far, cotangent[0]
-    )
+    unit_pack, normed_near, normed_far = tie(unit_pack, normed_near, normed_far)
     unit_pack = lax.all_gather(unit_pack, "fsdp", axis=0)
-    cot_near, cot_far = gather_blocks(out_grad)
+    mix_pack, normed_near, normed_far = tie(mix_pack, normed_near, normed_far)
 
     positions = jnp.arange(length, dtype=jnp.int32)
     starts = doc_starts[0]
@@ -1118,140 +1403,125 @@
         axis=0,
     )
 
-    mix_pack, cot_near, cot_far, normed_near, normed_far = tie(
-        mix_pack, cot_near, cot_far, normed_near, normed_far
-    )
     keep, got = exchange(mix_pack[:, near_model:].reshape(chips, 2, -1, 2 * width), chip, core, 0)
-    merged, *saved, weights = mix_forward(
+    keep, got, out_grad = tie(keep, got, cotangent[0])
+    cot_got = [chip_swap(out_grad, k) for k in range(1, chips)]
+    merged, middle_near, middle_far, *saved, weights = mix_forward(
         place_arg, normed_near, normed_far, age, chan, mix_pack, keep, got
     )
-    out_weights = weights[:, :model]
-    in_weights = mix_pack[:, :near_model].reshape(model, 2 * width)
-    far = dot_nn(merged[1].reshape(-1, width), out_weights).astype(bf16)
-    near = dot_nn(merged[0].reshape(-1, width), out_weights)
-    middle = values + scatter_blocks(
-        near.reshape(chips, rows, model), far.reshape(chips, rows, model)
-    )
-
-    scale2 = lax.rsqrt(jnp.mean(middle * middle, axis=-1, keepdims=True) + norm_eps)
-    near, far = gather_blocks((middle * scale2 * mlp_gain).astype(bf16))
+    middle_near, middle_far, *cot_got = tie(middle_near, middle_far, *cot_got)
+    cot_near = jnp.stack([out_grad, *cot_got])
+    cot_far = core_swap(cot_near)
+    middle, normed2 = middle_and_normed(
+        tokens[0], mlp_gain, spread_pairs(*pair_blocks(middle_near, middle_far))
+    )
+
+    near, far = gather_blocks(normed2)
     back_near, back_far, mixed_near, mixed_far, unit_grads = unit_back_and_forth(
         near, far, cot_near, cot_far, unit_pack, part
     )
     unit_sum = lax.psum_scatter(unit_grads, "fsdp", scatter_dimension=0, tiled=False)
-    normed2_grad = scatter_blocks(back_near, back_far)
-
-    mlp_gain_term = jnp.sum(normed2_grad * middle * scale2, axis=0)
-    middle_grad = out_grad.astype(f32) + norm_back(middle, scale2, mlp_gain, normed2_grad)
-    middle_low, mixed_near, mixed_far = tie(middle_grad.astype(bf16), mixed_near, mixed_far)
-    near, far = gather_blocks(middle_low)
-    mixed_low, mixed_own = pair_blocks(mixed_near, mixed_far)
-    near, far, mixed_low, mixed_own = tie(near, far, mixed_low, mixed_own)
-
-    both, small, *by_chip = mix_backward(place_arg, near, far, age, chan, weights, saved)
-    mixed = (middle + spread_pairs(mixed_low, mixed_own)).astype(bf16)
-    mixed, *by_chip = tie(mixed, *by_chip)
+
+    middle_grad, middle_low, mlp_gain_term = middle_back(
+        out_grad, middle, mlp_gain, spread_pairs(*pair_blocks(back_near, back_far))
+    )
+    middle_low, mixed_near, mixed_far = tie(middle_low, mixed_near, mixed_far)
+    mixed_own, *mixed_low = pair_blocks(mixed_near, mixed_far)
+    first, *others = [chip_swap(middle_low, k) for k in range(1, chips)]
+    first, mixed_own, *mixed_low = tie(first, mixed_own, *mixed_low)
+    near = jnp.stack([middle_low, first, *others])
+    far = core_swap(near)
+
+    both, small, back_near, back_far, *by_chip = mix_backward(
+        place_arg, near, far, age, chan, weights, mix_pack, merged, saved
+    )
+    mixed_got = [chip_swap(block, k + 1) for k, block in enumerate(mixed_low)]
+    held = tie(*mixed_got, *by_chip)
+    mixed_got, by_chip = held[: chips - 1], held[chips - 1 :]
     arrived = [by_chip[0]] + [chip_swap(by_chip[k], k) for k in range(1, chips)]
-    in_grad = dot_tn(normed_near.reshape(-1, model), both[0].reshape(-1, 2 * width)) + dot_tn(
-        normed_far.reshape(-1, model), both[1].reshape(-1, 2 * width)
-    )
-    *arrived, both = tie(*arrived, both)
+    arrived[1], both, back_near, back_far, small = tie(
+        arrived[1], both, back_near, back_far, small
+    )
+    in_pack, sums = in_grads(
+        place_arg,
+        normed_near,
+        normed_far,
+        both,
+        back_near,
+        back_far,
+        mix_gain,
+        mlp_gain_term,
+        small,
+        planes,
+    )
+    sums = sums + core_swap(sums)
+    *arrived, back_near, back_far = tie(*arrived, back_near, back_far)
+    normed_own, *normed_low = pair_blocks(back_near, back_far)
     away = core_swap(jnp.stack([block[1] for block in arrived]))
-    pack, unit_sum, small, both = tie(
+    held = tie(
         grad_pack(
             place_arg,
-            in_grad.astype(bf16).reshape(planes, near_model, 2 * width),
+            in_pack,
             [block[0] for block in arrived],
             [away[k] for k in range(chips)],
         ),
         unit_sum,
-        small,
-        both,
-    )
-    mix_sum = lax.psum_scatter(pack, "fsdp", scatter_dimension=0, tiled=False).astype(f32)
-    input_proj_grad = mix_sum[:near_model, :width]
-    gelu_proj_grad = mix_sum[:near_model, width:]
-    turned_sum = mix_sum[near_model:].T
-    slim = model // devices
-    output_proj_grad = turned_sum[:, :slim]
-    decay_gate_grad = turned_sum[:, slim : slim + piece]
-    input_gate_grad = turned_sum[:, slim + piece :]
-
-    normed_grad = scatter_blocks(
-        dot_nt(both[0].reshape(-1, 2 * width), in_weights).reshape(chips, rows, model),
-        dot_nt(both[1].reshape(-1, 2 * width), in_weights).astype(bf16).reshape(chips, rows, model),
-    )
-
-    up_first = unit_sum[part + near_model // 2 : 2 * part]
-    up_sum = jnp.concatenate([up_first, unit_sum[part : part + near_model // 2]], axis=0)
-    gate_up_sum = jnp.stack([unit_sum[:part], up_sum]).reshape(2, planes, span, near_model)
-    mlp_gate_grad, mlp_up_grad, mlp_down_grad = final_exchange(
-        gate_up_sum.swapaxes(0, 1),
-        unit_sum[2 * part :].reshape(planes, span, near_model),
-        chip,
-        core,
-        chips,
-    )
-
-    mix_gain_term = jnp.sum(in_grad * in_weights.astype(f32), axis=1) / mix_gain
-    gains = jnp.stack([mix_gain_term, mlp_gain_term]).reshape(-1, width)
-    small = over_planes(jnp.concatenate([small, gains], axis=0))
+        sums,
+        normed_own,
+        *normed_low,
+        *mixed_got,
+    )
+    pack, unit_sum, sums, normed_own = held[:4]
+    normed_low, mixed_got = held[4 : 3 + chips], held[3 + chips :]
+    mixed = mixed_own
+    for got in mixed_got:
+        mixed = mixed + got.astype(f32)
+    mixed = (middle + mixed).astype(bf16)
+    mix_sum = lax.psum_scatter(pack, "fsdp", scatter_dimension=0, tiled=False)
+    (
+        input_proj_grad,
+        gelu_proj_grad,
+        output_proj_grad,
+        decay_gate_grad,
+        input_gate_grad,
+    ) = mix_results(mix_sum, near_model, model // devices)
+
+    pieces = unit_pieces(unit_sum.reshape(planes, 3 * span, near_model), chip)
+    pieces[1], *normed_low = tie(pieces[1], *normed_low)
+    normed_grad = normed_own
+    for k in range(1, chips):
+        normed_grad = normed_grad + chip_swap(normed_low[k - 1], k).astype(f32)
     values_part = norm_back(values, scale1, mix_gain, normed_grad)
     tokens_grad = (middle_grad + values_part).astype(bf16)
-    where_mine = (jnp.arange(devices) == place)[None, :, None]
-    spread = jnp.where(where_mine, small[:8, None, :], 0.0).reshape(8, channels)
-    gains = jnp.pad(small[8:].reshape(2, model), ((0, 0), (0, channels - model)))
-    sums = total_over(jnp.concatenate([spread, gains], axis=0), ("seq",))
+
+    low = sums.astype(bf16)
+    for k in range(1, chips):
+        sums = sums + chip_swap(low, k).astype(f32)
+    sums, *pieces = tie(over_planes(sums), *pieces)
+    channel_sums = jnp.concatenate([sums[:8], sums[8:, : channels - model]], axis=1)
+    band = model // 3
+    gain_sums = sums[8:14, band : 2 * band].reshape(2, model)
+    mlp_gate_grad, mlp_up_grad, mlp_down_grad = unit_exchange(place_arg, pieces)
+
     return (
         mixed[None],
         tokens_grad[None],
-        sums[8, :model],
+        gain_sums[0],
         input_proj_grad,
         gelu_proj_grad,
-        sums[:4],
-        sums[4],
+        channel_sums[:4],
+        channel_sums[4],
         decay_gate_grad,
-        sums[5],
+        channel_sums[5],
         input_gate_grad,
-        sums[6],
-        sums[7],
+        channel_sums[6],
+        channel_sums[7],
         output_proj_grad,
-        sums[9, :model],
+        gain_sums[1],
         mlp_gate_grad,
         mlp_up_grad,
         mlp_down_grad,
     )
-
-
-def final_exchange(gate_up_sum, down_sum, chip, core, chips):
-    f32 = jnp.float32
-    span, cols = down_sum.shape[1:]
-    half = cols // 2
-    sent = jnp.concatenate([gate_up_sum, down_sum[:, None]], axis=1)
-    parts = [lax.dynamic_index_in_dim(sent, chip ^ k, 0, keepdims=False) for k in range(chips)]
-    got = [parts[0]] + [chip_swap(parts[k], k) for k in range(1, chips)]
-    turn = core ^ (chip // 2)
-    low, high = jnp.stack(got[:2]), jnp.stack(got[2:])
-    keep_gu = jnp.where(turn == 0, low[:, :2], high[:, :2])
-    give_gu = jnp.where(turn == 0, high[:, :2], low[:, :2])
-    downs = jnp.stack([g[2] for g in got])
-    keep_d = jnp.where(core == 0, downs[:, :, :half], downs[:, :, half:])
-    give_d = jnp.where(core == 0, downs[:, :, half:], downs[:, :, :half])
-    got_gu, got_d = core_swap(give_gu), core_swap(give_d)
-    home = reorder([keep_gu[0], keep_gu[1]], chip & 1)
-    away = reorder([got_gu[0], got_gu[1]], chip & 1)
-    blocks = []
-    for x in range(2):
-        blocks.append(jnp.where(core == 0, home[x], away[x]))
-        blocks.append(jnp.where(core == 0, away[x], home[x]))
-    gate_up = jnp.concatenate(blocks, axis=1).astype(f32)
-    home = reorder([keep_d[k] for k in range(chips)], chip)
-    away = reorder([got_d[k] for k in range(chips)], chip)
-    blocks = []
-    for k in range(chips):
-        blocks.append(jnp.where(core == 0, home[k], away[k]))
-        blocks.append(jnp.where(core == 0, away[k], home[k]))
-    return gate_up[0].T, gate_up[1].T, jnp.concatenate(blocks, axis=0).astype(f32)
 
 
 def choose_plan(mesh):

time: 379 us -> 361 us (0.953)
  Pallas kernels: 60.3 us -> 76.9 us
  other arithmetic: 25.6 us -> 9.31 us
  matrix products: 12.1 us -> 0 us
  waiting for transfers between devices: 190 us -> 183 us
    all_gather x1, waiting for transfers between devices: 10.5 us -> 32.3 us  [narrow_shards(): mix_pack = lax.all_gather(mix_pack, 'fsdp', axis=0)]
    ppermute x33 -> x36, waiting for transfers between devices: 142 us -> 122 us  [chip_swap(): return lax.ppermute(x, 'seq', [(i, i ^ 2 * k) for i in range(devices)])]
    pallas_call x0 -> x10, Pallas kernels: none -> 16.7 us  [the longest x1 3.65 us: middle_back(): pl.pallas_call(middle_back_kernel, in_specs=[whole] * (3 + len(parts)), o...]
    dot_general x6 -> x0, matrix products: 12.1 us -> none  [the longest x2 5.21 us: dot_tn(): lax.dot_general(a, b, (((0,), (0,)), ((), ())), preferred_element_type=jn...]
    ppermute x6 -> x3, waiting for transfers between devices: 14.1 us -> 4.12 us  [over_planes(): lax.ppermute(x.astype(jnp.bfloat16), 'fsdp', [(i, i ^ k) for i in range(p...]
    slice x19 -> x3, local copies, waits for them, and re-layouts: 9.94 us -> 0.01 us  [the longest x1 0.01 us: narrow_shards(): gain_sums[1]]
    unnamed x65 -> x134, local copies, waits for them, and re-layouts: 6.6 us -> 16 us
    all_gather x1, waiting for transfers between devices: 12.5 us -> 6.09 us  [narrow_shards(): unit_pack = lax.all_gather(unit_pack, 'fsdp', axis=0)]
  transfers between devices with their start and end apart: 55 -> 55, of which waited for: 35 -> 34; matrix products, arithmetic and copies ran while one was open for 14% -> 4% of each run, Pallas kernels for 8% -> 13%
where the time goes in v3:
time: 361 us; the launch traced here: 356 us
  waiting for transfers between devices  183 us (51%)
  Pallas kernels  76.9 us (21%)
  starting transfers between devices  49.1 us (14%)
  local copies, waits for them, and re-layouts  22.7 us (6%)
  between operations  15 us (4%)
  other arithmetic  9.31 us (3%)
    ppermute x36, waiting for transfers between devices, chip_swap(): return lax.ppermute(x, 'seq', [(i, i ^ 2 * k) for i in range(devices)])  122 us
    ppermute x36, starting transfers between devices, chip_swap(): return lax.ppermute(x, 'seq', [(i, i ^ 2 * k) for i in range(devices)])  43.4 us
    all_gather x1, waiting for transfers between devices, narrow_shards(): mix_pack = lax.all_gather(mix_pack, 'fsdp', axis=0)  32.3 us
    pallas_call x1, Pallas kernels, unit_back_and_forth(): pl.pallas_call(unit_kernel, in_specs=[there] * 5, out_specs=[there] * 5,...  25.7 us
    unnamed x134, local copies, waits for them, and re-layouts  16 us
    pallas_call x1, Pallas kernels, mix_backward(): pl.pallas_call(mix_backward_kernel, grid_spec=pltpu.PrefetchScalarGridSpe...  14.3 us
    pallas_call x1, Pallas kernels, mix_forward(): pl.pallas_call(mix_forward_kernel, grid_spec=pltpu.PrefetchScalarGridSpec...  14.2 us
    ppermute x12, waiting for transfers between devices, core_swap(): return lax.ppermute(x, 'seq', [(i, i ^ 1) for i in range(devices)])  12 us
  transfers between devices with their start and end apart: 55, of which 34 were waited for; matrix products, arithmetic and copies ran while one was open for 4% of the time, Pallas kernels for 13%

profile of v3, /device:TPU:0, one launch (start us, length us, event | category | flops | bytes accessed | tf_op | source)
XLA Modules:
  0.0 355.8 jit_solution(16521204766235829443)
XLA Ops:
  9.8 4.0 %collective-permute-start.2 = (bf16[128,1536]{1,0:T(8,128)(2,1)S(1)}, bf16[128,1536]{1,0:T(8,128)(2,1)S(1)}, u32[]{:S(2)}, u32[]{:S(2)}) collective-permute-start(bf16[128,1536]{1,0:T(8,128)(2,1)S(1)} %fusion.2), channel_id=1, source_target_pairs={{0,24},{4,28},{8,16},{12,20},{16,8},{20,12},{24,0},{28,4},{1,25},{... | collective-permute-start | bytes 1179656 | tf_op jit(solution)/shard_map/ppermute | solution.py:292
  14.4 9.3 %collective-permute-done.2 = bf16[128,1536]{1,0:T(8,128)(2,1)S(1)} collective-permute-done((bf16[128,1536]{1,0:T(8,128)(2,1)S(1)}, bf16[128,1536]{1,0:T(8,128)(2,1)S(1)}, u32[]{:S(2)}, u32[]{:S(2)}) %collective-permute-start.2) | collective-permute-done | bytes 393248 | tf_op jit(solution)/shard_map/ppermute | solution.py:292
  23.7 7.6 %collective-permute-done.1 = bf16[128,1536]{1,0:T(8,128)(2,1)S(1)} collective-permute-done((bf16[128,1536]{1,0:T(8,128)(2,1)S(1)}, bf16[128,1536]{1,0:T(8,128)(2,1)S(1)}, u32[]{:S(2)}, u32[]{:S(2)}) %collective-permute-start.1) | collective-permute-done | bytes 393248 | tf_op jit(solution)/shard_map/ppermute | solution.py:292
  35.4 32.3 %all-gather.5.cloned.1.call-done = bf16[2560,512]{1,0:T(8,128)(2,1)} async-done(((bf16[640,512]{1,0:T(8,128)(2,1)}), bf16[2560,512]{1,0:T(8,128)(2,1)}) %all-gather.5.cloned.1.call-update) | async-done | bytes 2621456 | tf_op jit(solution)/shard_map/all_gather | solution.py:1376
  69.1 2.4 collective-permute-start.6
  72.7 6.7 %collective-permute-done.6 = bf16[2,128,512]{2,1,0:T(8,128)(2,1)S(1)} collective-permute-done((bf16[2,128,512]{2,1,0:T(8,128)(2,1)S(1)}, bf16[2,128,512]{2,1,0:T(8,128)(2,1)S(1)}, u32[]{:S(2)}, u32[]{:S(2)}) %collective-permute-start.6) | collective-permute-done | bytes 262176 | tf_op jit(solution)/shard_map/ppermute | solution.py:292
  79.3 4.4 %collective-permute-done.5 = bf16[2,128,512]{2,1,0:T(8,128)(2,1)S(1)} collective-permute-done((bf16[2,128,512]{2,1,0:T(8,128)(2,1)S(1)}, bf16[2,128,512]{2,1,0:T(8,128)(2,1)S(1)}, u32[]{:S(2)}, u32[]{:S(2)}) %collective-permute-start.5) | collective-permute-done | bytes 262176 | tf_op jit(solution)/shard_map/ppermute | solution.py:292
  92.6 14.2 %mix_forward.1 = (bf16[2,4,128,256]{3,2,1,0:T(8,128)(2,1)}, bf16[4,128,1536]{2,1,0:T(8,128)(2,1)}, bf16[4,128,1536]{2,1,0:T(8,128)(2,1)}, bf16[1024,256]{1,0:T(8...) custom-call(s32[1]{0:T(128)} %bitcast.place_ref.seq_ref, ...), custom_call_target="tpu_custom_call" | custom-call | tf_op jit(solution)/shard_map/mix_forward/pallas_call | solution.py:521
  107.6 3.6 %collective-permute-done.11.refs_1_ = bf16[4,128,1536]{2,1,0:T(8,128)(2,1)S(1)} collective-permute-done((bf16[4,128,1536]{2,1,0:T(8,128)(2,1)}, bf16[4,128,1536]{2,1,0:T(8,128)(2,1)S(1)}, u32[]{:S(2)}, u32[]{:S(2)}) %collective-permute-start.11) | collective-permute-done | bytes 1572896 | tf_op jit(solution)/shard_map/ppermute | solution.py:297
  117.9 7.9 %collective-permute-done.12.refs_1_ = bf16[128,1536]{1,0:T(8,128)(2,1)S(1)} collective-permute-done((bf16[128,1536]{1,0:T(8,128)(2,1)S(1)}, bf16[128,1536]{1,0:T(8,128)(2,1)S(1)}, u32[]{:S(2)}, u32[]{:S(2)}) %collective-permute-start.12) | collective-permute-done | bytes 393248 | tf_op jit(solution)/shard_map/ppermute | solution.py:292
  125.8 8.2 %collective-permute-done.13.refs_2_ = bf16[128,1536]{1,0:T(8,128)(2,1)S(1)} collective-permute-done((bf16[128,1536]{1,0:T(8,128)(2,1)S(1)}, bf16[128,1536]{1,0:T(8,128)(2,1)S(1)}, u32[]{:S(2)}, u32[]{:S(2)}) %collective-permute-start.13) | collective-permute-done | bytes 393248 | tf_op jit(solution)/shard_map/ppermute | solution.py:292
  134.8 2.9 middle_and_normed.1
  141.5 9.4 %collective-permute-done.17 = bf16[128,1536]{1,0:T(8,128)(2,1)S(1)} collective-permute-done((bf16[128,1536]{1,0:T(8,128)(2,1)}, bf16[128,1536]{1,0:T(8,128)(2,1)S(1)}, u32[]{:S(2)}, u32[]{:S(2)}) %collective-permute-start.17) | collective-permute-done | bytes 393248 | tf_op jit(solution)/shard_map/ppermute | solution.py:292
  150.9 6.4 %collective-permute-done.16 = bf16[128,1536]{1,0:T(8,128)(2,1)S(1)} collective-permute-done((bf16[128,1536]{1,0:T(8,128)(2,1)}, bf16[128,1536]{1,0:T(8,128)(2,1)S(1)}, u32[]{:S(2)}, u32[]{:S(2)}) %collective-permute-start.16) | collective-permute-done | bytes 393248 | tf_op jit(solution)/shard_map/ppermute | solution.py:292
  161.1 6.1 %all-gather.7.cloned.1.call-done = bf16[6912,384]{1,0:T(8,128)(2,1)} async-done(((bf16[1728,384]{1,0:T(8,128)(2,1)}), bf16[6912,384]{1,0:T(8,128)(2,1)}) %all-gather.7.cloned.1.call-update) | async-done | bytes 5308432 | tf_op jit(solution)/shard_map/all_gather | solution.py:1386
  167.2 25.7 %unit_back_and_forth.1 = (bf16[4,128,1536]{2,1,0:T(8,128)(2,1)}, bf16[4,128,1536]{2,1,0:T(8,128)(2,1)}, bf16[4,128,1536]{2,1,0:T(8,128)(2,1)}, bf16[4,128,1536]{2,1,0:T(8,128)(2,1)}, bf16[4,1728,384]{2,1,0:T(8,128)(2,1)}) custom-call(bf16[4,128,1536]{2,1,0:T(8,128)(2,1)} %copy-done.35, bf16[4,128,1536]{2,1,0:T(8,128)(2,1)} %collective-permute-done.18.far_ref, ...), custom_call_target="tpu_custom_call" | custom-call | tf_op jit(solution)/shard_map/unit_back_and_forth/pallas_call | solution.py:869
  194.4 3.4 collective-permute-done.20.refs_1_
  202.5 8.5 %collective-permute-done.21.refs_1_ = bf16[128,1536]{1,0:T(8,128)(2,1)S(1)} collective-permute-done((bf16[128,1536]{1,0:T(8,128)(2,1)S(1)}, bf16[128,1536]{1,0:T(8,128)(2,1)S(1)}, u32[]{:S(2)}, u32[]{:S(2)}) %collective-permute-start.21) | collective-permute-done | bytes 393248 | tf_op jit(solution)/shard_map/ppermute | solution.py:292
  211.0 8.8 %collective-permute-done.22.refs_2_ = bf16[128,1536]{1,0:T(8,128)(2,1)S(1)} collective-permute-done((bf16[128,1536]{1,0:T(8,128)(2,1)S(1)}, bf16[128,1536]{1,0:T(8,128)(2,1)S(1)}, u32[]{:S(2)}, u32[]{:S(2)}) %collective-permute-start.22) | collective-permute-done | bytes 393248 | tf_op jit(solution)/shard_map/ppermute | solution.py:292
  220.6 3.6 %middle_back.1 = (f32[128,1536]{1,0:T(8,128)}, bf16[128,1536]{1,0:T(8,128)(2,1)}, f32[1,1536]{1,0:T(1,128)}) custom-call(bf16[128,1536]{1,0:T(8,128)(2,1)} %bitcast.98, f32[128,1536]{1,0:T(8,128)} %get-tuple-element.161.middle_ref, f32[1,1536]{1,0:T(1,128)} %broadcast_in_dim.52.gain_ref, f32[128,1536]{1,0:T(8,128)} %copy-done.25, ...), custom_call_target="tpu_custom_call" | custom-call | tf_op jit(solution)/shard_map/middle_back/pallas_call | solution.py:1158
  228.3 8.2 %collective-permute-done.24 = bf16[128,1536]{1,0:T(8,128)(2,1)S(1)} collective-permute-done((bf16[128,1536]{1,0:T(8,128)(2,1)}, bf16[128,1536]{1,0:T(8,128)(2,1)S(1)}, u32[]{:S(2)}, u32[]{:S(2)}) %collective-permute-start.24) | collective-permute-done | bytes 393248 | tf_op jit(solution)/shard_map/ppermute | solution.py:292
  236.5 9.0 %collective-permute-done.30 = bf16[128,1536]{1,0:T(8,128)(2,1)S(1)} collective-permute-done((bf16[128,1536]{1,0:T(8,128)(2,1)}, bf16[128,1536]{1,0:T(8,128)(2,1)S(1)}, u32[]{:S(2)}, u32[]{:S(2)}) %collective-permute-start.30) | collective-permute-done | bytes 393248 | tf_op jit(solution)/shard_map/ppermute | solution.py:292
  251.9 14.3 %mix_backward.1 = (bf16[2,4,128,512]{3,2,1,0:T(8,128)(2,1)}, f32[8,256]{1,0:T(8,128)S(1)}, bf16[4,128,1536]{2,1,0:T(8,128)(2,1)}, bf16[4,128,1536]{2,1,0:T(8,128...) custom-call(s32[1]{0:T(128)} %bitcast.place_ref.seq_ref, ...), custom_call_target="tpu_custom_call" | custom-call | flops 1000000000 | bytes 24000000 | tf_op jit(solution)/shard_map/mix_backward/pallas_call | solution.py:672
  271.0 5.8 %collective-permute-done.32 = bf16[2,256,256]{2,1,0:T(8,128)(2,1)S(1)} collective-permute-done((bf16[2,256,256]{2,1,0:T(8,128)(2,1)S(1)}, bf16[2,256,256]{2,1,0:T(8,128)(2,1)S(1)}, u32[]{:S(2)}, u32[]{:S(2)}) %collective-permute-start.32) | collective-permute-done | bytes 262176 | tf_op jit(solution)/shard_map/ppermute | solution.py:292
  277.1 4.6 %collective-permute-done.34 = bf16[2,256,256]{2,1,0:T(8,128)(2,1)S(1)} collective-permute-done((bf16[2,256,256]{2,1,0:T(8,128)(2,1)S(1)}, bf16[2,256,256]{2,1,0:T(8,128)(2,1)S(1)}, u32[]{:S(2)}, u32[]{:S(2)}) %collective-permute-start.34) | collective-permute-done | bytes 262176 | tf_op jit(solution)/shard_map/ppermute | solution.py:292
  302.2 3.6 %collective-permute-start.45 = (bf16[16,1536]{1,0:T(8,128)(2,1)S(1)}, bf16[16,1536]{1,0:T(8,128)(2,1)S(1)}, u32[]{:S(2)}, u32[]{:S(2)}) collective-permute-start(bf16[16,1536]{1,0:T(8,128)(2,1)S(1)} %fusion.14), channel_id=1, source_target_pairs={{0,1},{1,0},{2,3},{3,2},{4,5},{5,4},{6,7},{7,6},{8,9},{9,8},{10,11... | collective-permute-start | bytes 147464 | tf_op jit(solution)/shard_map/ppermute | solution.py:335
  312.3 4.7 %collective-permute-done.49.refs_3_ = bf16[432,384]{1,0:T(8,128)(2,1)S(1)} collective-permute-done((bf16[432,384]{1,0:T(8,128)(2,1)S(1)}, bf16[432,384]{1,0:T(8,128)(2,1)S(1)}, u32[]{:S(2)}, u32[]{:S(2)}) %collective-permute-start.49) | collective-permute-done | bytes 331808 | tf_op jit(solution)/shard_map/ppermute | solution.py:292
  321.8 2.5 unit_give.1
  325.6 4.4 %collective-permute-done.41 = bf16[128,1536]{1,0:T(8,128)(2,1)} collective-permute-done((bf16[128,1536]{1,0:T(8,128)(2,1)S(1)}, bf16[128,1536]{1,0:T(8,128)(2,1)}, u32[]{:S(2)}, u32[]{:S(2)}) %collective-permute-start.41) | collective-permute-done | bytes 393248 | tf_op jit(solution)/shard_map/ppermute | solution.py:292
  330.0 4.2 %collective-permute-done.40 = bf16[128,1536]{1,0:T(8,128)(2,1)} collective-permute-done((bf16[128,1536]{1,0:T(8,128)(2,1)S(1)}, bf16[128,1536]{1,0:T(8,128)(2,1)}, u32[]{:S(2)}, u32[]{:S(2)}) %collective-permute-start.40) | collective-permute-done | bytes 393248 | tf_op jit(solution)/shard_map/ppermute | solution.py:292
  335.8 2.5 fusion.9
  340.5 6.2 %reduce-scatter.5.cloned.1.call-done = bf16[1,640,512]{2,1,0:T(8,128)(2,1)} async-done(((bf16[4,640,512]{2,1,0:T(8,128)(2,1)}), bf16[1,640,512]{2,1,0:T(8,128)(2,1)}) %reduce-scatter.5.cloned.1.call-update) | async-done | bytes 655376 | tf_op jit(solution)/shard_map/reduce_scatter | solution.py:1480
  (271 shorter events, 95.4 us)
Async XLA Ops:
  7.2 60.5 %all-gather.5.cloned.1.call-start = ((), (), s32[]{:S(2)}) async-start(), calls=%async_computation.4 | async-start | bytes 3276800 | tf_op jit(solution)/shard_map/all_gather | solution.py:1376
  9.3 157.9 %all-gather.7.cloned.1.call-start = ((), (), s32[]{:S(2)}) async-start(), calls=%async_computation.5 | async-start | bytes 6635520 | tf_op jit(solution)/shard_map/all_gather | solution.py:1386
  9.8 13.9 %collective-permute-start.2 = (bf16[128,1536]{1,0:T(8,128)(2,1)S(1)}, bf16[128,1536]{1,0:T(8,128)(2,1)S(1)}, u32[]{:S(2)}, u32[]{:S(2)}) collective-permute-start(bf16[128,1536]{1,0:T(8,128)(2,1)S(1)} %fusion.2), channel_id=1, source_target_pairs={{0,24},{4,28},{8,16},{12,20},{16,8},{20,12},{24,0},{28,4},{1,25},{... | collective-permute-start | bytes 1179656 | tf_op jit(solution)/shard_map/ppermute | solution.py:292
  13.7 17.5 %collective-permute-start.1 = (bf16[128,1536]{1,0:T(8,128)(2,1)S(1)}, bf16[128,1536]{1,0:T(8,128)(2,1)S(1)}, u32[]{:S(2)}, u32[]{:S(2)}) collective-permute-start(bf16[128,1536]{1,0:T(8,128)(2,1)S(1)} %fusion.2), channel_id=1, source_target_pairs={{0,16},{4,20},{8,24},{12,28},{16,0},{20,4},{24,8},{28,12},{1,17},{... | collective-permute-start | bytes 1179656 | tf_op jit(solution)/shard_map/ppermute | solution.py:292
  14.2 17.3 %collective-permute-start = (bf16[128,1536]{1,0:T(8,128)(2,1)S(1)}, bf16[128,1536]{1,0:T(8,128)(2,1)S(1)}, u32[]{:S(2)}, u32[]{:S(2)}) collective-permute-start(bf16[128,1536]{1,0:T(8,128)(2,1)S(1)} %fusion.2), channel_id=1, source_target_pairs={{0,8},{4,12},{8,0},{12,4},{16,24},{20,28},{24,16},{28,20},{1,9},{5... | collective-permute-start | bytes 1179656 | tf_op jit(solution)/shard_map/ppermute | solution.py:292
  35.3 258.4 %reduce-scatter.3.cloned.1.call-start = ((), (), s32[]{:S(2)}) async-start(), calls=%async_computation.2 | async-start | bytes 6635520 | tf_op jit(solution)/shard_map/reduce_scatter | solution.py:1423
  71.5 12.1 %collective-permute-start.5 = (bf16[2,128,512]{2,1,0:T(8,128)(2,1)S(1)}, bf16[2,128,512]{2,1,0:T(8,128)(2,1)S(1)}, u32[]{:S(2)}, u32[]{:S(2)}) collective-permute-start(bf16[2,128,512]{2,1,0:T(8,128)(2,1)S(1)} %get-tuple-element.269), channel_id=1, source_target_pairs={{0,16},{4,20},{8,24},{12,28},{16,0},{20,4},{24,8},{28,12},{1,17},{... | collective-permute-start | bytes 786440 | tf_op jit(solution)/shard_map/ppermute | solution.py:292
  86.8 20.0 %collective-permute-start.8 = (bf16[128,1536]{1,0:T(8,128)(2,1)S(1)}, bf16[128,1536]{1,0:T(8,128)(2,1)S(1)}, u32[]{:S(2)}, u32[]{:S(2)}) collective-permute-start(bf16[128,1536]{1,0:T(8,128)(2,1)S(1)} %bitcast.99), channel_id=1, source_target_pairs={{0,8},{4,12},{8,0},{12,4},{16,24},{20,28},{24,16},{28,20},{1,9},{5... | collective-permute-start | bytes 1179656 | tf_op jit(solution)/shard_map/ppermute | solution.py:292
  88.3 19.3 %collective-permute-start.9 = (bf16[128,1536]{1,0:T(8,128)(2,1)S(1)}, bf16[128,1536]{1,0:T(8,128)(2,1)S(1)}, u32[]{:S(2)}, u32[]{:S(2)}) collective-permute-start(bf16[128,1536]{1,0:T(8,128)(2,1)S(1)} %bitcast.100), channel_id=1, source_target_pairs={{0,16},{4,20},{8,24},{12,28},{16,0},{20,4},{24,8},{28,12},{1,17},{... | collective-permute-start | bytes 1179656 | tf_op jit(solution)/shard_map/ppermute | solution.py:292
  89.0 18.5 %collective-permute-start.10 = (bf16[128,1536]{1,0:T(8,128)(2,1)S(1)}, bf16[128,1536]{1,0:T(8,128)(2,1)S(1)}, u32[]{:S(2)}, u32[]{:S(2)}) collective-permute-start(bf16[128,1536]{1,0:T(8,128)(2,1)S(1)} %bitcast.101), channel_id=1, source_target_pairs={{0,24},{4,28},{8,16},{12,20},{16,8},{20,12},{24,0},{28,4},{1,25},{... | collective-permute-start | bytes 1179656 | tf_op jit(solution)/shard_map/ppermute | solution.py:292
  114.7 19.3 %collective-permute-start.13 = (bf16[128,1536]{1,0:T(8,128)(2,1)S(1)}, bf16[128,1536]{1,0:T(8,128)(2,1)S(1)}, u32[]{:S(2)}, u32[]{:S(2)}) collective-permute-start(bf16[128,1536]{1,0:T(8,128)(2,1)S(1)} %get-tuple-element.159), channel_id=1, source_target_pairs={{0,16},{4,20},{8,24},{12,28},{16,0},{20,4},{24,8},{28,12},{1,17},{... | collective-permute-start | bytes 1179656 | tf_op jit(solution)/shard_map/ppermute | solution.py:292
  115.8 18.2 %collective-permute-start.14 = (bf16[128,1536]{1,0:T(8,128)(2,1)S(1)}, bf16[128,1536]{1,0:T(8,128)(2,1)S(1)}, u32[]{:S(2)}, u32[]{:S(2)}) collective-permute-start(bf16[128,1536]{1,0:T(8,128)(2,1)S(1)} %get-tuple-element.160), channel_id=1, source_target_pairs={{0,24},{4,28},{8,16},{12,20},{16,8},{20,12},{24,0},{28,4},{1,25},{... | collective-permute-start | bytes 1179656 | tf_op jit(solution)/shard_map/ppermute | solution.py:292
  137.7 13.2 %collective-permute-start.17 = (bf16[128,1536]{1,0:T(8,128)(2,1)}, bf16[128,1536]{1,0:T(8,128)(2,1)S(1)}, u32[]{:S(2)}, u32[]{:S(2)}) collective-permute-start(bf16[128,1536]{1,0:T(8,128)(2,1)} %get-tuple-element.162), channel_id=1, source_target_pairs={{0,24},{4,28},{8,16},{12,20},{16,8},{20,12},{24,0},{28,4},{1,25},{... | collective-permute-start | bytes 1179656 | tf_op jit(solution)/shard_map/ppermute | solution.py:292
  139.2 18.1 %collective-permute-start.16 = (bf16[128,1536]{1,0:T(8,128)(2,1)}, bf16[128,1536]{1,0:T(8,128)(2,1)S(1)}, u32[]{:S(2)}, u32[]{:S(2)}) collective-permute-start(bf16[128,1536]{1,0:T(8,128)(2,1)} %get-tuple-element.162), channel_id=1, source_target_pairs={{0,16},{4,20},{8,24},{12,28},{16,0},{20,4},{24,8},{28,12},{1,17},{... | collective-permute-start | bytes 1179656 | tf_op jit(solution)/shard_map/ppermute | solution.py:292
  140.4 16.9 %collective-permute-start.15 = (bf16[128,1536]{1,0:T(8,128)(2,1)}, bf16[128,1536]{1,0:T(8,128)(2,1)S(1)}, u32[]{:S(2)}, u32[]{:S(2)}) collective-permute-start(bf16[128,1536]{1,0:T(8,128)(2,1)} %get-tuple-element.162), channel_id=1, source_target_pairs={{0,8},{4,12},{8,0},{12,4},{16,24},{20,28},{24,16},{28,20},{1,9},{5... | collective-permute-start | bytes 1179656 | tf_op jit(solution)/shard_map/ppermute | solution.py:292
  141.4 16.3 %collective-permute-start.19 = (bf16[4,128,1536]{2,1,0:T(8,128)(2,1)S(1)}, bf16[4,128,1536]{2,1,0:T(8,128)(2,1)S(1)}, u32[]{:S(2)}, u32[]{:S(2)}) collective-permute-start(bf16[4,128,1536]{2,1,0:T(8,128)(2,1)S(1)} %pad_maximum_fusion.2.cot_near_ref), channel_id=1, source_target_pairs={{0,4},{4,0},{8,12},{12,8},{16,20},{20,16},{24,28},{28,24},{1,5},{5... | collective-permute-start | bytes 4718600 | tf_op jit(solution)/shard_map/ppermute | solution.py:297
  193.0 153.7 %reduce-scatter.5.cloned.1.call-start = ((), (), s32[]{:S(2)}) async-start(), calls=%async_computation.3 | async-start | bytes 3276800 | tf_op jit(solution)/shard_map/reduce_scatter | solution.py:1480
  200.5 19.3 %collective-permute-start.22 = (bf16[128,1536]{1,0:T(8,128)(2,1)S(1)}, bf16[128,1536]{1,0:T(8,128)(2,1)S(1)}, u32[]{:S(2)}, u32[]{:S(2)}) collective-permute-start(bf16[128,1536]{1,0:T(8,128)(2,1)S(1)} %get-tuple-element.171), channel_id=1, source_target_pairs={{0,16},{4,20},{8,24},{12,28},{16,0},{20,4},{24,8},{28,12},{1,17},{... | collective-permute-start | bytes 1179656 | tf_op jit(solution)/shard_map/ppermute | solution.py:292
  201.9 17.8 %collective-permute-start.23 = (bf16[128,1536]{1,0:T(8,128)(2,1)S(1)}, bf16[128,1536]{1,0:T(8,128)(2,1)S(1)}, u32[]{:S(2)}, u32[]{:S(2)}) collective-permute-start(bf16[128,1536]{1,0:T(8,128)(2,1)S(1)} %get-tuple-element.172), channel_id=1, source_target_pairs={{0,24},{4,28},{8,16},{12,20},{16,8},{20,12},{24,0},{28,4},{1,25},{... | collective-permute-start | bytes 1179656 | tf_op jit(solution)/shard_map/ppermute | solution.py:292
  224.3 12.2 %collective-permute-start.24 = (bf16[128,1536]{1,0:T(8,128)(2,1)}, bf16[128,1536]{1,0:T(8,128)(2,1)S(1)}, u32[]{:S(2)}, u32[]{:S(2)}) collective-permute-start(bf16[128,1536]{1,0:T(8,128)(2,1)} %get-tuple-element.176), channel_id=1, source_target_pairs={{0,8},{4,12},{8,0},{12,4},{16,24},{20,28},{24,16},{28,20},{1,9},{5... | collective-permute-start | bytes 1179656 | tf_op jit(solution)/shard_map/ppermute | solution.py:292
  225.4 20.1 %collective-permute-start.30 = (bf16[128,1536]{1,0:T(8,128)(2,1)}, bf16[128,1536]{1,0:T(8,128)(2,1)S(1)}, u32[]{:S(2)}, u32[]{:S(2)}) collective-permute-start(bf16[128,1536]{1,0:T(8,128)(2,1)} %get-tuple-element.176), channel_id=1, source_target_pairs={{0,24},{4,28},{8,16},{12,20},{16,8},{20,12},{24,0},{28,4},{1,25},{... | collective-permute-start | bytes 1179656 | tf_op jit(solution)/shard_map/ppermute | solution.py:292
  227.3 19.5 %collective-permute-start.29 = (bf16[128,1536]{1,0:T(8,128)(2,1)}, bf16[128,1536]{1,0:T(8,128)(2,1)S(1)}, u32[]{:S(2)}, u32[]{:S(2)}) collective-permute-start(bf16[128,1536]{1,0:T(8,128)(2,1)} %get-tuple-element.176), channel_id=1, source_target_pairs={{0,16},{4,20},{8,24},{12,28},{16,0},{20,4},{24,8},{28,12},{1,17},{... | collective-permute-start | bytes 1179656 | tf_op jit(solution)/shard_map/ppermute | solution.py:292
  247.2 19.0 %collective-permute-start.26 = (bf16[128,1536]{1,0:T(8,128)(2,1)S(1)}, bf16[128,1536]{1,0:T(8,128)(2,1)S(1)}, u32[]{:S(2)}, u32[]{:S(2)}) collective-permute-start(bf16[128,1536]{1,0:T(8,128)(2,1)S(1)} %get-tuple-element.184), channel_id=1, source_target_pairs={{0,8},{4,12},{8,0},{12,4},{16,24},{20,28},{24,16},{28,20},{1,9},{5... | collective-permute-start | bytes 1179656 | tf_op jit(solution)/shard_map/ppermute | solution.py:292
  247.8 19.6 %collective-permute-start.27 = (bf16[128,1536]{1,0:T(8,128)(2,1)S(1)}, bf16[128,1536]{1,0:T(8,128)(2,1)S(1)}, u32[]{:S(2)}, u32[]{:S(2)}) collective-permute-start(bf16[128,1536]{1,0:T(8,128)(2,1)S(1)} %get-tuple-element.185), channel_id=1, source_target_pairs={{0,16},{4,20},{8,24},{12,28},{16,0},{20,4},{24,8},{28,12},{1,17},{... | collective-permute-start | bytes 1179656 | tf_op jit(solution)/shard_map/ppermute | solution.py:292
  248.8 18.6 %collective-permute-start.28 = (bf16[128,1536]{1,0:T(8,128)(2,1)S(1)}, bf16[128,1536]{1,0:T(8,128)(2,1)S(1)}, u32[]{:S(2)}, u32[]{:S(2)}) collective-permute-start(bf16[128,1536]{1,0:T(8,128)(2,1)S(1)} %get-tuple-element.186), channel_id=1, source_target_pairs={{0,24},{4,28},{8,16},{12,20},{16,8},{20,12},{24,0},{28,4},{1,25},{... | collective-permute-start | bytes 1179656 | tf_op jit(solution)/shard_map/ppermute | solution.py:292
  269.5 12.1 %collective-permute-start.34 = (bf16[2,256,256]{2,1,0:T(8,128)(2,1)S(1)}, bf16[2,256,256]{2,1,0:T(8,128)(2,1)S(1)}, u32[]{:S(2)}, u32[]{:S(2)}) collective-permute-start(bf16[2,256,256]{2,1,0:T(8,128)(2,1)S(1)} %get-tuple-element.217), channel_id=1, source_target_pairs={{0,24},{4,28},{8,16},{12,20},{16,8},{20,12},{24,0},{28,4},{1,25},{... | collective-permute-start | bytes 786440 | tf_op jit(solution)/shard_map/ppermute | solution.py:292
  299.0 13.2 %collective-permute-start.38 = (bf16[432,384]{1,0:T(8,128)(2,1)S(1)}, bf16[432,384]{1,0:T(8,128)(2,1)S(1)}, u32[]{:S(2)}, u32[]{:S(2)}) collective-permute-start(bf16[432,384]{1,0:T(8,128)(2,1)S(1)} %get-tuple-element.264), channel_id=1, source_target_pairs={{0,8},{4,12},{8,0},{12,4},{16,24},{20,28},{24,16},{28,20},{1,9},{5... | collective-permute-start | bytes 995336 | tf_op jit(solution)/shard_map/ppermute | solution.py:292
  299.9 12.3 %collective-permute-start.48 = (bf16[432,384]{1,0:T(8,128)(2,1)S(1)}, bf16[432,384]{1,0:T(8,128)(2,1)S(1)}, u32[]{:S(2)}, u32[]{:S(2)}) collective-permute-start(bf16[432,384]{1,0:T(8,128)(2,1)S(1)} %get-tuple-element.262), channel_id=1, source_target_pairs={{0,16},{4,20},{8,24},{12,28},{16,0},{20,4},{24,8},{28,12},{1,17},{... | collective-permute-start | bytes 995336 | tf_op jit(solution)/shard_map/ppermute | solution.py:292
  317.0 13.0 %collective-permute-start.41 = (bf16[128,1536]{1,0:T(8,128)(2,1)S(1)}, bf16[128,1536]{1,0:T(8,128)(2,1)}, u32[]{:S(2)}, u32[]{:S(2)}) collective-permute-start(bf16[128,1536]{1,0:T(8,128)(2,1)S(1)} %get-tuple-element.244), channel_id=1, source_target_pairs={{0,24},{4,28},{8,16},{12,20},{16,8},{20,12},{24,0},{28,4},{1,25},{... | collective-permute-start | bytes 1179656 | tf_op jit(solution)/shard_map/ppermute | solution.py:292
  318.5 15.7 %collective-permute-start.40 = (bf16[128,1536]{1,0:T(8,128)(2,1)S(1)}, bf16[128,1536]{1,0:T(8,128)(2,1)}, u32[]{:S(2)}, u32[]{:S(2)}) collective-permute-start(bf16[128,1536]{1,0:T(8,128)(2,1)S(1)} %get-tuple-element.243), channel_id=1, source_target_pairs={{0,16},{4,20},{8,24},{12,28},{16,0},{20,4},{24,8},{28,12},{1,17},{... | collective-permute-start | bytes 1179656 | tf_op jit(solution)/shard_map/ppermute | solution.py:292
  319.7 14.4 %collective-permute-start.39 = (bf16[128,1536]{1,0:T(8,128)(2,1)S(1)}, bf16[128,1536]{1,0:T(8,128)(2,1)}, u32[]{:S(2)}, u32[]{:S(2)}) collective-permute-start(bf16[128,1536]{1,0:T(8,128)(2,1)S(1)} %get-tuple-element.242), channel_id=1, source_target_pairs={{0,8},{4,12},{8,0},{12,4},{16,24},{20,28},{24,16},{28,20},{1,9},{5... | collective-permute-start | bytes 1179656 | tf_op jit(solution)/shard_map/ppermute | solution.py:292
  324.3 14.0 %collective-permute-start.50 = (bf16[864,384]{1,0:T(8,128)(2,1)}, bf16[864,384]{1,0:T(8,128)(2,1)S(1)}, u32[]{:S(2)}, u32[]{:S(2)}) collective-permute-start(bf16[864,384]{1,0:T(8,128)(2,1)} %unit_give.1), channel_id=1, source_target_pairs={{0,4},{4,0},{8,12},{12,8},{16,20},{20,16},{24,28},{28,24},{1,5},{5... | collective-permute-start | bytes 1990664 | tf_op jit(solution)/shard_map/ppermute | solution.py:297
  (90 other events, 634.2 us)
Sparse Core Ops, SparseCore 0:
  10.2 57.4 all-gather.4
  69.3 97.9 all-gather.6
  193.1 93.1 reduce-scatter.2
  293.9 52.7 reduce-scatter.4

commit v4 on v3

--- a/solution.py
+++ b/solution.py
@@ -317,15 +317,23 @@
     return own, *[chip_swap(block, k + 1) for k, block in enumerate(low)]
 
 
-def exchange(x, chip, core, turn):
+def plane_swap(x, k):
+    if k == 0:
+        return x
+    return lax.ppermute(x, "fsdp", [(i, i ^ k) for i in range(lax.axis_size("fsdp"))])
+
+
+def exchange(x, chip, core, turn, beside):
     chips = x.shape[0]
     parts = [
         lax.dynamic_index_in_dim(x, chip ^ k ^ turn, 0, keepdims=False) for k in range(chips)
     ]
-    got = jnp.stack([parts[0]] + [chip_swap(parts[k], k) for k in range(1, chips)])
+    got = [chip_swap(parts[k], k) for k in range(1, chips)]
+    got[0], *beside = tie(got[0], *beside)
+    got = jnp.stack([parts[0], *got])
     keep = lax.dynamic_index_in_dim(got, core, 1, keepdims=False)
     give = lax.dynamic_index_in_dim(got, 1 - core, 1, keepdims=False)
-    return keep, core_swap(give)
+    return keep, core_swap(give), *beside
 
 
 def over_planes(x):
@@ -412,7 +420,6 @@
     far_ref,
     age_ref,
     chan_ref,
-    in_ref,
     keep_ref,
     got_ref,
     merged_ref,
@@ -432,14 +439,12 @@
     carry,
 ):
     place = seq_ref[0]
-    chips = near_ref.shape[0]
+    chips = keep_ref.shape[0]
     step = pl.program_id(0)
     chip, core = place // 2, place % 2
     rows, width = branch_ref.shape
-    planes, near_model, both = in_ref.shape
-    model = planes * near_model
-    parts = weights_ref.shape[1] // both
-    piece = keep_ref.shape[1] // parts
+    model = middle_near_ref.shape[1]
+    piece = keep_ref.shape[1]
 
     @pl.when(step == 0)
     def _():
@@ -448,18 +453,14 @@
         for k in range(chips):
             home = pl.multiple_of(piece * 2 * (chip ^ k) + piece * core, piece)
             away = pl.multiple_of(piece * 2 * (chip ^ k) + piece * (1 - core), piece)
-            for j in range(parts):
-                where = pl.ds(j * both, both)
-                weights_ref[pl.ds(home, piece), where] = keep_ref[k, pl.ds(j * piece, piece), :]
-                weights_ref[pl.ds(away, piece), where] = got_ref[k, pl.ds(j * piece, piece), :]
+            weights_ref[pl.ds(home, piece), :] = keep_ref[k]
+            weights_ref[pl.ds(away, piece), :] = got_ref[k]
 
     @pl.when(step > 0)
     def _():
         extended[pl.ds(0, 8), :] = extended[pl.ds(rows, 8), :]
 
-    turn = step ^ chip
-    normed = jnp.concatenate([near_ref[turn], far_ref[turn]], axis=0)
-    pre = in_time(dot_nn(normed, in_ref[...].reshape(model, both)), core)
+    pre = in_time(jnp.concatenate([near_ref[...], far_ref[...]], axis=0), core)
     branch = pre[:, :width].astype(jnp.bfloat16)
     gelu_pre = pre[:, width:]
     branch_ref[...] = branch
@@ -506,13 +507,14 @@
     decay_grad_ref[...] = -8.0 * soft * (1.0 - sig_d) * sig_grad
 
 
-def mix_forward(place, near, far, age, chan, pack, keep, got):
-    chips, rows, model = near.shape
-    planes, _, both = pack.shape
+def mix_forward(place, near, far, age, chan, keep, got):
+    chips, rows, both = near.shape
     width = both // 2
+    model = keep.shape[2] - both
     length = 2 * chips * rows
     chunk = 2 * rows
-    columns = keep.shape[1] * both // (width // (2 * chips))
+    columns = keep.shape[2]
+    one_block = lambda i, s: (i ^ (s[0] // 2), 0, 0)
     time_block = lambda i, s: (i, 0)
     token_block = lambda i, s: (0, i ^ (s[0] // 2), 0, 0)
     saved = lambda dtype: jax.ShapeDtypeStruct((length, width), dtype)
@@ -524,16 +526,15 @@
             num_scalar_prefetch=1,
             grid=(chips,),
             in_specs=[
-                fixed(near.shape),
-                fixed(far.shape),
+                pl.BlockSpec((None, rows, both), one_block),
+                pl.BlockSpec((None, rows, both), one_block),
                 pl.BlockSpec((chunk, 1), time_block),
                 pl.BlockSpec((chan.shape[0], width), lambda i, s: (0, s[0])),
-                fixed((planes, model // planes, both)),
                 fixed(keep.shape),
                 fixed(got.shape),
             ],
             out_specs=[pl.BlockSpec((2, None, rows, width), token_block)]
-            + [pl.BlockSpec((None, rows, model), lambda i, s: (i ^ (s[0] // 2), 0, 0))] * 2
+            + [pl.BlockSpec((None, rows, model), one_block)] * 2
             + [spec] * 9
             + [fixed((width, columns))],
             scratch_shapes=[
@@ -543,8 +544,8 @@
         ),
         out_shape=[
             jax.ShapeDtypeStruct((2, chips, rows, width), jnp.bfloat16),
-            jax.ShapeDtypeStruct(near.shape, jnp.bfloat16),
-            jax.ShapeDtypeStruct(near.shape, jnp.bfloat16),
+            jax.ShapeDtypeStruct((chips, rows, model), jnp.bfloat16),
+            jax.ShapeDtypeStruct((chips, rows, model), jnp.bfloat16),
             saved(jnp.bfloat16),
             saved(jnp.bfloat16),
         ]
@@ -552,7 +553,7 @@
         + [jax.ShapeDtypeStruct((width, columns), jnp.bfloat16)],
         compiler_params=pltpu.CompilerParams(vmem_limit_bytes=56 * 1024 * 1024),
         name="mix_forward",
-    )(place, near, far, age, chan, pack, keep, got)
+    )(place, near, far, age, chan, keep, got)
 
 
 def mix_backward_kernel(
@@ -745,6 +746,7 @@
     part = both // 2
     span = part // planes
     side = near_model // 2
+    spare = down.shape[0] - part
     half = chips * rows
     incoming, outgoing = [], []
 
@@ -797,7 +799,7 @@
         if i == 0:
             for copy in down_copies + cot_copies[0]:
                 copy.wait()
-            down[pl.ds(part, side), :] = down[pl.ds(part - side, side), :]
+            down[pl.ds(part, spare), :] = jnp.zeros((spare, down.shape[1]), bf16)
         above = dot_nt(cot[here, :], down[...])
         up = pre[:, 2 * near_model :]
         value, slope = gelu_parts(pre[:, :near_model])
@@ -806,13 +808,16 @@
         pair[here, first_unit] = (grad * up * slope).astype(bf16)
         pair[here, last_unit] = (grad * value).astype(bf16)
         mid = pre[:, near_model : 2 * near_model]
-        first = lax.broadcasted_iota(jnp.int32, mid.shape, 1) < side
-        turned = pltpu.roll(mid, side, 1)
-        gate, up = jnp.where(first, mid, turned), jnp.where(first, turned, mid)
-        value, slope = gelu_parts(gate)
+        broad = side + spare
+        up = pltpu.roll(mid, side, 1)[:, :broad]
+        value, slope = gelu_parts(mid[:, :broad])
         grad = above[:, near_model:]
         hidden[here, pl.ds(near_model, side)] = (value * up)[:, :side].astype(bf16)
-        pair[here, mid_unit] = jnp.where(first, grad * up * slope, grad * value).astype(bf16)
+        left, right = grad * up * slope, grad * value
+        left = jnp.concatenate([left, left[:, : near_model - broad]], axis=1)
+        right = jnp.concatenate([right, right[:, : near_model - broad]], axis=1)
+        lane = lax.broadcasted_iota(jnp.int32, left.shape, 1)
+        pair[here, mid_unit] = jnp.where(lane < side, left, pltpu.roll(right, side, 1)).astype(bf16)
         pair_t[:, here] = pair[here, :].T
         hidden_t[:, here] = hidden[here, :].T
     def unit_rows(start):
@@ -852,10 +857,12 @@
         for k in range(chips):
             send(mixed.at[pl.ds(i * half + k * rows, rows), :], out.at[k])
     for i, out in ((1, back_far_out), (0, back_near_out)):
-        here = pl.ds(i * half, half)
-        back[here, :] = dot_nt(pair[here, :], gate_up[...]).astype(bf16)
-        for k in range(chips):
-            send(back.at[pl.ds(i * half + k * rows, rows), :], out.at[k])
+        for k in range(0, chips, 2):
+            first_row = i * half + k * rows
+            here = pl.ds(first_row, chunk)
+            back[here, :] = dot_nt(pair[here, :], gate_up[...]).astype(bf16)
+            for e in range(2):
+                send(back.at[pl.ds(first_row + e * rows, rows), :], out.at[k + e])
     for copy in outgoing:
         copy.wait()
 
@@ -874,7 +881,7 @@
             pltpu.VMEM((length, model), bf16),
             pltpu.VMEM((length, model), bf16),
             pltpu.VMEM((model, 2 * part), bf16),
-            pltpu.VMEM((part + near_model // 2, model), bf16),
+            pltpu.VMEM((pl.cdiv(part, 128) * 128, model), bf16),
             pltpu.VMEM((length, 2 * part), bf16),
             pltpu.VMEM((length, part), bf16),
             pltpu.VMEM((2 * part, length), bf16),
@@ -892,19 +899,15 @@
     )(near, far, cot_near, cot_far, pack)
 
 
-def mix_pack_kernel(place_ref, input_ref, gelu_ref, out_ref, decay_ref, gate_ref, pack_ref):
-    near_model, width = input_ref.shape
-    heads, piece, model = out_ref.shape
-    pack_ref[pl.ds(0, near_model), pl.ds(0, width)] = input_ref[...]
-    pack_ref[pl.ds(0, near_model), pl.ds(width, width)] = gelu_ref[...]
-    row = near_model
-    for h in range(heads):
-        for j in range(model // (2 * width)):
-            pack_ref[pl.ds(row, piece), :] = out_ref[h, :, pl.ds(j * 2 * width, 2 * width)]
-            row += piece
-        pack_ref[pl.ds(row, piece), pl.ds(0, width)] = decay_ref[h]
-        pack_ref[pl.ds(row, piece), pl.ds(width, width)] = gate_ref[h]
-        row += piece
+def mix_pack_kernel(
+    place_ref, input_ref, gelu_ref, out_ref, decay_ref, gate_ref, in_own_ref, rows_ref
+):
+    width, model = input_ref.shape[1], out_ref.shape[2]
+    in_own_ref[:, pl.ds(0, width)] = input_ref[...]
+    in_own_ref[:, pl.ds(width, width)] = gelu_ref[...]
+    rows_ref[:, :, pl.ds(0, model)] = out_ref[...]
+    rows_ref[:, :, pl.ds(model, width)] = decay_ref[...]
+    rows_ref[:, :, pl.ds(model + width, width)] = gate_ref[...]
 
 
 def own_mix_pack(place, input_proj, gelu_proj, output_proj, decay_gate, input_gate):
@@ -913,18 +916,20 @@
     heads = decay_gate.shape[0] // width
     model = output_proj.shape[1]
     piece = width // (channels // width)
-    tall = near_model + heads * (model // (2 * width) + 1) * piece
     mine = pl.BlockSpec((near_model, width), lambda i, s: (0, s[0]))
     rows = lambda columns: pl.BlockSpec((heads, piece, columns), lambda i, s: (0, s[0], 0))
+    shapes = [(near_model, 2 * width), (heads, piece, model + 2 * width)]
     return pl.pallas_call(
         mix_pack_kernel,
         grid_spec=pltpu.PrefetchScalarGridSpec(
             num_scalar_prefetch=1,
             grid=(1,),
             in_specs=[mine, mine, rows(model), rows(width), rows(width)],
-            out_specs=pl.BlockSpec((tall, 2 * width), lambda i, s: (0, 0)),
+            out_specs=[
+                pl.BlockSpec(shape, lambda i, s, zeros=(0,) * len(shape): zeros) for shape in shapes
+            ],
         ),
-        out_shape=jax.ShapeDtypeStruct((tall, 2 * width), input_proj.dtype),
+        out_shape=[jax.ShapeDtypeStruct(shape, input_proj.dtype) for shape in shapes],
         name="own_mix_pack",
     )(
         place,
@@ -1289,7 +1294,7 @@
             out_specs=pl.BlockSpec((planes, near_model + tall, both), lambda i, s: (0, 0, 0)),
         ),
         out_shape=jax.ShapeDtypeStruct((planes, near_model + tall, both), jnp.bfloat16),
-        compiler_params=pltpu.CompilerParams(vmem_limit_bytes=32 * 1024 * 1024),
+        compiler_params=pltpu.CompilerParams(vmem_limit_bytes=16 * 1024 * 1024),
         name="grad_pack",
     )(place, in_grad, *home, *away)
 
@@ -1350,7 +1355,7 @@
     f32, bf16 = jnp.float32, jnp.bfloat16
     devices, planes = lax.axis_size("seq"), lax.axis_size("fsdp")
     chips = devices // 2
-    place = lax.axis_index("seq")
+    place, plane = lax.axis_index("seq"), lax.axis_index("fsdp")
     chip, core = place // 2, place % 2
     rows, model = tokens.shape[1:]
     length = rows * devices
@@ -1370,10 +1375,12 @@
         return lax.dynamic_slice_in_dim(x, start, size, axis=1)
 
     place_arg = place.astype(jnp.int32)[None]
-    mix_pack, tokens = tie(
-        own_mix_pack(place_arg, input_proj, gelu_proj, output_proj, decay_gate, input_gate), tokens
-    )
-    mix_pack = lax.all_gather(mix_pack, "fsdp", axis=0)
+    in_own, rowset = own_mix_pack(
+        place_arg, input_proj, gelu_proj, output_proj, decay_gate, input_gate
+    )
+    in_own, rowset, tokens = tie(in_own, rowset, tokens)
+    in_weights = lax.all_gather(in_own, "fsdp", axis=0)
+    by_plane = [plane_swap(rowset, k) for k in range(planes)]
 
     values = tokens[0].astype(f32)
     scale1 = lax.rsqrt(jnp.mean(values * values, axis=-1, keepdims=True) + norm_eps)
@@ -1384,8 +1391,6 @@
     unit_pack = own_unit_pack(place_arg, mlp_gate, mlp_up, mlp_down, planes, span)
     unit_pack, normed_near, normed_far = tie(unit_pack, normed_near, normed_far)
     unit_pack = lax.all_gather(unit_pack, "fsdp", axis=0)
-    mix_pack, normed_near, normed_far = tie(mix_pack, normed_near, normed_far)
-
     positions = jnp.arange(length, dtype=jnp.int32)
     starts = doc_starts[0]
     begin = jnp.max(jnp.where(starts[None, :] <= positions[:, None], starts[None, :], 0), axis=1)
@@ -1402,14 +1407,24 @@
         ],
         axis=0,
     )
-
-    keep, got = exchange(mix_pack[:, near_model:].reshape(chips, 2, -1, 2 * width), chip, core, 0)
-    keep, got, out_grad = tie(keep, got, cotangent[0])
+    normed_near, normed_far, out_grad = tie(normed_near, normed_far, cotangent[0])
     cot_got = [chip_swap(out_grad, k) for k in range(1, chips)]
+    held = tie(normed_near, normed_far, chan, age, *by_plane, *cot_got)
+    normed_near, normed_far, chan, age = held[:4]
+    by_plane, cot_got = held[4 : 4 + planes], held[4 + planes :]
+
+    pre_near, pre_far = (
+        dot_nn(x.reshape(-1, model), in_weights.reshape(model, 2 * width)).reshape(
+            chips, rows, 2 * width
+        )
+        for x in (normed_near, normed_far)
+    )
+    keep, got, pre_near, pre_far = exchange(
+        jnp.stack(by_plane), chip, core, plane, [pre_near, pre_far]
+    )
     merged, middle_near, middle_far, *saved, weights = mix_forward(
-        place_arg, normed_near, normed_far, age, chan, mix_pack, keep, got
-    )
-    middle_near, middle_far, *cot_got = tie(middle_near, middle_far, *cot_got)
+        place_arg, pre_near, pre_far, age, chan, keep, got
+    )
     cot_near = jnp.stack([out_grad, *cot_got])
     cot_far = core_swap(cot_near)
     middle, normed2 = middle_and_normed(
@@ -1433,7 +1448,7 @@
     far = core_swap(near)
 
     both, small, back_near, back_far, *by_chip = mix_backward(
-        place_arg, near, far, age, chan, weights, mix_pack, merged, saved
+        place_arg, near, far, age, chan, weights, in_weights, merged, saved
     )
     mixed_got = [chip_swap(block, k + 1) for k, block in enumerate(mixed_low)]
     held = tie(*mixed_got, *by_chip)
@@ -1455,10 +1470,9 @@
         planes,
     )
     sums = sums + core_swap(sums)
-    *arrived, back_near, back_far = tie(*arrived, back_near, back_far)
-    normed_own, *normed_low = pair_blocks(back_near, back_far)
+    *arrived, in_pack = tie(*arrived, in_pack)
     away = core_swap(jnp.stack([block[1] for block in arrived]))
-    held = tie(
+    pack, unit_sum, back_near, back_far, *mixed_got = tie(
         grad_pack(
             place_arg,
             in_pack,
@@ -1466,13 +1480,11 @@
             [away[k] for k in range(chips)],
         ),
         unit_sum,
-        sums,
-        normed_own,
-        *normed_low,
+        back_near,
+        back_far,
         *mixed_got,
     )
-    pack, unit_sum, sums, normed_own = held[:4]
-    normed_low, mixed_got = held[4 : 3 + chips], held[3 + chips :]
+    normed_own, *normed_low = pair_blocks(back_near, back_far)
     mixed = mixed_own
     for got in mixed_got:
         mixed = mixed + got.astype(f32)
@@ -1487,7 +1499,7 @@
     ) = mix_results(mix_sum, near_model, model // devices)
 
     pieces = unit_pieces(unit_sum.reshape(planes, 3 * span, near_model), chip)
-    pieces[1], *normed_low = tie(pieces[1], *normed_low)
+    pieces[1], sums, *normed_low = tie(pieces[1], sums, *normed_low)
     normed_grad = normed_own
     for k in range(1, chips):
         normed_grad = normed_grad + chip_swap(normed_low[k - 1], k).astype(f32)
@@ -1497,7 +1509,8 @@
     low = sums.astype(bf16)
     for k in range(1, chips):
         sums = sums + chip_swap(low, k).astype(f32)
-    sums, *pieces = tie(over_planes(sums), *pieces)
+    sums = over_planes(sums)
+    sums, *pieces = tie(sums, *pieces)
     channel_sums = jnp.concatenate([sums[:8], sums[8:, : channels - model]], axis=1)
     band = model // 3
     gain_sums = sums[8:14, band : 2 * band].reshape(2, model)

time: 361 us -> 355 us (0.983)
  waiting for transfers between devices: 183 us -> 152 us
  starting transfers between devices: 49.1 us -> 56.7 us
  other arithmetic: 9.31 us -> 15 us
  matrix products: 0 us -> 5.47 us
  local copies, waits for them, and re-layouts: 22.7 us -> 28.1 us
    all_gather x1, waiting for transfers between devices: 32.3 us -> 0.01 us  [narrow_shards(): in_weights = lax.all_gather(in_own, 'fsdp', axis=0)]
    ppermute x0 -> x3, waiting for transfers between devices: none -> 14.9 us  [plane_swap(): lax.ppermute(x, 'fsdp', [(i, i ^ k) for i in range(lax.axis_size('fsdp'))])]
    ppermute x36, waiting for transfers between devices: 122 us -> 110 us  [chip_swap(): return lax.ppermute(x, 'seq', [(i, i ^ 2 * k) for i in range(devices)])]
    ppermute x0 -> x3, starting transfers between devices: none -> 6.61 us  [plane_swap(): lax.ppermute(x, 'fsdp', [(i, i ^ k) for i in range(lax.axis_size('fsdp'))])]
    all_gather x1, waiting for transfers between devices: 6.09 us -> 0.01 us  [narrow_shards(): unit_pack = lax.all_gather(unit_pack, 'fsdp', axis=0)]
    dot_general x0 -> x2, matrix products: none -> 5.47 us  [dot_nn(): lax.dot_general(a, b, (((1,), (0,)), ((), ())), preferred_element_type=jn...]
    unnamed x134 -> x118, local copies, waits for them, and re-layouts: 16 us -> 16.7 us
  transfers between devices with their start and end apart: 55 -> 58, of which waited for: 34 -> 35; matrix products, arithmetic and copies ran while one was open for 4% -> 9% of each run, Pallas kernels for 13% -> 14%
where the time goes in v4:
time: 355 us; the launch traced here: 349 us
  waiting for transfers between devices  152 us (43%)
  Pallas kernels  76.4 us (22%)
  starting transfers between devices  56.7 us (16%)
  local copies, waits for them, and re-layouts  28.1 us (8%)
  other arithmetic  15 us (4%)
  between operations  14.9 us (4%)
  matrix products  5.47 us (2%)
    ppermute x36, waiting for transfers between devices, chip_swap(): return lax.ppermute(x, 'seq', [(i, i ^ 2 * k) for i in range(devices)])  110 us
    ppermute x36, starting transfers between devices, chip_swap(): return lax.ppermute(x, 'seq', [(i, i ^ 2 * k) for i in range(devices)])  44.4 us
    pallas_call x1, Pallas kernels, unit_back_and_forth(): pl.pallas_call(unit_kernel, in_specs=[there] * 5, out_specs=[there] * 5,...  25.1 us
    unnamed x118, local copies, waits for them, and re-layouts  16.7 us
    ppermute x3, waiting for transfers between devices, plane_swap(): lax.ppermute(x, 'fsdp', [(i, i ^ k) for i in range(lax.axis_size('fsdp'))])  14.9 us
    pallas_call x1, Pallas kernels, mix_backward(): pl.pallas_call(mix_backward_kernel, grid_spec=pltpu.PrefetchScalarGridSpe...  14.2 us
    ppermute x12, waiting for transfers between devices, core_swap(): return lax.ppermute(x, 'seq', [(i, i ^ 1) for i in range(devices)])  14 us
    pallas_call x1, Pallas kernels, mix_forward(): pl.pallas_call(mix_forward_kernel, grid_spec=pltpu.PrefetchScalarGridSpec...  11.4 us
  transfers between devices with their start and end apart: 58, of which 35 were waited for; matrix products, arithmetic and copies ran while one was open for 9% of the time, Pallas kernels for 14%

profile of v4, /device:TPU:0, one launch (start us, length us, event | category | flops | bytes accessed | tf_op | source)
XLA Modules:
  0.0 349.0 jit_solution(9214542169485767207)
XLA Ops:
  10.3 4.0 %collective-permute-start.2 = (bf16[128,1536]{1,0:T(8,128)(2,1)S(1)}, bf16[128,1536]{1,0:T(8,128)(2,1)S(1)}, u32[]{:S(2)}, u32[]{:S(2)}) collective-permute-start(bf16[128,1536]{1,0:T(8,128)(2,1)S(1)} %fusion.6), channel_id=1, source_target_pairs={{0,24},{4,28},{8,16},{12,20},{16,8},{20,12},{24,0},{28,4},{1,25},{... | collective-permute-start | bytes 1179656 | tf_op jit(solution)/shard_map/ppermute | solution.py:292
  14.9 9.3 %collective-permute-done.2 = bf16[128,1536]{1,0:T(8,128)(2,1)S(1)} collective-permute-done((bf16[128,1536]{1,0:T(8,128)(2,1)S(1)}, bf16[128,1536]{1,0:T(8,128)(2,1)S(1)}, u32[]{:S(2)}, u32[]{:S(2)}) %collective-permute-start.2) | collective-permute-done | bytes 393248 | tf_op jit(solution)/shard_map/ppermute | solution.py:292
  24.3 7.6 %collective-permute-done.1 = bf16[128,1536]{1,0:T(8,128)(2,1)S(1)} collective-permute-done((bf16[128,1536]{1,0:T(8,128)(2,1)S(1)}, bf16[128,1536]{1,0:T(8,128)(2,1)S(1)}, u32[]{:S(2)}, u32[]{:S(2)}) %collective-permute-start.1) | collective-permute-done | bytes 393248 | tf_op jit(solution)/shard_map/ppermute | solution.py:292
  32.4 3.0 own_unit_pack.1
  37.5 2.6 collective-permute-start.5
  44.9 14.9 %collective-permute-done.4 = bf16[2,32,2048]{2,1,0:T(8,128)(2,1)} collective-permute-done((bf16[2,32,2048]{2,1,0:T(8,128)(2,1)}, bf16[2,32,2048]{2,1,0:T(8,128)(2,1)}, u32[]{:S(2)}, u32[]{:S(2)}) %collective-permute-start.4) | collective-permute-done | bytes 262176 | tf_op jit(solution)/shard_map/ppermute | solution.py:323
  65.9 3.0 concatenate.6.chan_ref
  76.7 3.5 fusion.2.near_ref
  82.7 5.4 %collective-permute-done.12 = bf16[2,32,2048]{2,1,0:T(8,128)(2,1)} collective-permute-done((bf16[2,32,2048]{2,1,0:T(8,128)(2,1)}, bf16[2,32,2048]{2,1,0:T(8,128)(2,1)}, u32[]{:S(2)}, u32[]{:S(2)}) %collective-permute-start.12) | collective-permute-done | bytes 262176 | tf_op jit(solution)/shard_map/ppermute | solution.py:292
  94.3 11.4 %mix_forward.1 = (bf16[2,4,128,256]{3,2,1,0:T(8,128)(2,1)}, bf16[4,128,1536]{2,1,0:T(8,128)(2,1)}, bf16[4,128,1536]{2,1,0:T(8,128)(2,1)}, bf16[1024,256]{1,0:T(8...) custom-call(s32[1]{0:T(128)} %bitcast.place_ref.seq_ref, ...), custom_call_target="tpu_custom_call" | custom-call | tf_op jit(solution)/shard_map/mix_forward/pallas_call | solution.py:523
  105.9 3.5 collective-permute-done.14.refs_1_
  116.2 7.9 %collective-permute-done.15.refs_1_ = bf16[128,1536]{1,0:T(8,128)(2,1)S(1)} collective-permute-done((bf16[128,1536]{1,0:T(8,128)(2,1)S(1)}, bf16[128,1536]{1,0:T(8,128)(2,1)S(1)}, u32[]{:S(2)}, u32[]{:S(2)}) %collective-permute-start.15) | collective-permute-done | bytes 393248 | tf_op jit(solution)/shard_map/ppermute | solution.py:292
  124.0 9.0 %collective-permute-done.16.refs_2_ = bf16[128,1536]{1,0:T(8,128)(2,1)S(1)} collective-permute-done((bf16[128,1536]{1,0:T(8,128)(2,1)S(1)}, bf16[128,1536]{1,0:T(8,128)(2,1)S(1)}, u32[]{:S(2)}, u32[]{:S(2)}) %collective-permute-start.16) | collective-permute-done | bytes 393248 | tf_op jit(solution)/shard_map/ppermute | solution.py:292
  133.9 2.9 middle_and_normed.1
  141.8 8.1 %collective-permute-done.20 = bf16[128,1536]{1,0:T(8,128)(2,1)S(1)} collective-permute-done((bf16[128,1536]{1,0:T(8,128)(2,1)}, bf16[128,1536]{1,0:T(8,128)(2,1)S(1)}, u32[]{:S(2)}, u32[]{:S(2)}) %collective-permute-start.20) | collective-permute-done | bytes 393248 | tf_op jit(solution)/shard_map/ppermute | solution.py:292
  149.9 6.5 %collective-permute-done.19 = bf16[128,1536]{1,0:T(8,128)(2,1)S(1)} collective-permute-done((bf16[128,1536]{1,0:T(8,128)(2,1)}, bf16[128,1536]{1,0:T(8,128)(2,1)S(1)}, u32[]{:S(2)}, u32[]{:S(2)}) %collective-permute-start.19) | collective-permute-done | bytes 393248 | tf_op jit(solution)/shard_map/ppermute | solution.py:292
  160.2 25.1 %unit_back_and_forth.1 = (bf16[4,128,1536]{2,1,0:T(8,128)(2,1)}, bf16[4,128,1536]{2,1,0:T(8,128)(2,1)}, bf16[4,128,1536]{2,1,0:T(8,128)(2,1)}, bf16[4,128,1536]{2,1,0:T(8,128)(2,1)}, bf16[4,1728,384]{2,1,0:T(8,128)(2,1)}) custom-call(bf16[4,128,1536]{2,1,0:T(8,128)(2,1)} %copy-done.31, bf16[4,128,1536]{2,1,0:T(8,128)(2,1)} %collective-permute-done.21.far_ref, ...), custom_call_target="tpu_custom_call" | custom-call | tf_op jit(solution)/shard_map/unit_back_and_forth/pallas_call | solution.py:876
  185.6 3.5 collective-permute-done.23.refs_1_
  195.2 8.5 %collective-permute-done.24.refs_1_ = bf16[128,1536]{1,0:T(8,128)(2,1)S(1)} collective-permute-done((bf16[128,1536]{1,0:T(8,128)(2,1)S(1)}, bf16[128,1536]{1,0:T(8,128)(2,1)S(1)}, u32[]{:S(2)}, u32[]{:S(2)}) %collective-permute-start.24) | collective-permute-done | bytes 393248 | tf_op jit(solution)/shard_map/ppermute | solution.py:292
  203.7 8.3 %collective-permute-done.25.refs_2_ = bf16[128,1536]{1,0:T(8,128)(2,1)S(1)} collective-permute-done((bf16[128,1536]{1,0:T(8,128)(2,1)S(1)}, bf16[128,1536]{1,0:T(8,128)(2,1)S(1)}, u32[]{:S(2)}, u32[]{:S(2)}) %collective-permute-start.25) | collective-permute-done | bytes 393248 | tf_op jit(solution)/shard_map/ppermute | solution.py:292
  213.5 3.5 %middle_back.1 = (f32[128,1536]{1,0:T(8,128)}, bf16[128,1536]{1,0:T(8,128)(2,1)}, f32[1,1536]{1,0:T(1,128)}) custom-call(bf16[128,1536]{1,0:T(8,128)(2,1)} %bitcast.105, f32[128,1536]{1,0:T(8,128)} %get-tuple-element.176.middle_ref, f32[1,1536]{1,0:T(1,128)} %broadcast_in_dim.52.gain_ref, f32[128,1536]{1,0:T(8,128)} %copy-done.20, ...), custom_call_target="tpu_custom_call" | custom-call | tf_op jit(solution)/shard_map/middle_back/pallas_call | solution.py:1163
  222.4 6.7 %collective-permute-done.27 = bf16[128,1536]{1,0:T(8,128)(2,1)S(1)} collective-permute-done((bf16[128,1536]{1,0:T(8,128)(2,1)}, bf16[128,1536]{1,0:T(8,128)(2,1)S(1)}, u32[]{:S(2)}, u32[]{:S(2)}) %collective-permute-start.27) | collective-permute-done | bytes 393248 | tf_op jit(solution)/shard_map/ppermute | solution.py:292
  229.1 9.1 %collective-permute-done.33 = bf16[128,1536]{1,0:T(8,128)(2,1)S(1)} collective-permute-done((bf16[128,1536]{1,0:T(8,128)(2,1)}, bf16[128,1536]{1,0:T(8,128)(2,1)S(1)}, u32[]{:S(2)}, u32[]{:S(2)}) %collective-permute-start.33) | collective-permute-done | bytes 393248 | tf_op jit(solution)/shard_map/ppermute | solution.py:292
  244.6 14.2 %mix_backward.1 = (bf16[2,4,128,512]{3,2,1,0:T(8,128)(2,1)}, f32[8,256]{1,0:T(8,128)S(1)}, bf16[4,128,1536]{2,1,0:T(8,128)(2,1)}, bf16[4,128,1536]{2,1,0:T(8,128...) custom-call(s32[1]{0:T(128)} %bitcast.place_ref.seq_ref, ...), custom_call_target="tpu_custom_call" | custom-call | flops 1000000000 | bytes 24000000 | tf_op jit(solution)/shard_map/mix_backward/pallas_call | solution.py:673
  263.7 5.7 %collective-permute-done.35 = bf16[2,256,256]{2,1,0:T(8,128)(2,1)S(1)} collective-permute-done((bf16[2,256,256]{2,1,0:T(8,128)(2,1)S(1)}, bf16[2,256,256]{2,1,0:T(8,128)(2,1)S(1)}, u32[]{:S(2)}, u32[]{:S(2)}) %collective-permute-start.35) | collective-permute-done | bytes 262176 | tf_op jit(solution)/shard_map/ppermute | solution.py:292
  288.3 2.7 payloads.7
  291.0 3.4 collective-permute-done.40.refs_1_
  302.0 2.9 collective-permute-start.50
  310.7 4.3 %collective-permute-done.49 = bf16[16,1536]{1,0:T(8,128)(2,1)S(1)} collective-permute-done((bf16[16,1536]{1,0:T(8,128)(2,1)S(1)}, bf16[16,1536]{1,0:T(8,128)(2,1)S(1)}, u32[]{:S(2)}, u32[]{:S(2)}) %collective-permute-start.49) | collective-permute-done | bytes 49184 | tf_op jit(solution)/shard_map/ppermute | solution.py:343
  317.6 6.6 %collective-permute-done.51.refs_2_ = bf16[432,384]{1,0:T(8,128)(2,1)S(1)} collective-permute-done((bf16[432,384]{1,0:T(8,128)(2,1)S(1)}, bf16[432,384]{1,0:T(8,128)(2,1)S(1)}, u32[]{:S(2)}, u32[]{:S(2)}) %collective-permute-start.51) | collective-permute-done | bytes 331808 | tf_op jit(solution)/shard_map/ppermute | solution.py:292
  325.5 2.5 unit_give.1
  335.3 4.6 %reduce-scatter.5.cloned.1.call-done = bf16[1,640,512]{2,1,0:T(8,128)(2,1)} async-done(((bf16[4,640,512]{2,1,0:T(8,128)(2,1)}), bf16[1,640,512]{2,1,0:T(8,128)(2,1)}) %reduce-scatter.5.cloned.1.call-update) | async-done | bytes 655376 | tf_op jit(solution)/shard_map/reduce_scatter | solution.py:1492
  (263 shorter events, 120.1 us)
Async XLA Ops:
  7.2 69.5 %all-gather.5.cloned.1.call-start = ((), (), s32[]{:S(2)}) async-start(), calls=%async_computation.4 | async-start | bytes 1966080 | tf_op jit(solution)/shard_map/all_gather | solution.py:1382
  9.3 150.9 %all-gather.7.cloned.1.call-start = ((), (), s32[]{:S(2)}) async-start(), calls=%async_computation.5 | async-start | bytes 6635520 | tf_op jit(solution)/shard_map/all_gather | solution.py:1393
  10.3 13.9 %collective-permute-start.2 = (bf16[128,1536]{1,0:T(8,128)(2,1)S(1)}, bf16[128,1536]{1,0:T(8,128)(2,1)S(1)}, u32[]{:S(2)}, u32[]{:S(2)}) collective-permute-start(bf16[128,1536]{1,0:T(8,128)(2,1)S(1)} %fusion.6), channel_id=1, source_target_pairs={{0,24},{4,28},{8,16},{12,20},{16,8},{20,12},{24,0},{28,4},{1,25},{... | collective-permute-start | bytes 1179656 | tf_op jit(solution)/shard_map/ppermute | solution.py:292
  14.3 17.5 %collective-permute-start.1 = (bf16[128,1536]{1,0:T(8,128)(2,1)S(1)}, bf16[128,1536]{1,0:T(8,128)(2,1)S(1)}, u32[]{:S(2)}, u32[]{:S(2)}) collective-permute-start(bf16[128,1536]{1,0:T(8,128)(2,1)S(1)} %fusion.6), channel_id=1, source_target_pairs={{0,16},{4,20},{8,24},{12,28},{16,0},{20,4},{24,8},{28,12},{1,17},{... | collective-permute-start | bytes 1179656 | tf_op jit(solution)/shard_map/ppermute | solution.py:292
  14.8 17.3 %collective-permute-start = (bf16[128,1536]{1,0:T(8,128)(2,1)S(1)}, bf16[128,1536]{1,0:T(8,128)(2,1)S(1)}, u32[]{:S(2)}, u32[]{:S(2)}) collective-permute-start(bf16[128,1536]{1,0:T(8,128)(2,1)S(1)} %fusion.6), channel_id=1, source_target_pairs={{0,8},{4,12},{8,0},{12,4},{16,24},{20,28},{24,16},{28,20},{1,9},{5... | collective-permute-start | bytes 1179656 | tf_op jit(solution)/shard_map/ppermute | solution.py:292
  35.8 246.1 %reduce-scatter.3.cloned.1.call-start = ((), (), s32[]{:S(2)}) async-start(), calls=%async_computation.2 | async-start | bytes 6635520 | tf_op jit(solution)/shard_map/reduce_scatter | solution.py:1438
  35.9 24.0 %collective-permute-start.4 = (bf16[2,32,2048]{2,1,0:T(8,128)(2,1)}, bf16[2,32,2048]{2,1,0:T(8,128)(2,1)}, u32[]{:S(2)}, u32[]{:S(2)}) collective-permute-start(bf16[2,32,2048]{2,1,0:T(8,128)(2,1)} %get-tuple-element.158), channel_id=1, source_target_pairs={{0,1},{1,0},{2,3},{3,2},{4,5},{5,4},{6,7},{7,6},{8,9},{9,8},{10,11... | collective-permute-start | bytes 786440 | tf_op jit(solution)/shard_map/ppermute | solution.py:323
  37.5 33.2 %collective-permute-start.5 = (bf16[2,32,2048]{2,1,0:T(8,128)(2,1)}, bf16[2,32,2048]{2,1,0:T(8,128)(2,1)}, u32[]{:S(2)}, u32[]{:S(2)}) collective-permute-start(bf16[2,32,2048]{2,1,0:T(8,128)(2,1)} %get-tuple-element.158), channel_id=1, source_target_pairs={{0,2},{1,3},{2,0},{3,1},{4,6},{5,7},{6,4},{7,5},{8,10},{9,11},{10,... | collective-permute-start | bytes 786440 | tf_op jit(solution)/shard_map/ppermute | solution.py:323
  40.1 30.7 %collective-permute-start.7 = (bf16[128,1536]{1,0:T(8,128)(2,1)S(1)}, bf16[128,1536]{1,0:T(8,128)(2,1)}, u32[]{:S(2)}, u32[]{:S(2)}) collective-permute-start(bf16[128,1536]{1,0:T(8,128)(2,1)S(1)} %bitcast.106), channel_id=1, source_target_pairs={{0,8},{4,12},{8,0},{12,4},{16,24},{20,28},{24,16},{28,20},{1,9},{5... | collective-permute-start | bytes 1179656 | tf_op jit(solution)/shard_map/ppermute | solution.py:292
  41.6 29.2 %collective-permute-start.8 = (bf16[128,1536]{1,0:T(8,128)(2,1)S(1)}, bf16[128,1536]{1,0:T(8,128)(2,1)}, u32[]{:S(2)}, u32[]{:S(2)}) collective-permute-start(bf16[128,1536]{1,0:T(8,128)(2,1)S(1)} %bitcast.107), channel_id=1, source_target_pairs={{0,16},{4,20},{8,24},{12,28},{16,0},{20,4},{24,8},{28,12},{1,17},{... | collective-permute-start | bytes 1179656 | tf_op jit(solution)/shard_map/ppermute | solution.py:292
  42.3 28.5 %collective-permute-start.9 = (bf16[128,1536]{1,0:T(8,128)(2,1)S(1)}, bf16[128,1536]{1,0:T(8,128)(2,1)}, u32[]{:S(2)}, u32[]{:S(2)}) collective-permute-start(bf16[128,1536]{1,0:T(8,128)(2,1)S(1)} %bitcast.108), channel_id=1, source_target_pairs={{0,24},{4,28},{8,16},{12,20},{16,8},{20,12},{24,0},{28,4},{1,25},{... | collective-permute-start | bytes 1179656 | tf_op jit(solution)/shard_map/ppermute | solution.py:292
  74.7 13.4 %collective-permute-start.12 = (bf16[2,32,2048]{2,1,0:T(8,128)(2,1)}, bf16[2,32,2048]{2,1,0:T(8,128)(2,1)}, u32[]{:S(2)}, u32[]{:S(2)}) collective-permute-start(bf16[2,32,2048]{2,1,0:T(8,128)(2,1)} %get-tuple-element.280), channel_id=1, source_target_pairs={{0,24},{4,28},{8,16},{12,20},{16,8},{20,12},{24,0},{28,4},{1,25},{... | collective-permute-start | bytes 786440 | tf_op jit(solution)/shard_map/ppermute | solution.py:292
  113.7 19.3 %collective-permute-start.16 = (bf16[128,1536]{1,0:T(8,128)(2,1)S(1)}, bf16[128,1536]{1,0:T(8,128)(2,1)S(1)}, u32[]{:S(2)}, u32[]{:S(2)}) collective-permute-start(bf16[128,1536]{1,0:T(8,128)(2,1)S(1)} %get-tuple-element.174), channel_id=1, source_target_pairs={{0,16},{4,20},{8,24},{12,28},{16,0},{20,4},{24,8},{28,12},{1,17},{... | collective-permute-start | bytes 1179656 | tf_op jit(solution)/shard_map/ppermute | solution.py:292
  114.1 18.9 %collective-permute-start.17 = (bf16[128,1536]{1,0:T(8,128)(2,1)S(1)}, bf16[128,1536]{1,0:T(8,128)(2,1)S(1)}, u32[]{:S(2)}, u32[]{:S(2)}) collective-permute-start(bf16[128,1536]{1,0:T(8,128)(2,1)S(1)} %get-tuple-element.175), channel_id=1, source_target_pairs={{0,24},{4,28},{8,16},{12,20},{16,8},{20,12},{24,0},{28,4},{1,25},{... | collective-permute-start | bytes 1179656 | tf_op jit(solution)/shard_map/ppermute | solution.py:292
  137.8 18.6 %collective-permute-start.19 = (bf16[128,1536]{1,0:T(8,128)(2,1)}, bf16[128,1536]{1,0:T(8,128)(2,1)S(1)}, u32[]{:S(2)}, u32[]{:S(2)}) collective-permute-start(bf16[128,1536]{1,0:T(8,128)(2,1)} %get-tuple-element.177), channel_id=1, source_target_pairs={{0,16},{4,20},{8,24},{12,28},{16,0},{20,4},{24,8},{28,12},{1,17},{... | collective-permute-start | bytes 1179656 | tf_op jit(solution)/shard_map/ppermute | solution.py:292
  138.6 17.8 %collective-permute-start.18 = (bf16[128,1536]{1,0:T(8,128)(2,1)}, bf16[128,1536]{1,0:T(8,128)(2,1)S(1)}, u32[]{:S(2)}, u32[]{:S(2)}) collective-permute-start(bf16[128,1536]{1,0:T(8,128)(2,1)} %get-tuple-element.177), channel_id=1, source_target_pairs={{0,8},{4,12},{8,0},{12,4},{16,24},{20,28},{24,16},{28,20},{1,9},{5... | collective-permute-start | bytes 1179656 | tf_op jit(solution)/shard_map/ppermute | solution.py:292
  141.7 15.1 %collective-permute-start.22 = (bf16[4,128,1536]{2,1,0:T(8,128)(2,1)S(1)}, bf16[4,128,1536]{2,1,0:T(8,128)(2,1)S(1)}, u32[]{:S(2)}, u32[]{:S(2)}) collective-permute-start(bf16[4,128,1536]{2,1,0:T(8,128)(2,1)S(1)} %pad_maximum_fusion.2.cot_near_ref), channel_id=1, source_target_pairs={{0,4},{4,0},{8,12},{12,8},{16,20},{20,16},{24,28},{28,24},{1,5},{5... | collective-permute-start | bytes 4718600 | tf_op jit(solution)/shard_map/ppermute | solution.py:297
  185.3 154.6 %reduce-scatter.5.cloned.1.call-start = ((), (), s32[]{:S(2)}) async-start(), calls=%async_computation.3 | async-start | bytes 3276800 | tf_op jit(solution)/shard_map/reduce_scatter | solution.py:1492
  192.7 19.3 %collective-permute-start.25 = (bf16[128,1536]{1,0:T(8,128)(2,1)S(1)}, bf16[128,1536]{1,0:T(8,128)(2,1)S(1)}, u32[]{:S(2)}, u32[]{:S(2)}) collective-permute-start(bf16[128,1536]{1,0:T(8,128)(2,1)S(1)} %get-tuple-element.186), channel_id=1, source_target_pairs={{0,16},{4,20},{8,24},{12,28},{16,0},{20,4},{24,8},{28,12},{1,17},{... | collective-permute-start | bytes 1179656 | tf_op jit(solution)/shard_map/ppermute | solution.py:292
  194.1 17.8 %collective-permute-start.26 = (bf16[128,1536]{1,0:T(8,128)(2,1)S(1)}, bf16[128,1536]{1,0:T(8,128)(2,1)S(1)}, u32[]{:S(2)}, u32[]{:S(2)}) collective-permute-start(bf16[128,1536]{1,0:T(8,128)(2,1)S(1)} %get-tuple-element.187), channel_id=1, source_target_pairs={{0,24},{4,28},{8,16},{12,20},{16,8},{20,12},{24,0},{28,4},{1,25},{... | collective-permute-start | bytes 1179656 | tf_op jit(solution)/shard_map/ppermute | solution.py:292
  217.4 20.7 %collective-permute-start.33 = (bf16[128,1536]{1,0:T(8,128)(2,1)}, bf16[128,1536]{1,0:T(8,128)(2,1)S(1)}, u32[]{:S(2)}, u32[]{:S(2)}) collective-permute-start(bf16[128,1536]{1,0:T(8,128)(2,1)} %get-tuple-element.191), channel_id=1, source_target_pairs={{0,24},{4,28},{8,16},{12,20},{16,8},{20,12},{24,0},{28,4},{1,25},{... | collective-permute-start | bytes 1179656 | tf_op jit(solution)/shard_map/ppermute | solution.py:292
  219.9 19.6 %collective-permute-start.32 = (bf16[128,1536]{1,0:T(8,128)(2,1)}, bf16[128,1536]{1,0:T(8,128)(2,1)S(1)}, u32[]{:S(2)}, u32[]{:S(2)}) collective-permute-start(bf16[128,1536]{1,0:T(8,128)(2,1)} %get-tuple-element.191), channel_id=1, source_target_pairs={{0,16},{4,20},{8,24},{12,28},{16,0},{20,4},{24,8},{28,12},{1,17},{... | collective-permute-start | bytes 1179656 | tf_op jit(solution)/shard_map/ppermute | solution.py:292
  239.9 19.0 %collective-permute-start.29 = (bf16[128,1536]{1,0:T(8,128)(2,1)S(1)}, bf16[128,1536]{1,0:T(8,128)(2,1)S(1)}, u32[]{:S(2)}, u32[]{:S(2)}) collective-permute-start(bf16[128,1536]{1,0:T(8,128)(2,1)S(1)} %get-tuple-element.199), channel_id=1, source_target_pairs={{0,8},{4,12},{8,0},{12,4},{16,24},{20,28},{24,16},{28,20},{1,9},{5... | collective-permute-start | bytes 1179656 | tf_op jit(solution)/shard_map/ppermute | solution.py:292
  240.5 19.6 %collective-permute-start.30 = (bf16[128,1536]{1,0:T(8,128)(2,1)S(1)}, bf16[128,1536]{1,0:T(8,128)(2,1)S(1)}, u32[]{:S(2)}, u32[]{:S(2)}) collective-permute-start(bf16[128,1536]{1,0:T(8,128)(2,1)S(1)} %get-tuple-element.200), channel_id=1, source_target_pairs={{0,16},{4,20},{8,24},{12,28},{16,0},{20,4},{24,8},{28,12},{1,17},{... | collective-permute-start | bytes 1179656 | tf_op jit(solution)/shard_map/ppermute | solution.py:292
  240.9 19.2 %collective-permute-start.31 = (bf16[128,1536]{1,0:T(8,128)(2,1)S(1)}, bf16[128,1536]{1,0:T(8,128)(2,1)S(1)}, u32[]{:S(2)}, u32[]{:S(2)}) collective-permute-start(bf16[128,1536]{1,0:T(8,128)(2,1)S(1)} %get-tuple-element.201), channel_id=1, source_target_pairs={{0,24},{4,28},{8,16},{12,20},{16,8},{20,12},{24,0},{28,4},{1,25},{... | collective-permute-start | bytes 1179656 | tf_op jit(solution)/shard_map/ppermute | solution.py:292
  261.6 14.0 %collective-permute-start.36 = (bf16[2,256,256]{2,1,0:T(8,128)(2,1)S(1)}, bf16[2,256,256]{2,1,0:T(8,128)(2,1)S(1)}, u32[]{:S(2)}, u32[]{:S(2)}) collective-permute-start(bf16[2,256,256]{2,1,0:T(8,128)(2,1)S(1)} %get-tuple-element.225), channel_id=1, source_target_pairs={{0,16},{4,20},{8,24},{12,28},{16,0},{20,4},{24,8},{28,12},{1,17},{... | collective-permute-start | bytes 786440 | tf_op jit(solution)/shard_map/ppermute | solution.py:292
  262.2 13.5 %collective-permute-start.37 = (bf16[2,256,256]{2,1,0:T(8,128)(2,1)S(1)}, bf16[2,256,256]{2,1,0:T(8,128)(2,1)S(1)}, u32[]{:S(2)}, u32[]{:S(2)}) collective-permute-start(bf16[2,256,256]{2,1,0:T(8,128)(2,1)S(1)} %get-tuple-element.226), channel_id=1, source_target_pairs={{0,24},{4,28},{8,16},{12,20},{16,8},{20,12},{24,0},{28,4},{1,25},{... | collective-permute-start | bytes 786440 | tf_op jit(solution)/shard_map/ppermute | solution.py:292
  298.0 26.2 %collective-permute-start.51 = (bf16[432,384]{1,0:T(8,128)(2,1)S(1)}, bf16[432,384]{1,0:T(8,128)(2,1)S(1)}, u32[]{:S(2)}, u32[]{:S(2)}) collective-permute-start(bf16[432,384]{1,0:T(8,128)(2,1)S(1)} %get-tuple-element.274), channel_id=1, source_target_pairs={{0,16},{4,20},{8,24},{12,28},{16,0},{20,4},{24,8},{28,12},{1,17},{... | collective-permute-start | bytes 995336 | tf_op jit(solution)/shard_map/ppermute | solution.py:292
  299.5 24.7 %collective-permute-start.52 = (bf16[432,384]{1,0:T(8,128)(2,1)S(1)}, bf16[432,384]{1,0:T(8,128)(2,1)S(1)}, u32[]{:S(2)}, u32[]{:S(2)}) collective-permute-start(bf16[432,384]{1,0:T(8,128)(2,1)S(1)} %get-tuple-element.273), channel_id=1, source_target_pairs={{0,24},{4,28},{8,16},{12,20},{16,8},{20,12},{24,0},{28,4},{1,25},{... | collective-permute-start | bytes 995336 | tf_op jit(solution)/shard_map/ppermute | solution.py:292
  309.5 19.9 %collective-permute-start.44 = (bf16[128,1536]{1,0:T(8,128)(2,1)}, bf16[128,1536]{1,0:T(8,128)(2,1)S(1)}, u32[]{:S(2)}, u32[]{:S(2)}) collective-permute-start(bf16[128,1536]{1,0:T(8,128)(2,1)} %get-tuple-element.256), channel_id=1, source_target_pairs={{0,24},{4,28},{8,16},{12,20},{16,8},{20,12},{24,0},{28,4},{1,25},{... | collective-permute-start | bytes 1179656 | tf_op jit(solution)/shard_map/ppermute | solution.py:292
  314.9 16.6 %collective-permute-start.43 = (bf16[128,1536]{1,0:T(8,128)(2,1)}, bf16[128,1536]{1,0:T(8,128)(2,1)S(1)}, u32[]{:S(2)}, u32[]{:S(2)}) collective-permute-start(bf16[128,1536]{1,0:T(8,128)(2,1)} %get-tuple-element.255), channel_id=1, source_target_pairs={{0,16},{4,20},{8,24},{12,28},{16,0},{20,4},{24,8},{28,12},{1,17},{... | collective-permute-start | bytes 1179656 | tf_op jit(solution)/shard_map/ppermute | solution.py:292
  316.1 15.3 %collective-permute-start.42 = (bf16[128,1536]{1,0:T(8,128)(2,1)}, bf16[128,1536]{1,0:T(8,128)(2,1)S(1)}, u32[]{:S(2)}, u32[]{:S(2)}) collective-permute-start(bf16[128,1536]{1,0:T(8,128)(2,1)} %get-tuple-element.254), channel_id=1, source_target_pairs={{0,8},{4,12},{8,0},{12,4},{16,24},{20,28},{24,16},{28,20},{1,9},{5... | collective-permute-start | bytes 1179656 | tf_op jit(solution)/shard_map/ppermute | solution.py:292
  (85 other events, 620.4 us)
Sparse Core Ops, SparseCore 0:
  10.2 48.6 all-gather.4
  60.5 99.2 all-gather.6
  185.4 96.4 reduce-scatter.2
  284.2 55.6 reduce-scatter.4

commit v5 on v4

--- a/solution.py
+++ b/solution.py
@@ -412,6 +412,42 @@
     odd = core == 1
     ref[0] = jnp.where(odd, second, first).astype(ref.dtype)
     ref[1] = jnp.where(odd, first, second).astype(ref.dtype)
+
+
+def tables_kernel(starts_ref, taps_ref, conv_ref, decay_ref, input_ref, param_ref, chan_ref, age_ref):
+    chan_ref[...] = jnp.zeros_like(chan_ref)
+    chan_ref[0:4, :] = taps_ref[...]
+    chan_ref[4:5, :] = conv_ref[...]
+    chan_ref[5:6, :] = decay_ref[...]
+    chan_ref[6:7, :] = input_ref[...]
+    small = jnp.exp(-param_ref[...])
+    series = small * (
+        1.0
+        - small * (1 / 2 - small * (1 / 3 - small * (1 / 4 - small * (1 / 5 - small * (1 / 6)))))
+    )
+    chan_ref[7:8, :] = jnp.where(small < 0.1, series, jnp.log(1.0 + small))
+    chan_ref[8:9, :] = small / (1.0 + small)
+    positions = lax.broadcasted_iota(jnp.int32, age_ref.shape, 0)
+    begin = jnp.zeros(age_ref.shape, jnp.int32)
+    for j in range(starts_ref.shape[0]):
+        start = starts_ref[j]
+        begin = jnp.maximum(begin, jnp.where(start <= positions, start, 0))
+    age_ref[...] = (positions - begin).astype(jnp.float32)
+
+
+def tables(starts, taps, conv_bias, decay_bias, input_bias, param, length):
+    channels = taps.shape[1]
+    whole = pl.BlockSpec(memory_space=pltpu.VMEM)
+    return pl.pallas_call(
+        tables_kernel,
+        in_specs=[pl.BlockSpec(memory_space=pltpu.SMEM)] + [whole] * 5,
+        out_specs=[whole] * 2,
+        out_shape=[
+            jax.ShapeDtypeStruct((16, channels), jnp.float32),
+            jax.ShapeDtypeStruct((length, 1), jnp.float32),
+        ],
+        name="tables",
+    )(starts, taps, conv_bias[None], decay_bias[None], input_bias[None], param[None])
 
 
 def mix_forward_kernel(
@@ -775,8 +811,6 @@
         for j in range(3)
     ]
     normed_copies = [fetch_half(near_ref, normed, 0)]
-    for copy in gate_up_copies + normed_copies[0]:
-        copy.wait()
     down_copies = [
         fetch(
             pack_ref.at[z, pl.ds(3 * near_model + j * span, span), :],
@@ -786,6 +820,8 @@
         for j in range(planes)
     ]
     cot_copies = [fetch_half(cot_near_ref, cot, 0)]
+    for copy in gate_up_copies + normed_copies[0]:
+        copy.wait()
     normed_copies.append(fetch_half(far_ref, normed, 1))
     cot_copies.append(fetch_half(cot_far_ref, cot, 1))
     chunk = 2 * rows
@@ -1391,21 +1427,8 @@
     unit_pack = own_unit_pack(place_arg, mlp_gate, mlp_up, mlp_down, planes, span)
     unit_pack, normed_near, normed_far = tie(unit_pack, normed_near, normed_far)
     unit_pack = lax.all_gather(unit_pack, "fsdp", axis=0)
-    positions = jnp.arange(length, dtype=jnp.int32)
-    starts = doc_starts[0]
-    begin = jnp.max(jnp.where(starts[None, :] <= positions[:, None], starts[None, :], 0), axis=1)
-    age = (positions - begin).astype(f32)[:, None]
-    chan = jnp.concatenate(
-        [
-            conv_taps,
-            conv_bias[None],
-            decay_bias[None],
-            input_bias[None],
-            jax.nn.softplus(-decay_param)[None],
-            jax.nn.sigmoid(-decay_param)[None],
-            jnp.zeros((7, channels), f32),
-        ],
-        axis=0,
+    chan, age = tables(
+        doc_starts[0], conv_taps, conv_bias, decay_bias, input_bias, decay_param, length
     )
     normed_near, normed_far, out_grad = tie(normed_near, normed_far, cotangent[0])
     cot_got = [chip_swap(out_grad, k) for k in range(1, chips)]

time: 355 us -> 353 us (level)
  waiting for transfers between devices: 152 us -> 159 us
  other arithmetic: 15 us -> 9.79 us
  local copies, waits for them, and re-layouts: 28.1 us -> 23.8 us
    ppermute x3, waiting for transfers between devices: 14.9 us -> 22.6 us  [plane_swap(): lax.ppermute(x, 'fsdp', [(i, i ^ k) for i in range(lax.axis_size('fsdp'))])]
    unnamed x118 -> x112, local copies, waits for them, and re-layouts: 16.7 us -> 17.6 us
  transfers between devices with their start and end apart: 58 -> 58, of which waited for: 35 -> 36; matrix products, arithmetic and copies ran while one was open for 9% -> 6% of each run, Pallas kernels for 14% -> 14%
where the time goes in v5:
time: 353 us; the launch traced here: 347 us
  waiting for transfers between devices  159 us (45%)
  Pallas kernels  77.9 us (22%)
  starting transfers between devices  56.5 us (16%)
  local copies, waits for them, and re-layouts  23.8 us (7%)
  between operations  14.9 us (4%)
  other arithmetic  9.79 us (3%)
  matrix products  5.45 us (2%)
    ppermute x36, waiting for transfers between devices, chip_swap(): return lax.ppermute(x, 'seq', [(i, i ^ 2 * k) for i in range(devices)])  111 us
    ppermute x36, starting transfers between devices, chip_swap(): return lax.ppermute(x, 'seq', [(i, i ^ 2 * k) for i in range(devices)])  44.3 us
    pallas_call x1, Pallas kernels, unit_back_and_forth(): pl.pallas_call(unit_kernel, in_specs=[there] * 5, out_specs=[there] * 5,...  24.3 us
    ppermute x3, waiting for transfers between devices, plane_swap(): lax.ppermute(x, 'fsdp', [(i, i ^ k) for i in range(lax.axis_size('fsdp'))])  22.6 us
    unnamed x112, local copies, waits for them, and re-layouts  17.6 us
    pallas_call x1, Pallas kernels, mix_backward(): pl.pallas_call(mix_backward_kernel, grid_spec=pltpu.PrefetchScalarGridSpe...  14.2 us
    ppermute x12, waiting for transfers between devices, core_swap(): return lax.ppermute(x, 'seq', [(i, i ^ 1) for i in range(devices)])  14.1 us
    pallas_call x1, Pallas kernels, mix_forward(): pl.pallas_call(mix_forward_kernel, grid_spec=pltpu.PrefetchScalarGridSpec...  11.4 us
  transfers between devices with their start and end apart: 58, of which 36 were waited for; matrix products, arithmetic and copies ran while one was open for 6% of the time, Pallas kernels for 14%

profile of v5, /device:TPU:0, one launch (start us, length us, event | category | flops | bytes accessed | tf_op | source)
XLA Modules:
  0.0 347.0 jit_solution(3178421897449400179)
XLA Ops:
  9.7 4.0 %collective-permute-start.2 = (bf16[128,1536]{1,0:T(8,128)(2,1)S(1)}, bf16[128,1536]{1,0:T(8,128)(2,1)S(1)}, u32[]{:S(2)}, u32[]{:S(2)}) collective-permute-start(bf16[128,1536]{1,0:T(8,128)(2,1)S(1)} %fusion.6), channel_id=1, source_target_pairs={{0,24},{4,28},{8,16},{12,20},{16,8},{20,12},{24,0},{28,4},{1,25},{... | collective-permute-start | bytes 1179656 | tf_op jit(solution)/shard_map/ppermute | solution.py:292
  14.3 9.3 %collective-permute-done.2 = bf16[128,1536]{1,0:T(8,128)(2,1)S(1)} collective-permute-done((bf16[128,1536]{1,0:T(8,128)(2,1)S(1)}, bf16[128,1536]{1,0:T(8,128)(2,1)S(1)}, u32[]{:S(2)}, u32[]{:S(2)}) %collective-permute-start.2) | collective-permute-done | bytes 393248 | tf_op jit(solution)/shard_map/ppermute | solution.py:292
  23.7 7.6 %collective-permute-done.1 = bf16[128,1536]{1,0:T(8,128)(2,1)S(1)} collective-permute-done((bf16[128,1536]{1,0:T(8,128)(2,1)S(1)}, bf16[128,1536]{1,0:T(8,128)(2,1)S(1)}, u32[]{:S(2)}, u32[]{:S(2)}) %collective-permute-start.1) | collective-permute-done | bytes 393248 | tf_op jit(solution)/shard_map/ppermute | solution.py:292
  31.8 3.0 own_unit_pack.1
  40.4 2.6 collective-permute-start.5
  43.0 16.8 %collective-permute-done.4 = bf16[2,32,2048]{2,1,0:T(8,128)(2,1)} collective-permute-done((bf16[2,32,2048]{2,1,0:T(8,128)(2,1)}, bf16[2,32,2048]{2,1,0:T(8,128)(2,1)}, u32[]{:S(2)}, u32[]{:S(2)}) %collective-permute-start.4) | collective-permute-done | bytes 262176 | tf_op jit(solution)/shard_map/ppermute | solution.py:323
  64.4 5.7 %collective-permute-done.6 = bf16[2,32,2048]{2,1,0:T(8,128)(2,1)} collective-permute-done((bf16[2,32,2048]{2,1,0:T(8,128)(2,1)}, bf16[2,32,2048]{2,1,0:T(8,128)(2,1)}, u32[]{:S(2)}, u32[]{:S(2)}) %collective-permute-start.6) | collective-permute-done | bytes 262176 | tf_op jit(solution)/shard_map/ppermute | solution.py:323
  76.0 3.5 fusion.2.near_ref
  82.1 4.7 %collective-permute-done.12 = bf16[2,32,2048]{2,1,0:T(8,128)(2,1)} collective-permute-done((bf16[2,32,2048]{2,1,0:T(8,128)(2,1)}, bf16[2,32,2048]{2,1,0:T(8,128)(2,1)}, u32[]{:S(2)}, u32[]{:S(2)}) %collective-permute-start.12) | collective-permute-done | bytes 262176 | tf_op jit(solution)/shard_map/ppermute | solution.py:292
  93.0 11.4 %mix_forward.1 = (bf16[2,4,128,256]{3,2,1,0:T(8,128)(2,1)}, bf16[4,128,1536]{2,1,0:T(8,128)(2,1)}, bf16[4,128,1536]{2,1,0:T(8,128)(2,1)}, bf16[1024,256]{1,0:T(8...) custom-call(s32[1]{0:T(128)} %bitcast.place_ref.seq_ref, ...), custom_call_target="tpu_custom_call" | custom-call | tf_op jit(solution)/shard_map/mix_forward/pallas_call | solution.py:559
  104.6 3.5 collective-permute-done.14.refs_1_
  114.8 7.9 %collective-permute-done.15.refs_1_ = bf16[128,1536]{1,0:T(8,128)(2,1)S(1)} collective-permute-done((bf16[128,1536]{1,0:T(8,128)(2,1)S(1)}, bf16[128,1536]{1,0:T(8,128)(2,1)S(1)}, u32[]{:S(2)}, u32[]{:S(2)}) %collective-permute-start.15) | collective-permute-done | bytes 393248 | tf_op jit(solution)/shard_map/ppermute | solution.py:292
  122.7 9.1 %collective-permute-done.16.refs_2_ = bf16[128,1536]{1,0:T(8,128)(2,1)S(1)} collective-permute-done((bf16[128,1536]{1,0:T(8,128)(2,1)S(1)}, bf16[128,1536]{1,0:T(8,128)(2,1)S(1)}, u32[]{:S(2)}, u32[]{:S(2)}) %collective-permute-start.16) | collective-permute-done | bytes 393248 | tf_op jit(solution)/shard_map/ppermute | solution.py:292
  132.6 2.9 middle_and_normed.1
  140.5 8.1 %collective-permute-done.20 = bf16[128,1536]{1,0:T(8,128)(2,1)S(1)} collective-permute-done((bf16[128,1536]{1,0:T(8,128)(2,1)}, bf16[128,1536]{1,0:T(8,128)(2,1)S(1)}, u32[]{:S(2)}, u32[]{:S(2)}) %collective-permute-start.20) | collective-permute-done | bytes 393248 | tf_op jit(solution)/shard_map/ppermute | solution.py:292
  148.7 6.5 %collective-permute-done.19 = bf16[128,1536]{1,0:T(8,128)(2,1)S(1)} collective-permute-done((bf16[128,1536]{1,0:T(8,128)(2,1)}, bf16[128,1536]{1,0:T(8,128)(2,1)S(1)}, u32[]{:S(2)}, u32[]{:S(2)}) %collective-permute-start.19) | collective-permute-done | bytes 393248 | tf_op jit(solution)/shard_map/ppermute | solution.py:292
  160.3 24.3 %unit_back_and_forth.1 = (bf16[4,128,1536]{2,1,0:T(8,128)(2,1)}, bf16[4,128,1536]{2,1,0:T(8,128)(2,1)}, bf16[4,128,1536]{2,1,0:T(8,128)(2,1)}, bf16[4,128,1536]{2,1,0:T(8,128)(2,1)}, bf16[4,1728,384]{2,1,0:T(8,128)(2,1)}) custom-call(bf16[4,128,1536]{2,1,0:T(8,128)(2,1)} %copy-done.31, bf16[4,128,1536]{2,1,0:T(8,128)(2,1)} %collective-permute-done.21.far_ref, ...), custom_call_target="tpu_custom_call" | custom-call | tf_op jit(solution)/shard_map/unit_back_and_forth/pallas_call | solution.py:912
  184.7 3.6 %collective-permute-done.23.refs_1_ = bf16[4,128,1536]{2,1,0:T(8,128)(2,1)S(1)} collective-permute-done((bf16[4,128,1536]{2,1,0:T(8,128)(2,1)}, bf16[4,128,1536]{2,1,0:T(8,128)(2,1)S(1)}, u32[]{:S(2)}, u32[]{:S(2)}) %collective-permute-start.23) | collective-permute-done | bytes 1572896 | tf_op jit(solution)/shard_map/ppermute | solution.py:297
  194.5 8.5 %collective-permute-done.24.refs_1_ = bf16[128,1536]{1,0:T(8,128)(2,1)S(1)} collective-permute-done((bf16[128,1536]{1,0:T(8,128)(2,1)S(1)}, bf16[128,1536]{1,0:T(8,128)(2,1)S(1)}, u32[]{:S(2)}, u32[]{:S(2)}) %collective-permute-start.24) | collective-permute-done | bytes 393248 | tf_op jit(solution)/shard_map/ppermute | solution.py:292
  203.0 8.8 %collective-permute-done.25.refs_2_ = bf16[128,1536]{1,0:T(8,128)(2,1)S(1)} collective-permute-done((bf16[128,1536]{1,0:T(8,128)(2,1)S(1)}, bf16[128,1536]{1,0:T(8,128)(2,1)S(1)}, u32[]{:S(2)}, u32[]{:S(2)}) %collective-permute-start.25) | collective-permute-done | bytes 393248 | tf_op jit(solution)/shard_map/ppermute | solution.py:292
  213.3 3.5 %middle_back.1 = (f32[128,1536]{1,0:T(8,128)}, bf16[128,1536]{1,0:T(8,128)(2,1)}, f32[1,1536]{1,0:T(1,128)}) custom-call(bf16[128,1536]{1,0:T(8,128)(2,1)} %bitcast.103, f32[128,1536]{1,0:T(8,128)} %get-tuple-element.180.middle_ref, f32[1,1536]{1,0:T(1,128)} %broadcast_in_dim.34.gain_ref, f32[128,1536]{1,0:T(8,128)} %copy-done.19, ...), custom_call_target="tpu_custom_call" | custom-call | tf_op jit(solution)/shard_map/middle_back/pallas_call | solution.py:1199
  217.2 2.5 collective-permute-start.33
  222.2 6.7 %collective-permute-done.27 = bf16[128,1536]{1,0:T(8,128)(2,1)S(1)} collective-permute-done((bf16[128,1536]{1,0:T(8,128)(2,1)}, bf16[128,1536]{1,0:T(8,128)(2,1)S(1)}, u32[]{:S(2)}, u32[]{:S(2)}) %collective-permute-start.27) | collective-permute-done | bytes 393248 | tf_op jit(solution)/shard_map/ppermute | solution.py:292
  228.9 9.1 %collective-permute-done.33 = bf16[128,1536]{1,0:T(8,128)(2,1)S(1)} collective-permute-done((bf16[128,1536]{1,0:T(8,128)(2,1)}, bf16[128,1536]{1,0:T(8,128)(2,1)S(1)}, u32[]{:S(2)}, u32[]{:S(2)}) %collective-permute-start.33) | collective-permute-done | bytes 393248 | tf_op jit(solution)/shard_map/ppermute | solution.py:292
  244.4 14.2 %mix_backward.1 = (bf16[2,4,128,512]{3,2,1,0:T(8,128)(2,1)}, f32[8,256]{1,0:T(8,128)S(1)}, bf16[4,128,1536]{2,1,0:T(8,128)(2,1)}, bf16[4,128,1536]{2,1,0:T(8,128...) custom-call(s32[1]{0:T(128)} %bitcast.place_ref.seq_ref, ...), custom_call_target="tpu_custom_call" | custom-call | flops 1000000000 | bytes 24000000 | tf_op jit(solution)/shard_map/mix_backward/pallas_call | solution.py:709
  263.5 5.7 %collective-permute-done.35 = bf16[2,256,256]{2,1,0:T(8,128)(2,1)S(1)} collective-permute-done((bf16[2,256,256]{2,1,0:T(8,128)(2,1)S(1)}, bf16[2,256,256]{2,1,0:T(8,128)(2,1)S(1)}, u32[]{:S(2)}, u32[]{:S(2)}) %collective-permute-start.35) | collective-permute-done | bytes 262176 | tf_op jit(solution)/shard_map/ppermute | solution.py:292
  287.2 2.7 payloads.7
  289.9 3.4 collective-permute-done.40.refs_1_
  309.5 3.2 collective-permute-done.49
  315.4 7.5 %collective-permute-done.51.refs_2_ = bf16[432,384]{1,0:T(8,128)(2,1)S(1)} collective-permute-done((bf16[432,384]{1,0:T(8,128)(2,1)S(1)}, bf16[432,384]{1,0:T(8,128)(2,1)S(1)}, u32[]{:S(2)}, u32[]{:S(2)}) %collective-permute-start.51) | collective-permute-done | bytes 331808 | tf_op jit(solution)/shard_map/ppermute | solution.py:292
  324.2 2.5 unit_give.1
  333.8 4.0 %reduce-scatter.5.cloned.1.call-done = bf16[1,640,512]{2,1,0:T(8,128)(2,1)} async-done(((bf16[4,640,512]{2,1,0:T(8,128)(2,1)}), bf16[1,640,512]{2,1,0:T(8,128)(2,1)}) %reduce-scatter.5.cloned.1.call-update) | async-done | bytes 655376 | tf_op jit(solution)/shard_map/reduce_scatter | solution.py:1515
  (252 shorter events, 115.4 us)
Async XLA Ops:
  7.2 68.8 %all-gather.5.cloned.1.call-start = ((), (), s32[]{:S(2)}) async-start(), calls=%async_computation.4 | async-start | bytes 1966080 | tf_op jit(solution)/shard_map/all_gather | solution.py:1418
  9.3 151.0 %all-gather.7.cloned.1.call-start = ((), (), s32[]{:S(2)}) async-start(), calls=%async_computation.5 | async-start | bytes 6635520 | tf_op jit(solution)/shard_map/all_gather | solution.py:1429
  9.7 13.9 %collective-permute-start.2 = (bf16[128,1536]{1,0:T(8,128)(2,1)S(1)}, bf16[128,1536]{1,0:T(8,128)(2,1)S(1)}, u32[]{:S(2)}, u32[]{:S(2)}) collective-permute-start(bf16[128,1536]{1,0:T(8,128)(2,1)S(1)} %fusion.6), channel_id=1, source_target_pairs={{0,24},{4,28},{8,16},{12,20},{16,8},{20,12},{24,0},{28,4},{1,25},{... | collective-permute-start | bytes 1179656 | tf_op jit(solution)/shard_map/ppermute | solution.py:292
  13.7 17.5 %collective-permute-start.1 = (bf16[128,1536]{1,0:T(8,128)(2,1)S(1)}, bf16[128,1536]{1,0:T(8,128)(2,1)S(1)}, u32[]{:S(2)}, u32[]{:S(2)}) collective-permute-start(bf16[128,1536]{1,0:T(8,128)(2,1)S(1)} %fusion.6), channel_id=1, source_target_pairs={{0,16},{4,20},{8,24},{12,28},{16,0},{20,4},{24,8},{28,12},{1,17},{... | collective-permute-start | bytes 1179656 | tf_op jit(solution)/shard_map/ppermute | solution.py:292
  14.2 17.3 %collective-permute-start = (bf16[128,1536]{1,0:T(8,128)(2,1)S(1)}, bf16[128,1536]{1,0:T(8,128)(2,1)S(1)}, u32[]{:S(2)}, u32[]{:S(2)}) collective-permute-start(bf16[128,1536]{1,0:T(8,128)(2,1)S(1)} %fusion.6), channel_id=1, source_target_pairs={{0,8},{4,12},{8,0},{12,4},{16,24},{20,28},{24,16},{28,20},{1,9},{5... | collective-permute-start | bytes 1179656 | tf_op jit(solution)/shard_map/ppermute | solution.py:292
  35.2 244.6 %reduce-scatter.3.cloned.1.call-start = ((), (), s32[]{:S(2)}) async-start(), calls=%async_computation.2 | async-start | bytes 6635520 | tf_op jit(solution)/shard_map/reduce_scatter | solution.py:1461
  35.3 24.5 %collective-permute-start.4 = (bf16[2,32,2048]{2,1,0:T(8,128)(2,1)}, bf16[2,32,2048]{2,1,0:T(8,128)(2,1)}, u32[]{:S(2)}, u32[]{:S(2)}) collective-permute-start(bf16[2,32,2048]{2,1,0:T(8,128)(2,1)} %get-tuple-element.162), channel_id=1, source_target_pairs={{0,1},{1,0},{2,3},{3,2},{4,5},{5,4},{6,7},{7,6},{8,9},{9,8},{10,11... | collective-permute-start | bytes 786440 | tf_op jit(solution)/shard_map/ppermute | solution.py:323
  36.9 33.2 %collective-permute-start.7 = (bf16[128,1536]{1,0:T(8,128)(2,1)S(1)}, bf16[128,1536]{1,0:T(8,128)(2,1)}, u32[]{:S(2)}, u32[]{:S(2)}) collective-permute-start(bf16[128,1536]{1,0:T(8,128)(2,1)S(1)} %bitcast.104), channel_id=1, source_target_pairs={{0,8},{4,12},{8,0},{12,4},{16,24},{20,28},{24,16},{28,20},{1,9},{5... | collective-permute-start | bytes 1179656 | tf_op jit(solution)/shard_map/ppermute | solution.py:292
  38.4 31.7 %collective-permute-start.8 = (bf16[128,1536]{1,0:T(8,128)(2,1)S(1)}, bf16[128,1536]{1,0:T(8,128)(2,1)}, u32[]{:S(2)}, u32[]{:S(2)}) collective-permute-start(bf16[128,1536]{1,0:T(8,128)(2,1)S(1)} %bitcast.105), channel_id=1, source_target_pairs={{0,16},{4,20},{8,24},{12,28},{16,0},{20,4},{24,8},{28,12},{1,17},{... | collective-permute-start | bytes 1179656 | tf_op jit(solution)/shard_map/ppermute | solution.py:292
  39.2 31.0 %collective-permute-start.9 = (bf16[128,1536]{1,0:T(8,128)(2,1)S(1)}, bf16[128,1536]{1,0:T(8,128)(2,1)}, u32[]{:S(2)}, u32[]{:S(2)}) collective-permute-start(bf16[128,1536]{1,0:T(8,128)(2,1)S(1)} %bitcast.106), channel_id=1, source_target_pairs={{0,24},{4,28},{8,16},{12,20},{16,8},{20,12},{24,0},{28,4},{1,25},{... | collective-permute-start | bytes 1179656 | tf_op jit(solution)/shard_map/ppermute | solution.py:292
  40.4 24.0 %collective-permute-start.5 = (bf16[2,32,2048]{2,1,0:T(8,128)(2,1)}, bf16[2,32,2048]{2,1,0:T(8,128)(2,1)}, u32[]{:S(2)}, u32[]{:S(2)}) collective-permute-start(bf16[2,32,2048]{2,1,0:T(8,128)(2,1)} %get-tuple-element.162), channel_id=1, source_target_pairs={{0,2},{1,3},{2,0},{3,1},{4,6},{5,7},{6,4},{7,5},{8,10},{9,11},{10,... | collective-permute-start | bytes 786440 | tf_op jit(solution)/shard_map/ppermute | solution.py:323
  112.4 19.3 %collective-permute-start.16 = (bf16[128,1536]{1,0:T(8,128)(2,1)S(1)}, bf16[128,1536]{1,0:T(8,128)(2,1)S(1)}, u32[]{:S(2)}, u32[]{:S(2)}) collective-permute-start(bf16[128,1536]{1,0:T(8,128)(2,1)S(1)} %get-tuple-element.178), channel_id=1, source_target_pairs={{0,16},{4,20},{8,24},{12,28},{16,0},{20,4},{24,8},{28,12},{1,17},{... | collective-permute-start | bytes 1179656 | tf_op jit(solution)/shard_map/ppermute | solution.py:292
  112.8 18.9 %collective-permute-start.17 = (bf16[128,1536]{1,0:T(8,128)(2,1)S(1)}, bf16[128,1536]{1,0:T(8,128)(2,1)S(1)}, u32[]{:S(2)}, u32[]{:S(2)}) collective-permute-start(bf16[128,1536]{1,0:T(8,128)(2,1)S(1)} %get-tuple-element.179), channel_id=1, source_target_pairs={{0,24},{4,28},{8,16},{12,20},{16,8},{20,12},{24,0},{28,4},{1,25},{... | collective-permute-start | bytes 1179656 | tf_op jit(solution)/shard_map/ppermute | solution.py:292
  135.5 13.2 %collective-permute-start.20 = (bf16[128,1536]{1,0:T(8,128)(2,1)}, bf16[128,1536]{1,0:T(8,128)(2,1)S(1)}, u32[]{:S(2)}, u32[]{:S(2)}) collective-permute-start(bf16[128,1536]{1,0:T(8,128)(2,1)} %get-tuple-element.181), channel_id=1, source_target_pairs={{0,24},{4,28},{8,16},{12,20},{16,8},{20,12},{24,0},{28,4},{1,25},{... | collective-permute-start | bytes 1179656 | tf_op jit(solution)/shard_map/ppermute | solution.py:292
  136.5 18.6 %collective-permute-start.19 = (bf16[128,1536]{1,0:T(8,128)(2,1)}, bf16[128,1536]{1,0:T(8,128)(2,1)S(1)}, u32[]{:S(2)}, u32[]{:S(2)}) collective-permute-start(bf16[128,1536]{1,0:T(8,128)(2,1)} %get-tuple-element.181), channel_id=1, source_target_pairs={{0,16},{4,20},{8,24},{12,28},{16,0},{20,4},{24,8},{28,12},{1,17},{... | collective-permute-start | bytes 1179656 | tf_op jit(solution)/shard_map/ppermute | solution.py:292
  137.3 17.9 %collective-permute-start.18 = (bf16[128,1536]{1,0:T(8,128)(2,1)}, bf16[128,1536]{1,0:T(8,128)(2,1)S(1)}, u32[]{:S(2)}, u32[]{:S(2)}) collective-permute-start(bf16[128,1536]{1,0:T(8,128)(2,1)} %get-tuple-element.181), channel_id=1, source_target_pairs={{0,8},{4,12},{8,0},{12,4},{16,24},{20,28},{24,16},{28,20},{1,9},{5... | collective-permute-start | bytes 1179656 | tf_op jit(solution)/shard_map/ppermute | solution.py:292
  140.5 15.1 %collective-permute-start.22 = (bf16[4,128,1536]{2,1,0:T(8,128)(2,1)S(1)}, bf16[4,128,1536]{2,1,0:T(8,128)(2,1)S(1)}, u32[]{:S(2)}, u32[]{:S(2)}) collective-permute-start(bf16[4,128,1536]{2,1,0:T(8,128)(2,1)S(1)} %pad_maximum_fusion.2.cot_near_ref), channel_id=1, source_target_pairs={{0,4},{4,0},{8,12},{12,8},{16,20},{20,16},{24,28},{28,24},{1,5},{5... | collective-permute-start | bytes 4718600 | tf_op jit(solution)/shard_map/ppermute | solution.py:297
  184.6 153.2 %reduce-scatter.5.cloned.1.call-start = ((), (), s32[]{:S(2)}) async-start(), calls=%async_computation.3 | async-start | bytes 3276800 | tf_op jit(solution)/shard_map/reduce_scatter | solution.py:1515
  192.5 19.3 %collective-permute-start.25 = (bf16[128,1536]{1,0:T(8,128)(2,1)S(1)}, bf16[128,1536]{1,0:T(8,128)(2,1)S(1)}, u32[]{:S(2)}, u32[]{:S(2)}) collective-permute-start(bf16[128,1536]{1,0:T(8,128)(2,1)S(1)} %get-tuple-element.190), channel_id=1, source_target_pairs={{0,16},{4,20},{8,24},{12,28},{16,0},{20,4},{24,8},{28,12},{1,17},{... | collective-permute-start | bytes 1179656 | tf_op jit(solution)/shard_map/ppermute | solution.py:292
  193.9 17.8 %collective-permute-start.26 = (bf16[128,1536]{1,0:T(8,128)(2,1)S(1)}, bf16[128,1536]{1,0:T(8,128)(2,1)S(1)}, u32[]{:S(2)}, u32[]{:S(2)}) collective-permute-start(bf16[128,1536]{1,0:T(8,128)(2,1)S(1)} %get-tuple-element.191), channel_id=1, source_target_pairs={{0,24},{4,28},{8,16},{12,20},{16,8},{20,12},{24,0},{28,4},{1,25},{... | collective-permute-start | bytes 1179656 | tf_op jit(solution)/shard_map/ppermute | solution.py:292
  217.2 20.7 %collective-permute-start.33 = (bf16[128,1536]{1,0:T(8,128)(2,1)}, bf16[128,1536]{1,0:T(8,128)(2,1)S(1)}, u32[]{:S(2)}, u32[]{:S(2)}) collective-permute-start(bf16[128,1536]{1,0:T(8,128)(2,1)} %get-tuple-element.195), channel_id=1, source_target_pairs={{0,24},{4,28},{8,16},{12,20},{16,8},{20,12},{24,0},{28,4},{1,25},{... | collective-permute-start | bytes 1179656 | tf_op jit(solution)/shard_map/ppermute | solution.py:292
  219.7 19.6 %collective-permute-start.32 = (bf16[128,1536]{1,0:T(8,128)(2,1)}, bf16[128,1536]{1,0:T(8,128)(2,1)S(1)}, u32[]{:S(2)}, u32[]{:S(2)}) collective-permute-start(bf16[128,1536]{1,0:T(8,128)(2,1)} %get-tuple-element.195), channel_id=1, source_target_pairs={{0,16},{4,20},{8,24},{12,28},{16,0},{20,4},{24,8},{28,12},{1,17},{... | collective-permute-start | bytes 1179656 | tf_op jit(solution)/shard_map/ppermute | solution.py:292
  239.7 19.0 %collective-permute-start.29 = (bf16[128,1536]{1,0:T(8,128)(2,1)S(1)}, bf16[128,1536]{1,0:T(8,128)(2,1)S(1)}, u32[]{:S(2)}, u32[]{:S(2)}) collective-permute-start(bf16[128,1536]{1,0:T(8,128)(2,1)S(1)} %get-tuple-element.203), channel_id=1, source_target_pairs={{0,8},{4,12},{8,0},{12,4},{16,24},{20,28},{24,16},{28,20},{1,9},{5... | collective-permute-start | bytes 1179656 | tf_op jit(solution)/shard_map/ppermute | solution.py:292
  240.3 19.6 %collective-permute-start.30 = (bf16[128,1536]{1,0:T(8,128)(2,1)S(1)}, bf16[128,1536]{1,0:T(8,128)(2,1)S(1)}, u32[]{:S(2)}, u32[]{:S(2)}) collective-permute-start(bf16[128,1536]{1,0:T(8,128)(2,1)S(1)} %get-tuple-element.204), channel_id=1, source_target_pairs={{0,16},{4,20},{8,24},{12,28},{16,0},{20,4},{24,8},{28,12},{1,17},{... | collective-permute-start | bytes 1179656 | tf_op jit(solution)/shard_map/ppermute | solution.py:292
  240.7 19.2 %collective-permute-start.31 = (bf16[128,1536]{1,0:T(8,128)(2,1)S(1)}, bf16[128,1536]{1,0:T(8,128)(2,1)S(1)}, u32[]{:S(2)}, u32[]{:S(2)}) collective-permute-start(bf16[128,1536]{1,0:T(8,128)(2,1)S(1)} %get-tuple-element.205), channel_id=1, source_target_pairs={{0,24},{4,28},{8,16},{12,20},{16,8},{20,12},{24,0},{28,4},{1,25},{... | collective-permute-start | bytes 1179656 | tf_op jit(solution)/shard_map/ppermute | solution.py:292
  261.4 14.1 %collective-permute-start.36 = (bf16[2,256,256]{2,1,0:T(8,128)(2,1)S(1)}, bf16[2,256,256]{2,1,0:T(8,128)(2,1)S(1)}, u32[]{:S(2)}, u32[]{:S(2)}) collective-permute-start(bf16[2,256,256]{2,1,0:T(8,128)(2,1)S(1)} %get-tuple-element.229), channel_id=1, source_target_pairs={{0,16},{4,20},{8,24},{12,28},{16,0},{20,4},{24,8},{28,12},{1,17},{... | collective-permute-start | bytes 786440 | tf_op jit(solution)/shard_map/ppermute | solution.py:292
  262.0 13.5 %collective-permute-start.37 = (bf16[2,256,256]{2,1,0:T(8,128)(2,1)S(1)}, bf16[2,256,256]{2,1,0:T(8,128)(2,1)S(1)}, u32[]{:S(2)}, u32[]{:S(2)}) collective-permute-start(bf16[2,256,256]{2,1,0:T(8,128)(2,1)S(1)} %get-tuple-element.230), channel_id=1, source_target_pairs={{0,24},{4,28},{8,16},{12,20},{16,8},{20,12},{24,0},{28,4},{1,25},{... | collective-permute-start | bytes 786440 | tf_op jit(solution)/shard_map/ppermute | solution.py:292
  296.8 26.1 %collective-permute-start.51 = (bf16[432,384]{1,0:T(8,128)(2,1)S(1)}, bf16[432,384]{1,0:T(8,128)(2,1)S(1)}, u32[]{:S(2)}, u32[]{:S(2)}) collective-permute-start(bf16[432,384]{1,0:T(8,128)(2,1)S(1)} %get-tuple-element.278), channel_id=1, source_target_pairs={{0,16},{4,20},{8,24},{12,28},{16,0},{20,4},{24,8},{28,12},{1,17},{... | collective-permute-start | bytes 995336 | tf_op jit(solution)/shard_map/ppermute | solution.py:292
  297.9 25.0 %collective-permute-start.52 = (bf16[432,384]{1,0:T(8,128)(2,1)S(1)}, bf16[432,384]{1,0:T(8,128)(2,1)S(1)}, u32[]{:S(2)}, u32[]{:S(2)}) collective-permute-start(bf16[432,384]{1,0:T(8,128)(2,1)S(1)} %get-tuple-element.277), channel_id=1, source_target_pairs={{0,24},{4,28},{8,16},{12,20},{16,8},{20,12},{24,0},{28,4},{1,25},{... | collective-permute-start | bytes 995336 | tf_op jit(solution)/shard_map/ppermute | solution.py:292
  308.3 19.7 %collective-permute-start.44 = (bf16[128,1536]{1,0:T(8,128)(2,1)}, bf16[128,1536]{1,0:T(8,128)(2,1)S(1)}, u32[]{:S(2)}, u32[]{:S(2)}) collective-permute-start(bf16[128,1536]{1,0:T(8,128)(2,1)} %get-tuple-element.260), channel_id=1, source_target_pairs={{0,24},{4,28},{8,16},{12,20},{16,8},{20,12},{24,0},{28,4},{1,25},{... | collective-permute-start | bytes 1179656 | tf_op jit(solution)/shard_map/ppermute | solution.py:292
  312.7 17.3 %collective-permute-start.43 = (bf16[128,1536]{1,0:T(8,128)(2,1)}, bf16[128,1536]{1,0:T(8,128)(2,1)S(1)}, u32[]{:S(2)}, u32[]{:S(2)}) collective-permute-start(bf16[128,1536]{1,0:T(8,128)(2,1)} %get-tuple-element.259), channel_id=1, source_target_pairs={{0,16},{4,20},{8,24},{12,28},{16,0},{20,4},{24,8},{28,12},{1,17},{... | collective-permute-start | bytes 1179656 | tf_op jit(solution)/shard_map/ppermute | solution.py:292
  314.1 15.9 %collective-permute-start.42 = (bf16[128,1536]{1,0:T(8,128)(2,1)}, bf16[128,1536]{1,0:T(8,128)(2,1)S(1)}, u32[]{:S(2)}, u32[]{:S(2)}) collective-permute-start(bf16[128,1536]{1,0:T(8,128)(2,1)} %get-tuple-element.258), channel_id=1, source_target_pairs={{0,8},{4,12},{8,0},{12,4},{16,24},{20,28},{24,16},{28,20},{1,9},{5... | collective-permute-start | bytes 1179656 | tf_op jit(solution)/shard_map/ppermute | solution.py:292
  (82 other events, 584.8 us)
Sparse Core Ops, SparseCore 0:
  10.2 49.0 all-gather.4
  60.8 99.4 all-gather.6
  184.7 95.0 reduce-scatter.2
  282.1 55.6 reduce-scatter.4

commit v6 on v5

--- a/solution.py
+++ b/solution.py
@@ -758,8 +758,8 @@
     pack_ref,
     back_near_out,
     back_far_out,
-    mixed_near_out,
-    mixed_far_out,
+    hidden_out,
+    down_out,
     grads_out,
     normed,
     cot,
@@ -771,7 +771,6 @@
     hidden_t,
     grads,
     back,
-    mixed,
     in_sems,
     out_sems,
 ):
@@ -887,11 +886,8 @@
                     grads[z, pl.ds(row, count), :] = grad[first : first + count, columns]
                     row += count
             send(grads.at[z], grads_out.at[z])
-    for i, out in ((0, mixed_near_out), (1, mixed_far_out)):
-        here = pl.ds(i * half, half)
-        mixed[here, :] = dot_nn(hidden[here, :], down[pl.ds(0, part), :]).astype(bf16)
-        for k in range(chips):
-            send(mixed.at[pl.ds(i * half + k * rows, rows), :], out.at[k])
+    send(hidden, hidden_out)
+    send(down.at[pl.ds(0, part), :], down_out)
     for i, out in ((1, back_far_out), (0, back_near_out)):
         for k in range(0, chips, 2):
             first_row = i * half + k * rows
@@ -924,15 +920,41 @@
             pltpu.VMEM((part, length), bf16),
             pltpu.VMEM(pack.shape, bf16),
             pltpu.VMEM((length, model), bf16),
-            pltpu.VMEM((length, model), bf16),
             pltpu.SemaphoreType.DMA((4 * chips + planes * (3 + planes),)),
             pltpu.SemaphoreType.DMA((4 * chips + planes,)),
         ],
-        out_shape=[jax.ShapeDtypeStruct(near.shape, bf16)] * 4
-        + [jax.ShapeDtypeStruct(pack.shape, bf16)],
+        out_shape=[jax.ShapeDtypeStruct(near.shape, bf16)] * 2
+        + [
+            jax.ShapeDtypeStruct((length, part), bf16),
+            jax.ShapeDtypeStruct((part, model), bf16),
+            jax.ShapeDtypeStruct(pack.shape, bf16),
+        ],
         compiler_params=pltpu.CompilerParams(vmem_limit_bytes=58 * 1024 * 1024),
         name="unit_back_and_forth",
     )(near, far, cot_near, cot_far, pack)
+
+
+def mixed_kernel(hidden_ref, down_ref, near_ref, far_ref):
+    chips, rows, model = near_ref.shape
+    for i, ref in enumerate((near_ref, far_ref)):
+        here = pl.ds(i * chips * rows, chips * rows)
+        product = dot_nn(hidden_ref[here, :], down_ref[...])
+        ref[...] = product.reshape(chips, rows, model).astype(ref.dtype)
+
+
+def mixed_parts(hidden, down, chips):
+    length, model = hidden.shape[0], down.shape[1]
+    whole = pl.BlockSpec(memory_space=pltpu.VMEM)
+    shape = jax.ShapeDtypeStruct((chips, length // (2 * chips), model), jnp.bfloat16)
+    return pl.pallas_call(
+        mixed_kernel,
+        in_specs=[whole] * 2,
+        out_specs=[whole] * 2,
+        out_shape=[shape] * 2,
+        compiler_params=pltpu.CompilerParams(vmem_limit_bytes=24 * 1024 * 1024),
+        cost_estimate=little,
+        name="mixed_parts",
+    )(hidden, down)
 
 
 def mix_pack_kernel(
@@ -1455,7 +1477,7 @@
     )
 
     near, far = gather_blocks(normed2)
-    back_near, back_far, mixed_near, mixed_far, unit_grads = unit_back_and_forth(
+    back_near, back_far, hidden, down, unit_grads = unit_back_and_forth(
         near, far, cot_near, cot_far, unit_pack, part
     )
     unit_sum = lax.psum_scatter(unit_grads, "fsdp", scatter_dimension=0, tiled=False)
@@ -1463,7 +1485,8 @@
     middle_grad, middle_low, mlp_gain_term = middle_back(
         out_grad, middle, mlp_gain, spread_pairs(*pair_blocks(back_near, back_far))
     )
-    middle_low, mixed_near, mixed_far = tie(middle_low, mixed_near, mixed_far)
+    middle_low, hidden, down = tie(middle_low, hidden, down)
+    mixed_near, mixed_far = mixed_parts(hidden, down, chips)
     mixed_own, *mixed_low = pair_blocks(mixed_near, mixed_far)
     first, *others = [chip_swap(middle_low, k) for k in range(1, chips)]
     first, mixed_own, *mixed_low = tie(first, mixed_own, *mixed_low)

time: 353 us -> 351 us (level)
    unnamed x112 -> x116, local copies, waits for them, and re-layouts: 17.6 us -> 14.8 us
  transfers between devices with their start and end apart: 58 -> 58, of which waited for: 36 -> 34; matrix products, arithmetic and copies ran while one was open for 6% -> 6% of each run, Pallas kernels for 14% -> 15%
where the time goes in v6:
time: 351 us; the launch traced here: 345 us
  waiting for transfers between devices  161 us (46%)
  Pallas kernels  78.6 us (22%)
  starting transfers between devices  54.8 us (16%)
  local copies, waits for them, and re-layouts  20.9 us (6%)
  between operations  14.9 us (4%)
  other arithmetic  8.96 us (3%)
  matrix products  5.49 us (2%)
    ppermute x36, waiting for transfers between devices, chip_swap(): return lax.ppermute(x, 'seq', [(i, i ^ 2 * k) for i in range(devices)])  113 us
    ppermute x36, starting transfers between devices, chip_swap(): return lax.ppermute(x, 'seq', [(i, i ^ 2 * k) for i in range(devices)])  42.5 us
    ppermute x3, waiting for transfers between devices, plane_swap(): lax.ppermute(x, 'fsdp', [(i, i ^ k) for i in range(lax.axis_size('fsdp'))])  22.5 us
    pallas_call x1, Pallas kernels, unit_back_and_forth(): pl.pallas_call(unit_kernel, in_specs=[there] * 5, out_specs=[there] * 5,...  21.9 us
    ppermute x12, waiting for transfers between devices, core_swap(): return lax.ppermute(x, 'seq', [(i, i ^ 1) for i in range(devices)])  14.9 us
    unnamed x116, local copies, waits for them, and re-layouts  14.8 us
    pallas_call x1, Pallas kernels, mix_backward(): pl.pallas_call(mix_backward_kernel, grid_spec=pltpu.PrefetchScalarGridSpe...  14.4 us
    pallas_call x1, Pallas kernels, mix_forward(): pl.pallas_call(mix_forward_kernel, grid_spec=pltpu.PrefetchScalarGridSpec...  11.4 us
  transfers between devices with their start and end apart: 58, of which 34 were waited for; matrix products, arithmetic and copies ran while one was open for 6% of the time, Pallas kernels for 15%

profile of v6, /device:TPU:0, one launch (start us, length us, event | category | flops | bytes accessed | tf_op | source)
XLA Modules:
  0.0 344.7 jit_solution(7714266795105492735)
XLA Ops:
  9.7 4.0 %collective-permute-start.2 = (bf16[128,1536]{1,0:T(8,128)(2,1)S(1)}, bf16[128,1536]{1,0:T(8,128)(2,1)S(1)}, u32[]{:S(2)}, u32[]{:S(2)}) collective-permute-start(bf16[128,1536]{1,0:T(8,128)(2,1)S(1)} %fusion.6), channel_id=1, source_target_pairs={{0,24},{4,28},{8,16},{12,20},{16,8},{20,12},{24,0},{28,4},{1,25},{... | collective-permute-start | bytes 1179656 | tf_op jit(solution)/shard_map/ppermute | solution.py:292
  14.3 9.3 %collective-permute-done.2 = bf16[128,1536]{1,0:T(8,128)(2,1)S(1)} collective-permute-done((bf16[128,1536]{1,0:T(8,128)(2,1)S(1)}, bf16[128,1536]{1,0:T(8,128)(2,1)S(1)}, u32[]{:S(2)}, u32[]{:S(2)}) %collective-permute-start.2) | collective-permute-done | bytes 393248 | tf_op jit(solution)/shard_map/ppermute | solution.py:292
  23.7 7.6 %collective-permute-done.1 = bf16[128,1536]{1,0:T(8,128)(2,1)S(1)} collective-permute-done((bf16[128,1536]{1,0:T(8,128)(2,1)S(1)}, bf16[128,1536]{1,0:T(8,128)(2,1)S(1)}, u32[]{:S(2)}, u32[]{:S(2)}) %collective-permute-start.1) | collective-permute-done | bytes 393248 | tf_op jit(solution)/shard_map/ppermute | solution.py:292
  31.8 3.0 own_unit_pack.1
  40.4 2.6 collective-permute-start.5
  43.0 16.8 %collective-permute-done.4 = bf16[2,32,2048]{2,1,0:T(8,128)(2,1)} collective-permute-done((bf16[2,32,2048]{2,1,0:T(8,128)(2,1)}, bf16[2,32,2048]{2,1,0:T(8,128)(2,1)}, u32[]{:S(2)}, u32[]{:S(2)}) %collective-permute-start.4) | collective-permute-done | bytes 262176 | tf_op jit(solution)/shard_map/ppermute | solution.py:323
  64.5 5.7 %collective-permute-done.6 = bf16[2,32,2048]{2,1,0:T(8,128)(2,1)} collective-permute-done((bf16[2,32,2048]{2,1,0:T(8,128)(2,1)}, bf16[2,32,2048]{2,1,0:T(8,128)(2,1)}, u32[]{:S(2)}, u32[]{:S(2)}) %collective-permute-start.6) | collective-permute-done | bytes 262176 | tf_op jit(solution)/shard_map/ppermute | solution.py:323
  76.0 3.5 %fusion.2.near_ref = f32[4,128,512]{2,1,0:T(8,128)} fusion(bf16[4,128,1536]{2,1,0:T(8,128)(2,1)S(1)} %pad_maximum_fusion.near_ref, bf16[1536,512]{1,0:T(8,128)(2,1)} %all-gather.5.cloned.1.call-done), kind=kOutput, calls=%fused_computation.6 | convolution fusion | flops 805306368 | bytes 4194304 | tf_op jit(solution)/shard_map/dot_general | solution.py:369
  82.1 4.7 %collective-permute-done.12 = bf16[2,32,2048]{2,1,0:T(8,128)(2,1)} collective-permute-done((bf16[2,32,2048]{2,1,0:T(8,128)(2,1)}, bf16[2,32,2048]{2,1,0:T(8,128)(2,1)}, u32[]{:S(2)}, u32[]{:S(2)}) %collective-permute-start.12) | collective-permute-done | bytes 262176 | tf_op jit(solution)/shard_map/ppermute | solution.py:292
  93.0 11.4 %mix_forward.1 = (bf16[2,4,128,256]{3,2,1,0:T(8,128)(2,1)}, bf16[4,128,1536]{2,1,0:T(8,128)(2,1)}, bf16[4,128,1536]{2,1,0:T(8,128)(2,1)}, bf16[1024,256]{1,0:T(8...) custom-call(s32[1]{0:T(128)} %bitcast.place_ref.seq_ref, ...), custom_call_target="tpu_custom_call" | custom-call | tf_op jit(solution)/shard_map/mix_forward/pallas_call | solution.py:559
  104.6 3.5 %collective-permute-done.14.refs_1_ = bf16[4,128,1536]{2,1,0:T(8,128)(2,1)S(1)} collective-permute-done((bf16[4,128,1536]{2,1,0:T(8,128)(2,1)}, bf16[4,128,1536]{2,1,0:T(8,128)(2,1)S(1)}, u32[]{:S(2)}, u32[]{:S(2)}) %collective-permute-start.14) | collective-permute-done | bytes 1572896 | tf_op jit(solution)/shard_map/ppermute | solution.py:297
  114.8 7.9 %collective-permute-done.15.refs_1_ = bf16[128,1536]{1,0:T(8,128)(2,1)S(1)} collective-permute-done((bf16[128,1536]{1,0:T(8,128)(2,1)S(1)}, bf16[128,1536]{1,0:T(8,128)(2,1)S(1)}, u32[]{:S(2)}, u32[]{:S(2)}) %collective-permute-start.15) | collective-permute-done | bytes 393248 | tf_op jit(solution)/shard_map/ppermute | solution.py:292
  122.7 9.0 %collective-permute-done.16.refs_2_ = bf16[128,1536]{1,0:T(8,128)(2,1)S(1)} collective-permute-done((bf16[128,1536]{1,0:T(8,128)(2,1)S(1)}, bf16[128,1536]{1,0:T(8,128)(2,1)S(1)}, u32[]{:S(2)}, u32[]{:S(2)}) %collective-permute-start.16) | collective-permute-done | bytes 393248 | tf_op jit(solution)/shard_map/ppermute | solution.py:292
  132.6 2.9 middle_and_normed.1
  140.5 8.1 %collective-permute-done.20 = bf16[128,1536]{1,0:T(8,128)(2,1)S(1)} collective-permute-done((bf16[128,1536]{1,0:T(8,128)(2,1)}, bf16[128,1536]{1,0:T(8,128)(2,1)S(1)}, u32[]{:S(2)}, u32[]{:S(2)}) %collective-permute-start.20) | collective-permute-done | bytes 393248 | tf_op jit(solution)/shard_map/ppermute | solution.py:292
  148.7 6.5 %collective-permute-done.19 = bf16[128,1536]{1,0:T(8,128)(2,1)S(1)} collective-permute-done((bf16[128,1536]{1,0:T(8,128)(2,1)}, bf16[128,1536]{1,0:T(8,128)(2,1)S(1)}, u32[]{:S(2)}, u32[]{:S(2)}) %collective-permute-start.19) | collective-permute-done | bytes 393248 | tf_op jit(solution)/shard_map/ppermute | solution.py:292
  156.5 2.4 collective-permute-done.21.far_ref
  160.3 21.9 %unit_back_and_forth.1 = (bf16[4,128,1536]{2,1,0:T(8,128)(2,1)}, bf16[4,128,1536]{2,1,0:T(8,128)(2,1)}, bf16[1024,576]{1,0:T(8,128)(2,1)}, bf16[576,1536]{1,0:T(8,128)(2,1)}, bf16[4,1728,384]{2,1,0:T(8,128)(2,1)}) custom-call(bf16[4,128,1536]{2,1,0:T(8,128)(2,1)} %copy-done.33, bf16[4,128,1536]{2,1,0:T(8,128)(2,1)} %collective-permute-done.21.far_ref, ...), custom_call_target="tpu_custom_call" | custom-call | tf_op jit(solution)/shard_map/unit_back_and_forth/pallas_call | solution.py:908
  182.4 3.6 %collective-permute-done.23.refs_1_ = bf16[4,128,1536]{2,1,0:T(8,128)(2,1)S(1)} collective-permute-done((bf16[4,128,1536]{2,1,0:T(8,128)(2,1)}, bf16[4,128,1536]{2,1,0:T(8,128)(2,1)S(1)}, u32[]{:S(2)}, u32[]{:S(2)}) %collective-permute-start.23) | collective-permute-done | bytes 1572896 | tf_op jit(solution)/shard_map/ppermute | solution.py:297
  190.7 8.5 %collective-permute-done.24.refs_1_ = bf16[128,1536]{1,0:T(8,128)(2,1)S(1)} collective-permute-done((bf16[128,1536]{1,0:T(8,128)(2,1)S(1)}, bf16[128,1536]{1,0:T(8,128)(2,1)S(1)}, u32[]{:S(2)}, u32[]{:S(2)}) %collective-permute-start.24) | collective-permute-done | bytes 393248 | tf_op jit(solution)/shard_map/ppermute | solution.py:292
  199.2 8.8 %collective-permute-done.25.refs_2_ = bf16[128,1536]{1,0:T(8,128)(2,1)S(1)} collective-permute-done((bf16[128,1536]{1,0:T(8,128)(2,1)S(1)}, bf16[128,1536]{1,0:T(8,128)(2,1)S(1)}, u32[]{:S(2)}, u32[]{:S(2)}) %collective-permute-start.25) | collective-permute-done | bytes 393248 | tf_op jit(solution)/shard_map/ppermute | solution.py:292
  208.9 3.6 %middle_back.1 = (f32[128,1536]{1,0:T(8,128)}, bf16[128,1536]{1,0:T(8,128)(2,1)}, f32[1,1536]{1,0:T(1,128)}) custom-call(bf16[128,1536]{1,0:T(8,128)(2,1)} %bitcast.103, f32[128,1536]{1,0:T(8,128)} %get-tuple-element.182.middle_ref, f32[1,1536]{1,0:T(1,128)} %broadcast_in_dim.34.gain_ref, f32[128,1536]{1,0:T(8,128)} %copy-done.22, ...), custom_call_target="tpu_custom_call" | custom-call | tf_op jit(solution)/shard_map/middle_back/pallas_call | solution.py:1221
  213.9 2.6 mixed_parts.1
  220.5 8.1 %collective-permute-done.27 = bf16[128,1536]{1,0:T(8,128)(2,1)S(1)} collective-permute-done((bf16[128,1536]{1,0:T(8,128)(2,1)S(1)}, bf16[128,1536]{1,0:T(8,128)(2,1)S(1)}, u32[]{:S(2)}, u32[]{:S(2)}) %collective-permute-start.27) | collective-permute-done | bytes 393248 | tf_op jit(solution)/shard_map/ppermute | solution.py:292
  228.5 9.0 %collective-permute-done.33 = bf16[128,1536]{1,0:T(8,128)(2,1)S(1)} collective-permute-done((bf16[128,1536]{1,0:T(8,128)(2,1)S(1)}, bf16[128,1536]{1,0:T(8,128)(2,1)S(1)}, u32[]{:S(2)}, u32[]{:S(2)}) %collective-permute-start.33) | collective-permute-done | bytes 393248 | tf_op jit(solution)/shard_map/ppermute | solution.py:292
  244.0 14.4 %mix_backward.1 = (bf16[2,4,128,512]{3,2,1,0:T(8,128)(2,1)}, f32[8,256]{1,0:T(8,128)S(1)}, bf16[4,128,1536]{2,1,0:T(8,128)(2,1)}, bf16[4,128,1536]{2,1,0:T(8,128...) custom-call(s32[1]{0:T(128)} %bitcast.place_ref.seq_ref, ...), custom_call_target="tpu_custom_call" | custom-call | flops 1000000000 | bytes 24000000 | tf_op jit(solution)/shard_map/mix_backward/pallas_call | solution.py:709
  263.0 5.7 %collective-permute-done.35 = bf16[2,256,256]{2,1,0:T(8,128)(2,1)S(1)} collective-permute-done((bf16[2,256,256]{2,1,0:T(8,128)(2,1)S(1)}, bf16[2,256,256]{2,1,0:T(8,128)(2,1)S(1)}, u32[]{:S(2)}, u32[]{:S(2)}) %collective-permute-start.35) | collective-permute-done | bytes 262176 | tf_op jit(solution)/shard_map/ppermute | solution.py:292
  285.4 2.9 payloads.7
  288.3 4.3 %collective-permute-done.40.refs_1_ = bf16[432,384]{1,0:T(8,128)(2,1)S(1)} collective-permute-done((bf16[432,384]{1,0:T(8,128)(2,1)S(1)}, bf16[432,384]{1,0:T(8,128)(2,1)S(1)}, u32[]{:S(2)}, u32[]{:S(2)}) %collective-permute-start.40) | collective-permute-done | bytes 331808 | tf_op jit(solution)/shard_map/ppermute | solution.py:292
  308.9 4.6 %collective-permute-done.49 = bf16[16,1536]{1,0:T(8,128)(2,1)S(1)} collective-permute-done((bf16[16,1536]{1,0:T(8,128)(2,1)S(1)}, bf16[16,1536]{1,0:T(8,128)(2,1)S(1)}, u32[]{:S(2)}, u32[]{:S(2)}) %collective-permute-start.49) | collective-permute-done | bytes 49184 | tf_op jit(solution)/shard_map/ppermute | solution.py:343
  314.4 7.9 %collective-permute-done.51.refs_2_ = bf16[432,384]{1,0:T(8,128)(2,1)S(1)} collective-permute-done((bf16[432,384]{1,0:T(8,128)(2,1)S(1)}, bf16[432,384]{1,0:T(8,128)(2,1)S(1)}, u32[]{:S(2)}, u32[]{:S(2)}) %collective-permute-start.51) | collective-permute-done | bytes 331808 | tf_op jit(solution)/shard_map/ppermute | solution.py:292
  323.6 2.5 unit_give.1
  (257 shorter events, 112.6 us)
Async XLA Ops:
  7.2 68.8 %all-gather.5.cloned.1.call-start = ((), (), s32[]{:S(2)}) async-start(), calls=%async_computation.4 | async-start | bytes 1966080 | tf_op jit(solution)/shard_map/all_gather | solution.py:1440
  9.3 151.0 %all-gather.7.cloned.1.call-start = ((), (), s32[]{:S(2)}) async-start(), calls=%async_computation.5 | async-start | bytes 6635520 | tf_op jit(solution)/shard_map/all_gather | solution.py:1451
  9.7 13.9 %collective-permute-start.2 = (bf16[128,1536]{1,0:T(8,128)(2,1)S(1)}, bf16[128,1536]{1,0:T(8,128)(2,1)S(1)}, u32[]{:S(2)}, u32[]{:S(2)}) collective-permute-start(bf16[128,1536]{1,0:T(8,128)(2,1)S(1)} %fusion.6), channel_id=1, source_target_pairs={{0,24},{4,28},{8,16},{12,20},{16,8},{20,12},{24,0},{28,4},{1,25},{... | collective-permute-start | bytes 1179656 | tf_op jit(solution)/shard_map/ppermute | solution.py:292
  13.7 17.5 %collective-permute-start.1 = (bf16[128,1536]{1,0:T(8,128)(2,1)S(1)}, bf16[128,1536]{1,0:T(8,128)(2,1)S(1)}, u32[]{:S(2)}, u32[]{:S(2)}) collective-permute-start(bf16[128,1536]{1,0:T(8,128)(2,1)S(1)} %fusion.6), channel_id=1, source_target_pairs={{0,16},{4,20},{8,24},{12,28},{16,0},{20,4},{24,8},{28,12},{1,17},{... | collective-permute-start | bytes 1179656 | tf_op jit(solution)/shard_map/ppermute | solution.py:292
  14.2 17.3 %collective-permute-start = (bf16[128,1536]{1,0:T(8,128)(2,1)S(1)}, bf16[128,1536]{1,0:T(8,128)(2,1)S(1)}, u32[]{:S(2)}, u32[]{:S(2)}) collective-permute-start(bf16[128,1536]{1,0:T(8,128)(2,1)S(1)} %fusion.6), channel_id=1, source_target_pairs={{0,8},{4,12},{8,0},{12,4},{16,24},{20,28},{24,16},{28,20},{1,9},{5... | collective-permute-start | bytes 1179656 | tf_op jit(solution)/shard_map/ppermute | solution.py:292
  35.2 243.6 %reduce-scatter.3.cloned.1.call-start = ((), (), s32[]{:S(2)}) async-start(), calls=%async_computation.2 | async-start | bytes 6635520 | tf_op jit(solution)/shard_map/reduce_scatter | solution.py:1483
  35.3 24.5 %collective-permute-start.4 = (bf16[2,32,2048]{2,1,0:T(8,128)(2,1)}, bf16[2,32,2048]{2,1,0:T(8,128)(2,1)}, u32[]{:S(2)}, u32[]{:S(2)}) collective-permute-start(bf16[2,32,2048]{2,1,0:T(8,128)(2,1)} %get-tuple-element.164), channel_id=1, source_target_pairs={{0,1},{1,0},{2,3},{3,2},{4,5},{5,4},{6,7},{7,6},{8,9},{9,8},{10,11... | collective-permute-start | bytes 786440 | tf_op jit(solution)/shard_map/ppermute | solution.py:323
  36.9 33.2 %collective-permute-start.7 = (bf16[128,1536]{1,0:T(8,128)(2,1)S(1)}, bf16[128,1536]{1,0:T(8,128)(2,1)}, u32[]{:S(2)}, u32[]{:S(2)}) collective-permute-start(bf16[128,1536]{1,0:T(8,128)(2,1)S(1)} %bitcast.104), channel_id=1, source_target_pairs={{0,8},{4,12},{8,0},{12,4},{16,24},{20,28},{24,16},{28,20},{1,9},{5... | collective-permute-start | bytes 1179656 | tf_op jit(solution)/shard_map/ppermute | solution.py:292
  38.4 31.7 %collective-permute-start.8 = (bf16[128,1536]{1,0:T(8,128)(2,1)S(1)}, bf16[128,1536]{1,0:T(8,128)(2,1)}, u32[]{:S(2)}, u32[]{:S(2)}) collective-permute-start(bf16[128,1536]{1,0:T(8,128)(2,1)S(1)} %bitcast.105), channel_id=1, source_target_pairs={{0,16},{4,20},{8,24},{12,28},{16,0},{20,4},{24,8},{28,12},{1,17},{... | collective-permute-start | bytes 1179656 | tf_op jit(solution)/shard_map/ppermute | solution.py:292
  39.2 31.0 %collective-permute-start.9 = (bf16[128,1536]{1,0:T(8,128)(2,1)S(1)}, bf16[128,1536]{1,0:T(8,128)(2,1)}, u32[]{:S(2)}, u32[]{:S(2)}) collective-permute-start(bf16[128,1536]{1,0:T(8,128)(2,1)S(1)} %bitcast.106), channel_id=1, source_target_pairs={{0,24},{4,28},{8,16},{12,20},{16,8},{20,12},{24,0},{28,4},{1,25},{... | collective-permute-start | bytes 1179656 | tf_op jit(solution)/shard_map/ppermute | solution.py:292
  40.4 24.0 %collective-permute-start.5 = (bf16[2,32,2048]{2,1,0:T(8,128)(2,1)}, bf16[2,32,2048]{2,1,0:T(8,128)(2,1)}, u32[]{:S(2)}, u32[]{:S(2)}) collective-permute-start(bf16[2,32,2048]{2,1,0:T(8,128)(2,1)} %get-tuple-element.164), channel_id=1, source_target_pairs={{0,2},{1,3},{2,0},{3,1},{4,6},{5,7},{6,4},{7,5},{8,10},{9,11},{10,... | collective-permute-start | bytes 786440 | tf_op jit(solution)/shard_map/ppermute | solution.py:323
  112.4 19.3 %collective-permute-start.16 = (bf16[128,1536]{1,0:T(8,128)(2,1)S(1)}, bf16[128,1536]{1,0:T(8,128)(2,1)S(1)}, u32[]{:S(2)}, u32[]{:S(2)}) collective-permute-start(bf16[128,1536]{1,0:T(8,128)(2,1)S(1)} %get-tuple-element.180), channel_id=1, source_target_pairs={{0,16},{4,20},{8,24},{12,28},{16,0},{20,4},{24,8},{28,12},{1,17},{... | collective-permute-start | bytes 1179656 | tf_op jit(solution)/shard_map/ppermute | solution.py:292
  112.8 18.9 %collective-permute-start.17 = (bf16[128,1536]{1,0:T(8,128)(2,1)S(1)}, bf16[128,1536]{1,0:T(8,128)(2,1)S(1)}, u32[]{:S(2)}, u32[]{:S(2)}) collective-permute-start(bf16[128,1536]{1,0:T(8,128)(2,1)S(1)} %get-tuple-element.181), channel_id=1, source_target_pairs={{0,24},{4,28},{8,16},{12,20},{16,8},{20,12},{24,0},{28,4},{1,25},{... | collective-permute-start | bytes 1179656 | tf_op jit(solution)/shard_map/ppermute | solution.py:292
  135.5 13.2 %collective-permute-start.20 = (bf16[128,1536]{1,0:T(8,128)(2,1)}, bf16[128,1536]{1,0:T(8,128)(2,1)S(1)}, u32[]{:S(2)}, u32[]{:S(2)}) collective-permute-start(bf16[128,1536]{1,0:T(8,128)(2,1)} %get-tuple-element.183), channel_id=1, source_target_pairs={{0,24},{4,28},{8,16},{12,20},{16,8},{20,12},{24,0},{28,4},{1,25},{... | collective-permute-start | bytes 1179656 | tf_op jit(solution)/shard_map/ppermute | solution.py:292
  136.5 18.6 %collective-permute-start.19 = (bf16[128,1536]{1,0:T(8,128)(2,1)}, bf16[128,1536]{1,0:T(8,128)(2,1)S(1)}, u32[]{:S(2)}, u32[]{:S(2)}) collective-permute-start(bf16[128,1536]{1,0:T(8,128)(2,1)} %get-tuple-element.183), channel_id=1, source_target_pairs={{0,16},{4,20},{8,24},{12,28},{16,0},{20,4},{24,8},{28,12},{1,17},{... | collective-permute-start | bytes 1179656 | tf_op jit(solution)/shard_map/ppermute | solution.py:292
  137.3 17.8 %collective-permute-start.18 = (bf16[128,1536]{1,0:T(8,128)(2,1)}, bf16[128,1536]{1,0:T(8,128)(2,1)S(1)}, u32[]{:S(2)}, u32[]{:S(2)}) collective-permute-start(bf16[128,1536]{1,0:T(8,128)(2,1)} %get-tuple-element.183), channel_id=1, source_target_pairs={{0,8},{4,12},{8,0},{12,4},{16,24},{20,28},{24,16},{28,20},{1,9},{5... | collective-permute-start | bytes 1179656 | tf_op jit(solution)/shard_map/ppermute | solution.py:292
  140.5 15.1 %collective-permute-start.22 = (bf16[4,128,1536]{2,1,0:T(8,128)(2,1)S(1)}, bf16[4,128,1536]{2,1,0:T(8,128)(2,1)S(1)}, u32[]{:S(2)}, u32[]{:S(2)}) collective-permute-start(bf16[4,128,1536]{2,1,0:T(8,128)(2,1)S(1)} %pad_maximum_fusion.2.cot_near_ref), channel_id=1, source_target_pairs={{0,4},{4,0},{8,12},{12,8},{16,20},{20,16},{24,28},{28,24},{1,5},{5... | collective-permute-start | bytes 4718600 | tf_op jit(solution)/shard_map/ppermute | solution.py:297
  182.3 153.3 %reduce-scatter.5.cloned.1.call-start = ((), (), s32[]{:S(2)}) async-start(), calls=%async_computation.3 | async-start | bytes 3276800 | tf_op jit(solution)/shard_map/reduce_scatter | solution.py:1538
  188.7 19.3 %collective-permute-start.25 = (bf16[128,1536]{1,0:T(8,128)(2,1)S(1)}, bf16[128,1536]{1,0:T(8,128)(2,1)S(1)}, u32[]{:S(2)}, u32[]{:S(2)}) collective-permute-start(bf16[128,1536]{1,0:T(8,128)(2,1)S(1)} %get-tuple-element.192), channel_id=1, source_target_pairs={{0,16},{4,20},{8,24},{12,28},{16,0},{20,4},{24,8},{28,12},{1,17},{... | collective-permute-start | bytes 1179656 | tf_op jit(solution)/shard_map/ppermute | solution.py:292
  190.2 17.8 %collective-permute-start.26 = (bf16[128,1536]{1,0:T(8,128)(2,1)S(1)}, bf16[128,1536]{1,0:T(8,128)(2,1)S(1)}, u32[]{:S(2)}, u32[]{:S(2)}) collective-permute-start(bf16[128,1536]{1,0:T(8,128)(2,1)S(1)} %get-tuple-element.193), channel_id=1, source_target_pairs={{0,24},{4,28},{8,16},{12,20},{16,8},{20,12},{24,0},{28,4},{1,25},{... | collective-permute-start | bytes 1179656 | tf_op jit(solution)/shard_map/ppermute | solution.py:292
  217.7 19.8 %collective-permute-start.33 = (bf16[128,1536]{1,0:T(8,128)(2,1)S(1)}, bf16[128,1536]{1,0:T(8,128)(2,1)S(1)}, u32[]{:S(2)}, u32[]{:S(2)}) collective-permute-start(bf16[128,1536]{1,0:T(8,128)(2,1)S(1)} %copy-done.48), channel_id=1, source_target_pairs={{0,24},{4,28},{8,16},{12,20},{16,8},{20,12},{24,0},{28,4},{1,25},{... | collective-permute-start | bytes 1179656 | tf_op jit(solution)/shard_map/ppermute | solution.py:292
  219.6 19.3 %collective-permute-start.32 = (bf16[128,1536]{1,0:T(8,128)(2,1)S(1)}, bf16[128,1536]{1,0:T(8,128)(2,1)S(1)}, u32[]{:S(2)}, u32[]{:S(2)}) collective-permute-start(bf16[128,1536]{1,0:T(8,128)(2,1)S(1)} %copy-done.48), channel_id=1, source_target_pairs={{0,16},{4,20},{8,24},{12,28},{16,0},{20,4},{24,8},{28,12},{1,17},{... | collective-permute-start | bytes 1179656 | tf_op jit(solution)/shard_map/ppermute | solution.py:292
  239.2 19.1 %collective-permute-start.29 = (bf16[128,1536]{1,0:T(8,128)(2,1)S(1)}, bf16[128,1536]{1,0:T(8,128)(2,1)S(1)}, u32[]{:S(2)}, u32[]{:S(2)}) collective-permute-start(bf16[128,1536]{1,0:T(8,128)(2,1)S(1)} %get-tuple-element.207), channel_id=1, source_target_pairs={{0,8},{4,12},{8,0},{12,4},{16,24},{20,28},{24,16},{28,20},{1,9},{5... | collective-permute-start | bytes 1179656 | tf_op jit(solution)/shard_map/ppermute | solution.py:292
  239.8 19.6 %collective-permute-start.30 = (bf16[128,1536]{1,0:T(8,128)(2,1)S(1)}, bf16[128,1536]{1,0:T(8,128)(2,1)S(1)}, u32[]{:S(2)}, u32[]{:S(2)}) collective-permute-start(bf16[128,1536]{1,0:T(8,128)(2,1)S(1)} %get-tuple-element.208), channel_id=1, source_target_pairs={{0,16},{4,20},{8,24},{12,28},{16,0},{20,4},{24,8},{28,12},{1,17},{... | collective-permute-start | bytes 1179656 | tf_op jit(solution)/shard_map/ppermute | solution.py:292
  240.9 18.6 %collective-permute-start.31 = (bf16[128,1536]{1,0:T(8,128)(2,1)S(1)}, bf16[128,1536]{1,0:T(8,128)(2,1)S(1)}, u32[]{:S(2)}, u32[]{:S(2)}) collective-permute-start(bf16[128,1536]{1,0:T(8,128)(2,1)S(1)} %get-tuple-element.209), channel_id=1, source_target_pairs={{0,24},{4,28},{8,16},{12,20},{16,8},{20,12},{24,0},{28,4},{1,25},{... | collective-permute-start | bytes 1179656 | tf_op jit(solution)/shard_map/ppermute | solution.py:292
  261.0 13.9 %collective-permute-start.36 = (bf16[2,256,256]{2,1,0:T(8,128)(2,1)S(1)}, bf16[2,256,256]{2,1,0:T(8,128)(2,1)S(1)}, u32[]{:S(2)}, u32[]{:S(2)}) collective-permute-start(bf16[2,256,256]{2,1,0:T(8,128)(2,1)S(1)} %get-tuple-element.233), channel_id=1, source_target_pairs={{0,16},{4,20},{8,24},{12,28},{16,0},{20,4},{24,8},{28,12},{1,17},{... | collective-permute-start | bytes 786440 | tf_op jit(solution)/shard_map/ppermute | solution.py:292
  261.5 13.4 %collective-permute-start.37 = (bf16[2,256,256]{2,1,0:T(8,128)(2,1)S(1)}, bf16[2,256,256]{2,1,0:T(8,128)(2,1)S(1)}, u32[]{:S(2)}, u32[]{:S(2)}) collective-permute-start(bf16[2,256,256]{2,1,0:T(8,128)(2,1)S(1)} %get-tuple-element.234), channel_id=1, source_target_pairs={{0,24},{4,28},{8,16},{12,20},{16,8},{20,12},{24,0},{28,4},{1,25},{... | collective-permute-start | bytes 786440 | tf_op jit(solution)/shard_map/ppermute | solution.py:292
  296.2 26.1 %collective-permute-start.51 = (bf16[432,384]{1,0:T(8,128)(2,1)S(1)}, bf16[432,384]{1,0:T(8,128)(2,1)S(1)}, u32[]{:S(2)}, u32[]{:S(2)}) collective-permute-start(bf16[432,384]{1,0:T(8,128)(2,1)S(1)} %get-tuple-element.282), channel_id=1, source_target_pairs={{0,16},{4,20},{8,24},{12,28},{16,0},{20,4},{24,8},{28,12},{1,17},{... | collective-permute-start | bytes 995336 | tf_op jit(solution)/shard_map/ppermute | solution.py:292
  297.3 25.0 %collective-permute-start.52 = (bf16[432,384]{1,0:T(8,128)(2,1)S(1)}, bf16[432,384]{1,0:T(8,128)(2,1)S(1)}, u32[]{:S(2)}, u32[]{:S(2)}) collective-permute-start(bf16[432,384]{1,0:T(8,128)(2,1)S(1)} %get-tuple-element.281), channel_id=1, source_target_pairs={{0,24},{4,28},{8,16},{12,20},{16,8},{20,12},{24,0},{28,4},{1,25},{... | collective-permute-start | bytes 995336 | tf_op jit(solution)/shard_map/ppermute | solution.py:292
  307.9 19.5 %collective-permute-start.44 = (bf16[128,1536]{1,0:T(8,128)(2,1)}, bf16[128,1536]{1,0:T(8,128)(2,1)S(1)}, u32[]{:S(2)}, u32[]{:S(2)}) collective-permute-start(bf16[128,1536]{1,0:T(8,128)(2,1)} %get-tuple-element.264), channel_id=1, source_target_pairs={{0,24},{4,28},{8,16},{12,20},{16,8},{20,12},{24,0},{28,4},{1,25},{... | collective-permute-start | bytes 1179656 | tf_op jit(solution)/shard_map/ppermute | solution.py:292
  313.5 16.0 %collective-permute-start.43 = (bf16[128,1536]{1,0:T(8,128)(2,1)}, bf16[128,1536]{1,0:T(8,128)(2,1)S(1)}, u32[]{:S(2)}, u32[]{:S(2)}) collective-permute-start(bf16[128,1536]{1,0:T(8,128)(2,1)} %get-tuple-element.263), channel_id=1, source_target_pairs={{0,16},{4,20},{8,24},{12,28},{16,0},{20,4},{24,8},{28,12},{1,17},{... | collective-permute-start | bytes 1179656 | tf_op jit(solution)/shard_map/ppermute | solution.py:292
  314.3 15.1 %collective-permute-start.42 = (bf16[128,1536]{1,0:T(8,128)(2,1)S(1)}, bf16[128,1536]{1,0:T(8,128)(2,1)S(1)}, u32[]{:S(2)}, u32[]{:S(2)}) collective-permute-start(bf16[128,1536]{1,0:T(8,128)(2,1)S(1)} %get-tuple-element.262), channel_id=1, source_target_pairs={{0,8},{4,12},{8,0},{12,4},{16,24},{20,28},{24,16},{28,20},{1,9},{5... | collective-permute-start | bytes 1179656 | tf_op jit(solution)/shard_map/ppermute | solution.py:292
  (84 other events, 632.8 us)
Sparse Core Ops, SparseCore 0:
  10.2 49.0 all-gather.4
  60.8 99.4 all-gather.6
  182.4 95.0 reduce-scatter.2
  279.8 55.7 reduce-scatter.4
